TPU v7x, 32 devices: a whole 2x2x4 slice. The times are simulated.
32 devices in a mesh: section: 2 (over x), dp: 4 (over y, core), rep: 4 (over z).
Axes of the slice: x: 2, y: 2, z: 4, core: 2. Of those that a mesh axis runs over, the one named last changes fastest.
Arguments:
- query_input: bfloat16 [64, 256, 768], P(('dp', 'rep')), may hold values from -6 to 6
- key_input: bfloat16 [64, 256, 768], P(('dp', 'rep')), may hold values from -6 to 6
- query_lengths: int32 [64], P(('dp', 'rep')), may hold values from 64 to 256, as said below
- key_lengths: int32 [64], P(('dp', 'rep')), may hold values from 64 to 256, as said below
- cotangent: bfloat16 [64, 256, 768], P(('dp', 'rep')), may hold values from -8 to 8
- w_qkv: bfloat16 [2, 2, 768, 2304], P('section'), may hold values from -0.21875 to 0.21875
- w_out: bfloat16 [2, 2, 768, 768], P('section'), may hold values from -1.25 to 1.25
- w_up: bfloat16 [2, 2, 768, 3072], P('section'), may hold values from -0.21875 to 0.21875
- w_down: bfloat16 [2, 2, 3072, 768], P('section'), may hold values from -0.109375 to 0.109375
- b_up: float32 [2, 2, 3072], P('section'), may hold values from -1.5 to 1.5
- biases: float32 [2, 2, 6, 768], P('section'), may hold values from -1.5 to 1.5
- gains: float32 [2, 2, 2, 768], P('section'), may hold values from 0.25 to 1.75
Outputs:
- pooled_query: float32 [2, 64, 768], P('section')
- pooled_key: float32 [2, 64, 768], P('section')
- input_grad: float32 [2, 64, 256, 768], P('section', ('dp', 'rep'))
- grad_qkv: float32 [2, 768, 2304], P('section')
- grad_out: float32 [2, 768, 768], P('section')
- grad_up: float32 [2, 768, 3072], P('section')
- grad_down: float32 [2, 3072, 768], P('section')
- grad_b_up: float32 [2, 3072], P('section')
- grad_biases: float32 [2, 6, 768], P('section')
- grad_gains: float32 [2, 2, 768], P('section')
Inputs may be any that keep to these rules, and one draw needn't show every extreme that they name: `query_lengths`: positions before a crop's length are tokens, the rest padding; in every draw some crop has length 256 and some crop has length 64. `key_lengths`: as for query_lengths, drawn independently.
All inputs are finite; a program needn't handle non-finite values.
Results may differ from a plain program's by a relative error of at most 0.018.
Values may be sent and summed in bfloat16 or wider, within the bound.
No kernel may reach another device: no remote copies, remote signals or barrier semaphores. Data moves between devices by JAX's collectives and lax.ppermute only.
A program may use at most 384 MiB of HBM per device.

v0:
```python
import jax
import jax.numpy as jnp
from jax import lax
from jax.sharding import PartitionSpec as P

HEAD = 64
MICRO = 2


EPS = 1e-06
NEG = -1000000000.0


def shifted_2(value, axis, steps):
    count = lax.axis_size(axis)
    initial, last = (max(0, -steps), min(count, count - steps))
    return lax.ppermute(value, axis, [(source, source + steps) for source in range(initial, last)])


def crop_mask(lengths, crop_len):
    return lax.broadcasted_iota(jnp.int32, (lengths.shape[0], crop_len), 1) < lengths[:, None]


def layer_norm(hidden, norm_gain, norm_shift):
    centred = hidden - jnp.mean(hidden, -1, keepdims=True)
    inverse = lax.rsqrt(jnp.mean(centred * centred, -1, keepdims=True) + EPS)
    normed = centred * inverse
    return (normed * norm_gain + norm_shift, normed, inverse)


def norm_back(incoming, normed, inverse, norm_gain):
    scaled_grad = incoming * norm_gain
    pre_grad = (
        scaled_grad
        - jnp.mean(scaled_grad, -1, keepdims=True)
        - normed * jnp.mean(scaled_grad * normed, -1, keepdims=True)
    ) * inverse
    return (pre_grad, jnp.sum(incoming * normed, (0, 1)), jnp.sum(incoming, (0, 1)))


def exact_gelu(values):
    return jax.nn.gelu(values, approximate=False)


def forward_block(inputs, lengths, weights):
    w_qkv, w_out, w_up, w_down, b_up, biases, gains = weights
    crop_count, crop_len, model_width = inputs.shape
    head_count = model_width // HEAD
    heads_shape = (crop_count, crop_len, head_count, HEAD)
    key_mask = crop_mask(lengths, crop_len)
    projected = jnp.einsum("cld,de->cle", inputs, w_qkv, preferred_element_type=jnp.float32)
    query_heads = (
        (projected[..., :model_width] + biases[0]).astype(jnp.bfloat16).reshape(heads_shape)
    )
    key_heads = (
        projected[..., model_width : 2 * model_width].astype(jnp.bfloat16).reshape(heads_shape)
    )
    value_heads = (
        (projected[..., 2 * model_width :] + biases[1]).astype(jnp.bfloat16).reshape(heads_shape)
    )
    scores = jnp.einsum(
        "cqhe,ckhe->chqk", query_heads, key_heads, preferred_element_type=jnp.float32
    ) * HEAD ** (-0.5)
    scores = jnp.where(key_mask[:, None, None, :], scores, NEG)
    row_max = jnp.max(scores, -1, keepdims=True)
    shifted = jnp.exp(scores - row_max)
    attention = shifted / jnp.sum(shifted, -1, keepdims=True)
    mixture = (
        jnp.einsum(
            "chqk,ckhe->cqhe",
            attention.astype(jnp.bfloat16),
            value_heads,
            preferred_element_type=jnp.float32,
        )
        .astype(jnp.bfloat16)
        .reshape(crop_count, crop_len, model_width)
    )
    attended = (
        jnp.einsum("cld,de->cle", mixture, w_out, preferred_element_type=jnp.float32) + biases[2]
    )
    after_attn, normed_one, inverse_one = layer_norm(
        inputs.astype(jnp.float32) + attended, gains[0], biases[3]
    )
    attn_low = after_attn.astype(jnp.bfloat16)
    pre_active = (
        jnp.einsum("cld,df->clf", attn_low, w_up, preferred_element_type=jnp.float32) + b_up
    )
    active = exact_gelu(pre_active).astype(jnp.bfloat16)
    branch = (
        jnp.einsum("clf,fd->cld", active, w_down, preferred_element_type=jnp.float32) + biases[4]
    )
    block_out, normed_two, inverse_two = layer_norm(after_attn + branch, gains[1], biases[5])
    saved = (
        query_heads,
        key_heads,
        value_heads,
        attention,
        mixture,
        normed_one,
        inverse_one,
        attn_low,
        pre_active,
        active,
        normed_two,
        inverse_two,
    )
    return (block_out, saved)


def backward_block(inputs, lengths, out_grad, weights):
    w_qkv, w_out, w_up, w_down, b_up, biases, gains = weights
    crop_count, crop_len, model_width = inputs.shape
    head_count = model_width // HEAD
    heads_shape = (crop_count, crop_len, head_count, HEAD)
    flat_shape = (crop_count, crop_len, model_width)
    scale = HEAD ** (-0.5)
    unused_out, saved = forward_block(inputs, lengths, weights)
    (
        query_heads,
        key_heads,
        value_heads,
        attention,
        mixture,
        normed_one,
        inverse_one,
        attn_low,
        pre_active,
        active,
        normed_two,
        inverse_two,
    ) = saved
    sum_two, gain_two, shift_two = norm_back(out_grad, normed_two, inverse_two, gains[1])
    branch_grad = sum_two.astype(jnp.bfloat16)
    grad_down = jnp.einsum("clf,cld->fd", active, branch_grad, preferred_element_type=jnp.float32)
    bias_down = jnp.sum(branch_grad.astype(jnp.float32), (0, 1))
    active_grad = jnp.einsum("cld,fd->clf", branch_grad, w_down, preferred_element_type=jnp.float32)
    gelu_back = jax.vjp(exact_gelu, pre_active)[1]
    upper_grad = gelu_back(active_grad)[0].astype(jnp.bfloat16)
    grad_up = jnp.einsum("cld,clf->df", attn_low, upper_grad, preferred_element_type=jnp.float32)
    bias_up = jnp.sum(upper_grad.astype(jnp.float32), (0, 1))
    attn_side = sum_two + jnp.einsum(
        "clf,df->cld", upper_grad, w_up, preferred_element_type=jnp.float32
    )
    sum_one, gain_one, shift_one = norm_back(attn_side, normed_one, inverse_one, gains[0])
    attn_grad = sum_one.astype(jnp.bfloat16)
    grad_out = jnp.einsum("cld,cle->de", mixture, attn_grad, preferred_element_type=jnp.float32)
    bias_out = jnp.sum(attn_grad.astype(jnp.float32), (0, 1))
    mixture_grad = (
        jnp.einsum("cle,de->cld", attn_grad, w_out, preferred_element_type=jnp.float32)
        .astype(jnp.bfloat16)
        .reshape(heads_shape)
    )
    attention_grad = jnp.einsum(
        "cqhe,ckhe->chqk", mixture_grad, value_heads, preferred_element_type=jnp.float32
    )
    value_grad = jnp.einsum(
        "chqk,cqhe->ckhe",
        attention.astype(jnp.bfloat16),
        mixture_grad,
        preferred_element_type=jnp.float32,
    ).astype(jnp.bfloat16)
    score_grad = (
        attention * (attention_grad - jnp.sum(attention * attention_grad, -1, keepdims=True))
    ).astype(jnp.bfloat16)
    query_grad = (
        jnp.einsum("chqk,ckhe->cqhe", score_grad, key_heads, preferred_element_type=jnp.float32)
        * scale
    ).astype(jnp.bfloat16)
    key_grad = (
        jnp.einsum("chqk,cqhe->ckhe", score_grad, query_heads, preferred_element_type=jnp.float32)
        * scale
    ).astype(jnp.bfloat16)
    qkv_grad = jnp.concatenate(
        [
            query_grad.reshape(flat_shape),
            key_grad.reshape(flat_shape),
            value_grad.reshape(flat_shape),
        ],
        -1,
    )
    grad_qkv = jnp.einsum("cld,cle->de", inputs, qkv_grad, preferred_element_type=jnp.float32)
    input_grad = sum_one + jnp.einsum(
        "cle,de->cld", qkv_grad, w_qkv, preferred_element_type=jnp.float32
    )
    bias_query = jnp.sum(query_grad.astype(jnp.float32), (0, 1)).reshape(model_width)
    bias_value = jnp.sum(value_grad.astype(jnp.float32), (0, 1)).reshape(model_width)
    bias_rows = jnp.stack([bias_query, bias_value, bias_out, shift_one, bias_down, shift_two])
    gain_rows = jnp.stack([gain_one, gain_two])
    return (input_grad, (grad_qkv, grad_out, grad_up, grad_down, bias_up, bias_rows, gain_rows))


def on_device(
    query_input,
    key_input,
    query_lengths,
    key_lengths,
    cotangent,
    w_qkv,
    w_out,
    w_up,
    w_down,
    b_up,
    biases,
    gains,
):
    section_index = lax.axis_index("section")
    at_first = section_index == 0
    micro_count = MICRO
    per_micro = query_input.shape[0] // micro_count
    crop_len = query_input.shape[1]
    model_width = query_input.shape[2]

    def encoder(member):
        return (
            w_qkv[0, member],
            w_out[0, member],
            w_up[0, member],
            w_down[0, member],
            b_up[0, member],
            biases[0, member],
            gains[0, member],
        )

    query_weights = encoder(0)
    key_weights = encoder(1)

    def micro_part(source, micro_slot):
        return lax.dynamic_slice_in_dim(source, micro_slot * per_micro, per_micro, 0)

    def pooled_of(block_out, lengths):
        weights_mask = crop_mask(lengths, crop_len).astype(jnp.float32)
        return (
            jnp.sum(block_out * weights_mask[..., None], 1) / lengths.astype(jnp.float32)[:, None]
        )

    act_shape = (per_micro, crop_len, model_width)
    arrived_query = jnp.zeros(act_shape, jnp.bfloat16)
    arrived_key = jnp.zeros(act_shape, jnp.bfloat16)
    pool_query = jnp.zeros((query_input.shape[0], model_width), jnp.float32)
    pool_key = jnp.zeros((query_input.shape[0], model_width), jnp.float32)
    kept_inputs = []
    for clock in range(micro_count + 1):
        micro_index = clock - section_index
        is_live = (micro_index >= 0) & (micro_index < micro_count)
        micro_slot = jnp.clip(micro_index, 0, micro_count - 1)
        own_query = jnp.where(at_first, micro_part(query_input, micro_slot), arrived_query)
        own_key = jnp.where(at_first, micro_part(key_input, micro_slot), arrived_key)
        query_len = micro_part(query_lengths, micro_slot)
        key_len = micro_part(key_lengths, micro_slot)
        kept_inputs.append(own_query)

        def compute(operands):
            return (
                forward_block(operands[0], query_len, query_weights)[0],
                forward_block(operands[1], key_len, key_weights)[0],
            )

        def nothing(operands):
            return (jnp.zeros(act_shape, jnp.float32), jnp.zeros(act_shape, jnp.float32))

        out_query, out_key = lax.cond(is_live, compute, nothing, (own_query, own_key))
        pool_query = jnp.where(
            is_live,
            lax.dynamic_update_slice_in_dim(
                pool_query, pooled_of(out_query, query_len), micro_slot * per_micro, 0
            ),
            pool_query,
        )
        pool_key = jnp.where(
            is_live,
            lax.dynamic_update_slice_in_dim(
                pool_key, pooled_of(out_key, key_len), micro_slot * per_micro, 0
            ),
            pool_key,
        )
        if clock < micro_count:
            arrived_query, arrived_key = shifted_2(
                (out_query.astype(jnp.bfloat16), out_key.astype(jnp.bfloat16)), "section", 1
            )
    inputs_stack = jnp.stack(kept_inputs)
    returned = jnp.zeros(act_shape, jnp.bfloat16)
    input_grads = jnp.zeros(query_input.shape, jnp.float32)
    totals = None
    for clock in range(micro_count + 1):
        micro_index = clock - 1 + section_index
        is_live = (micro_index >= 0) & (micro_index < micro_count)
        micro_slot = jnp.clip(micro_index, 0, micro_count - 1)
        source_clock = jnp.clip(clock - 1 + 2 * section_index, 0, micro_count)
        own_input = lax.dynamic_index_in_dim(inputs_stack, source_clock, 0, keepdims=False)
        query_len = micro_part(query_lengths, micro_slot)
        weights_mask = crop_mask(query_len, crop_len).astype(jnp.float32)
        out_grad = jnp.where(
            at_first,
            returned.astype(jnp.float32),
            micro_part(cotangent, micro_slot).astype(jnp.float32) * weights_mask[..., None],
        )

        def compute_back(operands):
            return backward_block(operands[0], query_len, operands[1], query_weights)

        def nothing_back(operands):
            return (
                jnp.zeros(act_shape, jnp.float32),
                tuple((jnp.zeros(weight.shape, jnp.float32) for weight in query_weights)),
            )

        grad_input, grads = lax.cond(is_live, compute_back, nothing_back, (own_input, out_grad))
        sent_grad = grad_input.astype(jnp.bfloat16)
        stored = jnp.where(at_first, grad_input, sent_grad.astype(jnp.float32))
        input_grads = jnp.where(
            is_live,
            lax.dynamic_update_slice_in_dim(input_grads, stored, micro_slot * per_micro, 0),
            input_grads,
        )
        flattened = tuple((grad_part.reshape(-1) for grad_part in grads))
        totals = (
            flattened
            if totals is None
            else tuple((older + newer for older, newer in zip(totals, flattened)))
        )
        if clock < micro_count:
            returned = shifted_2(sent_grad, "section", -1)
    summed = (
        lax.psum_scatter(totals[0], ("dp", "rep"), scatter_dimension=0, tiled=True),
        lax.psum_scatter(totals[1], ("dp", "rep"), scatter_dimension=0, tiled=True),
        lax.psum_scatter(totals[2], ("dp", "rep"), scatter_dimension=0, tiled=True),
        lax.psum_scatter(totals[3], ("dp", "rep"), scatter_dimension=0, tiled=True),
        lax.psum_scatter(totals[4], ("dp", "rep"), scatter_dimension=0, tiled=True),
        lax.psum_scatter(totals[5], ("dp", "rep"), scatter_dimension=0, tiled=True),
        lax.psum_scatter(totals[6], ("dp", "rep"), scatter_dimension=0, tiled=True),
    )
    gathered = (
        lax.all_gather(summed[0].astype(jnp.bfloat16), ("dp", "rep"), axis=0, tiled=True).astype(
            jnp.float32
        ),
        lax.all_gather(summed[1].astype(jnp.bfloat16), ("dp", "rep"), axis=0, tiled=True).astype(
            jnp.float32
        ),
        lax.all_gather(summed[2].astype(jnp.bfloat16), ("dp", "rep"), axis=0, tiled=True).astype(
            jnp.float32
        ),
        lax.all_gather(summed[3].astype(jnp.bfloat16), ("dp", "rep"), axis=0, tiled=True).astype(
            jnp.float32
        ),
        lax.all_gather(summed[4].astype(jnp.bfloat16), ("dp", "rep"), axis=0, tiled=True).astype(
            jnp.float32
        ),
        lax.all_gather(summed[5].astype(jnp.bfloat16), ("dp", "rep"), axis=0, tiled=True).astype(
            jnp.float32
        ),
        lax.all_gather(summed[6].astype(jnp.bfloat16), ("dp", "rep"), axis=0, tiled=True).astype(
            jnp.float32
        ),
    )
    grad_list = [gathered[number].reshape(query_weights[number].shape)[None] for number in range(7)]
    pooled_all = (
        lax.all_gather(pool_query, ("dp", "rep"), axis=0, tiled=True),
        lax.all_gather(pool_key, ("dp", "rep"), axis=0, tiled=True),
    )
    return (
        pooled_all[0][None],
        pooled_all[1][None],
        input_grads[None],
        grad_list[0],
        grad_list[1],
        grad_list[2],
        grad_list[3],
        grad_list[4],
        grad_list[5],
        grad_list[6],
    )


def solution(mesh):
    placed = (
        P(("dp", "rep"), None, None),
        P(("dp", "rep"), None, None),
        P(("dp", "rep")),
        P(("dp", "rep")),
        P(("dp", "rep"), None, None),
        P("section", None, None, None),
        P("section", None, None, None),
        P("section", None, None, None),
        P("section", None, None, None),
        P("section", None, None),
        P("section", None, None, None),
        P("section", None, None, None),
    )
    return jax.shard_map(
        on_device,
        mesh=mesh,
        in_specs=placed,
        out_specs=(
            P("section", None, None),
            P("section", None, None),
            P("section", ("dp", "rep"), None, None),
            P("section", None, None),
            P("section", None, None),
            P("section", None, None),
            P("section", None, None),
            P("section", None),
            P("section", None, None),
            P("section", None, None),
        ),
        check_vma=False,
    )
```

profile of v0, /device:TPU:3, one launch (start us, length us, event | category | flops | bytes accessed | tf_op | source)
XLA Modules:
  0.0 2265.8 jit_solution(52028763051105207)
XLA Ops:
  7.3 7.3 slice_bitcast_fusion.4
  17.2 4.4 slice_bitcast_fusion.1
  21.7 8.1 slice_bitcast_fusion
  32.2 9.6 conditional.6
  47.1 92.7 %collective-permute-done = bf16[2,256,768]{2,1,0:T(8,128)(2,1)S(1)} collective-permute-done((bf16[2,256,768]{2,1,0:T(8,128)(2,1)}, bf16[2,256,768]{2,1,0:T(8,128)(2,1)S(1)}, u32[]{:S(2)}, u32[]{:S(2)}) %collective-permute-start) | collective-permute-done | bytes 786464 | tf_op jit(solution)/shard_map/ppermute | solution.py:17
  141.8 14.8 collective-permute-done.1
  156.6 87.2 %conditional.7 = (f32[2,256,768]{2,1,0:T(8,128)S(1)}, f32[2,256,768]{2,1,0:T(8,128)S(1)}) conditional(s32[]{:T(128)} %convert_element_type.683, () %tuple.114, (bf16[2,256,768]{2,1,0:T(8,128)(2,1)}, bf16[768,2304]{1,0:T(8,128)(2,1)}, f32[6,768]{1,0:T(8,128)S(1)}, s32[2]{0:T(128)S(1)}, bf16[768,768]{1,0:T(8,128)(2,1)}, ...), branch_computations={%region_15.16_spmd, %region_16.29_spmd} | conditional | flops 15609105408 | bytes 297663040 | solution.py:261
  156.7 4.5 fusion.245
  166.1 5.0 fusion.862
  177.2 4.5 fusion.325
  181.8 17.1 fusion.864
  209.8 6.2 fusion.865
  221.3 5.0 fusion.326
  226.3 16.9 fusion.867
  253.1 13.6 collective-permute-done.2
  271.5 154.2 %conditional.9 = (f32[2,256,768]{2,1,0:T(8,128)}, f32[3072]{0:T(1024)}, bf16[2,256,768]{2,1,0:T(8,128)(2,1)S(1)}, f32[1769472]{0:T(1024)}, f32[589824]{0:T(1024)...) conditional(s32[]{:T(128)} %convert_element_type.699, ...), branch_computations={%region_48.49_spmd, %region_49.70_spmd} | conditional | flops 23187146752 | bytes 455264832 | solution.py:307
  287.8 7.0 fusion.874
  300.1 4.5 fusion.671
  304.7 15.0 multiply_convert_fusion.1
  325.8 9.1 convert_reduce_fusion
  334.9 7.4 multiply_reduce_fusion.14
  346.3 5.7 convert_reduce_fusion.3
  371.2 7.5 fusion.839
  378.7 6.4 convolution_bitcast_fusion
  385.1 8.0 reshape.1037
  396.5 5.3 convolution_bitcast_fusion.2
  401.9 6.0 copy.303
  407.8 5.1 convolution_bitcast_fusion.1
  413.0 10.8 reshape.1040
  428.3 14.3 collective-permute-done.4
  442.7 148.5 %conditional.10 = (f32[2,256,768]{2,1,0:T(8,128)}, f32[3072]{0:T(1024)}, bf16[2,256,768]{2,1,0:T(8,128)(2,1)}, f32[1769472]{0:T(1024)}, f32[589824]{0:T(1024)}, ...) conditional(s32[]{:T(128)} %convert_element_type.702, ...), branch_computations={%region_70.71_spmd, %region_71.92_spmd} | conditional | flops 23187146752 | bytes 439552704 | solution.py:307
  457.2 5.6 fusion.877
  469.4 4.5 fusion.737
  474.0 14.8 multiply_convert_fusion.5
  494.7 9.1 convert_reduce_fusion.5
  503.9 7.4 multiply_reduce_fusion.23
  514.4 4.6 convert_reduce_fusion.8
  536.9 7.5 fusion.843
  544.4 6.5 convolution_bitcast_fusion.4
  550.9 8.0 reshape.1058
  562.4 5.3 convolution_bitcast_fusion.6
  567.8 5.9 copy.304
  573.6 5.2 convolution_bitcast_fusion.5
  578.8 10.8 reshape.1061
  598.6 11.6 collective-permute-done.5
  610.4 19.6 conditional.11
  630.0 10.7 add_add_fusion.20
  644.1 13.6 add_add_fusion.19
  657.7 13.6 add_add_fusion.18
  673.6 1168.2 %all-reduce.13 = (bf16[1769472]{0:T(1024)(128)(2,1)}, bf16[589824]{0:T(1024)(128)(2,1)}, bf16[2359296]{0:T(1024)(128)(2,1)}, bf16[2359296]{0:T(1024)(128)(2,1)},...) all-reduce(f32[1769472]{0:T(1024)} %add_add_fusion.20, ...), channel_id=2, replica_groups=mesh['section'=2,'dp'=4,'rep'=4] {'dp','rep'}, use_global_device_ids=true, to_apply=%region_114.115.clone | all-reduce | flops 7087104 | bytes 42522624
  1858.9 145.9 %collective-permute-done.3 = bf16[2,256,768]{2,1,0:T(8,128)(2,1)S(1)} collective-permute-done((bf16[2,256,768]{2,1,0:T(8,128)(2,1)S(1)}, bf16[2,256,768]{2,1,0:T(8,128)(2,1)S(1)}, u32[]{:S(2)}, u32[]{:S(2)}) %collective-permute-start.3) | collective-permute-done | bytes 786464 | tf_op jit(solution)/shard_map/ppermute | solution.py:17
  2004.8 87.5 %conditional.8 = (f32[2,256,768]{2,1,0:T(8,128)S(1)}, f32[2,256,768]{2,1,0:T(8,128)S(1)}) conditional(s32[]{:T(128)} %convert_element_type.688, () %tuple.116, (bf16[2,256,768]{2,1,0:T(8,128)(2,1)}, bf16[768,2304]{1,0:T(8,128)(2,1)}, f32[6,768]{1,0:T(8,128)S(1)}, s32[2]{0:T(128)S(1)}, bf16[768,768]{1,0:T(8,128)(2,1)}, ...), branch_computations={%region_30.31_spmd, %region_31.44_spmd} | conditional | flops 15609105408 | bytes 300808832 | solution.py:261
  2015.3 5.0 fusion.868
  2025.3 4.5 fusion.538
  2029.9 17.1 fusion.870
  2057.9 6.2 fusion.871
  2069.5 5.0 fusion.539
  2074.5 16.9 fusion.873
  2092.6 30.7 %all-gather = f32[16,4,768]{2,1,0:T(4,128)S(1)} all-gather(f32[1,4,768]{2,1,0:T(4,128)S(1)} %bitcast_dynamic-update-slice_fusion.2), channel_id=1, replica_groups=mesh['section'=2,'dp'=4,'rep'=4] {'dp','rep'}, dimensions={0}, use_global_device_ids=true | all-gather | bytes 208896 | tf_op jit(solution)/shard_map/all_gather | solution.py:357
  2125.1 31.4 %all-gather.1 = f32[16,4,768]{2,1,0:T(4,128)S(1)} all-gather(f32[1,4,768]{2,1,0:T(4,128)S(1)} %bitcast_dynamic-update-slice_fusion.1), channel_id=1, replica_groups=mesh['section'=2,'dp'=4,'rep'=4] {'dp','rep'}, dimensions={0}, use_global_device_ids=true | all-gather | bytes 208896 | tf_op jit(solution)/shard_map/all_gather | solution.py:358
  2165.6 58.3 %all-reduce.11 = (bf16[3072]{0:T(1024)(128)(2,1)S(1)}, bf16[4608]{0:T(1024)(128)(2,1)S(1)}, bf16[1536]{0:T(1024)(128)(2,1)S(1)}) all-reduce(bf16[3072]{0:T(1024)(128)(2,1)S(1)} %dynamic-update-slice.10, bf16[4608]{0:T(1024)(128)(2,1)S(1)} %dynamic-update-slice.11, ...), channel_id=1, replica_groups=mesh['section'=2,'dp'=4,'rep'=4] {'dp','rep'}, use_global_device_ids=true, to_apply=%add | all-reduce | flops 9216 | bytes 36864
  2232.4 7.9 reshape.1087
  2240.3 8.7 reshape.1089
  2249.1 10.0 reshape.1090
  (637 shorter events, 256.5 us)
Async XLA Ops:
  7.2 2221.9 %all-gather.9.cloned.1.call-start = ((), (), s32[]{:S(2)}) async-start(), calls=%async_computation.1 | async-start | bytes 1253376 | tf_op jit(solution)/shard_map/all_gather | solution.py:336
  17.2 139.4 %copy-start.100 = (f32[2,768]{1,0:T(2,128)}, f32[2,768]{1,0:T(2,128)S(1)}, u32[]{:S(2)}) copy-start(f32[2,768]{1,0:T(2,128)S(1)} %get-tuple-element.1005) | copy-start | bytes 18436
  21.6 135.0 %copy-start.93 = (f32[1,1,3072]{2,1,0:T(1,128)}, f32[1,1,3072]{2,1,0:T(1,128)S(1)}, u32[]{:S(2)}) copy-start(f32[1,1,3072]{2,1,0:T(1,128)S(1)} %get-tuple-element.1004) | copy-start | bytes 36868
  21.7 135.0 %copy-start.145 = (f32[1,1,3072]{2,1,0:T(1,128)}, f32[1,1,3072]{2,1,0:T(1,128)S(1)}, u32[]{:S(2)}) copy-start(f32[1,1,3072]{2,1,0:T(1,128)S(1)} %get-tuple-element.1003) | copy-start | bytes 36868
  31.2 125.4 %copy-start.88 = (f32[6,768]{1,0:T(8,128)}, f32[6,768]{1,0:T(8,128)S(1)}, u32[]{:S(2)}) copy-start(f32[6,768]{1,0:T(8,128)S(1)} %get-tuple-element.1032) | copy-start | bytes 55300
  31.2 125.4 %copy-start.91 = (f32[6,768]{1,0:T(8,128)}, f32[6,768]{1,0:T(8,128)S(1)}, u32[]{:S(2)}) copy-start(f32[6,768]{1,0:T(8,128)S(1)} %get-tuple-element.1031) | copy-start | bytes 55300
  41.8 114.8 %copy-start.167 = (s32[2]{0:T(128)S(1)}, s32[2]{0:T(128)}, u32[]{:S(2)}) copy-start(s32[2]{0:T(128)} %get-tuple-element.1021) | copy-start | bytes 28
  43.6 96.2 %collective-permute-start = (bf16[2,256,768]{2,1,0:T(8,128)(2,1)}, bf16[2,256,768]{2,1,0:T(8,128)(2,1)S(1)}, u32[]{:S(2)}, u32[]{:S(2)}) collective-permute-start(bf16[2,256,768]{2,1,0:T(8,128)(2,1)} %get-tuple-element.999), channel_id=1, source_target_pairs={{0,16},{1,17},{2,18},{3,19},{4,20},{5,21},{6,22},{7,23},{8,24},{9,... | collective-permute-start | bytes 2359304 | tf_op jit(solution)/shard_map/ppermute | solution.py:17
  45.7 110.9 %collective-permute-start.1 = (bf16[2,256,768]{2,1,0:T(8,128)(2,1)S(1)}, bf16[2,256,768]{2,1,0:T(8,128)(2,1)S(1)}, u32[]{:S(2)}, u32[]{:S(2)}) collective-permute-start(bf16[2,256,768]{2,1,0:T(8,128)(2,1)S(1)} %get-tuple-element.996), channel_id=1, source_target_pairs={{0,16},{1,17},{2,18},{3,19},{4,20},{5,21},{6,22},{7,23},{8,24},{9,... | collective-permute-start | bytes 2359304 | tf_op jit(solution)/shard_map/ppermute | solution.py:17
  156.6 91.9 %copy-start.192 = (s32[2]{0:T(128)S(1)}, s32[2]{0:T(128)}, u32[]{:S(2)}) copy-start(s32[2]{0:T(128)} %get-tuple-element.1029) | copy-start | bytes 28
  181.8 17.9 copy-start.195
  245.9 20.8 copy-start.8
  245.9 20.8 collective-permute-start.2
  253.1 18.0 copy-start.89
  271.7 27.0 %copy-start.1 = (bf16[3,2,256,768]{3,2,1,0:T(8,128)(2,1)}, bf16[3,2,256,768]{3,2,1,0:T(8,128)(2,1)S(1)}, u32[]{:S(2)}) copy-start(bf16[3,2,256,768]{3,2,1,0:T(8,128)(2,1)S(1)} %get-tuple-element.575) | copy-start | bytes 7077892 | tf_op jit(solution)/shard_map/cond
  299.7 42.6 %copy-start.4 = (f32[2,256,768]{2,1,0:T(8,128)}, f32[2,256,768]{2,1,0:T(8,128)S(1)}, u32[]{:S(2)}) copy-start(f32[2,256,768]{2,1,0:T(8,128)S(1)} %get-tuple-element.925) | copy-start | bytes 4718596 | tf_op jit(solution)/shard_map/cond
  299.7 42.6 %copy-start.113 = (f32[2,256]{1,0:T(2,128)}, f32[2,256]{1,0:T(2,128)S(1)}, u32[]{:S(2)}) copy-start(f32[2,256]{1,0:T(2,128)S(1)} %broadcast_multiply_fusion.16) | copy-start | bytes 6148 | tf_op jit(solution)/shard_map/cond
  299.7 20.0 slice-start.31
  300.0 19.7 copy-start.152
  300.1 19.6 slice-start.32
  304.6 15.1 copy-start.176
  412.9 11.0 copy-start.184
  412.9 11.0 copy-start.140
  412.9 11.0 copy-start.137
  412.9 11.7 copy-start.134
  412.9 11.7 copy-start.182
  413.0 12.3 copy-start.76
  425.7 16.9 collective-permute-start.4
  469.0 42.3 %copy-start.5 = (f32[2,256,768]{2,1,0:T(8,128)}, f32[2,256,768]{2,1,0:T(8,128)S(1)}, u32[]{:S(2)}) copy-start(f32[2,256,768]{2,1,0:T(8,128)S(1)} %get-tuple-element.946) | copy-start | bytes 4718596 | tf_op jit(solution)/shard_map/cond
  469.0 19.8 copy-start.114
  469.0 19.8 slice-start.33
  469.3 19.4 copy-start.154
  469.4 19.4 slice-start.34
  473.9 14.8 copy-start.178
  578.8 11.0 copy-start.141
  578.8 11.0 copy-start.138
  578.8 11.7 copy-start.135
  578.8 11.7 copy-start.183
  591.1 19.1 collective-permute-start.5
  673.6 1180.0 %copy-start.168 = (s32[2]{0:T(128)S(1)}, s32[2]{0:T(128)}, u32[]{:S(2)}) copy-start(s32[2]{0:T(128)} %get-tuple-element.1021) | copy-start | bytes 28
  673.6 1180.1 %copy-start.166 = (s32[2]{0:T(128)S(1)}, s32[2]{0:T(128)}, u32[]{:S(2)}) copy-start(s32[2]{0:T(128)} %get-tuple-element.1028) | copy-start | bytes 28
  673.6 1180.8 %copy-start.110 = (f32[2,768]{1,0:T(2,128)S(1)}, f32[2,768]{1,0:T(2,128)}, u32[]{:S(2)}) copy-start(f32[2,768]{1,0:T(2,128)} %get-tuple-element.1000) | copy-start | bytes 18436
  673.6 1180.8 %copy-start.187 = (f32[2]{0:T(128)S(1)}, f32[2]{0:T(128)}, u32[]{:S(2)}) copy-start(f32[2]{0:T(128)} %get-tuple-element.1023) | copy-start | bytes 28
  1841.8 16.1 copy-start.165
  1841.8 16.2 copy-start.109
  1841.8 16.2 copy-start.186
  1841.8 16.3 copy-start.111
  1841.8 16.3 copy-start.191
  1841.8 16.4 copy-start.190
  1841.8 163.0 %copy-start.90 = (f32[6,768]{1,0:T(8,128)S(1)}, f32[6,768]{1,0:T(8,128)}, u32[]{:S(2)}) copy-start(f32[6,768]{1,0:T(8,128)} %copy-done.88) | copy-start | bytes 55300
  1841.8 162.9 %copy-start.92 = (f32[6,768]{1,0:T(8,128)S(1)}, f32[6,768]{1,0:T(8,128)}, u32[]{:S(2)}) copy-start(f32[6,768]{1,0:T(8,128)} %copy-done.91) | copy-start | bytes 55300
  1841.8 162.9 %copy-start.94 = (f32[1,1,3072]{2,1,0:T(1,128)S(1)}, f32[1,1,3072]{2,1,0:T(1,128)}, u32[]{:S(2)}) copy-start(f32[1,1,3072]{2,1,0:T(1,128)} %copy-done.93) | copy-start | bytes 36868
  1841.8 162.9 %copy-start.101 = (f32[2,768]{1,0:T(2,128)S(1)}, f32[2,768]{1,0:T(2,128)}, u32[]{:S(2)}) copy-start(f32[2,768]{1,0:T(2,128)} %copy-done.100) | copy-start | bytes 18436
  1841.9 162.9 %copy-start.146 = (f32[1,1,3072]{2,1,0:T(1,128)S(1)}, f32[1,1,3072]{2,1,0:T(1,128)}, u32[]{:S(2)}) copy-start(f32[1,1,3072]{2,1,0:T(1,128)} %copy-done.145) | copy-start | bytes 36868
  1843.5 388.9 %all-gather.7.cloned.1.call-start = ((), (), s32[]{:S(2)}) async-start(), calls=%async_computation | async-start | bytes 3760128 | tf_op jit(solution)/shard_map/all_gather | solution.py:333
  1845.8 394.5 %all-gather.11.cloned.1.call-start = ((), (), s32[]{:S(2)}) async-start(), calls=%async_computation.2 | async-start | bytes 5013504 | tf_op jit(solution)/shard_map/all_gather | solution.py:339
  1848.2 400.9 %all-gather.13.cloned.1.call-start = ((), (), s32[]{:S(2)}) async-start(), calls=%async_computation.3 | async-start | bytes 5013504 | tf_op jit(solution)/shard_map/all_gather | solution.py:342
  1856.6 148.1 %collective-permute-start.3 = (bf16[2,256,768]{2,1,0:T(8,128)(2,1)S(1)}, bf16[2,256,768]{2,1,0:T(8,128)(2,1)S(1)}, u32[]{:S(2)}, u32[]{:S(2)}) collective-permute-start(bf16[2,256,768]{2,1,0:T(8,128)(2,1)S(1)} %get-tuple-element.994), channel_id=1, source_target_pairs={{0,16},{1,17},{2,18},{3,19},{4,20},{5,21},{6,22},{7,23},{8,24},{9,... | collective-permute-start | bytes 2359304 | tf_op jit(solution)/shard_map/ppermute | solution.py:17
  1858.3 146.5 %copy-start.99 = (f32[4,768]{1,0:T(4,128)}, f32[4,768]{1,0:T(4,128)S(1)}, u32[]{:S(2)}) copy-start(f32[4,768]{1,0:T(4,128)S(1)} %fusion.838) | copy-start | bytes 36868
  2004.8 87.5 %copy-start.150 = (f32[2,256]{1,0:T(2,128)S(1)}, f32[2,256]{1,0:T(2,128)}, u32[]{:S(2)}) copy-start(f32[2,256]{1,0:T(2,128)} %compare_convert_fusion.6) | copy-start | bytes 6148
  2004.8 87.7 %copy-start.189 = (f32[2]{0:T(128)S(1)}, f32[2]{0:T(128)}, u32[]{:S(2)}) copy-start(f32[2]{0:T(128)} %get-tuple-element.1027) | copy-start | bytes 28
  2004.8 119.5 %copy-start.102 = (f32[1,4,768]{2,1,0:T(4,128)S(1)}, f32[1,4,768]{2,1,0:T(4,128)}, u32[]{:S(2)}) copy-start(f32[1,4,768]{2,1,0:T(4,128)} %copy.325) | copy-start | bytes 36868
  2004.8 119.5 %copy-start.188 = (f32[2]{0:T(128)S(1)}, f32[2]{0:T(128)}, u32[]{:S(2)}) copy-start(f32[2]{0:T(128)} %get-tuple-element.836) | copy-start | bytes 28
  2029.9 17.9 copy-start.197
  (129 other events, 689.3 us)
Sparse Core Ops, SparseCore 0:
  1843.6 166.4 all-gather.8
  2012.4 46.0 all-gather.6
  2061.4 52.9 all-gather.10
  2116.5 53.0 all-gather.12
where the time goes:
time: 2280 us; the launch traced here: 2270 us
  blocking collectives  1290 us (57%)
  matrix products  303 us (13%)
  waiting for transfers between devices  293 us (13%)
  local copies, waits for them, and re-layouts  203 us (9%)
  other arithmetic  131 us (6%)
    unnamed x2, blocking collectives  1230 us
    ppermute x6, waiting for transfers between devices, shifted_2(): lax.ppermute(value, axis, [(source, source + steps) for source in range(i...  293 us
    dot_general x6, matrix products, forward_block(): jnp.einsum('clf,fd->cld', active, w_down, preferred_element_type=jnp.floa...  73.8 us
    reshape x16, local copies, waits for them, and re-layouts, on_device(): flattened = tuple((grad_part.reshape(-1) for grad_part in grads))  56.8 us
  transfers between devices with their start and end apart: 10, of which 6 were waited for; matrix products, arithmetic and copies ran while one was open for 6% of the time, Pallas kernels for 0%

commit v1 on v0

v1 whole, which is shorter than its diff:
```python
import functools
import math

import jax
import jax.numpy as jnp
from jax import lax
from jax.experimental import pallas as pl
from jax.experimental.pallas import tpu as pltpu
from jax.sharding import PartitionSpec as P

HEAD = 64
EPS = 1e-06
NEG = -1000000000.0
CHUNK = 256
VMEM_LIMIT = 60 * 1024 * 1024
NT = (((1,), (1,)), ((), ()))
TN = (((0,), (0,)), ((), ()))
F32 = jnp.float32
BF16 = jnp.bfloat16
ANY = pl.BlockSpec(memory_space=pl.ANY)
SMEM = pl.BlockSpec(memory_space=pltpu.SMEM)


def mm(left, right, dims=(((1,), (0,)), ((), ()))):
    return lax.dot_general(left, right, dims, preferred_element_type=F32)


def row_variants(crop_len):
    return [crop_len]


def gelu_pair(values):
    cdf = 0.5 + 0.5 * lax.erf(values * (2.0**-0.5))
    density = jnp.exp(-0.5 * values * values) * (2.0 * math.pi) ** -0.5
    return values * cdf, cdf + values * density


def norm_forward(hidden):
    centred = hidden - jnp.mean(hidden, -1, keepdims=True)
    inverse = lax.rsqrt(jnp.mean(centred * centred, -1, keepdims=True) + EPS)
    return centred * inverse, inverse


def norm_backward(scaled, normed, inverse):
    return (
        scaled
        - jnp.mean(scaled, -1, keepdims=True)
        - normed * jnp.mean(scaled * normed, -1, keepdims=True)
    ) * inverse


def dispatch(length, crop_len, body):
    lower = 0
    for rows in row_variants(crop_len):
        pl.when((length > lower) & (length <= rows))(functools.partial(body, rows))
        lower = rows


def save_shapes(crops, crop_len, width, hidden):
    heads = width // HEAD
    return {
        "xs": ((crops, crop_len, width), BF16),
        "qkv": ((crops, crop_len, 3 * width), BF16),
        "att": ((crops, heads, crop_len, crop_len), BF16),
        "mix": ((crops, crop_len, width), BF16),
        "n1": ((crops, crop_len, width), F32),
        "low": ((crops, crop_len, width), BF16),
        "act": ((crops, crop_len, hidden), BF16),
        "gp": ((crops, crop_len, hidden), BF16),
        "n2": ((crops, crop_len, width), F32),
        "inv": ((crops, crop_len, 128), F32),
    }


def forward_kernel(member, names, first, n_alias, info, own, *refs):
    recv, refs = (None, refs) if first else (refs[0], refs[1:])
    wqkv, wout, wup, wdown, bup, biases, gains = refs[:7]
    refs = refs[7 + n_alias :]
    y_ref, pool_ref = refs[:2]
    saved = dict(zip(names, refs[2 : 2 + len(names)]))
    (bx, bwqkv, bwout, bwup, bwdown, bqkv, batt, bmix, blow, bact, bgp, bn1, bn2, binv, by, wsem, xsem, osem) = refs[2 + len(names) :]
    crop_len, width = by.shape
    hidden = bact.shape[1]
    heads = width // HEAD
    live, crop, length, section = info[0], info[1], info[2], info[3]

    def weight_copy(number):
        source = (wqkv, wout, wup, wdown)[number]
        return pltpu.make_async_copy(source.at[0, member], (bwqkv, bwout, bwup, bwdown)[number], wsem.at[number])

    def out_copy(number, name, buffer):
        return pltpu.make_async_copy(buffer, saved[name].at[crop], osem.at[number])

    def body(rows):
        keys = -(-rows // 128) * 128
        started = []

        def finish(number, name, buffer):
            if rows < crop_len:
                if name == "att":
                    pass
                else:
                    buffer[rows:, :] = jnp.zeros((crop_len - rows, buffer.shape[1]), buffer.dtype)
            if name in saved:
                copy = out_copy(number, name, buffer)
                copy.start()
                started.append(copy)

        weight_copy(0).wait()
        weight_copy(1).start()
        weight_copy(2).start()
        x = bx[:rows, :]
        finish(0, "xs", bx)
        bias_of = {0: biases[0, member, 0:1, :], 2: biases[0, member, 1:2, :]}
        for segment in range(3):
            for start in range(0, width, CHUNK):
                cols = slice(segment * width + start, segment * width + start + CHUNK)
                part = mm(x, bwqkv[:, cols])
                if segment in bias_of:
                    part = part + bias_of[segment][:, start : start + CHUNK]
                bqkv[:rows, cols] = part.astype(BF16)
        weight_copy(3).start()
        finish(1, "qkv", bqkv)
        lane = lax.broadcasted_iota(jnp.int32, (1, 128), 1)
        masks = (lane < HEAD, lane >= HEAD)
        key_valid = lax.broadcasted_iota(jnp.int32, (1, keys), 1) < length
        scale = HEAD**-0.5
        for pair in range(heads // 2):
            lo = pair * 128
            q2 = bqkv[:rows, lo : lo + 128]
            k2 = bqkv[:keys, width + lo : width + lo + 128]
            v2 = bqkv[:keys, 2 * width + lo : 2 * width + lo + 128]
            mixed = None
            for half in range(2):
                scores = mm(q2, jnp.where(masks[half], k2, 0), NT) * scale
                scores = jnp.where(key_valid, scores, NEG)
                weight = jnp.exp(scores - jnp.max(scores, -1, keepdims=True))
                weight = weight * (1.0 / jnp.sum(weight, -1, keepdims=True))
                weight = weight.astype(BF16)
                if "att" in saved:
                    batt[2 * pair + half, :rows, :keys] = weight
                part = mm(weight, jnp.where(masks[half], v2, 0))
                mixed = part if mixed is None else mixed + part
            bmix[:rows, lo : lo + 128] = mixed.astype(BF16)
        finish(2, "att", batt)
        finish(3, "mix", bmix)
        weight_copy(1).wait()
        attended = mm(bmix[:rows, :], bwout[...]) + biases[0, member, 2:3, :]
        n1, inv1 = norm_forward(x.astype(F32) + attended)
        bn1[:rows, :] = n1
        finish(4, "n1", bn1)
        after = n1 * gains[0, member, 0:1, :] + biases[0, member, 3:4, :]
        low = after.astype(BF16)
        blow[:rows, :] = low
        finish(5, "low", blow)
        weight_copy(2).wait()
        weight_copy(3).wait()
        branch = None
        for start in range(0, hidden, CHUNK):
            cols = slice(start, start + CHUNK)
            pre = mm(low, bwup[:, cols]) + bup[0, member : member + 1, cols]
            act, slope = gelu_pair(pre)
            act = act.astype(BF16)
            bact[:rows, cols] = act
            if "gp" in saved:
                bgp[:rows, cols] = slope.astype(BF16)
            part = mm(act, bwdown[cols, :])
            branch = part if branch is None else branch + part
        finish(6, "act", bact)
        finish(7, "gp", bgp)
        n2, inv2 = norm_forward(after + branch + biases[0, member, 4:5, :])
        bn2[:rows, :] = n2
        finish(8, "n2", bn2)
        if "inv" in saved:
            wide = lax.broadcasted_iota(jnp.int32, (1, 128), 1)
            binv[:rows, :] = jnp.where(wide == 0, inv1, inv2)
            finish(9, "inv", binv)
        out = n2 * gains[0, member, 1:2, :] + biases[0, member, 5:6, :]
        by[:rows, :] = out.astype(BF16)
        if rows < crop_len:
            by[rows:, :] = jnp.zeros((crop_len - rows, width), BF16)
        ycopy = pltpu.make_async_copy(by, y_ref, osem.at[10])
        ycopy.start()
        valid = lax.broadcasted_iota(jnp.int32, (rows, 1), 0) < length
        total = jnp.sum(jnp.where(valid, out, 0.0), 0, keepdims=True)
        pool_ref[...] = total / length.astype(F32)
        for copy in started:
            copy.wait()
        ycopy.wait()

    @pl.when(live == 1)
    def _():
        @pl.when(section == 0)
        def _():
            pltpu.make_async_copy(own.at[crop], bx, xsem).start()

        if recv is not None:

            @pl.when(section != 0)
            def _():
                pltpu.make_async_copy(recv, bx, xsem).start()

        weight_copy(0).start()
        pltpu.make_async_copy(own.at[crop], bx, xsem).wait()

        dispatch(length, crop_len, body)


def forward_call(member, info, own, recv, weights, state, save, order=()):
    wqkv, wout, wup, wdown, bup, biases, gains = weights
    crops, crop_len, width = own.shape
    hidden = wup.shape[-1]
    heads = width // HEAD
    shapes = save_shapes(crops, crop_len, width, hidden)
    names = tuple(shapes) if save else ()
    aliased = [state[name] for name in names] if state else []
    order = list(order)
    arrived = [] if recv is None else [recv]
    operands = [info, own, *arrived, *weights, *order, *aliased]
    whole = lambda a: pl.BlockSpec(a.shape, lambda n=len(a.shape): (0,) * n)
    in_specs = [SMEM, ANY] + [ANY] * len(arrived) + [ANY] * 4 + [whole(bup), whole(biases), whole(gains)]
    in_specs += [ANY] * (len(order) + len(aliased))
    out_shape = [
        jax.ShapeDtypeStruct((crop_len, width), BF16),
        jax.ShapeDtypeStruct((1, width), F32),
    ] + [jax.ShapeDtypeStruct(*shapes[name]) for name in names]
    first = 9 + len(arrived) + len(order)
    tokens = crop_len
    cost = pl.CostEstimate(
        flops=2 * tokens * (wqkv[0, 0].size + wout[0, 0].size + 2 * wup[0, 0].size),
        bytes_accessed=20_000_000,
        transcendentals=0,
    )
    outs = pl.pallas_call(
        functools.partial(forward_kernel, member, names, recv is None, len(order) + len(aliased)),
        out_shape=out_shape,
        in_specs=in_specs,
        out_specs=[ANY, pl.BlockSpec((1, width), lambda: (0, 0))] + [ANY] * len(names),
        input_output_aliases={first + i: 2 + i for i in range(len(aliased))},
        scratch_shapes=[
            pltpu.VMEM((crop_len, width), BF16),
            pltpu.VMEM((width, 3 * width), BF16),
            pltpu.VMEM((width, width), BF16),
            pltpu.VMEM((width, hidden), BF16),
            pltpu.VMEM((hidden, width), BF16),
            pltpu.VMEM((crop_len, 3 * width), BF16),
            pltpu.VMEM((heads, crop_len, crop_len) if save else (1, 16, 128), BF16),
            pltpu.VMEM((crop_len, width), BF16),
            pltpu.VMEM((crop_len, width), BF16),
            pltpu.VMEM((crop_len, hidden), BF16),
            pltpu.VMEM((crop_len, hidden), BF16),
            pltpu.VMEM((crop_len, width), F32),
            pltpu.VMEM((crop_len, width), F32),
            pltpu.VMEM((crop_len, 128), F32),
            pltpu.VMEM((crop_len, width), BF16),
            pltpu.SemaphoreType.DMA((4,)),
            pltpu.SemaphoreType.DMA,
            pltpu.SemaphoreType.DMA((11,)),
        ],
        compiler_params=pltpu.CompilerParams(vmem_limit_bytes=VMEM_LIMIT),
        cost_estimate=cost,
        name="forward_crop",
    )(*operands)
    return outs[0], outs[1], dict(zip(names, outs[2:]))


BACK_READ = ("qkv", "att", "n1", "gp", "n2", "inv")


def backward_kernel(first, n_alias, info, cot, *refs):
    recv, refs = (None, refs) if first else (refs[0], refs[1:])
    wqkv, wout, wup, wdown, biases, gains = refs[:6]
    refs = refs[6:]
    saved = dict(zip(BACK_READ, refs[: len(BACK_READ)]))
    refs = refs[len(BACK_READ) + n_alias :]
    dx_ref, vec_ref, ig_ref, bg_ref, ug_ref, ag_ref, qg_ref = refs[:7]
    (bg_in, bwqkv, bwout, bwup, bwdown, bqkv, batt, bn1, bgp, bn2, binv, bbg, bug, bag, bqg, bmg, bxg, bdx, wsem, ssem, gsem, osem) = refs[7:]
    crop_len, width = bbg.shape
    hidden = bug.shape[1]
    heads = width // HEAD
    live, crop, length, section = info[0], info[1], info[2], info[3]

    def weight_copy(number):
        source = (wup, wout, wqkv)[number]
        return pltpu.make_async_copy(source.at[0, 0], (bwup, bwout, bwqkv)[number], wsem.at[number])

    def down_copy(part):
        size = hidden // 4
        return pltpu.make_async_copy(
            wdown.at[0, 0, pl.ds(part * size, size)], bwdown.at[pl.ds(part * size, size)], wsem.at[3 + part]
        )

    def state_copy(name):
        buffers = {"qkv": bqkv, "att": batt, "n1": bn1, "gp": bgp, "n2": bn2, "inv": binv}
        return pltpu.make_async_copy(saved[name].at[crop], buffers[name], ssem.at[BACK_READ.index(name)])

    def body(rows):
        keys = -(-rows // 128) * 128
        started = []

        def finish(number, buffer, target):
            if rows < crop_len:
                buffer[rows:, :] = jnp.zeros((crop_len - rows, buffer.shape[1]), buffer.dtype)
            copy = pltpu.make_async_copy(buffer, target, osem.at[number])
            copy.start()
            started.append(copy)

        def column(values):
            return jnp.sum(values, 0, keepdims=True)

        valid = lax.broadcasted_iota(jnp.int32, (rows, 1), 0) < length
        g = jnp.where(valid, bg_in[:rows, :].astype(F32), 0.0)
        state_copy("n2").wait()
        state_copy("inv").wait()
        n2 = bn2[:rows, :]
        inv1 = binv[:rows, 0:1]
        inv2 = binv[:rows, 1:2]
        base = hidden // width
        vec_ref[base + 5 : base + 6, :] = column(g)
        vec_ref[base + 7 : base + 8, :] = column(g * n2)
        sum_two = norm_backward(g * gains[0, 0, 1:2, :], n2, inv2)
        bg = sum_two.astype(BF16)
        bbg[:rows, :] = bg
        finish(0, bbg, bg_ref.at[crop])
        vec_ref[base + 4 : base + 5, :] = column(bg.astype(F32))
        weight_copy(0).start()
        state_copy("gp").wait()
        for start in range(0, hidden, CHUNK):
            cols = slice(start, start + CHUNK)
            if start % (hidden // 4) == 0:
                down_copy(start // (hidden // 4)).wait()
            grad = mm(bg, bwdown[cols, :], NT) * bgp[:rows, cols].astype(F32)
            grad = grad.astype(BF16)
            bug[:rows, cols] = grad
            vec_ref[start // width : start // width + 1, start % width : start % width + CHUNK] = column(grad.astype(F32))
        weight_copy(0).wait()
        weight_copy(1).start()
        state_copy("n1").start()
        state_copy("qkv").start()
        state_copy("att").start()
        weight_copy(2).start()
        side = sum_two + mm(bug[:rows, :], bwup[...], NT)
        finish(1, bug, ug_ref.at[crop])
        state_copy("n1").wait()
        n1 = bn1[:rows, :]
        vec_ref[base + 3 : base + 4, :] = column(side)
        vec_ref[base + 6 : base + 7, :] = column(side * n1)
        sum_one = norm_backward(side * gains[0, 0, 0:1, :], n1, inv1)
        ag = sum_one.astype(BF16)
        bag[:rows, :] = ag
        finish(2, bag, ag_ref.at[crop])
        vec_ref[base + 2 : base + 3, :] = column(ag.astype(F32))
        weight_copy(1).wait()
        bmg[:rows, :] = mm(ag, bwout[...], NT).astype(BF16)
        state_copy("qkv").wait()
        state_copy("att").wait()
        lane = lax.broadcasted_iota(jnp.int32, (1, 128), 1)
        masks = (lane < HEAD, lane >= HEAD)
        scale = HEAD**-0.5
        zero = jnp.zeros((), BF16)
        for pair in range(heads // 2):
            lo = pair * 128
            q2 = bqkv[:rows, lo : lo + 128]
            k2 = bqkv[:keys, width + lo : width + lo + 128]
            v2 = bqkv[:keys, 2 * width + lo : 2 * width + lo + 128]
            m2 = bmg[:rows, lo : lo + 128]
            dq = dk = dv = None
            for half in range(2):
                weight = batt[2 * pair + half, :rows, :keys]
                wide = weight.astype(F32)
                grad = mm(m2, jnp.where(masks[half], v2, zero), NT)
                mean = jnp.sum(wide * grad, -1, keepdims=True)
                score = (wide * (grad - mean)).astype(BF16)
                parts = (
                    mm(score, jnp.where(masks[half], k2, zero)),
                    mm(score, jnp.where(masks[half], q2, zero), TN),
                    mm(weight, jnp.where(masks[half], m2, zero), TN),
                )
                dq, dk, dv = parts if dq is None else (dq + parts[0], dk + parts[1], dv + parts[2])
            dq = (dq * scale).astype(BF16)
            dk = (dk[:rows] * scale).astype(BF16)
            dv = dv[:rows].astype(BF16)
            bqg[:rows, lo : lo + 128] = dq
            bqg[:rows, width + lo : width + lo + 128] = dk
            bqg[:rows, 2 * width + lo : 2 * width + lo + 128] = dv
            vec_ref[base : base + 1, lo : lo + 128] = column(dq.astype(F32))
            vec_ref[base + 1 : base + 2, lo : lo + 128] = column(dv.astype(F32))
        finish(3, bqg, qg_ref.at[crop])
        weight_copy(2).wait()
        xg = sum_one + mm(bqg[:rows, :], bwqkv[...], NT)
        dx = xg.astype(BF16)
        bdx[:rows, :] = dx
        finish(4, bdx, dx_ref)
        bxg[:rows, :] = jnp.where(section == 0, xg, dx.astype(F32))
        finish(5, bxg, ig_ref.at[crop])
        for copy in started:
            copy.wait()

    @pl.when(live != 1)
    def _():
        vec_ref[...] = jnp.zeros(vec_ref.shape, F32)

    @pl.when(live == 1)
    def _():
        if recv is not None:

            @pl.when(section == 0)
            def _():
                pltpu.make_async_copy(recv, bg_in, gsem).start()

        @pl.when(section != 0)
        def _():
            pltpu.make_async_copy(cot.at[crop], bg_in, gsem).start()

        state_copy("n2").start()
        state_copy("inv").start()
        for part in range(4):
            down_copy(part).start()
        state_copy("gp").start()
        pltpu.make_async_copy(cot.at[crop], bg_in, gsem).wait()
        dispatch(length, crop_len, body)


def backward_call(info, cot, recv, weights, state, grads):
    wqkv, wout, wup, wdown, bup, biases, gains = weights
    crops, crop_len, width = cot.shape
    hidden = wup.shape[-1]
    heads = width // HEAD
    shapes = {
        "ig": ((crops, crop_len, width), F32),
        "bg": ((crops, crop_len, width), BF16),
        "ug": ((crops, crop_len, hidden), BF16),
        "ag": ((crops, crop_len, width), BF16),
        "qg": ((crops, crop_len, 3 * width), BF16),
    }
    names = tuple(shapes)
    aliased = [grads[name] for name in names] if grads else []
    arrived = [] if recv is None else [recv]
    operands = [info, cot, *arrived, wqkv, wout, wup, wdown, biases, gains]
    operands += [state[name] for name in BACK_READ] + aliased
    whole = lambda a: pl.BlockSpec(a.shape, lambda n=len(a.shape): (0,) * n)
    in_specs = [SMEM, ANY] + [ANY] * (len(arrived) + 4) + [whole(biases), whole(gains)]
    in_specs += [ANY] * (len(BACK_READ) + len(aliased))
    first = 8 + len(arrived) + len(BACK_READ)
    rows = hidden // width + 8
    cost = pl.CostEstimate(
        flops=2 * crop_len * (wqkv[0, 0].size + wout[0, 0].size + 2 * wup[0, 0].size),
        bytes_accessed=20_000_000,
        transcendentals=0,
    )
    outs = pl.pallas_call(
        functools.partial(backward_kernel, recv is None, len(aliased)),
        out_shape=[
            jax.ShapeDtypeStruct((crop_len, width), BF16),
            jax.ShapeDtypeStruct((rows, width), F32),
        ]
        + [jax.ShapeDtypeStruct(*shapes[name]) for name in names],
        in_specs=in_specs,
        out_specs=[ANY, pl.BlockSpec((rows, width), lambda: (0, 0))] + [ANY] * len(names),
        input_output_aliases={first + i: 2 + i for i in range(len(aliased))},
        scratch_shapes=[
            pltpu.VMEM((crop_len, width), BF16),
            pltpu.VMEM((width, 3 * width), BF16),
            pltpu.VMEM((width, width), BF16),
            pltpu.VMEM((width, hidden), BF16),
            pltpu.VMEM((hidden, width), BF16),
            pltpu.VMEM((crop_len, 3 * width), BF16),
            pltpu.VMEM((heads, crop_len, crop_len), BF16),
            pltpu.VMEM((crop_len, width), F32),
            pltpu.VMEM((crop_len, hidden), BF16),
            pltpu.VMEM((crop_len, width), F32),
            pltpu.VMEM((crop_len, 128), F32),
            pltpu.VMEM((crop_len, width), BF16),
            pltpu.VMEM((crop_len, hidden), BF16),
            pltpu.VMEM((crop_len, width), BF16),
            pltpu.VMEM((crop_len, 3 * width), BF16),
            pltpu.VMEM((crop_len, width), BF16),
            pltpu.VMEM((crop_len, width), F32),
            pltpu.VMEM((crop_len, width), BF16),
            pltpu.SemaphoreType.DMA((7,)),
            pltpu.SemaphoreType.DMA((len(BACK_READ),)),
            pltpu.SemaphoreType.DMA,
            pltpu.SemaphoreType.DMA((6,)),
        ],
        compiler_params=pltpu.CompilerParams(vmem_limit_bytes=VMEM_LIMIT),
        cost_estimate=cost,
        name="backward_crop",
    )(*operands)
    return outs[0], outs[1], dict(zip(names, outs[2:]))


def weight_kernel(info, left, right, out):
    out[...] = mm(left[...], right[...], TN).astype(BF16)


def weight_call(info, left, right, mine):
    left = left.reshape(-1, left.shape[-1])
    right = right.reshape(-1, right.shape[-1])
    tokens, rows, columns = left.shape[0], left.shape[1] // 2, right.shape[1]
    if rows >= columns:
        tile, count = rows // (rows // 384), rows // 384
        spec_left = pl.BlockSpec((tokens, tile), lambda i, info: (0, (info[0] if mine else 1 - info[0]) * count + i))
        spec_right = pl.BlockSpec((tokens, columns), lambda i, info: (0, 0))
        spec_out = pl.BlockSpec((tile, columns), lambda i, info: (i, 0))
    else:
        tile = 768
        count = columns // tile
        spec_left = pl.BlockSpec((tokens, rows), lambda i, info: (0, info[0] if mine else 1 - info[0]))
        spec_right = pl.BlockSpec((tokens, tile), lambda i, info: (0, i))
        spec_out = pl.BlockSpec((rows, tile), lambda i, info: (0, i))
    return pl.pallas_call(
        weight_kernel,
        out_shape=jax.ShapeDtypeStruct((rows, columns), BF16),
        grid_spec=pltpu.PrefetchScalarGridSpec(
            num_scalar_prefetch=1, grid=(count,), in_specs=[spec_left, spec_right], out_specs=spec_out
        ),
        compiler_params=pltpu.CompilerParams(vmem_limit_bytes=VMEM_LIMIT, dimension_semantics=("arbitrary",)),
        cost_estimate=pl.CostEstimate(flops=2 * tokens * rows * columns, bytes_accessed=2 * tokens * (rows + columns) + 2 * rows * columns, transcendentals=0),
        name="weight_half",
    )(info, left, right)


def last_weight_kernel(info, left, right, left_out, right_out, out):
    step = pl.program_id(0)

    @pl.when(step < pl.num_programs(0) - 1)
    def _():
        out[...] = mm(left[...], right[...], TN).astype(BF16)

    @pl.when(step == pl.num_programs(0) - 1)
    def _():
        out[...] = mm(left_out[...], right_out[...], TN).astype(BF16)


def last_weight_call(info, left, right, left_out, right_out, mine):
    left, right, left_out, right_out = (a.reshape(-1, a.shape[-1]) for a in (left, right, left_out, right_out))
    tokens, width = left.shape
    rows, parts = width // 2, right.shape[1] // width
    half = lambda info: info[0] if mine else 1 - info[0]
    return pl.pallas_call(
        last_weight_kernel,
        out_shape=jax.ShapeDtypeStruct((rows, (parts + 1) * width), BF16),
        grid_spec=pltpu.PrefetchScalarGridSpec(
            num_scalar_prefetch=1,
            grid=(parts + 1,),
            in_specs=[
                pl.BlockSpec((tokens, rows), lambda i, info: (0, half(info))),
                pl.BlockSpec((tokens, width), lambda i, info: (0, jnp.minimum(i, parts - 1))),
                pl.BlockSpec((tokens, rows), lambda i, info: (0, half(info))),
                pl.BlockSpec((tokens, width), lambda i, info: (0, 0)),
            ],
            out_specs=pl.BlockSpec((rows, width), lambda i, info: (0, i)),
        ),
        compiler_params=pltpu.CompilerParams(vmem_limit_bytes=VMEM_LIMIT),
        cost_estimate=pl.CostEstimate(flops=2 * tokens * rows * width * (parts + 1), bytes_accessed=12_000_000, transcendentals=0),
        name="weight_half_two",
    )(info, left, right, left_out, right_out)


def ring_plan(dp, rep):
    chips = [(0, z) for z in range(rep)] + [(1, z) for z in reversed(range(rep))]
    count = len(chips)
    position = [0] * (dp * rep)
    pairs = []
    for core in range(2):
        order = chips if core == 0 else chips[::-1]
        index = [(2 * y + core) * rep + z for y, z in order]
        for place, device in enumerate(index):
            position[device] = place
            pairs.append((device, index[(place + 1) % count]))
    return count, position, pairs


def sum_over_ring(halves, place, count, pairs):
    own, other = (a.reshape(count, -1, a.shape[-1]) for a in halves)

    def block(number):
        number = jnp.mod(number, count)
        take = lambda a: lax.dynamic_index_in_dim(a, number, 0, keepdims=False).astype(F32)
        return take(own) + take(other)

    moving = block(place).astype(BF16)
    for step in range(1, count):
        moving = lax.ppermute(moving, AXES, pairs)
        moving = (moving.astype(F32) + block(place - step)).astype(BF16)
        yield None
    result = jnp.zeros(own.shape, BF16)
    for step in range(count):
        if step > 0:
            moving = lax.ppermute(moving, AXES, pairs)
        result = lax.dynamic_update_index_in_dim(result, moving, jnp.mod(place + 1 - step, count), 0)
        yield None
    yield result.reshape(halves[0].shape)


AXES = ("dp", "rep")


def on_device(
    query_input,
    key_input,
    query_lengths,
    key_lengths,
    cotangent,
    w_qkv,
    w_out,
    w_up,
    w_down,
    b_up,
    biases,
    gains,
):
    section = lax.axis_index("section")
    dp, rep = lax.axis_size("dp"), lax.axis_size("rep")
    crops, crop_len, width = query_input.shape
    hidden = w_up.shape[-1]
    weights = (w_qkv, w_out, w_up, w_down, b_up, biases, gains)

    def info_of(crop, lengths):
        live = (crop >= 0) & (crop < crops)
        slot = jnp.clip(crop, 0, crops - 1)
        length = lax.dynamic_index_in_dim(lengths, slot, 0, keepdims=False)
        return jnp.stack([live.astype(jnp.int32), slot, length, section]).astype(jnp.int32)

    def up(value):
        return lax.ppermute(value, "section", [(0, 1)])

    def down(value):
        return lax.ppermute(value, "section", [(1, 0)])

    def picked(rows, first):
        return lax.dynamic_slice_in_dim(jnp.concatenate(rows), first, crops, 0)

    state, grads = {}, {}
    pools, vectors = [], []
    arrived = returned = None
    for slot in range(crops + 1):
        sent, pooled, state = forward_call(
            0, info_of(slot - section, query_lengths), query_input, arrived, weights, state, True, vectors[-1:]
        )
        pools.append(pooled)
        if slot < crops:
            arrived = up(sent)
        if slot >= 1:
            back, vector, grads = backward_call(
                info_of(slot - 2 + section, query_lengths), cotangent, returned, weights, state, grads
            )
            vectors.append(vector)
            returned = down(back)
    back, vector, grads = backward_call(
        info_of(crops - 1 + section, query_lengths), cotangent, returned, weights, state, grads
    )
    vectors.append(vector)

    core = jnp.mod(lax.axis_index("dp"), 2)
    core_info = core.astype(jnp.int32)[None]
    swap = [(d * rep + z, (d ^ 1) * rep + z) for d in range(dp) for z in range(rep)]
    products = (
        lambda mine: weight_call(core_info, state["act"], grads["bg"], mine),
        lambda mine: weight_call(core_info, state["low"], grads["ug"], mine),
        lambda mine: last_weight_call(core_info, state["xs"], grads["qg"], state["mix"], grads["ag"], mine),
    )
    halves = []
    for product in products:
        theirs = product(False)
        halves.append((product(True), lax.ppermute(theirs, AXES, swap), theirs))

    pooled_query = lax.all_gather(picked(pools, section), AXES, axis=0, tiled=True)
    small = lax.psum(sum(vectors), AXES)

    key_pools = []
    arrived = None
    for slot in range(crops + 1):
        sent, pooled, _ = forward_call(
            1, info_of(slot - section, key_lengths), key_input, arrived, weights, {}, False, [halves[-1][0]]
        )
        key_pools.append(pooled)
        if slot < crops:
            arrived = up(sent)
    pooled_key = lax.all_gather(picked(key_pools, section), AXES, axis=0, tiled=True)

    def joined(half, other):
        both = jnp.where(core == 0, jnp.stack([half, other]), jnp.stack([other, half]))
        return both.reshape(-1, half.shape[-1])

    if dp == 4:
        count, position, pairs = ring_plan(dp, rep)
        place = jnp.asarray(position, jnp.int32)[lax.axis_index(AXES)]
        rings = [sum_over_ring(half[:2], place, count, pairs) for half in halves]
        for step in range(2 * count):
            results = [next(ring) for ring in rings]
        totals = [joined(half, lax.ppermute(half, AXES, swap)) for half in results]
    else:
        totals = [lax.psum(joined(mine, theirs), AXES) for mine, _, theirs in halves]
    totals = [total.astype(F32) for total in totals]
    ratio = hidden // width
    return (
        pooled_query[None],
        pooled_key[None],
        grads["ig"][None],
        totals[2][None, :, : 3 * width],
        totals[2][None, :, 3 * width :],
        totals[1][None],
        totals[0][None],
        small[:ratio].reshape(1, hidden),
        small[None, ratio : ratio + 6],
        small[None, ratio + 6 : ratio + 8],
    )


def solution(mesh):
    placed = (
        P(("dp", "rep"), None, None),
        P(("dp", "rep"), None, None),
        P(("dp", "rep")),
        P(("dp", "rep")),
        P(("dp", "rep"), None, None),
        P("section", None, None, None),
        P("section", None, None, None),
        P("section", None, None, None),
        P("section", None, None, None),
        P("section", None, None),
        P("section", None, None, None),
        P("section", None, None, None),
    )
    return jax.shard_map(
        on_device,
        mesh=mesh,
        in_specs=placed,
        out_specs=(
            P("section", None, None),
            P("section", None, None),
            P("section", ("dp", "rep"), None, None),
            P("section", None, None),
            P("section", None, None),
            P("section", None, None),
            P("section", None, None),
            P("section", None),
            P("section", None, None),
            P("section", None, None),
        ),
        check_vma=False,
    )
```

time: 2280 us -> 611 us (0.27)
  blocking collectives: 1290 us -> 129 us
  matrix products: 303 us -> 0 us
  Pallas kernels: 0 us -> 225 us
  waiting for transfers between devices: 293 us -> 74.2 us
  local copies, waits for them, and re-layouts: 203 us -> 23.9 us
  other arithmetic: 131 us -> 57.4 us
  starting transfers between devices: 10.9 us -> 83.7 us
    unnamed x2 -> x0, blocking collectives: 1230 us -> none
    dot_general x54 -> x0, matrix products: 268 us -> none  [the longest x6 73.8 us: forward_block(): jnp.einsum('clf,fd->cld', active, w_down, preferred_element_type=jnp.floa...]
    pallas_call x0 -> x21, Pallas kernels: none -> 225 us  [the longest x10 108 us: forward_call(): pl.pallas_call(functools.partial(forward_kernel, member, names, recv is N...]
    ppermute x6 -> x60, waiting for transfers between devices: 293 us -> 74.2 us  [the longest x42 61 us: sum_over_ring(): moving = lax.ppermute(moving, AXES, pairs)]
    ppermute x6 -> x60, starting transfers between devices: 10.8 us -> 83.7 us  [the longest x42 53.8 us: sum_over_ring(): moving = lax.ppermute(moving, AXES, pairs)]
    reshape x26 -> x0, local copies, waits for them, and re-layouts: 68 us -> none  [the longest x16 56.8 us: on_device(): flattened = tuple((grad_part.reshape(-1) for grad_part in grads))]
    psum x0 -> x1, blocking collectives: none -> 60.3 us  [on_device(): small = lax.psum(sum(vectors), AXES)]
    add x11 -> x1, other arithmetic: 44.9 us -> 0.02 us  [on_device(): small = lax.psum(sum(vectors), AXES)]
  transfers between devices with their start and end apart: 10 -> 60, of which waited for: 6 -> 43; matrix products, arithmetic and copies ran while one was open for 6% -> 10% of each run, Pallas kernels for 0% -> 28%
where the time goes in v1:
time: 611 us; the launch traced here: 603 us
  Pallas kernels  225 us (37%)
  blocking collectives  129 us (21%)
  starting transfers between devices  83.7 us (14%)
  waiting for transfers between devices  74.2 us (12%)
  other arithmetic  57.4 us (9%)
  local copies, waits for them, and re-layouts  23.9 us (4%)
  between operations  8.95 us (1%)
    pallas_call x10, Pallas kernels, forward_call(): pl.pallas_call(functools.partial(forward_kernel, member, names, recv is N...  108 us
    pallas_call x5, Pallas kernels, backward_call(): pl.pallas_call(functools.partial(backward_kernel, recv is None, len(alias...  76.7 us
    ppermute x42, waiting for transfers between devices, sum_over_ring(): moving = lax.ppermute(moving, AXES, pairs)  61 us
    psum x1, blocking collectives, on_device(): small = lax.psum(sum(vectors), AXES)  60.3 us
    ppermute x42, starting transfers between devices, sum_over_ring(): moving = lax.ppermute(moving, AXES, pairs)  53.8 us
    all_gather x1, blocking collectives, on_device(): lax.all_gather(picked(key_pools, section), AXES, axis=0, tiled=True)  36.5 us
    all_gather x1, blocking collectives, on_device(): lax.all_gather(picked(pools, section), AXES, axis=0, tiled=True)  32.6 us
    pallas_call x4, Pallas kernels, weight_call(): pl.pallas_call(weight_kernel, out_shape=jax.ShapeDtypeStruct((rows, colum...  26.2 us
  transfers between devices with their start and end apart: 60, of which 43 were waited for; matrix products, arithmetic and copies ran while one was open for 10% of the time, Pallas kernels for 28%

profile of v1, /device:TPU:3, one launch (start us, length us, event | category | flops | bytes accessed | tf_op | source)
XLA Modules:
  0.0 602.7 jit_solution(2521284329070844481)
XLA Ops:
  2.1 1.7 fusion.30
  5.0 1.6 forward_crop.10
  17.2 2.0 add_add_fusion.2
  19.2 9.4 %collective-permute-done.refs_0_ = bf16[256,768]{1,0:T(8,128)(2,1)S(1)} collective-permute-done((bf16[256,768]{1,0:T(8,128)(2,1)}, bf16[256,768]{1,0:T(8,128)(2,1)S(1)}, u32[]{:S(2)}, u32[]{:S(2)}) %collective-permute-start) | collective-permute-done | bytes 393248 | tf_op jit(solution)/shard_map/ppermute | solution.py:626
  29.3 13.5 %forward_crop.11 = (bf16[256,768]{1,0:T(8,128)(2,1)}, f32[1,768]{1,0:T(1,128)}, bf16[4,256,768]{2,1,0:T(8,128)(2,1)}, bf16[4,256,2304]{2,1,0:T(8,128)(2,1)}, bf1...) custom-call(s32[4]{0:T(128)} %get-tuple-element.255.info, ...), custom_call_target="tpu_custom_call", output_to_operand_aliasing={{2}: (10, {}), {3}: (11, {}), {4}: (12, {}), {5}: (13, {}),... | custom-call | flops 3623878656 | bytes 20000000 | tf_op jit(solution)/shard_map/forward_crop/pallas_call | solution.py:234
  44.1 16.5 %backward_crop.5 = (bf16[256,768]{1,0:T(8,128)(2,1)}, f32[12,768]{1,0:T(8,128)}, f32[4,256,768]{2,1,0:T(8,128)}, bf16[4,256,768]{2,1,0:T(8,128)(2,1)}, bf16[4,25...) custom-call(s32[4]{0:T(128)} %get-tuple-element.256.info, ...), custom_call_target="tpu_custom_call" | custom-call | flops 3623878656 | bytes 20000000 | tf_op jit(solution)/shard_map/backward_crop/pallas_call | solution.py:451
  63.9 13.7 %forward_crop.12 = (bf16[256,768]{1,0:T(8,128)(2,1)}, f32[1,768]{1,0:T(1,128)}, bf16[4,256,768]{2,1,0:T(8,128)(2,1)}, bf16[4,256,2304]{2,1,0:T(8,128)(2,1)}, bf1...) custom-call(s32[4]{0:T(128)} %add_add_fusion.3.info, ...), custom_call_target="tpu_custom_call", output_to_operand_aliasing={{2}: (11, {}), {3}: (12, {}), {4}: (13, {}), {5}: (14, {}),... | custom-call | flops 3623878656 | bytes 20000000 | tf_op jit(solution)/shard_map/forward_crop/pallas_call | solution.py:234
  79.7 16.8 %backward_crop.6 = (bf16[256,768]{1,0:T(8,128)(2,1)}, f32[12,768]{1,0:T(8,128)}, f32[4,256,768]{2,1,0:T(8,128)}, bf16[4,256,768]{2,1,0:T(8,128)(2,1)}, bf16[4,25...) custom-call(s32[4]{0:T(128)} %add_add_fusion.6.info, ...), custom_call_target="tpu_custom_call", output_to_operand_aliasing={{2}: (15, {}), {3}: (16, {}), {4}: (17, {}), {5}: (18, {}),... | custom-call | flops 3623878656 | bytes 20000000 | tf_op jit(solution)/shard_map/backward_crop/pallas_call | solution.py:451
  96.5 3.5 collective-permute-start.5
  102.1 13.5 %forward_crop.13 = (bf16[256,768]{1,0:T(8,128)(2,1)}, f32[1,768]{1,0:T(1,128)}, bf16[4,256,768]{2,1,0:T(8,128)(2,1)}, bf16[4,256,2304]{2,1,0:T(8,128)(2,1)}, bf1...) custom-call(s32[4]{0:T(128)} %add_add_fusion.5.info, ...), custom_call_target="tpu_custom_call", output_to_operand_aliasing={{2}: (11, {}), {3}: (12, {}), {4}: (13, {}), {5}: (14, {}),... | custom-call | flops 3623878656 | bytes 20000000 | tf_op jit(solution)/shard_map/forward_crop/pallas_call | solution.py:234
  117.7 16.8 %backward_crop.7 = (bf16[256,768]{1,0:T(8,128)(2,1)}, f32[12,768]{1,0:T(8,128)}, f32[4,256,768]{2,1,0:T(8,128)}, bf16[4,256,768]{2,1,0:T(8,128)(2,1)}, bf16[4,25...) custom-call(s32[4]{0:T(128)} %add_add_fusion.8.info, ...), custom_call_target="tpu_custom_call", output_to_operand_aliasing={{2}: (15, {}), {3}: (16, {}), {4}: (17, {}), {5}: (18, {}),... | custom-call | flops 3623878656 | bytes 20000000 | tf_op jit(solution)/shard_map/backward_crop/pallas_call | solution.py:451
  134.6 3.5 collective-permute-start.6
  147.6 13.7 %forward_crop.14 = (bf16[256,768]{1,0:T(8,128)(2,1)}, f32[1,768]{1,0:T(1,128)}, bf16[4,256,768]{2,1,0:T(8,128)(2,1)}, bf16[4,256,2304]{2,1,0:T(8,128)(2,1)}, bf1...) custom-call(s32[4]{0:T(128)} %add_add_fusion.7.info, ...), custom_call_target="tpu_custom_call", output_to_operand_aliasing={{2}: (11, {}), {3}: (12, {}), {4}: (13, {}), {5}: (14, {}),... | custom-call | flops 3623878656 | bytes 20000000 | tf_op jit(solution)/shard_map/forward_crop/pallas_call | solution.py:234
  162.1 16.9 %backward_crop.8 = (bf16[256,768]{1,0:T(8,128)(2,1)}, f32[12,768]{1,0:T(8,128)}, f32[4,256,768]{2,1,0:T(8,128)}, bf16[4,256,768]{2,1,0:T(8,128)(2,1)}, bf16[4,25...) custom-call(s32[4]{0:T(128)} %add_add_fusion.11.info, ...), custom_call_target="tpu_custom_call", output_to_operand_aliasing={{2}: (15, {}), {3}: (16, {}), {4}: (17, {}), {5}: (18, {}),... | custom-call | flops 3623878656 | bytes 20000000 | tf_op jit(solution)/shard_map/backward_crop/pallas_call | solution.py:451
  182.9 32.6 %all-gather = f32[16,4,768]{2,1,0:T(4,128)S(1)} all-gather(f32[1,4,768]{2,1,0:T(4,128)S(1)} %fusion.24), channel_id=1, replica_groups=mesh['section'=2,'dp'=4,'rep'=4] {'dp','rep'}, dimensions={0}, use_global_device_ids=true | all-gather | bytes 208896 | tf_op jit(solution)/shard_map/all_gather | solution.py:668
  217.0 9.7 %backward_crop.9 = (bf16[256,768]{1,0:T(8,128)(2,1)}, f32[12,768]{1,0:T(8,128)}, f32[4,256,768]{2,1,0:T(8,128)}, bf16[4,256,768]{2,1,0:T(8,128)(2,1)}, bf16[4,25...) custom-call(s32[4]{0:T(128)} %add_add_fusion.10.info, ...), custom_call_target="tpu_custom_call", output_to_operand_aliasing={{2}: (15, {}), {3}: (16, {}), {4}: (17, {}), {5}: (18, {}),... | custom-call | flops 3623878656 | bytes 20000000 | tf_op jit(solution)/shard_map/backward_crop/pallas_call | solution.py:451
  226.7 7.4 %weight_half_two.2.refs_7_.refs_8_ = bf16[384,3072]{1,0:T(8,128)(2,1)} custom-call(s32[1]{0:T(128)} %bitcast.18.info, bf16[1024,768]{1,0:T(8,128)(2,1)} %bitcast.233, bf16[1024,2304]{1,0:T(8,128)(2,1)} %bitcast.219, bf16[1024,768]{1,0:T(8,128)(2,1)} %bitcast.235, bf16[1024,768]{1,0:T(8,128)(2,1)} %bitcast.237), custom_call_target="tpu_custom_call" | custom-call | flops 2415919104 | bytes 12000000 | tf_op jit(solution)/shard_map/weight_half_two/pallas_call | solution.py:540
  234.1 7.3 %weight_half_two.3 = bf16[384,3072]{1,0:T(8,128)(2,1)} custom-call(s32[1]{0:T(128)} %bitcast.18.info, bf16[1024,768]{1,0:T(8,128)(2,1)} %bitcast.234, bf16[1024,2304]{1,0:T(8,128)(2,1)} %bitcast.220, bf16[1024,768]{1,0:T(8,128)(2,1)} %bitcast.236, bf16[1024,768]{1,0:T(8,128)(2,1)} %bitcast.238), custom_call_target="tpu_custom_call" | custom-call | flops 2415919104 | bytes 12000000 | tf_op jit(solution)/shard_map/weight_half_two/pallas_call | solution.py:540
  241.4 1.5 forward_crop.15
  244.3 2.5 collective-permute-start.12
  246.7 6.7 %weight_half.5 = bf16[384,3072]{1,0:T(8,128)(2,1)} custom-call(s32[1]{0:T(128)} %bitcast.18.info, bf16[1024,768]{1,0:T(8,128)(2,1)} %bitcast.229, bf16[1024,3072]{1,0:T(8,128)(2,1)} %bitcast.217), custom_call_target="tpu_custom_call" | custom-call | flops 2415919104 | bytes 9437184 | tf_op jit(solution)/shard_map/weight_half/pallas_call | solution.py:511
  253.5 6.4 %weight_half.7 = bf16[1536,768]{1,0:T(8,128)(2,1)} custom-call(s32[1]{0:T(128)} %bitcast.18.info, bf16[1024,3072]{1,0:T(8,128)(2,1)} %bitcast.215, bf16[1024,768]{1,0:T(8,128)(2,1)} %bitcast.231), custom_call_target="tpu_custom_call" | custom-call | flops 2415919104 | bytes 7077888 | tf_op jit(solution)/shard_map/weight_half/pallas_call | solution.py:511
  261.7 12.8 %forward_crop.16 = (bf16[256,768]{1,0:T(8,128)(2,1)}, f32[1,768]{1,0:T(1,128)}) custom-call(s32[4]{0:T(128)} %add_add_fusion.12.info, bf16[4,256,768]{2,1,0:T(8,128)(2,1)} %own.19, bf16[256,768]{1,0:T(8,128)(2,1)} %copy-done.11, bf16[1,2,768,2304]{3,2,1,0:T(8,128)(2,1)} %refs_1_.29, bf16[1,2,768,768]{3,2,1,0:T(8,128)(2,1)} %refs_2_.29, ...), custom_call_target="tpu_custom_call" | custom-call | flops 3623878656 | bytes 20000000 | tf_op jit(solution)/shard_map/forward_crop/pallas_call | solution.py:234
  275.9 60.3 %psum.7 = f32[12,768]{1,0:T(8,128)S(1)} all-reduce(f32[12,768]{1,0:T(8,128)S(1)} %add_add_fusion), channel_id=1, replica_groups=mesh['section'=2,'dp'=4,'rep'=4] {'dp','rep'}, use_global_device_ids=true, to_apply=%region_0.1 | all-reduce | flops 9216 | bytes 73728 | tf_op jit(solution)/shard_map/psum | solution.py:669
  337.0 12.2 %forward_crop.17 = (bf16[256,768]{1,0:T(8,128)(2,1)}, f32[1,768]{1,0:T(1,128)}) custom-call(s32[4]{0:T(128)} %add_add_fusion.13.info, bf16[4,256,768]{2,1,0:T(8,128)(2,1)} %own.19, bf16[256,768]{1,0:T(8,128)(2,1)} %copy-done.12, bf16[1,2,768,2304]{3,2,1,0:T(8,128)(2,1)} %refs_1_.29, bf16[1,2,768,768]{3,2,1,0:T(8,128)(2,1)} %refs_2_.29, ...), custom_call_target="tpu_custom_call" | custom-call | flops 3623878656 | bytes 20000000 | tf_op jit(solution)/shard_map/forward_crop/pallas_call | solution.py:234
  351.8 6.7 %weight_half.4 = bf16[384,3072]{1,0:T(8,128)(2,1)} custom-call(s32[1]{0:T(128)} %bitcast.18.info, bf16[1024,768]{1,0:T(8,128)(2,1)} %bitcast.230, bf16[1024,3072]{1,0:T(8,128)(2,1)} %bitcast.218), custom_call_target="tpu_custom_call" | custom-call | flops 2415919104 | bytes 9437184 | tf_op jit(solution)/shard_map/weight_half/pallas_call | solution.py:511
  358.5 2.8 collective-permute-done.10.refs_0_
  362.1 12.6 %forward_crop.18 = (bf16[256,768]{1,0:T(8,128)(2,1)}, f32[1,768]{1,0:T(1,128)}) custom-call(s32[4]{0:T(128)} %add_add_fusion.14.info, bf16[4,256,768]{2,1,0:T(8,128)(2,1)} %own.19, bf16[256,768]{1,0:T(8,128)(2,1)} %copy-done.13, bf16[1,2,768,2304]{3,2,1,0:T(8,128)(2,1)} %refs_1_.29, bf16[1,2,768,768]{3,2,1,0:T(8,128)(2,1)} %refs_2_.29, ...), custom_call_target="tpu_custom_call" | custom-call | flops 3623878656 | bytes 20000000 | tf_op jit(solution)/shard_map/forward_crop/pallas_call | solution.py:234
  376.6 6.4 %weight_half.6 = bf16[1536,768]{1,0:T(8,128)(2,1)} custom-call(s32[1]{0:T(128)} %bitcast.18.info, bf16[1024,3072]{1,0:T(8,128)(2,1)} %bitcast.216, bf16[1024,768]{1,0:T(8,128)(2,1)} %bitcast.232), custom_call_target="tpu_custom_call" | custom-call | flops 2415919104 | bytes 7077888 | tf_op jit(solution)/shard_map/weight_half/pallas_call | solution.py:511
  384.2 12.2 %forward_crop.19 = (bf16[256,768]{1,0:T(8,128)(2,1)}, f32[1,768]{1,0:T(1,128)}) custom-call(s32[4]{0:T(128)} %add_add_fusion.15.info, bf16[4,256,768]{2,1,0:T(8,128)(2,1)} %own.19, bf16[256,768]{1,0:T(8,128)(2,1)} %copy-done.14, bf16[1,2,768,2304]{3,2,1,0:T(8,128)(2,1)} %refs_1_.29, bf16[1,2,768,768]{3,2,1,0:T(8,128)(2,1)} %refs_2_.29, ...), custom_call_target="tpu_custom_call" | custom-call | flops 3623878656 | bytes 20000000 | tf_op jit(solution)/shard_map/forward_crop/pallas_call | solution.py:234
  397.2 36.5 %all-gather.1 = f32[16,4,768]{2,1,0:T(4,128)S(1)} all-gather(f32[1,4,768]{2,1,0:T(4,128)S(1)} %fusion.25), channel_id=1, replica_groups=mesh['section'=2,'dp'=4,'rep'=4] {'dp','rep'}, dimensions={0}, use_global_device_ids=true | all-gather | bytes 208896 | tf_op jit(solution)/shard_map/all_gather | solution.py:680
  439.8 1.5 collective-permute-done.13
  442.4 1.7 collective-permute-start.14
  449.0 1.4 collective-permute-start.46
  452.2 1.4 collective-permute-start.15
  461.7 1.4 collective-permute-start.16
  471.1 1.4 collective-permute-start.17
  477.5 1.4 collective-permute-start.49
  486.9 1.4 collective-permute-start.50
  490.1 1.7 collective-permute-start.19
  493.3 1.4 collective-permute-start.35
  509.4 1.7 collective-permute-done.36
  512.6 1.7 collective-permute-done.52
  515.7 1.7 collective-permute-done.21
  518.9 1.7 collective-permute-done.37
  522.0 1.7 collective-permute-done.53
  525.2 1.7 collective-permute-done.22
  528.4 1.7 collective-permute-done.38
  531.5 1.7 collective-permute-done.54
  534.7 1.7 collective-permute-done.23
  537.8 1.7 collective-permute-done.39
  541.0 1.7 collective-permute-done.55
  544.1 1.8 collective-permute-done.24
  547.3 1.7 collective-permute-done.40
  550.5 4.9 collective-permute-done.25
  556.8 4.9 collective-permute-done.26
  561.7 4.9 collective-permute-start.27
  566.8 8.9 %collective-permute-done.42 = bf16[48,3072]{1,0:T(8,128)(2,1)S(1)} collective-permute-done((bf16[48,3072]{1,0:T(8,128)(2,1)S(1)}, bf16[48,3072]{1,0:T(8,128)(2,1)S(1)}, u32[]{:S(2)}, u32[]{:S(2)}) %collective-permute-start.42) | collective-permute-done | bytes 294944 | tf_op jit(solution)/shard_map/ppermute | solution.py:590
  576.9 5.8 collective-permute-done.58
  584.4 1.6 bitcast_convert_fusion.2
  586.7 1.6 slice_bitcast_fusion.1
  588.4 5.0 bitcast_convert_fusion.1
  593.4 3.5 slice_bitcast_fusion
  597.7 4.5 bitcast_convert_fusion
  (228 shorter events, 130.3 us)
Async XLA Ops:
  6.6 22.0 %collective-permute-start = (bf16[256,768]{1,0:T(8,128)(2,1)}, bf16[256,768]{1,0:T(8,128)(2,1)S(1)}, u32[]{:S(2)}, u32[]{:S(2)}) collective-permute-start(bf16[256,768]{1,0:T(8,128)(2,1)} %get-tuple-element.113), channel_id=1, source_target_pairs={{0,16},{1,17},{2,18},{3,19},{4,20},{5,21},{6,22},{7,23},{8,24},{9,... | collective-permute-start | bytes 1179656 | tf_op jit(solution)/shard_map/ppermute | solution.py:626
  42.8 20.3 %collective-permute-start.1 = (bf16[256,768]{1,0:T(8,128)(2,1)}, bf16[256,768]{1,0:T(8,128)(2,1)S(1)}, u32[]{:S(2)}, u32[]{:S(2)}) collective-permute-start(bf16[256,768]{1,0:T(8,128)(2,1)} %get-tuple-element.125), channel_id=1, source_target_pairs={{0,16},{1,17},{2,18},{3,19},{4,20},{5,21},{6,22},{7,23},{8,24},{9,... | collective-permute-start | bytes 1179656 | tf_op jit(solution)/shard_map/ppermute | solution.py:626
  60.6 18.3 %collective-permute-start.3 = (bf16[256,768]{1,0:T(8,128)(2,1)}, bf16[256,768]{1,0:T(8,128)(2,1)S(1)}, u32[]{:S(2)}, u32[]{:S(2)}) collective-permute-start(bf16[256,768]{1,0:T(8,128)(2,1)} %get-tuple-element.139), channel_id=1, source_target_pairs={{16,0},{17,1},{18,2},{19,3},{20,4},{21,5},{22,6},{23,7},{24,8},{25... | collective-permute-start | bytes 1179656 | tf_op jit(solution)/shard_map/ppermute | solution.py:629
  77.6 23.7 %collective-permute-start.2 = (bf16[256,768]{1,0:T(8,128)(2,1)}, bf16[256,768]{1,0:T(8,128)(2,1)S(1)}, u32[]{:S(2)}, u32[]{:S(2)}) collective-permute-start(bf16[256,768]{1,0:T(8,128)(2,1)} %get-tuple-element.138), channel_id=1, source_target_pairs={{0,16},{1,17},{2,18},{3,19},{4,20},{5,21},{6,22},{7,23},{8,24},{9,... | collective-permute-start | bytes 1179656 | tf_op jit(solution)/shard_map/ppermute | solution.py:626
  96.5 20.4 %collective-permute-start.5 = (bf16[256,768]{1,0:T(8,128)(2,1)}, bf16[256,768]{1,0:T(8,128)(2,1)S(1)}, u32[]{:S(2)}, u32[]{:S(2)}) collective-permute-start(bf16[256,768]{1,0:T(8,128)(2,1)} %get-tuple-element.158), channel_id=1, source_target_pairs={{16,0},{17,1},{18,2},{19,3},{20,4},{21,5},{22,6},{23,7},{24,8},{25... | collective-permute-start | bytes 1179656 | tf_op jit(solution)/shard_map/ppermute | solution.py:629
  115.6 31.2 %collective-permute-start.4 = (bf16[256,768]{1,0:T(8,128)(2,1)}, bf16[256,768]{1,0:T(8,128)(2,1)S(1)}, u32[]{:S(2)}, u32[]{:S(2)}) collective-permute-start(bf16[256,768]{1,0:T(8,128)(2,1)} %get-tuple-element.157), channel_id=1, source_target_pairs={{0,16},{1,17},{2,18},{3,19},{4,20},{5,21},{6,22},{7,23},{8,24},{9,... | collective-permute-start | bytes 1179656 | tf_op jit(solution)/shard_map/ppermute | solution.py:626
  117.7 21.6 %copy-start.30 = (s32[16]{0:T(128)S(1)}, s32[16]{0:T(128)}, u32[]{:S(2)}) copy-start(s32[16]{0:T(128)} %constant.400.clone) | copy-start | bytes 196
  134.6 26.8 %collective-permute-start.6 = (bf16[256,768]{1,0:T(8,128)(2,1)}, bf16[256,768]{1,0:T(8,128)(2,1)S(1)}, u32[]{:S(2)}, u32[]{:S(2)}) collective-permute-start(bf16[256,768]{1,0:T(8,128)(2,1)} %get-tuple-element.177), channel_id=1, source_target_pairs={{16,0},{17,1},{18,2},{19,3},{20,4},{21,5},{22,6},{23,7},{24,8},{25... | collective-permute-start | bytes 1179656 | tf_op jit(solution)/shard_map/ppermute | solution.py:629
  162.1 20.7 %copy-start.24 = (f32[1,768]{1,0:T(1,128)S(1)}, f32[1,768]{1,0:T(1,128)}, u32[]{:S(2)}) copy-start(f32[1,768]{1,0:T(1,128)} %get-tuple-element.156) | copy-start | bytes 9220
  162.1 20.7 %copy-start.27 = (f32[1,768]{1,0:T(1,128)S(1)}, f32[1,768]{1,0:T(1,128)}, u32[]{:S(2)}) copy-start(f32[1,768]{1,0:T(1,128)} %get-tuple-element.175) | copy-start | bytes 9220
  179.0 37.2 %collective-permute-start.7 = (bf16[256,768]{1,0:T(8,128)(2,1)}, bf16[256,768]{1,0:T(8,128)(2,1)S(1)}, u32[]{:S(2)}, u32[]{:S(2)}) collective-permute-start(bf16[256,768]{1,0:T(8,128)(2,1)} %get-tuple-element.189), channel_id=1, source_target_pairs={{16,0},{17,1},{18,2},{19,3},{20,4},{21,5},{22,6},{23,7},{24,8},{25... | collective-permute-start | bytes 1179656 | tf_op jit(solution)/shard_map/ppermute | solution.py:629
  243.0 18.0 %collective-permute-start.8 = (bf16[256,768]{1,0:T(8,128)(2,1)}, bf16[256,768]{1,0:T(8,128)(2,1)S(1)}, u32[]{:S(2)}, u32[]{:S(2)}) collective-permute-start(bf16[256,768]{1,0:T(8,128)(2,1)} %get-tuple-element.199), channel_id=1, source_target_pairs={{0,16},{1,17},{2,18},{3,19},{4,20},{5,21},{6,22},{7,23},{8,24},{9,... | collective-permute-start | bytes 1179656 | tf_op jit(solution)/shard_map/ppermute | solution.py:626
  244.3 190.2 %collective-permute-start.12 = (bf16[384,3072]{1,0:T(8,128)(2,1)}, bf16[384,3072]{1,0:T(8,128)(2,1)}, u32[]{:S(2)}, u32[]{:S(2)}) collective-permute-start(bf16[384,3072]{1,0:T(8,128)(2,1)} %weight_half_two.3), channel_id=1, source_target_pairs={{0,4},{1,5},{2,6},{3,7},{4,0},{5,1},{6,2},{7,3},{8,12},{9,13},{10,... | collective-permute-start | bytes 7077896 | tf_op jit(solution)/shard_map/ppermute | solution.py:666
  253.4 183.7 %collective-permute-start.28 = (bf16[384,3072]{1,0:T(8,128)(2,1)}, bf16[384,3072]{1,0:T(8,128)(2,1)}, u32[]{:S(2)}, u32[]{:S(2)}) collective-permute-start(bf16[384,3072]{1,0:T(8,128)(2,1)} %weight_half.5), channel_id=1, source_target_pairs={{0,4},{1,5},{2,6},{3,7},{4,0},{5,1},{6,2},{7,3},{8,12},{9,13},{10,... | collective-permute-start | bytes 7077896 | tf_op jit(solution)/shard_map/ppermute | solution.py:666
  259.9 178.7 %collective-permute-start.44 = (bf16[1536,768]{1,0:T(8,128)(2,1)}, bf16[1536,768]{1,0:T(8,128)(2,1)}, u32[]{:S(2)}, u32[]{:S(2)}) collective-permute-start(bf16[1536,768]{1,0:T(8,128)(2,1)} %weight_half.7), channel_id=1, source_target_pairs={{0,4},{1,5},{2,6},{3,7},{4,0},{5,1},{6,2},{7,3},{8,12},{9,13},{10,... | collective-permute-start | bytes 7077896 | tf_op jit(solution)/shard_map/ppermute | solution.py:666
  274.6 61.7 %collective-permute-start.9 = (bf16[256,768]{1,0:T(8,128)(2,1)}, bf16[256,768]{1,0:T(8,128)(2,1)S(1)}, u32[]{:S(2)}, u32[]{:S(2)}) collective-permute-start(bf16[256,768]{1,0:T(8,128)(2,1)} %get-tuple-element.201), channel_id=1, source_target_pairs={{0,16},{1,17},{2,18},{3,19},{4,20},{5,21},{6,22},{7,23},{8,24},{9,... | collective-permute-start | bytes 1179656 | tf_op jit(solution)/shard_map/ppermute | solution.py:626
  349.2 12.1 %collective-permute-start.10 = (bf16[256,768]{1,0:T(8,128)(2,1)}, bf16[256,768]{1,0:T(8,128)(2,1)S(1)}, u32[]{:S(2)}, u32[]{:S(2)}) collective-permute-start(bf16[256,768]{1,0:T(8,128)(2,1)} %get-tuple-element.203), channel_id=1, source_target_pairs={{0,16},{1,17},{2,18},{3,19},{4,20},{5,21},{6,22},{7,23},{8,24},{9,... | collective-permute-start | bytes 1179656 | tf_op jit(solution)/shard_map/ppermute | solution.py:626
  374.7 8.7 %collective-permute-start.11 = (bf16[256,768]{1,0:T(8,128)(2,1)}, bf16[256,768]{1,0:T(8,128)(2,1)S(1)}, u32[]{:S(2)}, u32[]{:S(2)}) collective-permute-start(bf16[256,768]{1,0:T(8,128)(2,1)} %get-tuple-element.205), channel_id=1, source_target_pairs={{0,16},{1,17},{2,18},{3,19},{4,20},{5,21},{6,22},{7,23},{8,24},{9,... | collective-permute-start | bytes 1179656 | tf_op jit(solution)/shard_map/ppermute | solution.py:626
  383.1 51.4 %copy-start = (bf16[384,3072]{1,0:T(8,128)(2,1)S(1)}, bf16[384,3072]{1,0:T(8,128)(2,1)}, u32[]{:S(2)}) copy-start(bf16[384,3072]{1,0:T(8,128)(2,1)} %weight_half_two.2.refs_7_.refs_8_) | copy-start | bytes 7077892
  435.7 5.6 collective-permute-start.13
  438.3 6.5 %collective-permute-start.29 = (bf16[48,3072]{1,0:T(8,128)(2,1)S(1)}, bf16[48,3072]{1,0:T(8,128)(2,1)S(1)}, u32[]{:S(2)}, u32[]{:S(2)}) collective-permute-start(bf16[48,3072]{1,0:T(8,128)(2,1)S(1)} %fusion.22), channel_id=1, source_target_pairs={{0,1},{1,2},{2,3},{3,11},{11,10},{10,9},{9,8},{8,0},{12,13},{13,14... | collective-permute-start | bytes 884744 | tf_op jit(solution)/shard_map/ppermute | solution.py:584
  439.7 8.2 %collective-permute-start.45 = (bf16[192,768]{1,0:T(8,128)(2,1)S(1)}, bf16[192,768]{1,0:T(8,128)(2,1)S(1)}, u32[]{:S(2)}, u32[]{:S(2)}) collective-permute-start(bf16[192,768]{1,0:T(8,128)(2,1)S(1)} %fusion.23), channel_id=1, source_target_pairs={{0,1},{1,2},{2,3},{3,11},{11,10},{10,9},{9,8},{8,0},{12,13},{13,14... | collective-permute-start | bytes 884744 | tf_op jit(solution)/shard_map/ppermute | solution.py:584
  442.4 8.7 %collective-permute-start.14 = (bf16[48,3072]{1,0:T(8,128)(2,1)S(1)}, bf16[48,3072]{1,0:T(8,128)(2,1)S(1)}, u32[]{:S(2)}, u32[]{:S(2)}) collective-permute-start(bf16[48,3072]{1,0:T(8,128)(2,1)S(1)} %fusion.20), channel_id=1, source_target_pairs={{0,1},{1,2},{2,3},{3,11},{11,10},{10,9},{9,8},{8,0},{12,13},{13,14... | collective-permute-start | bytes 884744 | tf_op jit(solution)/shard_map/ppermute | solution.py:584
  445.9 8.4 %collective-permute-start.30 = (bf16[48,3072]{1,0:T(8,128)(2,1)S(1)}, bf16[48,3072]{1,0:T(8,128)(2,1)S(1)}, u32[]{:S(2)}, u32[]{:S(2)}) collective-permute-start(bf16[48,3072]{1,0:T(8,128)(2,1)S(1)} %fusion.13), channel_id=1, source_target_pairs={{0,1},{1,2},{2,3},{3,11},{11,10},{10,9},{9,8},{8,0},{12,13},{13,14... | collective-permute-start | bytes 884744 | tf_op jit(solution)/shard_map/ppermute | solution.py:584
  449.0 8.4 %collective-permute-start.46 = (bf16[192,768]{1,0:T(8,128)(2,1)S(1)}, bf16[192,768]{1,0:T(8,128)(2,1)S(1)}, u32[]{:S(2)}, u32[]{:S(2)}) collective-permute-start(bf16[192,768]{1,0:T(8,128)(2,1)S(1)} %fusion.6), channel_id=1, source_target_pairs={{0,1},{1,2},{2,3},{3,11},{11,10},{10,9},{9,8},{8,0},{12,13},{13,14... | collective-permute-start | bytes 884744 | tf_op jit(solution)/shard_map/ppermute | solution.py:584
  452.2 8.4 %collective-permute-start.15 = (bf16[48,3072]{1,0:T(8,128)(2,1)S(1)}, bf16[48,3072]{1,0:T(8,128)(2,1)S(1)}, u32[]{:S(2)}, u32[]{:S(2)}) collective-permute-start(bf16[48,3072]{1,0:T(8,128)(2,1)S(1)} %fusion.19), channel_id=1, source_target_pairs={{0,1},{1,2},{2,3},{3,11},{11,10},{10,9},{9,8},{8,0},{12,13},{13,14... | collective-permute-start | bytes 884744 | tf_op jit(solution)/shard_map/ppermute | solution.py:584
  455.3 8.4 %collective-permute-start.31 = (bf16[48,3072]{1,0:T(8,128)(2,1)S(1)}, bf16[48,3072]{1,0:T(8,128)(2,1)S(1)}, u32[]{:S(2)}, u32[]{:S(2)}) collective-permute-start(bf16[48,3072]{1,0:T(8,128)(2,1)S(1)} %fusion.12), channel_id=1, source_target_pairs={{0,1},{1,2},{2,3},{3,11},{11,10},{10,9},{9,8},{8,0},{12,13},{13,14... | collective-permute-start | bytes 884744 | tf_op jit(solution)/shard_map/ppermute | solution.py:584
  458.5 8.4 %collective-permute-start.47 = (bf16[192,768]{1,0:T(8,128)(2,1)S(1)}, bf16[192,768]{1,0:T(8,128)(2,1)S(1)}, u32[]{:S(2)}, u32[]{:S(2)}) collective-permute-start(bf16[192,768]{1,0:T(8,128)(2,1)S(1)} %fusion.5), channel_id=1, source_target_pairs={{0,1},{1,2},{2,3},{3,11},{11,10},{10,9},{9,8},{8,0},{12,13},{13,14... | collective-permute-start | bytes 884744 | tf_op jit(solution)/shard_map/ppermute | solution.py:584
  461.7 8.4 %collective-permute-start.16 = (bf16[48,3072]{1,0:T(8,128)(2,1)S(1)}, bf16[48,3072]{1,0:T(8,128)(2,1)S(1)}, u32[]{:S(2)}, u32[]{:S(2)}) collective-permute-start(bf16[48,3072]{1,0:T(8,128)(2,1)S(1)} %fusion.18), channel_id=1, source_target_pairs={{0,1},{1,2},{2,3},{3,11},{11,10},{10,9},{9,8},{8,0},{12,13},{13,14... | collective-permute-start | bytes 884744 | tf_op jit(solution)/shard_map/ppermute | solution.py:584
  464.8 8.4 %collective-permute-start.32 = (bf16[48,3072]{1,0:T(8,128)(2,1)S(1)}, bf16[48,3072]{1,0:T(8,128)(2,1)S(1)}, u32[]{:S(2)}, u32[]{:S(2)}) collective-permute-start(bf16[48,3072]{1,0:T(8,128)(2,1)S(1)} %fusion.11), channel_id=1, source_target_pairs={{0,1},{1,2},{2,3},{3,11},{11,10},{10,9},{9,8},{8,0},{12,13},{13,14... | collective-permute-start | bytes 884744 | tf_op jit(solution)/shard_map/ppermute | solution.py:584
  468.0 8.4 %collective-permute-start.48 = (bf16[192,768]{1,0:T(8,128)(2,1)S(1)}, bf16[192,768]{1,0:T(8,128)(2,1)S(1)}, u32[]{:S(2)}, u32[]{:S(2)}) collective-permute-start(bf16[192,768]{1,0:T(8,128)(2,1)S(1)} %fusion.4), channel_id=1, source_target_pairs={{0,1},{1,2},{2,3},{3,11},{11,10},{10,9},{9,8},{8,0},{12,13},{13,14... | collective-permute-start | bytes 884744 | tf_op jit(solution)/shard_map/ppermute | solution.py:584
  471.1 8.4 %collective-permute-start.17 = (bf16[48,3072]{1,0:T(8,128)(2,1)S(1)}, bf16[48,3072]{1,0:T(8,128)(2,1)S(1)}, u32[]{:S(2)}, u32[]{:S(2)}) collective-permute-start(bf16[48,3072]{1,0:T(8,128)(2,1)S(1)} %fusion.17), channel_id=1, source_target_pairs={{0,1},{1,2},{2,3},{3,11},{11,10},{10,9},{9,8},{8,0},{12,13},{13,14... | collective-permute-start | bytes 884744 | tf_op jit(solution)/shard_map/ppermute | solution.py:584
  474.3 8.4 %collective-permute-start.33 = (bf16[48,3072]{1,0:T(8,128)(2,1)S(1)}, bf16[48,3072]{1,0:T(8,128)(2,1)S(1)}, u32[]{:S(2)}, u32[]{:S(2)}) collective-permute-start(bf16[48,3072]{1,0:T(8,128)(2,1)S(1)} %fusion.10), channel_id=1, source_target_pairs={{0,1},{1,2},{2,3},{3,11},{11,10},{10,9},{9,8},{8,0},{12,13},{13,14... | collective-permute-start | bytes 884744 | tf_op jit(solution)/shard_map/ppermute | solution.py:584
  477.5 8.4 %collective-permute-start.49 = (bf16[192,768]{1,0:T(8,128)(2,1)S(1)}, bf16[192,768]{1,0:T(8,128)(2,1)S(1)}, u32[]{:S(2)}, u32[]{:S(2)}) collective-permute-start(bf16[192,768]{1,0:T(8,128)(2,1)S(1)} %fusion.3), channel_id=1, source_target_pairs={{0,1},{1,2},{2,3},{3,11},{11,10},{10,9},{9,8},{8,0},{12,13},{13,14... | collective-permute-start | bytes 884744 | tf_op jit(solution)/shard_map/ppermute | solution.py:584
  480.6 8.4 %collective-permute-start.18 = (bf16[48,3072]{1,0:T(8,128)(2,1)S(1)}, bf16[48,3072]{1,0:T(8,128)(2,1)S(1)}, u32[]{:S(2)}, u32[]{:S(2)}) collective-permute-start(bf16[48,3072]{1,0:T(8,128)(2,1)S(1)} %fusion.16), channel_id=1, source_target_pairs={{0,1},{1,2},{2,3},{3,11},{11,10},{10,9},{9,8},{8,0},{12,13},{13,14... | collective-permute-start | bytes 884744 | tf_op jit(solution)/shard_map/ppermute | solution.py:584
  483.8 8.4 %collective-permute-start.34 = (bf16[48,3072]{1,0:T(8,128)(2,1)S(1)}, bf16[48,3072]{1,0:T(8,128)(2,1)S(1)}, u32[]{:S(2)}, u32[]{:S(2)}) collective-permute-start(bf16[48,3072]{1,0:T(8,128)(2,1)S(1)} %fusion.9), channel_id=1, source_target_pairs={{0,1},{1,2},{2,3},{3,11},{11,10},{10,9},{9,8},{8,0},{12,13},{13,14... | collective-permute-start | bytes 884744 | tf_op jit(solution)/shard_map/ppermute | solution.py:584
  486.9 8.4 %collective-permute-start.50 = (bf16[192,768]{1,0:T(8,128)(2,1)S(1)}, bf16[192,768]{1,0:T(8,128)(2,1)S(1)}, u32[]{:S(2)}, u32[]{:S(2)}) collective-permute-start(bf16[192,768]{1,0:T(8,128)(2,1)S(1)} %fusion.2), channel_id=1, source_target_pairs={{0,1},{1,2},{2,3},{3,11},{11,10},{10,9},{9,8},{8,0},{12,13},{13,14... | collective-permute-start | bytes 884744 | tf_op jit(solution)/shard_map/ppermute | solution.py:584
  490.1 8.4 %collective-permute-start.19 = (bf16[48,3072]{1,0:T(8,128)(2,1)S(1)}, bf16[48,3072]{1,0:T(8,128)(2,1)S(1)}, u32[]{:S(2)}, u32[]{:S(2)}) collective-permute-start(bf16[48,3072]{1,0:T(8,128)(2,1)S(1)} %fusion.15), channel_id=1, source_target_pairs={{0,1},{1,2},{2,3},{3,11},{11,10},{10,9},{9,8},{8,0},{12,13},{13,14... | collective-permute-start | bytes 884744 | tf_op jit(solution)/shard_map/ppermute | solution.py:584
  493.3 8.4 %collective-permute-start.35 = (bf16[48,3072]{1,0:T(8,128)(2,1)S(1)}, bf16[48,3072]{1,0:T(8,128)(2,1)S(1)}, u32[]{:S(2)}, u32[]{:S(2)}) collective-permute-start(bf16[48,3072]{1,0:T(8,128)(2,1)S(1)} %fusion.8), channel_id=1, source_target_pairs={{0,1},{1,2},{2,3},{3,11},{11,10},{10,9},{9,8},{8,0},{12,13},{13,14... | collective-permute-start | bytes 884744 | tf_op jit(solution)/shard_map/ppermute | solution.py:584
  496.4 8.4 %collective-permute-start.51 = (bf16[192,768]{1,0:T(8,128)(2,1)S(1)}, bf16[192,768]{1,0:T(8,128)(2,1)S(1)}, u32[]{:S(2)}, u32[]{:S(2)}) collective-permute-start(bf16[192,768]{1,0:T(8,128)(2,1)S(1)} %fusion.1), channel_id=1, source_target_pairs={{0,1},{1,2},{2,3},{3,11},{11,10},{10,9},{9,8},{8,0},{12,13},{13,14... | collective-permute-start | bytes 884744 | tf_op jit(solution)/shard_map/ppermute | solution.py:584
  499.9 8.1 %collective-permute-start.20 = (bf16[48,3072]{1,0:T(8,128)(2,1)S(1)}, bf16[48,3072]{1,0:T(8,128)(2,1)S(1)}, u32[]{:S(2)}, u32[]{:S(2)}) collective-permute-start(bf16[48,3072]{1,0:T(8,128)(2,1)S(1)} %get-tuple-element.239), channel_id=1, source_target_pairs={{0,1},{1,2},{2,3},{3,11},{11,10},{10,9},{9,8},{8,0},{12,13},{13,14... | collective-permute-start | bytes 884744 | tf_op jit(solution)/shard_map/ppermute | solution.py:590
  503.0 8.1 %collective-permute-start.36 = (bf16[48,3072]{1,0:T(8,128)(2,1)S(1)}, bf16[48,3072]{1,0:T(8,128)(2,1)S(1)}, u32[]{:S(2)}, u32[]{:S(2)}) collective-permute-start(bf16[48,3072]{1,0:T(8,128)(2,1)S(1)} %get-tuple-element.237), channel_id=1, source_target_pairs={{0,1},{1,2},{2,3},{3,11},{11,10},{10,9},{9,8},{8,0},{12,13},{13,14... | collective-permute-start | bytes 884744 | tf_op jit(solution)/shard_map/ppermute | solution.py:590
  506.1 8.2 %collective-permute-start.52 = (bf16[192,768]{1,0:T(8,128)(2,1)S(1)}, bf16[192,768]{1,0:T(8,128)(2,1)S(1)}, u32[]{:S(2)}, u32[]{:S(2)}) collective-permute-start(bf16[192,768]{1,0:T(8,128)(2,1)S(1)} %get-tuple-element.235), channel_id=1, source_target_pairs={{0,1},{1,2},{2,3},{3,11},{11,10},{10,9},{9,8},{8,0},{12,13},{13,14... | collective-permute-start | bytes 884744 | tf_op jit(solution)/shard_map/ppermute | solution.py:590
  508.0 9.5 %collective-permute-start.21 = (bf16[48,3072]{1,0:T(8,128)(2,1)S(1)}, bf16[48,3072]{1,0:T(8,128)(2,1)S(1)}, u32[]{:S(2)}, u32[]{:S(2)}) collective-permute-start(bf16[48,3072]{1,0:T(8,128)(2,1)S(1)} %collective-permute-done.20), channel_id=1, source_target_pairs={{0,1},{1,2},{2,3},{3,11},{11,10},{10,9},{9,8},{8,0},{12,13},{13,14... | collective-permute-start | bytes 884744 | tf_op jit(solution)/shard_map/ppermute | solution.py:590
  511.1 9.5 %collective-permute-start.37 = (bf16[48,3072]{1,0:T(8,128)(2,1)S(1)}, bf16[48,3072]{1,0:T(8,128)(2,1)S(1)}, u32[]{:S(2)}, u32[]{:S(2)}) collective-permute-start(bf16[48,3072]{1,0:T(8,128)(2,1)S(1)} %collective-permute-done.36), channel_id=1, source_target_pairs={{0,1},{1,2},{2,3},{3,11},{11,10},{10,9},{9,8},{8,0},{12,13},{13,14... | collective-permute-start | bytes 884744 | tf_op jit(solution)/shard_map/ppermute | solution.py:590
  514.3 9.5 %collective-permute-start.53 = (bf16[192,768]{1,0:T(8,128)(2,1)S(1)}, bf16[192,768]{1,0:T(8,128)(2,1)S(1)}, u32[]{:S(2)}, u32[]{:S(2)}) collective-permute-start(bf16[192,768]{1,0:T(8,128)(2,1)S(1)} %collective-permute-done.52), channel_id=1, source_target_pairs={{0,1},{1,2},{2,3},{3,11},{11,10},{10,9},{9,8},{8,0},{12,13},{13,14... | collective-permute-start | bytes 884744 | tf_op jit(solution)/shard_map/ppermute | solution.py:590
  517.5 9.5 %collective-permute-start.22 = (bf16[48,3072]{1,0:T(8,128)(2,1)S(1)}, bf16[48,3072]{1,0:T(8,128)(2,1)S(1)}, u32[]{:S(2)}, u32[]{:S(2)}) collective-permute-start(bf16[48,3072]{1,0:T(8,128)(2,1)S(1)} %collective-permute-done.21), channel_id=1, source_target_pairs={{0,1},{1,2},{2,3},{3,11},{11,10},{10,9},{9,8},{8,0},{12,13},{13,14... | collective-permute-start | bytes 884744 | tf_op jit(solution)/shard_map/ppermute | solution.py:590
  520.6 9.5 %collective-permute-start.38 = (bf16[48,3072]{1,0:T(8,128)(2,1)S(1)}, bf16[48,3072]{1,0:T(8,128)(2,1)S(1)}, u32[]{:S(2)}, u32[]{:S(2)}) collective-permute-start(bf16[48,3072]{1,0:T(8,128)(2,1)S(1)} %collective-permute-done.37), channel_id=1, source_target_pairs={{0,1},{1,2},{2,3},{3,11},{11,10},{10,9},{9,8},{8,0},{12,13},{13,14... | collective-permute-start | bytes 884744 | tf_op jit(solution)/shard_map/ppermute | solution.py:590
  523.8 9.5 %collective-permute-start.54 = (bf16[192,768]{1,0:T(8,128)(2,1)S(1)}, bf16[192,768]{1,0:T(8,128)(2,1)S(1)}, u32[]{:S(2)}, u32[]{:S(2)}) collective-permute-start(bf16[192,768]{1,0:T(8,128)(2,1)S(1)} %collective-permute-done.53), channel_id=1, source_target_pairs={{0,1},{1,2},{2,3},{3,11},{11,10},{10,9},{9,8},{8,0},{12,13},{13,14... | collective-permute-start | bytes 884744 | tf_op jit(solution)/shard_map/ppermute | solution.py:590
  526.9 9.5 %collective-permute-start.23 = (bf16[48,3072]{1,0:T(8,128)(2,1)S(1)}, bf16[48,3072]{1,0:T(8,128)(2,1)S(1)}, u32[]{:S(2)}, u32[]{:S(2)}) collective-permute-start(bf16[48,3072]{1,0:T(8,128)(2,1)S(1)} %collective-permute-done.22), channel_id=1, source_target_pairs={{0,1},{1,2},{2,3},{3,11},{11,10},{10,9},{9,8},{8,0},{12,13},{13,14... | collective-permute-start | bytes 884744 | tf_op jit(solution)/shard_map/ppermute | solution.py:590
  530.1 9.5 %collective-permute-start.39 = (bf16[48,3072]{1,0:T(8,128)(2,1)S(1)}, bf16[48,3072]{1,0:T(8,128)(2,1)S(1)}, u32[]{:S(2)}, u32[]{:S(2)}) collective-permute-start(bf16[48,3072]{1,0:T(8,128)(2,1)S(1)} %collective-permute-done.38), channel_id=1, source_target_pairs={{0,1},{1,2},{2,3},{3,11},{11,10},{10,9},{9,8},{8,0},{12,13},{13,14... | collective-permute-start | bytes 884744 | tf_op jit(solution)/shard_map/ppermute | solution.py:590
  533.3 9.5 %collective-permute-start.55 = (bf16[192,768]{1,0:T(8,128)(2,1)S(1)}, bf16[192,768]{1,0:T(8,128)(2,1)S(1)}, u32[]{:S(2)}, u32[]{:S(2)}) collective-permute-start(bf16[192,768]{1,0:T(8,128)(2,1)S(1)} %collective-permute-done.54), channel_id=1, source_target_pairs={{0,1},{1,2},{2,3},{3,11},{11,10},{10,9},{9,8},{8,0},{12,13},{13,14... | collective-permute-start | bytes 884744 | tf_op jit(solution)/shard_map/ppermute | solution.py:590
  536.4 9.5 %collective-permute-start.24 = (bf16[48,3072]{1,0:T(8,128)(2,1)S(1)}, bf16[48,3072]{1,0:T(8,128)(2,1)S(1)}, u32[]{:S(2)}, u32[]{:S(2)}) collective-permute-start(bf16[48,3072]{1,0:T(8,128)(2,1)S(1)} %collective-permute-done.23), channel_id=1, source_target_pairs={{0,1},{1,2},{2,3},{3,11},{11,10},{10,9},{9,8},{8,0},{12,13},{13,14... | collective-permute-start | bytes 884744 | tf_op jit(solution)/shard_map/ppermute | solution.py:590
  539.6 9.5 %collective-permute-start.40 = (bf16[48,3072]{1,0:T(8,128)(2,1)S(1)}, bf16[48,3072]{1,0:T(8,128)(2,1)S(1)}, u32[]{:S(2)}, u32[]{:S(2)}) collective-permute-start(bf16[48,3072]{1,0:T(8,128)(2,1)S(1)} %collective-permute-done.39), channel_id=1, source_target_pairs={{0,1},{1,2},{2,3},{3,11},{11,10},{10,9},{9,8},{8,0},{12,13},{13,14... | collective-permute-start | bytes 884744 | tf_op jit(solution)/shard_map/ppermute | solution.py:590
  542.7 23.9 %collective-permute-start.56 = (bf16[192,768]{1,0:T(8,128)(2,1)S(1)}, bf16[192,768]{1,0:T(8,128)(2,1)S(1)}, u32[]{:S(2)}, u32[]{:S(2)}) collective-permute-start(bf16[192,768]{1,0:T(8,128)(2,1)S(1)} %collective-permute-done.55), channel_id=1, source_target_pairs={{0,1},{1,2},{2,3},{3,11},{11,10},{10,9},{9,8},{8,0},{12,13},{13,14... | collective-permute-start | bytes 884744 | tf_op jit(solution)/shard_map/ppermute | solution.py:590
  545.9 9.5 %collective-permute-start.25 = (bf16[48,3072]{1,0:T(8,128)(2,1)S(1)}, bf16[48,3072]{1,0:T(8,128)(2,1)S(1)}, u32[]{:S(2)}, u32[]{:S(2)}) collective-permute-start(bf16[48,3072]{1,0:T(8,128)(2,1)S(1)} %collective-permute-done.24), channel_id=1, source_target_pairs={{0,1},{1,2},{2,3},{3,11},{11,10},{10,9},{9,8},{8,0},{12,13},{13,14... | collective-permute-start | bytes 884744 | tf_op jit(solution)/shard_map/ppermute | solution.py:590
  549.1 17.6 %collective-permute-start.41 = (bf16[48,3072]{1,0:T(8,128)(2,1)S(1)}, bf16[48,3072]{1,0:T(8,128)(2,1)S(1)}, u32[]{:S(2)}, u32[]{:S(2)}) collective-permute-start(bf16[48,3072]{1,0:T(8,128)(2,1)S(1)} %collective-permute-done.40), channel_id=1, source_target_pairs={{0,1},{1,2},{2,3},{3,11},{11,10},{10,9},{9,8},{8,0},{12,13},{13,14... | collective-permute-start | bytes 884744 | tf_op jit(solution)/shard_map/ppermute | solution.py:590
  555.4 6.3 %collective-permute-start.26 = (bf16[48,3072]{1,0:T(8,128)(2,1)S(1)}, bf16[48,3072]{1,0:T(8,128)(2,1)S(1)}, u32[]{:S(2)}, u32[]{:S(2)}) collective-permute-start(bf16[48,3072]{1,0:T(8,128)(2,1)S(1)} %collective-permute-done.25), channel_id=1, source_target_pairs={{0,1},{1,2},{2,3},{3,11},{11,10},{10,9},{9,8},{8,0},{12,13},{13,14... | collective-permute-start | bytes 884744 | tf_op jit(solution)/shard_map/ppermute | solution.py:590
  561.7 21.9 %collective-permute-start.27 = (bf16[384,3072]{1,0:T(8,128)(2,1)S(1)}, bf16[384,3072]{1,0:T(8,128)(2,1)S(1)}, u32[]{:S(2)}, u32[]{:S(2)}) collective-permute-start(bf16[384,3072]{1,0:T(8,128)(2,1)S(1)} %bitcast.260), channel_id=1, source_target_pairs={{0,4},{1,5},{2,6},{3,7},{4,0},{5,1},{6,2},{7,3},{8,12},{9,13},{10,... | collective-permute-start | bytes 7077896 | tf_op jit(solution)/shard_map/ppermute | solution.py:692
  566.6 10.1 %collective-permute-start.57 = (bf16[192,768]{1,0:T(8,128)(2,1)S(1)}, bf16[192,768]{1,0:T(8,128)(2,1)S(1)}, u32[]{:S(2)}, u32[]{:S(2)}) collective-permute-start(bf16[192,768]{1,0:T(8,128)(2,1)S(1)} %collective-permute-done.56), channel_id=1, source_target_pairs={{0,1},{1,2},{2,3},{3,11},{11,10},{10,9},{9,8},{8,0},{12,13},{13,14... | collective-permute-start | bytes 884744 | tf_op jit(solution)/shard_map/ppermute | solution.py:590
  566.7 9.0 %collective-permute-start.42 = (bf16[48,3072]{1,0:T(8,128)(2,1)S(1)}, bf16[48,3072]{1,0:T(8,128)(2,1)S(1)}, u32[]{:S(2)}, u32[]{:S(2)}) collective-permute-start(bf16[48,3072]{1,0:T(8,128)(2,1)S(1)} %collective-permute-done.41), channel_id=1, source_target_pairs={{0,1},{1,2},{2,3},{3,11},{11,10},{10,9},{9,8},{8,0},{12,13},{13,14... | collective-permute-start | bytes 884744 | tf_op jit(solution)/shard_map/ppermute | solution.py:590
  575.7 10.2 %collective-permute-start.43 = (bf16[384,3072]{1,0:T(8,128)(2,1)S(1)}, bf16[384,3072]{1,0:T(8,128)(2,1)S(1)}, u32[]{:S(2)}, u32[]{:S(2)}) collective-permute-start(bf16[384,3072]{1,0:T(8,128)(2,1)S(1)} %bitcast.262), channel_id=1, source_target_pairs={{0,4},{1,5},{2,6},{3,7},{4,0},{5,1},{6,2},{7,3},{8,12},{9,13},{10,... | collective-permute-start | bytes 7077896 | tf_op jit(solution)/shard_map/ppermute | solution.py:692
  576.7 5.9 collective-permute-start.58
  582.7 14.3 %collective-permute-start.59 = (bf16[1536,768]{1,0:T(8,128)(2,1)S(1)}, bf16[1536,768]{1,0:T(8,128)(2,1)S(1)}, u32[]{:S(2)}, u32[]{:S(2)}) collective-permute-start(bf16[1536,768]{1,0:T(8,128)(2,1)S(1)} %bitcast.258), channel_id=1, source_target_pairs={{0,4},{1,5},{2,6},{3,7},{4,0},{5,1},{6,2},{7,3},{8,12},{9,13},{10,... | collective-permute-start | bytes 7077896 | tf_op jit(solution)/shard_map/ppermute | solution.py:692
  (27 other events, 231.6 us)

commit v2 on v1

--- a/solution.py
+++ b/solution.py
@@ -72,7 +72,7 @@
     }
 
 
-def forward_kernel(member, names, first, n_alias, info, own, *refs):
+def forward_kernel(member, names, call, first, n_alias, info, own, *refs):
     recv, refs = (None, refs) if first else (refs[0], refs[1:])
     wqkv, wout, wup, wdown, bup, biases, gains = refs[:7]
     refs = refs[7 + n_alias :]
@@ -82,7 +82,7 @@
     crop_len, width = by.shape
     hidden = bact.shape[1]
     heads = width // HEAD
-    live, crop, length, section = info[0], info[1], info[2], info[3]
+    live, crop, length, section = (info[call, number] for number in range(4))
 
     def weight_copy(number):
         source = (wqkv, wout, wup, wdown)[number]
@@ -206,7 +206,7 @@
         dispatch(length, crop_len, body)
 
 
-def forward_call(member, info, own, recv, weights, state, save, order=()):
+def forward_call(member, info, call, own, recv, weights, state, save, order=()):
     wqkv, wout, wup, wdown, bup, biases, gains = weights
     crops, crop_len, width = own.shape
     hidden = wup.shape[-1]
@@ -232,7 +232,7 @@
         transcendentals=0,
     )
     outs = pl.pallas_call(
-        functools.partial(forward_kernel, member, names, recv is None, len(order) + len(aliased)),
+        functools.partial(forward_kernel, member, names, call, recv is None, len(order) + len(aliased)),
         out_shape=out_shape,
         in_specs=in_specs,
         out_specs=[ANY, pl.BlockSpec((1, width), lambda: (0, 0))] + [ANY] * len(names),
@@ -267,7 +267,7 @@
 BACK_READ = ("qkv", "att", "n1", "gp", "n2", "inv")
 
 
-def backward_kernel(first, n_alias, info, cot, *refs):
+def backward_kernel(call, first, n_alias, info, cot, *refs):
     recv, refs = (None, refs) if first else (refs[0], refs[1:])
     wqkv, wout, wup, wdown, biases, gains = refs[:6]
     refs = refs[6:]
@@ -278,7 +278,7 @@
     crop_len, width = bbg.shape
     hidden = bug.shape[1]
     heads = width // HEAD
-    live, crop, length, section = info[0], info[1], info[2], info[3]
+    live, crop, length, section = (info[call, number] for number in range(4))
 
     def weight_copy(number):
         source = (wup, wout, wqkv)[number]
@@ -421,7 +421,7 @@
         dispatch(length, crop_len, body)
 
 
-def backward_call(info, cot, recv, weights, state, grads):
+def backward_call(info, call, cot, recv, weights, state, grads):
     wqkv, wout, wup, wdown, bup, biases, gains = weights
     crops, crop_len, width = cot.shape
     hidden = wup.shape[-1]
@@ -449,7 +449,7 @@
         transcendentals=0,
     )
     outs = pl.pallas_call(
-        functools.partial(backward_kernel, recv is None, len(aliased)),
+        functools.partial(backward_kernel, call, recv is None, len(aliased)),
         out_shape=[
             jax.ShapeDtypeStruct((crop_len, width), BF16),
             jax.ShapeDtypeStruct((rows, width), F32),
@@ -497,15 +497,17 @@
     left = left.reshape(-1, left.shape[-1])
     right = right.reshape(-1, right.shape[-1])
     tokens, rows, columns = left.shape[0], left.shape[1] // 2, right.shape[1]
+    half = lambda info: info[0] if mine else 1 - info[0]
     if rows >= columns:
-        tile, count = rows // (rows // 384), rows // 384
-        spec_left = pl.BlockSpec((tokens, tile), lambda i, info: (0, (info[0] if mine else 1 - info[0]) * count + i))
+        count = rows // 384
+        tile = rows // count
+        spec_left = pl.BlockSpec((tokens, tile), lambda i, info: (0, half(info) * count + i))
         spec_right = pl.BlockSpec((tokens, columns), lambda i, info: (0, 0))
         spec_out = pl.BlockSpec((tile, columns), lambda i, info: (i, 0))
     else:
         tile = 768
         count = columns // tile
-        spec_left = pl.BlockSpec((tokens, rows), lambda i, info: (0, info[0] if mine else 1 - info[0]))
+        spec_left = pl.BlockSpec((tokens, rows), lambda i, info: (0, half(info)))
         spec_right = pl.BlockSpec((tokens, tile), lambda i, info: (0, i))
         spec_out = pl.BlockSpec((rows, tile), lambda i, info: (0, i))
     return pl.pallas_call(
@@ -514,7 +516,7 @@
         grid_spec=pltpu.PrefetchScalarGridSpec(
             num_scalar_prefetch=1, grid=(count,), in_specs=[spec_left, spec_right], out_specs=spec_out
         ),
-        compiler_params=pltpu.CompilerParams(vmem_limit_bytes=VMEM_LIMIT, dimension_semantics=("arbitrary",)),
+        compiler_params=pltpu.CompilerParams(vmem_limit_bytes=VMEM_LIMIT),
         cost_estimate=pl.CostEstimate(flops=2 * tokens * rows * columns, bytes_accessed=2 * tokens * (rows + columns) + 2 * rows * columns, transcendentals=0),
         name="weight_half",
     )(info, left, right)
@@ -571,26 +573,74 @@
     return count, position, pairs
 
 
-def sum_over_ring(halves, place, count, pairs):
-    own, other = (a.reshape(count, -1, a.shape[-1]) for a in halves)
-
-    def block(number):
-        number = jnp.mod(number, count)
+def tied(value, *others):
+    return lax.optimization_barrier((value, *others))[0]
+
+
+class RingSum:
+    def __init__(self, own, other, core, place, plan, swap):
+        self.count, _, self.pairs = plan
+        self.own, self.other = (a.reshape(self.count, -1, a.shape[-1]) for a in (own, other))
+        self.core, self.place, self.swap = core, place, swap
+        self.moving = self.block(place).astype(BF16)
+        self.step, self.half = 0, None
+
+    def block(self, number):
+        number = jnp.mod(number, self.count)
         take = lambda a: lax.dynamic_index_in_dim(a, number, 0, keepdims=False).astype(F32)
-        return take(own) + take(other)
-
-    moving = block(place).astype(BF16)
-    for step in range(1, count):
-        moving = lax.ppermute(moving, AXES, pairs)
-        moving = (moving.astype(F32) + block(place - step)).astype(BF16)
-        yield None
-    result = jnp.zeros(own.shape, BF16)
-    for step in range(count):
-        if step > 0:
-            moving = lax.ppermute(moving, AXES, pairs)
-        result = lax.dynamic_update_index_in_dim(result, moving, jnp.mod(place + 1 - step, count), 0)
-        yield None
-    yield result.reshape(halves[0].shape)
+        return take(self.own) + take(self.other)
+
+    def done(self):
+        return self.step == 2 * self.count - 2
+
+    def put(self, number):
+        self.half = lax.dynamic_update_index_in_dim(self.half, self.moving, jnp.mod(number, self.count), 0)
+
+    def advance(self, last):
+        self.step += 1
+        moving = tied(lax.ppermute(self.moving, AXES, self.pairs), last)
+        if self.step < self.count:
+            self.moving = (moving.astype(F32) + self.block(self.place - self.step)).astype(BF16)
+            if self.step == self.count - 1:
+                self.half = jnp.zeros(self.own.shape, BF16)
+                self.put(self.place + 1)
+            return
+        self.moving = moving
+        self.put(self.place - (self.step - self.count))
+
+    def result(self):
+        half = self.half.reshape(-1, self.own.shape[-1])
+        other = lax.ppermute(half, AXES, self.swap)
+        both = jnp.where(self.core == 0, jnp.stack([half, other]), jnp.stack([other, half]))
+        return both.reshape(-1, half.shape[-1]).astype(F32)
+
+
+class RingGather:
+    def __init__(self, value, place, plan, swap):
+        self.count, _, self.pairs = plan
+        self.place, self.swap = place, swap
+        self.moving = value
+        self.parts = [value]
+
+    def done(self):
+        return len(self.parts) == self.count
+
+    def advance(self, last):
+        self.moving = tied(lax.ppermute(self.moving, AXES, self.pairs), last)
+        self.parts.append(self.moving)
+
+    def result(self, core, rep):
+        count = self.count
+        own = jnp.stack(self.parts[::-1])
+        own = jnp.roll(own, self.place + 1, 0)
+        other = lax.ppermute(own, AXES, self.swap)
+        first = jnp.where(core == 0, own, other)
+        second = jnp.where(core == 0, other, own)[::-1]
+        both = jnp.stack([first, second], 1)
+        low, high = both[: count // 2], both[count // 2 :][::-1]
+        whole = jnp.stack([low, high])
+        whole = jnp.moveaxis(whole, 1, 2)
+        return whole.reshape((2 * 2, rep) + whole.shape[3:])
 
 
 AXES = ("dp", "rep")
@@ -616,11 +666,19 @@
     hidden = w_up.shape[-1]
     weights = (w_qkv, w_out, w_up, w_down, b_up, biases, gains)
 
-    def info_of(crop, lengths):
-        live = (crop >= 0) & (crop < crops)
-        slot = jnp.clip(crop, 0, crops - 1)
-        length = lax.dynamic_index_in_dim(lengths, slot, 0, keepdims=False)
-        return jnp.stack([live.astype(jnp.int32), slot, length, section]).astype(jnp.int32)
+    slots = list(range(crops + 1))
+    calls = [(slot, slot - 1) for slot in slots] + [(slot - 1, slot) for slot in slots]
+    early = min(2, crops)
+    key_calls = [(slot, -1) for slot in range(early)] + [(-1, slot) for slot in range(early)]
+    key_calls += [(slot, slot - 1 if slot > early else -1) for slot in range(early, crops + 1)]
+    table = jnp.asarray(calls + key_calls, jnp.int32)
+    lives = jnp.where(section == 0, table[:, 0], table[:, 1])
+    crop_of = jnp.clip(lives, 0, crops - 1)
+    is_query = jnp.arange(len(calls) + len(key_calls)) < len(calls)
+    lengths = jnp.where(is_query, query_lengths[crop_of], key_lengths[crop_of])
+    info = jnp.stack(
+        [(lives == crop_of).astype(jnp.int32), crop_of, lengths, jnp.full(lives.shape, section)], 1
+    ).astype(jnp.int32)
 
     def up(value):
         return lax.ppermute(value, "section", [(0, 1)])
@@ -633,66 +691,112 @@
 
     state, grads = {}, {}
     pools, vectors = [], []
+    key_sent, key_pools = {}, [None] * len(key_calls)
+
+    def key_crop(number, info):
+        first, second = key_calls[number]
+        arrived = key_sent.get(second)
+        sent, key_pools[number], _ = forward_call(
+            1, info, len(calls) + number, key_input, arrived, weights, {}, False
+        )
+        if 0 <= first < crops:
+            key_sent[first] = up(sent)
+
+    def key_pool():
+        rows = []
+        for crop in range(crops):
+            first = [key_pools[n] for n, call in enumerate(key_calls) if call[0] == crop][0]
+            second = [key_pools[n] for n, call in enumerate(key_calls) if call[1] == crop][0]
+            rows.append(jnp.where(section == 0, first, second))
+        return jnp.concatenate(rows)
+
     arrived = returned = None
-    for slot in range(crops + 1):
-        sent, pooled, state = forward_call(
-            0, info_of(slot - section, query_lengths), query_input, arrived, weights, state, True, vectors[-1:]
-        )
-        pools.append(pooled)
+    for slot in range(crops + 2):
+        if slot <= crops:
+            sent, pooled, state = forward_call(
+                0, info, slot, query_input, arrived, weights, state, True, vectors[-1:]
+            )
+            pools.append(pooled)
         if slot < crops:
             arrived = up(sent)
+        if slot == 1:
+            key_crop(0, tied(info, pooled))
+        if slot == crops:
+            for number in range(1, early):
+                key_crop(number, tied(info, pooled))
+        if slot == crops + 1:
+            for number in range(early, 2 * early):
+                key_crop(number, tied(info, vectors[-1]))
         if slot >= 1:
-            back, vector, grads = backward_call(
-                info_of(slot - 2 + section, query_lengths), cotangent, returned, weights, state, grads
-            )
+            late = info
+            if slot == 1:
+                late = tied(info, key_pools[0])
+            if slot == crops:
+                late = tied(info, *key_pools[1:early])
+            if slot == crops + 1:
+                late = tied(info, *key_pools[early : 2 * early])
+            back, vector, grads = backward_call(late, crops + slot, cotangent, returned, weights, state, grads)
             vectors.append(vector)
             returned = down(back)
-    back, vector, grads = backward_call(
-        info_of(crops - 1 + section, query_lengths), cotangent, returned, weights, state, grads
-    )
-    vectors.append(vector)
 
     core = jnp.mod(lax.axis_index("dp"), 2)
     core_info = core.astype(jnp.int32)[None]
     swap = [(d * rep + z, (d ^ 1) * rep + z) for d in range(dp) for z in range(rep)]
     products = (
-        lambda mine: weight_call(core_info, state["act"], grads["bg"], mine),
-        lambda mine: weight_call(core_info, state["low"], grads["ug"], mine),
-        lambda mine: last_weight_call(core_info, state["xs"], grads["qg"], state["mix"], grads["ag"], mine),
+        lambda mine, core_info: weight_call(core_info, state["act"], grads["bg"], mine),
+        lambda mine, core_info: weight_call(core_info, state["low"], grads["ug"], mine),
+        lambda mine, core_info: last_weight_call(
+            core_info, state["xs"], grads["qg"], state["mix"], grads["ag"], mine
+        ),
     )
-    halves = []
-    for product in products:
-        theirs = product(False)
-        halves.append((product(True), lax.ppermute(theirs, AXES, swap), theirs))
-
-    pooled_query = lax.all_gather(picked(pools, section), AXES, axis=0, tiled=True)
-    small = lax.psum(sum(vectors), AXES)
-
-    key_pools = []
-    arrived = None
-    for slot in range(crops + 1):
-        sent, pooled, _ = forward_call(
-            1, info_of(slot - section, key_lengths), key_input, arrived, weights, {}, False, [halves[-1][0]]
-        )
-        key_pools.append(pooled)
-        if slot < crops:
-            arrived = up(sent)
-    pooled_key = lax.all_gather(picked(key_pools, section), AXES, axis=0, tiled=True)
-
-    def joined(half, other):
-        both = jnp.where(core == 0, jnp.stack([half, other]), jnp.stack([other, half]))
-        return both.reshape(-1, half.shape[-1])
-
+    vector = sum(vectors)
+    late_keys = range(2 * early, len(key_calls))
     if dp == 4:
-        count, position, pairs = ring_plan(dp, rep)
-        place = jnp.asarray(position, jnp.int32)[lax.axis_index(AXES)]
-        rings = [sum_over_ring(half[:2], place, count, pairs) for half in halves]
-        for step in range(2 * count):
-            results = [next(ring) for ring in rings]
-        totals = [joined(half, lax.ppermute(half, AXES, swap)) for half in results]
+        plan = ring_plan(dp, rep)
+        place = jnp.asarray(plan[1], jnp.int32)[lax.axis_index(AXES)]
+        rings, last = [], vector
+
+        def advance(last):
+            for ring in rings:
+                if not ring.done():
+                    ring.advance(last)
+                    last = ring.moving
+            return last
+
+        for product in products:
+            theirs = product(False, tied(core_info, last))
+            last = advance(theirs)
+            other = lax.ppermute(theirs, AXES, swap)
+            own = product(True, tied(core_info, last))
+            last = advance(own)
+            rings.append(RingSum(own, other, core, place, plan, swap))
+        sums = list(rings)
+        for number in late_keys:
+            key_crop(number, tied(info, last))
+            last = advance(key_pools[number])
+        small = jnp.concatenate([vector, picked(pools, section), key_pool()])
+        gather = RingGather(small, place, plan, swap)
+        rings.insert(0, gather)
+        while not all(ring.done() for ring in rings):
+            last = advance(last)
+        small = gather.result(core, rep)
+        totals = [ring.result() for ring in sums]
+        ratio = vector.shape[0]
+        every = small.reshape((dp * rep,) + small.shape[2:])
+        vector = jnp.sum(every[:, :ratio], 0)
+        pooled_query = every[:, ratio : ratio + crops].reshape(-1, width)
+        pooled_key = every[:, ratio + crops :].reshape(-1, width)
     else:
-        totals = [lax.psum(joined(mine, theirs), AXES) for mine, _, theirs in halves]
-    totals = [total.astype(F32) for total in totals]
+        totals = []
+        for product in products:
+            theirs, own = product(False, core_info), product(True, core_info)
+            both = jnp.where(core == 0, jnp.stack([own, theirs]), jnp.stack([theirs, own]))
+            totals.append(lax.psum(both.reshape(-1, own.shape[-1]), AXES).astype(F32))
+        for number in late_keys:
+            key_crop(number, info)
+        vector = lax.psum(vector, AXES)
+        pooled_query = lax.all_gather(picked(pools, section), AXES, axis=0, tiled=True)
+        pooled_key = lax.all_gather(key_pool(), AXES, axis=0, tiled=True)
     ratio = hidden // width
     return (
         pooled_query[None],
@@ -702,9 +806,9 @@
         totals[2][None, :, 3 * width :],
         totals[1][None],
         totals[0][None],
-        small[:ratio].reshape(1, hidden),
-        small[None, ratio : ratio + 6],
-        small[None, ratio + 6 : ratio + 8],
+        vector[:ratio].reshape(1, hidden),
+        vector[None, ratio : ratio + 6],
+        vector[None, ratio + 6 : ratio + 8],
     )
 
 

time: 611 us -> 513 us (0.84)
  blocking collectives: 129 us -> 0 us
  Pallas kernels: 225 us -> 242 us
  local copies, waits for them, and re-layouts: 23.9 us -> 40.3 us
    all_gather x2 -> x0, blocking collectives: 69.1 us -> none  [the longest x1 36.5 us: on_device(): lax.all_gather(picked(key_pools, section), AXES, axis=0, tiled=True)]
    psum x1 -> x0, blocking collectives: 60.3 us -> none  [on_device(): small = lax.psum(sum(vectors), AXES)]
    another operation x14 -> x4, other arithmetic: 18 us -> 0.47 us  [the longest x2 0.2 us: result(): whole = jnp.stack([low, high])]
    pallas_call x15 -> x17, Pallas kernels: 184 us -> 201 us  [the longest x12 125 us: forward_call(): pl.pallas_call(functools.partial(forward_kernel, member, names, call, rec...]
    ppermute x48 -> x56, waiting for transfers between devices: 61 us -> 47.3 us  [the longest x42 45.4 us: advance(): moving = tied(lax.ppermute(self.moving, AXES, self.pairs), last)]
    ppermute x8, waiting for transfers between devices: 13.2 us -> 26.6 us  [up(): return lax.ppermute(value, 'section', [(0, 1)])]
    dynamic_update_slice x21, local copies, waits for them, and re-layouts: 0.5 us -> 8.15 us  [put(): lax.dynamic_update_index_in_dim(self.half, self.moving, jnp.mod(number, s...]
    convert_element_type x24 -> x25, other arithmetic: 33.9 us -> 40.1 us  [the longest x18 25 us: advance(): (moving.astype(F32) + self.block(self.place - self.step)).astype(BF16)]
  transfers between devices with their start and end apart: 60 -> 68, of which waited for: 43 -> 27; matrix products, arithmetic and copies ran while one was open for 10% -> 14% of each run, Pallas kernels for 28% -> 42%
where the time goes in v2:
time: 513 us; the launch traced here: 504 us
  Pallas kernels  242 us (47%)
  starting transfers between devices  85.8 us (17%)
  waiting for transfers between devices  73.9 us (14%)
  other arithmetic  52.9 us (10%)
  local copies, waits for them, and re-layouts  40.3 us (8%)
  between operations  9.36 us (2%)
    pallas_call x12, Pallas kernels, forward_call(): pl.pallas_call(functools.partial(forward_kernel, member, names, call, rec...  125 us
    pallas_call x5, Pallas kernels, backward_call(): pl.pallas_call(functools.partial(backward_kernel, call, recv is None, len...  76.5 us
    ppermute x42, waiting for transfers between devices, advance(): moving = tied(lax.ppermute(self.moving, AXES, self.pairs), last)  45.4 us
    ppermute x42, starting transfers between devices, advance(): moving = tied(lax.ppermute(self.moving, AXES, self.pairs), last)  40.6 us
    ppermute x8, waiting for transfers between devices, up(): return lax.ppermute(value, 'section', [(0, 1)])  26.6 us
    pallas_call x4, Pallas kernels, weight_call(): pl.pallas_call(weight_kernel, out_shape=jax.ShapeDtypeStruct((rows, colum...  26.4 us
    convert_element_type x18, other arithmetic, advance(): (moving.astype(F32) + self.block(self.place - self.step)).astype(BF16)  25 us
    ppermute x4, starting transfers between devices, down(): return lax.ppermute(value, 'section', [(1, 0)])  15.4 us
  transfers between devices with their start and end apart: 68, of which 27 were waited for; matrix products, arithmetic and copies ran while one was open for 14% of the time, Pallas kernels for 42%

profile of v2, /device:TPU:3, one launch (start us, length us, event | category | flops | bytes accessed | tf_op | source)
XLA Modules:
  0.0 504.4 jit_solution(18161930106125930081)
XLA Ops:
  6.3 1.7 forward_crop.12
  9.4 20.7 %collective-permute-done.refs_0_ = bf16[256,768]{1,0:T(8,128)(2,1)S(1)} collective-permute-done((bf16[256,768]{1,0:T(8,128)(2,1)}, bf16[256,768]{1,0:T(8,128)(2,1)S(1)}, u32[]{:S(2)}, u32[]{:S(2)}) %collective-permute-start) | collective-permute-done | bytes 393248 | tf_op jit(solution)/shard_map/ppermute | solution.py:684
  30.8 14.1 %forward_crop.13 = (bf16[256,768]{1,0:T(8,128)(2,1)}, f32[1,768]{1,0:T(1,128)}, bf16[4,256,768]{2,1,0:T(8,128)(2,1)}, bf16[4,256,2304]{2,1,0:T(8,128)(2,1)}, bf1...) custom-call(s32[17,4]{1,0:T(8,128)} %copy.124.info, ...), custom_call_target="tpu_custom_call", output_to_operand_aliasing={{2}: (10, {}), {3}: (11, {}), {4}: (12, {}), {5}: (13, {}),... | custom-call | flops 3623878656 | bytes 20000000 | tf_op jit(solution)/shard_map/forward_crop/pallas_call | solution.py:234
  46.8 1.7 forward_crop.14
  49.3 17.0 %backward_crop.5 = (bf16[256,768]{1,0:T(8,128)(2,1)}, f32[12,768]{1,0:T(8,128)}, f32[4,256,768]{2,1,0:T(8,128)}, bf16[4,256,768]{2,1,0:T(8,128)(2,1)}, bf16[4,25...) custom-call(s32[17,4]{1,0:T(8,128)} %copy.128.info, bf16[4,256,768]{2,1,0:T(8,128)(2,1)} %cot.9, ...), custom_call_target="tpu_custom_call" | custom-call | flops 3623878656 | bytes 20000000 | tf_op jit(solution)/shard_map/backward_crop/pallas_call | solution.py:451
  66.3 5.2 %collective-permute-start.1 = (bf16[256,768]{1,0:T(8,128)(2,1)}, bf16[256,768]{1,0:T(8,128)(2,1)S(1)}, u32[]{:S(2)}, u32[]{:S(2)}) collective-permute-start(bf16[256,768]{1,0:T(8,128)(2,1)} %get-tuple-element.200), channel_id=1, source_target_pairs={{16,0},{17,1},{18,2},{19,3},{20,4},{21,5},{22,6},{23,7},{24,8},{25... | collective-permute-start | bytes 1179656 | tf_op jit(solution)/shard_map/ppermute | solution.py:687
  72.2 13.3 %forward_crop.15 = (bf16[256,768]{1,0:T(8,128)(2,1)}, f32[1,768]{1,0:T(1,128)}, bf16[4,256,768]{2,1,0:T(8,128)(2,1)}, bf16[4,256,2304]{2,1,0:T(8,128)(2,1)}, bf1...) custom-call(s32[17,4]{1,0:T(8,128)} %copy.124.info, ...), custom_call_target="tpu_custom_call", output_to_operand_aliasing={{2}: (11, {}), {3}: (12, {}), {4}: (13, {}), {5}: (14, {}),... | custom-call | flops 3623878656 | bytes 20000000 | tf_op jit(solution)/shard_map/forward_crop/pallas_call | solution.py:234
  87.6 17.6 %backward_crop.6 = (bf16[256,768]{1,0:T(8,128)(2,1)}, f32[12,768]{1,0:T(8,128)}, f32[4,256,768]{2,1,0:T(8,128)}, bf16[4,256,768]{2,1,0:T(8,128)(2,1)}, bf16[4,25...) custom-call(s32[17,4]{1,0:T(8,128)} %copy.124.info, ...), custom_call_target="tpu_custom_call", output_to_operand_aliasing={{2}: (15, {}), {3}: (16, {}), {4}: (17, {}), {5}: (18, {}),... | custom-call | flops 3623878656 | bytes 20000000 | tf_op jit(solution)/shard_map/backward_crop/pallas_call | solution.py:451
  105.1 3.3 collective-permute-start.3
  109.2 13.3 %forward_crop.16 = (bf16[256,768]{1,0:T(8,128)(2,1)}, f32[1,768]{1,0:T(1,128)}, bf16[4,256,768]{2,1,0:T(8,128)(2,1)}, bf16[4,256,2304]{2,1,0:T(8,128)(2,1)}, bf1...) custom-call(s32[17,4]{1,0:T(8,128)} %copy.124.info, ...), custom_call_target="tpu_custom_call", output_to_operand_aliasing={{2}: (11, {}), {3}: (12, {}), {4}: (13, {}), {5}: (14, {}),... | custom-call | flops 3623878656 | bytes 20000000 | tf_op jit(solution)/shard_map/forward_crop/pallas_call | solution.py:234
  125.9 17.2 %backward_crop.7 = (bf16[256,768]{1,0:T(8,128)(2,1)}, f32[12,768]{1,0:T(8,128)}, f32[4,256,768]{2,1,0:T(8,128)}, bf16[4,256,768]{2,1,0:T(8,128)(2,1)}, bf16[4,25...) custom-call(s32[17,4]{1,0:T(8,128)} %copy.124.info, ...), custom_call_target="tpu_custom_call", output_to_operand_aliasing={{2}: (15, {}), {3}: (16, {}), {4}: (17, {}), {5}: (18, {}),... | custom-call | flops 3623878656 | bytes 20000000 | tf_op jit(solution)/shard_map/backward_crop/pallas_call | solution.py:451
  143.1 3.4 collective-permute-start.6
  147.3 13.3 %forward_crop.17 = (bf16[256,768]{1,0:T(8,128)(2,1)}, f32[1,768]{1,0:T(1,128)}, bf16[4,256,768]{2,1,0:T(8,128)(2,1)}, bf16[4,256,2304]{2,1,0:T(8,128)(2,1)}, bf1...) custom-call(s32[17,4]{1,0:T(8,128)} %copy.124.info, ...), custom_call_target="tpu_custom_call", output_to_operand_aliasing={{2}: (11, {}), {3}: (12, {}), {4}: (13, {}), {5}: (14, {}),... | custom-call | flops 3623878656 | bytes 20000000 | tf_op jit(solution)/shard_map/forward_crop/pallas_call | solution.py:234
  161.2 8.4 %forward_crop.18 = (bf16[256,768]{1,0:T(8,128)(2,1)}, f32[1,768]{1,0:T(1,128)}) custom-call(s32[17,4]{1,0:T(8,128)} %copy.140.info, bf16[4,256,768]{2,1,0:T(8,128)(2,1)} %own.23, bf16[1,2,768,2304]{3,2,1,0:T(8,128)(2,1)} %refs_1_.33, bf16[1,2,768,768]{3,2,1,0:T(8,128)(2,1)} %refs_2_.33, bf16[1,2,768,3072]{3,2,1,0:T(8,128)(2,1)} %refs_3_.33, ...), custom_call_target="tpu_custom_call" | custom-call | flops 3623878656 | bytes 20000000 | tf_op jit(solution)/shard_map/forward_crop/pallas_call | solution.py:234
  172.4 16.9 %backward_crop.8 = (bf16[256,768]{1,0:T(8,128)(2,1)}, f32[12,768]{1,0:T(8,128)}, f32[4,256,768]{2,1,0:T(8,128)}, bf16[4,256,768]{2,1,0:T(8,128)(2,1)}, bf16[4,25...) custom-call(s32[17,4]{1,0:T(8,128)} %copy.142.info, ...), custom_call_target="tpu_custom_call", output_to_operand_aliasing={{2}: (15, {}), {3}: (16, {}), {4}: (17, {}), {5}: (18, {}),... | custom-call | flops 3623878656 | bytes 20000000 | tf_op jit(solution)/shard_map/backward_crop/pallas_call | solution.py:451
  189.9 3.5 collective-permute-start.9
  194.2 12.8 %forward_crop.19 = (bf16[256,768]{1,0:T(8,128)(2,1)}, f32[1,768]{1,0:T(1,128)}) custom-call(s32[17,4]{1,0:T(8,128)} %copy.144.info, bf16[4,256,768]{2,1,0:T(8,128)(2,1)} %own.23, bf16[256,768]{1,0:T(8,128)(2,1)} %copy-done.8, bf16[1,2,768,2304]{3,2,1,0:T(8,128)(2,1)} %refs_1_.33, bf16[1,2,768,768]{3,2,1,0:T(8,128)(2,1)} %refs_2_.33, ...), custom_call_target="tpu_custom_call" | custom-call | flops 3623878656 | bytes 20000000 | tf_op jit(solution)/shard_map/forward_crop/pallas_call | solution.py:234
  207.7 12.4 %forward_crop.20 = (bf16[256,768]{1,0:T(8,128)(2,1)}, f32[1,768]{1,0:T(1,128)}) custom-call(s32[17,4]{1,0:T(8,128)} %copy.144.info, bf16[4,256,768]{2,1,0:T(8,128)(2,1)} %own.23, bf16[256,768]{1,0:T(8,128)(2,1)} %copy-done.17, bf16[1,2,768,2304]{3,2,1,0:T(8,128)(2,1)} %refs_1_.33, bf16[1,2,768,768]{3,2,1,0:T(8,128)(2,1)} %refs_2_.33, ...), custom_call_target="tpu_custom_call" | custom-call | flops 3623878656 | bytes 20000000 | tf_op jit(solution)/shard_map/forward_crop/pallas_call | solution.py:234
  221.6 7.8 %backward_crop.9 = (bf16[256,768]{1,0:T(8,128)(2,1)}, f32[12,768]{1,0:T(8,128)}, f32[4,256,768]{2,1,0:T(8,128)}, bf16[4,256,768]{2,1,0:T(8,128)(2,1)}, bf16[4,25...) custom-call(s32[17,4]{1,0:T(8,128)} %copy.148.info, ...), custom_call_target="tpu_custom_call", output_to_operand_aliasing={{2}: (15, {}), {3}: (16, {}), {4}: (17, {}), {5}: (18, {}),... | custom-call | flops 3623878656 | bytes 20000000 | tf_op jit(solution)/shard_map/backward_crop/pallas_call | solution.py:451
  230.3 6.4 %weight_half.4 = bf16[1536,768]{1,0:T(8,128)(2,1)} custom-call(s32[1]{0:T(128)} %bitcast.3.info, bf16[1024,3072]{1,0:T(8,128)(2,1)} %bitcast.230, bf16[1024,768]{1,0:T(8,128)(2,1)} %bitcast.236), custom_call_target="tpu_custom_call" | custom-call | flops 2415919104 | bytes 7077888 | tf_op jit(solution)/shard_map/weight_half/pallas_call | solution.py:513
  236.7 2.9 collective-permute-start.10
  239.6 6.4 %weight_half.5 = bf16[1536,768]{1,0:T(8,128)(2,1)} custom-call(s32[1]{0:T(128)} %bitcast.3.info, bf16[1024,3072]{1,0:T(8,128)(2,1)} %bitcast.231, bf16[1024,768]{1,0:T(8,128)(2,1)} %bitcast.237), custom_call_target="tpu_custom_call" | custom-call | flops 2415919104 | bytes 7077888 | tf_op jit(solution)/shard_map/weight_half/pallas_call | solution.py:513
  246.1 6.8 %weight_half.6 = bf16[384,3072]{1,0:T(8,128)(2,1)} custom-call(s32[1]{0:T(128)} %bitcast.3.info, bf16[1024,768]{1,0:T(8,128)(2,1)} %bitcast.238, bf16[1024,3072]{1,0:T(8,128)(2,1)} %bitcast.232), custom_call_target="tpu_custom_call" | custom-call | flops 2415919104 | bytes 9437184 | tf_op jit(solution)/shard_map/weight_half/pallas_call | solution.py:513
  256.6 2.1 collective-permute-start.11
  266.7 6.7 %weight_half.7 = bf16[384,3072]{1,0:T(8,128)(2,1)} custom-call(s32[1]{0:T(128)} %bitcast.3.info, bf16[1024,768]{1,0:T(8,128)(2,1)} %bitcast.239, bf16[1024,3072]{1,0:T(8,128)(2,1)} %bitcast.233), custom_call_target="tpu_custom_call" | custom-call | flops 2415919104 | bytes 9437184 | tf_op jit(solution)/shard_map/weight_half/pallas_call | solution.py:513
  278.3 7.3 %weight_half_two.2 = bf16[384,3072]{1,0:T(8,128)(2,1)} custom-call(s32[1]{0:T(128)} %bitcast.3.info, bf16[1024,768]{1,0:T(8,128)(2,1)} %bitcast.242, bf16[1024,2304]{1,0:T(8,128)(2,1)} %bitcast.234, bf16[1024,768]{1,0:T(8,128)(2,1)} %bitcast.244, bf16[1024,768]{1,0:T(8,128)(2,1)} %bitcast.240), custom_call_target="tpu_custom_call" | custom-call | flops 2415919104 | bytes 12000000 | tf_op jit(solution)/shard_map/weight_half_two/pallas_call | solution.py:542
  290.0 7.3 %weight_half_two.3 = bf16[384,3072]{1,0:T(8,128)(2,1)} custom-call(s32[1]{0:T(128)} %bitcast.3.info, bf16[1024,768]{1,0:T(8,128)(2,1)} %bitcast.243, bf16[1024,2304]{1,0:T(8,128)(2,1)} %bitcast.235, bf16[1024,768]{1,0:T(8,128)(2,1)} %bitcast.245, bf16[1024,768]{1,0:T(8,128)(2,1)} %bitcast.241), custom_call_target="tpu_custom_call" | custom-call | flops 2415919104 | bytes 12000000 | tf_op jit(solution)/shard_map/weight_half_two/pallas_call | solution.py:542
  298.7 1.9 fusion.18
  302.2 8.4 %forward_crop.21 = (bf16[256,768]{1,0:T(8,128)(2,1)}, f32[1,768]{1,0:T(1,128)}) custom-call(s32[17,4]{1,0:T(8,128)} %copy.150.info, bf16[4,256,768]{2,1,0:T(8,128)(2,1)} %own.23, bf16[1,2,768,2304]{3,2,1,0:T(8,128)(2,1)} %refs_1_.33, bf16[1,2,768,768]{3,2,1,0:T(8,128)(2,1)} %refs_2_.33, bf16[1,2,768,3072]{3,2,1,0:T(8,128)(2,1)} %refs_3_.33, ...), custom_call_target="tpu_custom_call" | custom-call | flops 3623878656 | bytes 20000000 | tf_op jit(solution)/shard_map/forward_crop/pallas_call | solution.py:234
  316.9 2.0 fusion.16
  320.2 2.0 collective-permute-done.19
  322.2 1.9 fusion.15
  326.8 12.4 %forward_crop.22 = (bf16[256,768]{1,0:T(8,128)(2,1)}, f32[1,768]{1,0:T(1,128)}) custom-call(s32[17,4]{1,0:T(8,128)} %copy.152.info, bf16[4,256,768]{2,1,0:T(8,128)(2,1)} %own.23, bf16[256,768]{1,0:T(8,128)(2,1)} %copy-done.14, bf16[1,2,768,2304]{3,2,1,0:T(8,128)(2,1)} %refs_1_.33, bf16[1,2,768,768]{3,2,1,0:T(8,128)(2,1)} %refs_2_.33, ...), custom_call_target="tpu_custom_call" | custom-call | flops 3623878656 | bytes 20000000 | tf_op jit(solution)/shard_map/forward_crop/pallas_call | solution.py:234
  339.2 1.8 fusion.14
  342.3 2.0 fusion.13
  349.4 5.9 %collective-permute-done.26.refs_0_ = bf16[256,768]{1,0:T(8,128)(2,1)S(1)} collective-permute-done((bf16[256,768]{1,0:T(8,128)(2,1)}, bf16[256,768]{1,0:T(8,128)(2,1)S(1)}, u32[]{:S(2)}, u32[]{:S(2)}) %collective-permute-start.26) | collective-permute-done | bytes 393248 | tf_op jit(solution)/shard_map/ppermute | solution.py:684
  356.1 12.8 %forward_crop.23 = (bf16[256,768]{1,0:T(8,128)(2,1)}, f32[1,768]{1,0:T(1,128)}) custom-call(s32[17,4]{1,0:T(8,128)} %copy.154.info, bf16[4,256,768]{2,1,0:T(8,128)(2,1)} %own.23, bf16[256,768]{1,0:T(8,128)(2,1)} %copy-done.19, bf16[1,2,768,2304]{3,2,1,0:T(8,128)(2,1)} %refs_1_.33, bf16[1,2,768,768]{3,2,1,0:T(8,128)(2,1)} %refs_2_.33, ...), custom_call_target="tpu_custom_call" | custom-call | flops 3623878656 | bytes 20000000 | tf_op jit(solution)/shard_map/forward_crop/pallas_call | solution.py:234
  370.5 1.8 bitcast_dynamic-update-slice_fusion.7
  372.3 2.4 collective-permute-start.34
  374.7 2.0 fusion.10
  378.4 1.9 collective-permute-done.27
  381.4 2.0 collective-permute-done.33
  388.9 1.6 collective-permute-done.38
  391.6 2.1 collective-permute-done.37
  399.2 1.7 collective-permute-done.42
  401.9 2.1 collective-permute-done.41
  409.4 1.7 collective-permute-done.46
  412.1 2.1 collective-permute-done.45
  422.4 2.1 collective-permute-done.49
  429.5 2.1 collective-permute-done.54
  432.7 2.1 collective-permute-done.53
  439.5 1.9 collective-permute-start.55
  442.6 2.2 collective-permute-start.67
  446.1 2.1 collective-permute-done.56
  449.3 2.2 collective-permute-done.60
  458.9 1.7 bitcast_dynamic-update-slice_fusion.8
  460.6 2.9 collective-permute-start.66
  464.5 5.5 %collective-permute-done.63 = bf16[48,3072]{1,0:T(8,128)(2,1)S(1)} collective-permute-done((bf16[48,3072]{1,0:T(8,128)(2,1)S(1)}, bf16[48,3072]{1,0:T(8,128)(2,1)S(1)}, u32[]{:S(2)}, u32[]{:S(2)}) %collective-permute-start.63) | collective-permute-done | bytes 294944 | tf_op jit(solution)/shard_map/ppermute | solution.py:601
  470.1 5.5 %collective-permute-done.64 = bf16[48,3072]{1,0:T(8,128)(2,1)S(1)} collective-permute-done((bf16[48,3072]{1,0:T(8,128)(2,1)S(1)}, bf16[48,3072]{1,0:T(8,128)(2,1)S(1)}, u32[]{:S(2)}, u32[]{:S(2)}) %collective-permute-start.64) | collective-permute-done | bytes 294944 | tf_op jit(solution)/shard_map/ppermute | solution.py:601
  475.6 5.5 %collective-permute-start.65 = (bf16[384,3072]{1,0:T(8,128)(2,1)S(1)}, bf16[384,3072]{1,0:T(8,128)(2,1)S(1)}, u32[]{:S(2)}, u32[]{:S(2)}) collective-permute-start(bf16[384,3072]{1,0:T(8,128)(2,1)S(1)} %bitcast.273), channel_id=1, source_target_pairs={{0,4},{1,5},{2,6},{3,7},{4,0},{5,1},{6,2},{7,3},{8,12},{9,13},{10,... | collective-permute-start | bytes 7077896 | tf_op jit(solution)/shard_map/ppermute | solution.py:613
  481.1 5.2 %maximum_select_fusion.2 = bf16[2,1536,768]{2,1,0:T(8,128)(2,1)S(1)} fusion(bf16[1,1536,768]{2,1,0:T(8,128)(2,1)} %bitcast.96, bf16[1,1536,768]{2,1,0:T(8,128)(2,1)} %bitcast.94, pred[]{:T(512)S(6)} %eq.71), kind=kLoop, calls=%fused_computation.5 | loop fusion | flops 7077888 | bytes 9437185 | tf_op jit(solution)/shard_map/jit(_where)/select_n | solution.py:614
  486.3 4.5 bitcast_convert_fusion
  491.6 5.1 %bitcast_convert_fusion.1 = f32[1,768,3072]{2,1,0:T(8,128)} fusion(bf16[1,768,3072]{2,1,0:T(8,128)(2,1)S(1)} %bitcast.248), kind=kLoop, calls=%fused_computation.7 | loop fusion | flops 2359296 | bytes 14155776 | tf_op jit(solution)/shard_map/convert_element_type | solution.py:615
  499.0 3.5 slice_bitcast_fusion
  (285 shorter events, 119.2 us)
Async XLA Ops:
  8.1 22.0 %collective-permute-start = (bf16[256,768]{1,0:T(8,128)(2,1)}, bf16[256,768]{1,0:T(8,128)(2,1)S(1)}, u32[]{:S(2)}, u32[]{:S(2)}) collective-permute-start(bf16[256,768]{1,0:T(8,128)(2,1)} %get-tuple-element.178), channel_id=1, source_target_pairs={{0,16},{1,17},{2,18},{3,19},{4,20},{5,21},{6,22},{7,23},{8,24},{9,... | collective-permute-start | bytes 1179656 | tf_op jit(solution)/shard_map/ppermute | solution.py:684
  45.6 25.9 %collective-permute-start.2 = (bf16[256,768]{1,0:T(8,128)(2,1)}, bf16[256,768]{1,0:T(8,128)(2,1)S(1)}, u32[]{:S(2)}, u32[]{:S(2)}) collective-permute-start(bf16[256,768]{1,0:T(8,128)(2,1)} %get-tuple-element.201), channel_id=1, source_target_pairs={{0,16},{1,17},{2,18},{3,19},{4,20},{5,21},{6,22},{7,23},{8,24},{9,... | collective-permute-start | bytes 1179656 | tf_op jit(solution)/shard_map/ppermute | solution.py:684
  66.3 20.5 %collective-permute-start.1 = (bf16[256,768]{1,0:T(8,128)(2,1)}, bf16[256,768]{1,0:T(8,128)(2,1)S(1)}, u32[]{:S(2)}, u32[]{:S(2)}) collective-permute-start(bf16[256,768]{1,0:T(8,128)(2,1)} %get-tuple-element.200), channel_id=1, source_target_pairs={{16,0},{17,1},{18,2},{19,3},{20,4},{21,5},{22,6},{23,7},{24,8},{25... | collective-permute-start | bytes 1179656 | tf_op jit(solution)/shard_map/ppermute | solution.py:687
  85.5 22.9 %collective-permute-start.4 = (bf16[256,768]{1,0:T(8,128)(2,1)}, bf16[256,768]{1,0:T(8,128)(2,1)S(1)}, u32[]{:S(2)}, u32[]{:S(2)}) collective-permute-start(bf16[256,768]{1,0:T(8,128)(2,1)} %get-tuple-element.219), channel_id=1, source_target_pairs={{0,16},{1,17},{2,18},{3,19},{4,20},{5,21},{6,22},{7,23},{8,24},{9,... | collective-permute-start | bytes 1179656 | tf_op jit(solution)/shard_map/ppermute | solution.py:684
  105.1 20.0 %collective-permute-start.3 = (bf16[256,768]{1,0:T(8,128)(2,1)}, bf16[256,768]{1,0:T(8,128)(2,1)S(1)}, u32[]{:S(2)}, u32[]{:S(2)}) collective-permute-start(bf16[256,768]{1,0:T(8,128)(2,1)} %get-tuple-element.218), channel_id=1, source_target_pairs={{16,0},{17,1},{18,2},{19,3},{20,4},{21,5},{22,6},{23,7},{24,8},{25... | collective-permute-start | bytes 1179656 | tf_op jit(solution)/shard_map/ppermute | solution.py:687
  122.5 24.0 %collective-permute-start.5 = (bf16[256,768]{1,0:T(8,128)(2,1)}, bf16[256,768]{1,0:T(8,128)(2,1)S(1)}, u32[]{:S(2)}, u32[]{:S(2)}) collective-permute-start(bf16[256,768]{1,0:T(8,128)(2,1)} %get-tuple-element.236), channel_id=1, source_target_pairs={{0,16},{1,17},{2,18},{3,19},{4,20},{5,21},{6,22},{7,23},{8,24},{9,... | collective-permute-start | bytes 1179656 | tf_op jit(solution)/shard_map/ppermute | solution.py:684
  123.8 69.7 %collective-permute-start.7 = (bf16[256,768]{1,0:T(8,128)(2,1)S(1)}, bf16[256,768]{1,0:T(8,128)(2,1)S(1)}, u32[]{:S(2)}, u32[]{:S(2)}) collective-permute-start(bf16[256,768]{1,0:T(8,128)(2,1)S(1)} %copy-done.36), channel_id=1, source_target_pairs={{0,16},{1,17},{2,18},{3,19},{4,20},{5,21},{6,22},{7,23},{8,24},{9,... | collective-permute-start | bytes 1179656 | tf_op jit(solution)/shard_map/ppermute | solution.py:684
  143.1 28.5 %collective-permute-start.6 = (bf16[256,768]{1,0:T(8,128)(2,1)}, bf16[256,768]{1,0:T(8,128)(2,1)S(1)}, u32[]{:S(2)}, u32[]{:S(2)}) collective-permute-start(bf16[256,768]{1,0:T(8,128)(2,1)} %get-tuple-element.245), channel_id=1, source_target_pairs={{16,0},{17,1},{18,2},{19,3},{20,4},{21,5},{22,6},{23,7},{24,8},{25... | collective-permute-start | bytes 1179656 | tf_op jit(solution)/shard_map/ppermute | solution.py:687
  170.3 36.7 %collective-permute-start.8 = (bf16[256,768]{1,0:T(8,128)(2,1)}, bf16[256,768]{1,0:T(8,128)(2,1)S(1)}, u32[]{:S(2)}, u32[]{:S(2)}) collective-permute-start(bf16[256,768]{1,0:T(8,128)(2,1)} %get-tuple-element.261), channel_id=1, source_target_pairs={{0,16},{1,17},{2,18},{3,19},{4,20},{5,21},{6,22},{7,23},{8,24},{9,... | collective-permute-start | bytes 1179656 | tf_op jit(solution)/shard_map/ppermute | solution.py:684
  189.9 30.9 %collective-permute-start.9 = (bf16[256,768]{1,0:T(8,128)(2,1)}, bf16[256,768]{1,0:T(8,128)(2,1)S(1)}, u32[]{:S(2)}, u32[]{:S(2)}) collective-permute-start(bf16[256,768]{1,0:T(8,128)(2,1)} %get-tuple-element.264), channel_id=1, source_target_pairs={{16,0},{17,1},{18,2},{19,3},{20,4},{21,5},{22,6},{23,7},{24,8},{25... | collective-permute-start | bytes 1179656 | tf_op jit(solution)/shard_map/ppermute | solution.py:687
  236.7 18.9 %collective-permute-start.10 = (bf16[1536,768]{1,0:T(8,128)(2,1)}, bf16[1536,768]{1,0:T(8,128)(2,1)}, u32[]{:S(2)}, u32[]{:S(2)}) collective-permute-start(bf16[1536,768]{1,0:T(8,128)(2,1)} %weight_half.4), channel_id=1, source_target_pairs={{0,4},{1,5},{2,6},{3,7},{4,0},{5,1},{6,2},{7,3},{8,12},{9,13},{10,... | collective-permute-start | bytes 7077896 | tf_op jit(solution)/shard_map/ppermute | solution.py:769
  252.9 22.9 %collective-permute-start.12 = (bf16[384,3072]{1,0:T(8,128)(2,1)}, bf16[384,3072]{1,0:T(8,128)(2,1)}, u32[]{:S(2)}, u32[]{:S(2)}) collective-permute-start(bf16[384,3072]{1,0:T(8,128)(2,1)} %weight_half.6), channel_id=1, source_target_pairs={{0,4},{1,5},{2,6},{3,7},{4,0},{5,1},{6,2},{7,3},{8,12},{9,13},{10,... | collective-permute-start | bytes 7077896 | tf_op jit(solution)/shard_map/ppermute | solution.py:769
  256.6 7.6 %collective-permute-start.11 = (bf16[192,768]{1,0:T(8,128)(2,1)S(1)}, bf16[192,768]{1,0:T(8,128)(2,1)S(1)}, u32[]{:S(2)}, u32[]{:S(2)}) collective-permute-start(bf16[192,768]{1,0:T(8,128)(2,1)S(1)} %fusion.24), channel_id=1, source_target_pairs={{0,1},{1,2},{2,3},{3,11},{11,10},{10,9},{9,8},{8,0},{12,13},{13,14... | collective-permute-start | bytes 884744 | tf_op jit(solution)/shard_map/ppermute | solution.py:601
  265.3 8.1 %collective-permute-start.14 = (bf16[192,768]{1,0:T(8,128)(2,1)S(1)}, bf16[192,768]{1,0:T(8,128)(2,1)S(1)}, u32[]{:S(2)}, u32[]{:S(2)}) collective-permute-start(bf16[192,768]{1,0:T(8,128)(2,1)S(1)} %fusion.23), channel_id=1, source_target_pairs={{0,1},{1,2},{2,3},{3,11},{11,10},{10,9},{9,8},{8,0},{12,13},{13,14... | collective-permute-start | bytes 884744 | tf_op jit(solution)/shard_map/ppermute | solution.py:601
  274.5 12.8 %collective-permute-start.15 = (bf16[192,768]{1,0:T(8,128)(2,1)S(1)}, bf16[192,768]{1,0:T(8,128)(2,1)S(1)}, u32[]{:S(2)}, u32[]{:S(2)}) collective-permute-start(bf16[192,768]{1,0:T(8,128)(2,1)S(1)} %fusion.22), channel_id=1, source_target_pairs={{0,1},{1,2},{2,3},{3,11},{11,10},{10,9},{9,8},{8,0},{12,13},{13,14... | collective-permute-start | bytes 884744 | tf_op jit(solution)/shard_map/ppermute | solution.py:601
  277.0 11.7 %collective-permute-start.13 = (bf16[48,3072]{1,0:T(8,128)(2,1)S(1)}, bf16[48,3072]{1,0:T(8,128)(2,1)S(1)}, u32[]{:S(2)}, u32[]{:S(2)}) collective-permute-start(bf16[48,3072]{1,0:T(8,128)(2,1)S(1)} %fusion.25), channel_id=1, source_target_pairs={{0,1},{1,2},{2,3},{3,11},{11,10},{10,9},{9,8},{8,0},{12,13},{13,14... | collective-permute-start | bytes 884744 | tf_op jit(solution)/shard_map/ppermute | solution.py:601
  285.7 28.8 %collective-permute-start.18 = (bf16[384,3072]{1,0:T(8,128)(2,1)}, bf16[384,3072]{1,0:T(8,128)(2,1)}, u32[]{:S(2)}, u32[]{:S(2)}) collective-permute-start(bf16[384,3072]{1,0:T(8,128)(2,1)} %weight_half_two.2), channel_id=1, source_target_pairs={{0,4},{1,5},{2,6},{3,7},{4,0},{5,1},{6,2},{7,3},{8,12},{9,13},{10,... | collective-permute-start | bytes 7077896 | tf_op jit(solution)/shard_map/ppermute | solution.py:769
  288.3 9.0 %collective-permute-start.17 = (bf16[192,768]{1,0:T(8,128)(2,1)S(1)}, bf16[192,768]{1,0:T(8,128)(2,1)S(1)}, u32[]{:S(2)}, u32[]{:S(2)}) collective-permute-start(bf16[192,768]{1,0:T(8,128)(2,1)S(1)} %fusion.21), channel_id=1, source_target_pairs={{0,1},{1,2},{2,3},{3,11},{11,10},{10,9},{9,8},{8,0},{12,13},{13,14... | collective-permute-start | bytes 884744 | tf_op jit(solution)/shard_map/ppermute | solution.py:601
  289.8 8.9 %collective-permute-start.16 = (bf16[48,3072]{1,0:T(8,128)(2,1)S(1)}, bf16[48,3072]{1,0:T(8,128)(2,1)S(1)}, u32[]{:S(2)}, u32[]{:S(2)}) collective-permute-start(bf16[48,3072]{1,0:T(8,128)(2,1)S(1)} %fusion.20), channel_id=1, source_target_pairs={{0,1},{1,2},{2,3},{3,11},{11,10},{10,9},{9,8},{8,0},{12,13},{13,14... | collective-permute-start | bytes 884744 | tf_op jit(solution)/shard_map/ppermute | solution.py:601
  298.5 13.5 %collective-permute-start.21 = (bf16[192,768]{1,0:T(8,128)(2,1)S(1)}, bf16[192,768]{1,0:T(8,128)(2,1)S(1)}, u32[]{:S(2)}, u32[]{:S(2)}) collective-permute-start(bf16[192,768]{1,0:T(8,128)(2,1)S(1)} %fusion.19), channel_id=1, source_target_pairs={{0,1},{1,2},{2,3},{3,11},{11,10},{10,9},{9,8},{8,0},{12,13},{13,14... | collective-permute-start | bytes 884744 | tf_op jit(solution)/shard_map/ppermute | solution.py:601
  300.6 13.8 %collective-permute-start.20 = (bf16[48,3072]{1,0:T(8,128)(2,1)}, bf16[48,3072]{1,0:T(8,128)(2,1)}, u32[]{:S(2)}, u32[]{:S(2)}) collective-permute-start(bf16[48,3072]{1,0:T(8,128)(2,1)} %fusion.18), channel_id=1, source_target_pairs={{0,1},{1,2},{2,3},{3,11},{11,10},{10,9},{9,8},{8,0},{12,13},{13,14... | collective-permute-start | bytes 884744 | tf_op jit(solution)/shard_map/ppermute | solution.py:601
  310.7 15.4 %collective-permute-start.22 = (bf16[256,768]{1,0:T(8,128)(2,1)}, bf16[256,768]{1,0:T(8,128)(2,1)S(1)}, u32[]{:S(2)}, u32[]{:S(2)}) collective-permute-start(bf16[256,768]{1,0:T(8,128)(2,1)} %get-tuple-element.300), channel_id=1, source_target_pairs={{0,16},{1,17},{2,18},{3,19},{4,20},{5,21},{6,22},{7,23},{8,24},{9,... | collective-permute-start | bytes 1179656 | tf_op jit(solution)/shard_map/ppermute | solution.py:684
  313.1 26.1 %collective-permute-start.25 = (bf16[192,768]{1,0:T(8,128)(2,1)S(1)}, bf16[192,768]{1,0:T(8,128)(2,1)S(1)}, u32[]{:S(2)}, u32[]{:S(2)}) collective-permute-start(bf16[192,768]{1,0:T(8,128)(2,1)S(1)} %fusion.17), channel_id=1, source_target_pairs={{0,1},{1,2},{2,3},{3,11},{11,10},{10,9},{9,8},{8,0},{12,13},{13,14... | collective-permute-start | bytes 884744 | tf_op jit(solution)/shard_map/ppermute | solution.py:601
  315.6 6.6 %collective-permute-start.19 = (bf16[48,3072]{1,0:T(8,128)(2,1)S(1)}, bf16[48,3072]{1,0:T(8,128)(2,1)S(1)}, u32[]{:S(2)}, u32[]{:S(2)}) collective-permute-start(bf16[48,3072]{1,0:T(8,128)(2,1)S(1)} %fusion.26), channel_id=1, source_target_pairs={{0,1},{1,2},{2,3},{3,11},{11,10},{10,9},{9,8},{8,0},{12,13},{13,14... | collective-permute-start | bytes 884744 | tf_op jit(solution)/shard_map/ppermute | solution.py:601
  318.9 23.4 %collective-permute-start.24 = (bf16[48,3072]{1,0:T(8,128)(2,1)}, bf16[48,3072]{1,0:T(8,128)(2,1)}, u32[]{:S(2)}, u32[]{:S(2)}) collective-permute-start(bf16[48,3072]{1,0:T(8,128)(2,1)} %fusion.16), channel_id=1, source_target_pairs={{0,1},{1,2},{2,3},{3,11},{11,10},{10,9},{9,8},{8,0},{12,13},{13,14... | collective-permute-start | bytes 884744 | tf_op jit(solution)/shard_map/ppermute | solution.py:601
  324.0 22.9 %collective-permute-start.23 = (bf16[48,3072]{1,0:T(8,128)(2,1)}, bf16[48,3072]{1,0:T(8,128)(2,1)}, u32[]{:S(2)}, u32[]{:S(2)}) collective-permute-start(bf16[48,3072]{1,0:T(8,128)(2,1)} %fusion.15), channel_id=1, source_target_pairs={{0,1},{1,2},{2,3},{3,11},{11,10},{10,9},{9,8},{8,0},{12,13},{13,14... | collective-permute-start | bytes 884744 | tf_op jit(solution)/shard_map/ppermute | solution.py:601
  341.0 27.9 %collective-permute-start.30 = (bf16[192,768]{1,0:T(8,128)(2,1)}, bf16[192,768]{1,0:T(8,128)(2,1)S(1)}, u32[]{:S(2)}, u32[]{:S(2)}) collective-permute-start(bf16[192,768]{1,0:T(8,128)(2,1)} %fusion.14), channel_id=1, source_target_pairs={{0,1},{1,2},{2,3},{3,11},{11,10},{10,9},{9,8},{8,0},{12,13},{13,14... | collective-permute-start | bytes 884744 | tf_op jit(solution)/shard_map/ppermute | solution.py:601
  344.3 11.0 %collective-permute-start.26 = (bf16[256,768]{1,0:T(8,128)(2,1)}, bf16[256,768]{1,0:T(8,128)(2,1)S(1)}, u32[]{:S(2)}, u32[]{:S(2)}) collective-permute-start(bf16[256,768]{1,0:T(8,128)(2,1)} %get-tuple-element.306), channel_id=1, source_target_pairs={{0,16},{1,17},{2,18},{3,19},{4,20},{5,21},{6,22},{7,23},{8,24},{9,... | collective-permute-start | bytes 1179656 | tf_op jit(solution)/shard_map/ppermute | solution.py:684
  345.6 29.1 %collective-permute-start.29 = (bf16[48,3072]{1,0:T(8,128)(2,1)}, bf16[48,3072]{1,0:T(8,128)(2,1)}, u32[]{:S(2)}, u32[]{:S(2)}) collective-permute-start(bf16[48,3072]{1,0:T(8,128)(2,1)} %fusion.13), channel_id=1, source_target_pairs={{0,1},{1,2},{2,3},{3,11},{11,10},{10,9},{9,8},{8,0},{12,13},{13,14... | collective-permute-start | bytes 884744 | tf_op jit(solution)/shard_map/ppermute | solution.py:601
  348.2 28.9 %collective-permute-start.28 = (bf16[48,3072]{1,0:T(8,128)(2,1)S(1)}, bf16[48,3072]{1,0:T(8,128)(2,1)}, u32[]{:S(2)}, u32[]{:S(2)}) collective-permute-start(bf16[48,3072]{1,0:T(8,128)(2,1)S(1)} %fusion.12), channel_id=1, source_target_pairs={{0,1},{1,2},{2,3},{3,11},{11,10},{10,9},{9,8},{8,0},{12,13},{13,14... | collective-permute-start | bytes 884744 | tf_op jit(solution)/shard_map/ppermute | solution.py:601
  372.3 9.0 %collective-permute-start.34 = (bf16[192,768]{1,0:T(8,128)(2,1)S(1)}, bf16[192,768]{1,0:T(8,128)(2,1)S(1)}, u32[]{:S(2)}, u32[]{:S(2)}) collective-permute-start(bf16[192,768]{1,0:T(8,128)(2,1)S(1)} %get-tuple-element.347), channel_id=1, source_target_pairs={{0,1},{1,2},{2,3},{3,11},{11,10},{10,9},{9,8},{8,0},{12,13},{13,14... | collective-permute-start | bytes 884744 | tf_op jit(solution)/shard_map/ppermute | solution.py:601
  377.0 6.4 %collective-permute-start.33 = (bf16[48,3072]{1,0:T(8,128)(2,1)}, bf16[48,3072]{1,0:T(8,128)(2,1)S(1)}, u32[]{:S(2)}, u32[]{:S(2)}) collective-permute-start(bf16[48,3072]{1,0:T(8,128)(2,1)} %fusion.10), channel_id=1, source_target_pairs={{0,1},{1,2},{2,3},{3,11},{11,10},{10,9},{9,8},{8,0},{12,13},{13,14... | collective-permute-start | bytes 884744 | tf_op jit(solution)/shard_map/ppermute | solution.py:601
  378.3 8.3 %collective-permute-start.32 = (bf16[48,3072]{1,0:T(8,128)(2,1)S(1)}, bf16[48,3072]{1,0:T(8,128)(2,1)S(1)}, u32[]{:S(2)}, u32[]{:S(2)}) collective-permute-start(bf16[48,3072]{1,0:T(8,128)(2,1)S(1)} %fusion.9), channel_id=1, source_target_pairs={{0,1},{1,2},{2,3},{3,11},{11,10},{10,9},{9,8},{8,0},{12,13},{13,14... | collective-permute-start | bytes 884744 | tf_op jit(solution)/shard_map/ppermute | solution.py:601
  380.3 8.5 %collective-permute-start.31 = (f32[20,768]{1,0:T(8,128)S(1)}, f32[20,768]{1,0:T(8,128)S(1)}, u32[]{:S(2)}, u32[]{:S(2)}) collective-permute-start(f32[20,768]{1,0:T(8,128)S(1)} %collective-permute-done.27), channel_id=1, source_target_pairs={{0,1},{1,2},{2,3},{3,11},{11,10},{10,9},{9,8},{8,0},{12,13},{13,14... | collective-permute-start | bytes 184328 | tf_op jit(solution)/shard_map/ppermute | solution.py:629
  381.3 9.2 %collective-permute-start.38 = (bf16[192,768]{1,0:T(8,128)(2,1)S(1)}, bf16[192,768]{1,0:T(8,128)(2,1)S(1)}, u32[]{:S(2)}, u32[]{:S(2)}) collective-permute-start(bf16[192,768]{1,0:T(8,128)(2,1)S(1)} %collective-permute-done.34), channel_id=1, source_target_pairs={{0,1},{1,2},{2,3},{3,11},{11,10},{10,9},{9,8},{8,0},{12,13},{13,14... | collective-permute-start | bytes 884744 | tf_op jit(solution)/shard_map/ppermute | solution.py:601
  384.6 9.1 %collective-permute-start.37 = (bf16[48,3072]{1,0:T(8,128)(2,1)S(1)}, bf16[48,3072]{1,0:T(8,128)(2,1)S(1)}, u32[]{:S(2)}, u32[]{:S(2)}) collective-permute-start(bf16[48,3072]{1,0:T(8,128)(2,1)S(1)} %fusion.8), channel_id=1, source_target_pairs={{0,1},{1,2},{2,3},{3,11},{11,10},{10,9},{9,8},{8,0},{12,13},{13,14... | collective-permute-start | bytes 884744 | tf_op jit(solution)/shard_map/ppermute | solution.py:601
  387.7 9.3 %collective-permute-start.36 = (bf16[48,3072]{1,0:T(8,128)(2,1)S(1)}, bf16[48,3072]{1,0:T(8,128)(2,1)S(1)}, u32[]{:S(2)}, u32[]{:S(2)}) collective-permute-start(bf16[48,3072]{1,0:T(8,128)(2,1)S(1)} %fusion.7), channel_id=1, source_target_pairs={{0,1},{1,2},{2,3},{3,11},{11,10},{10,9},{9,8},{8,0},{12,13},{13,14... | collective-permute-start | bytes 884744 | tf_op jit(solution)/shard_map/ppermute | solution.py:601
  388.8 10.3 %collective-permute-start.35 = (f32[20,768]{1,0:T(8,128)S(1)}, f32[20,768]{1,0:T(8,128)S(1)}, u32[]{:S(2)}, u32[]{:S(2)}) collective-permute-start(f32[20,768]{1,0:T(8,128)S(1)} %collective-permute-done.31), channel_id=1, source_target_pairs={{0,1},{1,2},{2,3},{3,11},{11,10},{10,9},{9,8},{8,0},{12,13},{13,14... | collective-permute-start | bytes 184328 | tf_op jit(solution)/shard_map/ppermute | solution.py:629
  390.5 10.3 %collective-permute-start.42 = (bf16[192,768]{1,0:T(8,128)(2,1)S(1)}, bf16[192,768]{1,0:T(8,128)(2,1)S(1)}, u32[]{:S(2)}, u32[]{:S(2)}) collective-permute-start(bf16[192,768]{1,0:T(8,128)(2,1)S(1)} %collective-permute-done.38), channel_id=1, source_target_pairs={{0,1},{1,2},{2,3},{3,11},{11,10},{10,9},{9,8},{8,0},{12,13},{13,14... | collective-permute-start | bytes 884744 | tf_op jit(solution)/shard_map/ppermute | solution.py:601
  395.1 8.8 %collective-permute-start.41 = (bf16[48,3072]{1,0:T(8,128)(2,1)S(1)}, bf16[48,3072]{1,0:T(8,128)(2,1)S(1)}, u32[]{:S(2)}, u32[]{:S(2)}) collective-permute-start(bf16[48,3072]{1,0:T(8,128)(2,1)S(1)} %get-tuple-element.349), channel_id=1, source_target_pairs={{0,1},{1,2},{2,3},{3,11},{11,10},{10,9},{9,8},{8,0},{12,13},{13,14... | collective-permute-start | bytes 884744 | tf_op jit(solution)/shard_map/ppermute | solution.py:601
  398.1 9.1 %collective-permute-start.40 = (bf16[48,3072]{1,0:T(8,128)(2,1)S(1)}, bf16[48,3072]{1,0:T(8,128)(2,1)S(1)}, u32[]{:S(2)}, u32[]{:S(2)}) collective-permute-start(bf16[48,3072]{1,0:T(8,128)(2,1)S(1)} %fusion.5), channel_id=1, source_target_pairs={{0,1},{1,2},{2,3},{3,11},{11,10},{10,9},{9,8},{8,0},{12,13},{13,14... | collective-permute-start | bytes 884744 | tf_op jit(solution)/shard_map/ppermute | solution.py:601
  399.1 10.3 %collective-permute-start.39 = (f32[20,768]{1,0:T(8,128)S(1)}, f32[20,768]{1,0:T(8,128)S(1)}, u32[]{:S(2)}, u32[]{:S(2)}) collective-permute-start(f32[20,768]{1,0:T(8,128)S(1)} %collective-permute-done.35), channel_id=1, source_target_pairs={{0,1},{1,2},{2,3},{3,11},{11,10},{10,9},{9,8},{8,0},{12,13},{13,14... | collective-permute-start | bytes 184328 | tf_op jit(solution)/shard_map/ppermute | solution.py:629
  400.8 10.3 %collective-permute-start.46 = (bf16[192,768]{1,0:T(8,128)(2,1)S(1)}, bf16[192,768]{1,0:T(8,128)(2,1)S(1)}, u32[]{:S(2)}, u32[]{:S(2)}) collective-permute-start(bf16[192,768]{1,0:T(8,128)(2,1)S(1)} %collective-permute-done.42), channel_id=1, source_target_pairs={{0,1},{1,2},{2,3},{3,11},{11,10},{10,9},{9,8},{8,0},{12,13},{13,14... | collective-permute-start | bytes 884744 | tf_op jit(solution)/shard_map/ppermute | solution.py:601
  404.0 10.3 %collective-permute-start.45 = (bf16[48,3072]{1,0:T(8,128)(2,1)S(1)}, bf16[48,3072]{1,0:T(8,128)(2,1)S(1)}, u32[]{:S(2)}, u32[]{:S(2)}) collective-permute-start(bf16[48,3072]{1,0:T(8,128)(2,1)S(1)} %collective-permute-done.41), channel_id=1, source_target_pairs={{0,1},{1,2},{2,3},{3,11},{11,10},{10,9},{9,8},{8,0},{12,13},{13,14... | collective-permute-start | bytes 884744 | tf_op jit(solution)/shard_map/ppermute | solution.py:601
  408.2 9.2 %collective-permute-start.44 = (bf16[48,3072]{1,0:T(8,128)(2,1)S(1)}, bf16[48,3072]{1,0:T(8,128)(2,1)S(1)}, u32[]{:S(2)}, u32[]{:S(2)}) collective-permute-start(bf16[48,3072]{1,0:T(8,128)(2,1)S(1)} %fusion.4), channel_id=1, source_target_pairs={{0,1},{1,2},{2,3},{3,11},{11,10},{10,9},{9,8},{8,0},{12,13},{13,14... | collective-permute-start | bytes 884744 | tf_op jit(solution)/shard_map/ppermute | solution.py:601
  409.3 10.6 %collective-permute-start.43 = (f32[20,768]{1,0:T(8,128)S(1)}, f32[20,768]{1,0:T(8,128)S(1)}, u32[]{:S(2)}, u32[]{:S(2)}) collective-permute-start(f32[20,768]{1,0:T(8,128)S(1)} %collective-permute-done.39), channel_id=1, source_target_pairs={{0,1},{1,2},{2,3},{3,11},{11,10},{10,9},{9,8},{8,0},{12,13},{13,14... | collective-permute-start | bytes 184328 | tf_op jit(solution)/shard_map/ppermute | solution.py:629
  411.1 10.3 %collective-permute-start.50 = (bf16[192,768]{1,0:T(8,128)(2,1)S(1)}, bf16[192,768]{1,0:T(8,128)(2,1)S(1)}, u32[]{:S(2)}, u32[]{:S(2)}) collective-permute-start(bf16[192,768]{1,0:T(8,128)(2,1)S(1)} %collective-permute-done.46), channel_id=1, source_target_pairs={{0,1},{1,2},{2,3},{3,11},{11,10},{10,9},{9,8},{8,0},{12,13},{13,14... | collective-permute-start | bytes 884744 | tf_op jit(solution)/shard_map/ppermute | solution.py:601
  414.2 10.3 %collective-permute-start.49 = (bf16[48,3072]{1,0:T(8,128)(2,1)S(1)}, bf16[48,3072]{1,0:T(8,128)(2,1)S(1)}, u32[]{:S(2)}, u32[]{:S(2)}) collective-permute-start(bf16[48,3072]{1,0:T(8,128)(2,1)S(1)} %collective-permute-done.45), channel_id=1, source_target_pairs={{0,1},{1,2},{2,3},{3,11},{11,10},{10,9},{9,8},{8,0},{12,13},{13,14... | collective-permute-start | bytes 884744 | tf_op jit(solution)/shard_map/ppermute | solution.py:601
  418.8 8.9 %collective-permute-start.48 = (bf16[48,3072]{1,0:T(8,128)(2,1)S(1)}, bf16[48,3072]{1,0:T(8,128)(2,1)S(1)}, u32[]{:S(2)}, u32[]{:S(2)}) collective-permute-start(bf16[48,3072]{1,0:T(8,128)(2,1)S(1)} %get-tuple-element.351), channel_id=1, source_target_pairs={{0,1},{1,2},{2,3},{3,11},{11,10},{10,9},{9,8},{8,0},{12,13},{13,14... | collective-permute-start | bytes 884744 | tf_op jit(solution)/shard_map/ppermute | solution.py:601
  419.9 8.8 %collective-permute-start.47 = (f32[20,768]{1,0:T(8,128)S(1)}, f32[20,768]{1,0:T(8,128)S(1)}, u32[]{:S(2)}, u32[]{:S(2)}) collective-permute-start(f32[20,768]{1,0:T(8,128)S(1)} %collective-permute-done.43), channel_id=1, source_target_pairs={{0,1},{1,2},{2,3},{3,11},{11,10},{10,9},{9,8},{8,0},{12,13},{13,14... | collective-permute-start | bytes 184328 | tf_op jit(solution)/shard_map/ppermute | solution.py:629
  421.3 10.3 %collective-permute-start.54 = (bf16[192,768]{1,0:T(8,128)(2,1)S(1)}, bf16[192,768]{1,0:T(8,128)(2,1)S(1)}, u32[]{:S(2)}, u32[]{:S(2)}) collective-permute-start(bf16[192,768]{1,0:T(8,128)(2,1)S(1)} %collective-permute-done.50), channel_id=1, source_target_pairs={{0,1},{1,2},{2,3},{3,11},{11,10},{10,9},{9,8},{8,0},{12,13},{13,14... | collective-permute-start | bytes 884744 | tf_op jit(solution)/shard_map/ppermute | solution.py:601
  424.5 10.3 %collective-permute-start.53 = (bf16[48,3072]{1,0:T(8,128)(2,1)S(1)}, bf16[48,3072]{1,0:T(8,128)(2,1)S(1)}, u32[]{:S(2)}, u32[]{:S(2)}) collective-permute-start(bf16[48,3072]{1,0:T(8,128)(2,1)S(1)} %collective-permute-done.49), channel_id=1, source_target_pairs={{0,1},{1,2},{2,3},{3,11},{11,10},{10,9},{9,8},{8,0},{12,13},{13,14... | collective-permute-start | bytes 884744 | tf_op jit(solution)/shard_map/ppermute | solution.py:601
  427.7 10.3 %collective-permute-start.52 = (bf16[48,3072]{1,0:T(8,128)(2,1)S(1)}, bf16[48,3072]{1,0:T(8,128)(2,1)S(1)}, u32[]{:S(2)}, u32[]{:S(2)}) collective-permute-start(bf16[48,3072]{1,0:T(8,128)(2,1)S(1)} %collective-permute-done.48), channel_id=1, source_target_pairs={{0,1},{1,2},{2,3},{3,11},{11,10},{10,9},{9,8},{8,0},{12,13},{13,14... | collective-permute-start | bytes 884744 | tf_op jit(solution)/shard_map/ppermute | solution.py:601
  428.7 10.3 %collective-permute-start.51 = (f32[20,768]{1,0:T(8,128)S(1)}, f32[20,768]{1,0:T(8,128)S(1)}, u32[]{:S(2)}, u32[]{:S(2)}) collective-permute-start(f32[20,768]{1,0:T(8,128)S(1)} %collective-permute-done.47), channel_id=1, source_target_pairs={{0,1},{1,2},{2,3},{3,11},{11,10},{10,9},{9,8},{8,0},{12,13},{13,14... | collective-permute-start | bytes 184328 | tf_op jit(solution)/shard_map/ppermute | solution.py:629
  431.6 10.3 %collective-permute-start.58 = (bf16[192,768]{1,0:T(8,128)(2,1)S(1)}, bf16[192,768]{1,0:T(8,128)(2,1)S(1)}, u32[]{:S(2)}, u32[]{:S(2)}) collective-permute-start(bf16[192,768]{1,0:T(8,128)(2,1)S(1)} %collective-permute-done.54), channel_id=1, source_target_pairs={{0,1},{1,2},{2,3},{3,11},{11,10},{10,9},{9,8},{8,0},{12,13},{13,14... | collective-permute-start | bytes 884744 | tf_op jit(solution)/shard_map/ppermute | solution.py:601
  434.8 10.3 %collective-permute-start.57 = (bf16[48,3072]{1,0:T(8,128)(2,1)S(1)}, bf16[48,3072]{1,0:T(8,128)(2,1)S(1)}, u32[]{:S(2)}, u32[]{:S(2)}) collective-permute-start(bf16[48,3072]{1,0:T(8,128)(2,1)S(1)} %collective-permute-done.53), channel_id=1, source_target_pairs={{0,1},{1,2},{2,3},{3,11},{11,10},{10,9},{9,8},{8,0},{12,13},{13,14... | collective-permute-start | bytes 884744 | tf_op jit(solution)/shard_map/ppermute | solution.py:601
  437.9 10.3 %collective-permute-start.56 = (bf16[48,3072]{1,0:T(8,128)(2,1)S(1)}, bf16[48,3072]{1,0:T(8,128)(2,1)S(1)}, u32[]{:S(2)}, u32[]{:S(2)}) collective-permute-start(bf16[48,3072]{1,0:T(8,128)(2,1)S(1)} %collective-permute-done.52), channel_id=1, source_target_pairs={{0,1},{1,2},{2,3},{3,11},{11,10},{10,9},{9,8},{8,0},{12,13},{13,14... | collective-permute-start | bytes 884744 | tf_op jit(solution)/shard_map/ppermute | solution.py:601
  439.5 14.1 %collective-permute-start.55 = (f32[8,20,768]{2,0,1:T(8,128)S(1)}, f32[8,20,768]{2,0,1:T(8,128)S(1)}, u32[]{:S(2)}, u32[]{:S(2)}) collective-permute-start(f32[8,20,768]{2,0,1:T(8,128)S(1)} %copy.156), channel_id=1, source_target_pairs={{0,4},{1,5},{2,6},{3,7},{4,0},{5,1},{6,2},{7,3},{8,12},{9,13},{10,... | collective-permute-start | bytes 1474568 | tf_op jit(solution)/shard_map/ppermute | solution.py:636
  442.6 38.5 %collective-permute-start.67 = (bf16[1536,768]{1,0:T(8,128)(2,1)}, bf16[1536,768]{1,0:T(8,128)(2,1)}, u32[]{:S(2)}, u32[]{:S(2)}) collective-permute-start(bf16[1536,768]{1,0:T(8,128)(2,1)} %bitcast.95), channel_id=1, source_target_pairs={{0,4},{1,5},{2,6},{3,7},{4,0},{5,1},{6,2},{7,3},{8,12},{9,13},{10,... | collective-permute-start | bytes 7077896 | tf_op jit(solution)/shard_map/ppermute | solution.py:613
  445.0 6.4 %collective-permute-start.60 = (bf16[48,3072]{1,0:T(8,128)(2,1)S(1)}, bf16[48,3072]{1,0:T(8,128)(2,1)}, u32[]{:S(2)}, u32[]{:S(2)}) collective-permute-start(bf16[48,3072]{1,0:T(8,128)(2,1)S(1)} %collective-permute-done.57), channel_id=1, source_target_pairs={{0,1},{1,2},{2,3},{3,11},{11,10},{10,9},{9,8},{8,0},{12,13},{13,14... | collective-permute-start | bytes 884744 | tf_op jit(solution)/shard_map/ppermute | solution.py:601
  448.2 10.4 %collective-permute-start.59 = (bf16[48,3072]{1,0:T(8,128)(2,1)S(1)}, bf16[48,3072]{1,0:T(8,128)(2,1)S(1)}, u32[]{:S(2)}, u32[]{:S(2)}) collective-permute-start(bf16[48,3072]{1,0:T(8,128)(2,1)S(1)} %collective-permute-done.56), channel_id=1, source_target_pairs={{0,1},{1,2},{2,3},{3,11},{11,10},{10,9},{9,8},{8,0},{12,13},{13,14... | collective-permute-start | bytes 884744 | tf_op jit(solution)/shard_map/ppermute | solution.py:601
  451.5 7.5 %collective-permute-start.62 = (bf16[48,3072]{1,0:T(8,128)(2,1)}, bf16[48,3072]{1,0:T(8,128)(2,1)}, u32[]{:S(2)}, u32[]{:S(2)}) collective-permute-start(bf16[48,3072]{1,0:T(8,128)(2,1)} %collective-permute-done.60), channel_id=1, source_target_pairs={{0,1},{1,2},{2,3},{3,11},{11,10},{10,9},{9,8},{8,0},{12,13},{13,14... | collective-permute-start | bytes 884744 | tf_op jit(solution)/shard_map/ppermute | solution.py:601
  460.6 30.1 %collective-permute-start.66 = (bf16[384,3072]{1,0:T(8,128)(2,1)}, bf16[384,3072]{1,0:T(8,128)(2,1)S(1)}, u32[]{:S(2)}, u32[]{:S(2)}) collective-permute-start(bf16[384,3072]{1,0:T(8,128)(2,1)} %bitcast.275), channel_id=1, source_target_pairs={{0,4},{1,5},{2,6},{3,7},{4,0},{5,1},{6,2},{7,3},{8,12},{9,13},{10,... | collective-permute-start | bytes 7077896 | tf_op jit(solution)/shard_map/ppermute | solution.py:613
  475.6 21.0 %collective-permute-start.65 = (bf16[384,3072]{1,0:T(8,128)(2,1)S(1)}, bf16[384,3072]{1,0:T(8,128)(2,1)S(1)}, u32[]{:S(2)}, u32[]{:S(2)}) collective-permute-start(bf16[384,3072]{1,0:T(8,128)(2,1)S(1)} %bitcast.273), channel_id=1, source_target_pairs={{0,4},{1,5},{2,6},{3,7},{4,0},{5,1},{6,2},{7,3},{8,12},{9,13},{10,... | collective-permute-start | bytes 7077896 | tf_op jit(solution)/shard_map/ppermute | solution.py:613
  (42 other events, 296.1 us)

commit v3 on v2

v3 whole, which is shorter than its diff:
```python
import functools
import math

import jax
import jax.numpy as jnp
from jax import lax
from jax.experimental import pallas as pl
from jax.experimental.pallas import tpu as pltpu
from jax.sharding import PartitionSpec as P

HEAD = 64
EPS = 1e-06
NEG = -1000000000.0
VMEM_LIMIT = 16 * 1024 * 1024
HELD_CROPS = 3
HELD_LIMIT = 10 * 1024 * 1024
PASS_LIMIT = 22 * 1024 * 1024
NT = (((1,), (1,)), ((), ()))
TN = (((0,), (0,)), ((), ()))
F32 = jnp.float32
BF16 = jnp.bfloat16
ANY = pl.BlockSpec(memory_space=pl.ANY)
SMEM = pl.BlockSpec(memory_space=pltpu.SMEM)


def mm(left, right, dims=(((1,), (0,)), ((), ()))):
    return lax.dot_general(left, right, dims, preferred_element_type=F32)


def row_variants(crop_len):
    return [crop_len]


def gelu_pair(values):
    cdf = 0.5 + 0.5 * lax.erf(values * (2.0**-0.5))
    density = jnp.exp(-0.5 * values * values) * (2.0 * math.pi) ** -0.5
    return values * cdf, cdf + values * density


def norm_forward(hidden):
    centred = hidden - jnp.mean(hidden, -1, keepdims=True)
    inverse = lax.rsqrt(jnp.mean(centred * centred, -1, keepdims=True) + EPS)
    return centred * inverse, inverse


def norm_backward(scaled, normed, inverse):
    return (
        scaled
        - jnp.mean(scaled, -1, keepdims=True)
        - normed * jnp.mean(scaled * normed, -1, keepdims=True)
    ) * inverse


def dispatch(length, crop_len, body):
    lower = 0
    for rows in row_variants(crop_len):
        pl.when((length > lower) & (length <= rows))(functools.partial(body, rows))
        lower = rows


VMEM_NAMES = ("qkv", "n1", "gp", "n2", "inv")
HBM_NAMES = ("att", "xs", "mix", "low", "act")


def save_shapes(crops, crop_len, width, hidden):
    heads = width // HEAD
    held = min(HELD_CROPS, crops)
    return {
        "qkv": ((held, crop_len, 3 * width), BF16),
        "att": ((crops + 1, heads, crop_len, crop_len), BF16),
        "n1": ((held, crop_len, width), BF16),
        "gp": ((held, crop_len, hidden), BF16),
        "n2": ((held, crop_len, width), BF16),
        "inv": ((held, crop_len, 128), F32),
        "xs": ((crops + 1, crop_len, width), BF16),
        "mix": ((crops + 1, crop_len, width), BF16),
        "low": ((crops + 1, crop_len, width), BF16),
        "act": ((crops + 1, crop_len, hidden), BF16),
    }


VMEM = pl.BlockSpec(memory_space=pltpu.VMEM)


def in_hbm(*values):
    return [pltpu.with_memory_space_constraint(value, pltpu.HBM) for value in values]


def in_vmem(*values):
    return [pltpu.with_memory_space_constraint(value, pltpu.VMEM) for value in values]


def each_lagged(count, first, second, third):
    ahead, waiting = first(0), None
    for number in range(count):
        current, ahead = ahead, first(number + 1) if number + 1 < count else None
        if waiting is not None:
            third(*waiting)
        waiting = (number, second(number, current))
    third(*waiting)


def assigned(crops, query_lengths, key_lengths):
    section = lax.axis_index("section")
    member = jnp.where(section == 0, crops[0][0], crops[1][0])
    crop = jnp.where(section == 0, crops[0][1], crops[1][1])
    live = crop >= 0
    crop = jnp.maximum(crop, 0)
    return section, live, member, crop, jnp.where(member == 0, query_lengths[crop], key_lengths[crop])


def head_masks():
    lane = lax.broadcasted_iota(jnp.int32, (1, 2 * HEAD), 1)
    return lane < HEAD, lane >= HEAD


def forward_kernel(mode, crops, first, n_alias, query_lengths, key_lengths, own, *refs):
    refs = list(refs)
    take = lambda count: [refs.pop(0) for _ in range(count)]
    recv = None if first else take(1)[0]
    weights = take(4)
    bup, biases, gains = take(3)
    take(n_alias)
    y_ref, pool_ref = take(2)
    save = mode != "pass"
    kept = dict(zip(VMEM_NAMES + HBM_NAMES, take(10))) if save else {}
    if mode == "held":
        held = weights
    else:
        held = take(4)
    if not save:
        kept["qkv"] = take(1)[0]
    batt = take(1)[0] if save else None
    bx, bmix, blow, bact, wsem, xsem, osem = refs
    wqkv, wout, wup, wdown = held
    crop_len, width = bx.shape
    hidden = bact.shape[1]
    heads = width // HEAD
    base = hidden // width
    section, live, member, crop, length = assigned(crops, query_lengths, key_lengths)
    which = member if save else 0
    place = jnp.where(member == 0, lax.rem(crop, HELD_CROPS), 1) if save else 0

    loaded = crops[0][0]

    def weight_copy(number):
        target = held[number].at[loaded if save else 0]
        return pltpu.make_async_copy(weights[number].at[0, loaded if save else 1], target, wsem.at[number])

    def weight_ready(number):
        if mode != "held":
            weight_copy(number).wait()

    def bias(row):
        return biases[0, member, row : row + 1, :]

    def gain(row):
        return gains[0, member, row : row + 1, :]

    def rise_bias(cols):
        return jnp.where(member == 0, bup[0, 0:1, cols], bup[0, 1:2, cols])

    def body(rows):
        keys = -(-rows // 128) * 128
        qkv = kept["qkv"]
        started = []

        def clear(ref, *index):
            if rows < crop_len:
                ref[(*index, slice(rows, crop_len))] = jnp.zeros((crop_len - rows, ref.shape[-1]), ref.dtype)

        def finish(number, name, buffer):
            if name != "att":
                clear(buffer)
            if save:
                slot = jnp.where(member == 0, crop, kept[name].shape[0] - 1)
                copy = pltpu.make_async_copy(buffer, kept[name].at[slot], osem.at[number])
                copy.start()
                started.append(copy)

        x = bx[:rows, :]
        finish(0, "xs", bx)
        weight_ready(0)
        for segment in range(3):
            cols = slice(segment * width, (segment + 1) * width)
            part = mm(x, wqkv[which, :, cols])
            if segment != 1:
                part = part + bias(segment // 2)
            qkv[place, :rows, cols] = part.astype(BF16)
        clear(qkv, place)
        masks = head_masks()
        key_valid = lax.broadcasted_iota(jnp.int32, (1, keys), 1) < length
        mixed = [None]

        def pair(part, head, row_count):
            start = part * width + head // 2 * 2 * HEAD
            return qkv[place, :row_count, start : start + 2 * HEAD]

        def score(head):
            return mm(pair(0, head, rows), jnp.where(masks[head % 2], pair(1, head, keys), 0), NT)

        def soften(head, scores):
            scores = jnp.where(key_valid, scores * HEAD**-0.5, NEG)
            weight = jnp.exp(scores - jnp.max(scores, -1, keepdims=True))
            weight = (weight * (1.0 / jnp.sum(weight, -1, keepdims=True))).astype(BF16)
            if save:
                batt[head, :rows, :keys] = weight
            return weight

        def mix(head, weight):
            part = mm(weight, jnp.where(masks[head % 2], pair(2, head, keys), 0))
            if head % 2 == 0:
                mixed[0] = part
            else:
                start = head // 2 * 2 * HEAD
                bmix[:rows, start : start + 2 * HEAD] = (mixed[0] + part).astype(BF16)

        each_lagged(heads, score, soften, mix)
        if save:
            finish(4, "att", batt)
        finish(1, "mix", bmix)
        weight_ready(1)
        attended = mm(bmix[:rows, :], wout[which]) + bias(2)
        n1, inv1 = norm_forward(x.astype(F32) + attended)
        after = n1 * gain(0) + bias(3)
        low = after.astype(BF16)
        blow[:rows, :] = low
        finish(2, "low", blow)
        weight_ready(2)
        weight_ready(3)
        branch = [after + bias(4)]

        def cols(part):
            return slice(part * width, (part + 1) * width)

        def rise(part):
            return mm(low, wup[which, :, cols(part)]) + rise_bias(cols(part))

        def activate(part, pre):
            act, slope = gelu_pair(pre)
            act = act.astype(BF16)
            bact[:rows, cols(part)] = act
            if save:
                kept["gp"][place, :rows, cols(part)] = slope.astype(BF16)
            return act

        def fall(part, act):
            branch[0] = branch[0] + mm(act, wdown[which, cols(part), :])

        each_lagged(base, rise, activate, fall)
        finish(3, "act", bact)
        n2, inv2 = norm_forward(branch[0])
        out = n2 * gain(1) + bias(5)
        y_ref[:rows, :] = out.astype(BF16)
        clear(y_ref)
        valid = lax.broadcasted_iota(jnp.int32, (rows, 1), 0) < length
        total = jnp.sum(jnp.where(valid, out, 0.0), 0, keepdims=True)
        pool_ref[...] = total / length.astype(F32)
        if save:
            kept["n1"][place, :rows, :] = n1.astype(BF16)
            kept["n2"][place, :rows, :] = n2.astype(BF16)
            wide = lax.broadcasted_iota(jnp.int32, (1, 128), 1)
            kept["inv"][place, :rows, :] = jnp.where(wide == 0, inv1, inv2)
        for copy in started:
            copy.wait()

    @pl.when(live)
    def _():
        @pl.when(section == 0)
        def _():
            copy = pltpu.make_async_copy(own.at[crop], bx, xsem)
            copy.start()

        if mode != "held":
            for number in range(4):
                weight_copy(number).start()

        @pl.when(section == 0)
        def _():
            pltpu.make_async_copy(own.at[crop], bx, xsem).wait()

        if recv is not None:

            @pl.when(section != 0)
            def _():
                bx[...] = recv[...]

        dispatch(length, crop_len, body)

    if mode == "load":

        @pl.when(jnp.logical_not(live))
        def _():
            for number in range(4):
                weight_copy(number).start()
            for number in range(4):
                weight_copy(number).wait()


def forward_call(mode, lengths, crops, own, recv, weights, held, state, order=()):
    crop_count, crop_len, width = own.shape
    hidden = weights[2].shape[-1]
    shapes = save_shapes(crop_count, crop_len, width, hidden)
    names = VMEM_NAMES + HBM_NAMES if mode != "pass" else ()
    pinned = lambda name, value: (in_vmem if name in VMEM_NAMES else in_hbm)(value)[0]
    aliased = [pinned(name, state[name]) for name in names] if state else []
    order = list(order)
    arrived = [] if recv is None else [recv]
    read = in_vmem(*held) if mode == "held" else in_hbm(*weights[:4])
    grown = in_vmem(*held) if mode == "load" and held else []
    operands = [*lengths, *in_hbm(own), *arrived, *read, *weights[4:], *order, *aliased, *grown]
    first = 10 + len(arrived) + len(order)
    shape_of = lambda name: (pltpu.VMEM if name in VMEM_NAMES else pltpu.HBM)(*shapes[name])
    spec_of = lambda name: VMEM if name in VMEM_NAMES else ANY
    copies = 1 if mode == "pass" else 2
    weight_shapes = [pltpu.VMEM((copies, *weight.shape[2:]), BF16) for weight in weights[:4]]
    outs = pl.pallas_call(
        functools.partial(forward_kernel, mode, crops, recv is None, len(order) + len(aliased) + len(grown)),
        out_shape=[
            jax.ShapeDtypeStruct((crop_len, width), BF16),
            jax.ShapeDtypeStruct((1, width), F32),
        ]
        + [shape_of(name) for name in names]
        + (weight_shapes if mode == "load" else []),
        in_specs=[SMEM, SMEM, ANY]
        + [VMEM] * len(arrived)
        + [VMEM if mode == "held" else ANY] * 4
        + [VMEM] * 3
        + [ANY] * len(order)
        + [spec_of(name) for name in names][: len(aliased)]
        + [VMEM] * len(grown),
        out_specs=[VMEM, VMEM] + [spec_of(name) for name in names] + ([VMEM] * 4 if mode == "load" else []),
        input_output_aliases={first + i: 2 + i for i in range(len(aliased) + len(grown))},
        scratch_shapes=(weight_shapes if mode == "pass" else [])
        + [
            pltpu.VMEM((1, crop_len, 3 * width), BF16)
            if mode == "pass"
            else pltpu.VMEM((width // HEAD, crop_len, crop_len), BF16)
        ]
        + [
            pltpu.VMEM((crop_len, width), BF16),
            pltpu.VMEM((crop_len, width), BF16),
            pltpu.VMEM((crop_len, width), BF16),
            pltpu.VMEM((crop_len, hidden), BF16),
            pltpu.SemaphoreType.DMA((4,)),
            pltpu.SemaphoreType.DMA,
            pltpu.SemaphoreType.DMA((5,)),
        ],
        compiler_params=pltpu.CompilerParams(vmem_limit_bytes=PASS_LIMIT if mode == "pass" else HELD_LIMIT),
        cost_estimate=crop_cost(weights, crop_len),
        name="forward_crop",
    )(*operands)
    return outs[0], outs[1], outs[2 + len(names) :], dict(zip(names, outs[2:]))


def crop_cost(weights, crop_len):
    size = sum(weight[0, 0].size for weight in weights[:4])
    return pl.CostEstimate(flops=2 * crop_len * size, bytes_accessed=8_000_000, transcendentals=0)


def backward_kernel(crops, first, n_alias, lengths, cot, *refs):
    refs = list(refs)
    take = lambda count: [refs.pop(0) for _ in range(count)]
    recv = None if first else take(1)[0]
    wqkv, wout, wup, wdown, gains = take(5)
    kept = dict(zip(VMEM_NAMES, take(len(VMEM_NAMES))))
    att = take(1)[0]
    take(n_alias)
    dx_ref, vec_ref, ig_ref, bg_ref, ug_ref, ag_ref, qg_ref = take(7)
    batt, bgin, bbg, bug, bag, bqg, bmg, bxg, asem, gsem, osem = refs
    crop_len, width = bbg.shape
    hidden = bug.shape[1]
    heads = width // HEAD
    base = hidden // width
    section, live, _, crop, length = assigned([(0, crop) for crop in crops], lengths, lengths)
    place = lax.rem(crop, HELD_CROPS)

    def gain(row):
        return gains[0, 0, row : row + 1, :]

    def att_copy():
        return pltpu.make_async_copy(att.at[crop], batt, asem)

    def body(rows):
        keys = -(-rows // 128) * 128
        started = []

        def clear(buffer):
            if rows < crop_len:
                buffer[rows:, :] = jnp.zeros((crop_len - rows, buffer.shape[1]), buffer.dtype)

        def finish(number, buffer, target):
            clear(buffer)
            copy = pltpu.make_async_copy(buffer, target, osem.at[number])
            copy.start()
            started.append(copy)

        def column(row, values, start=0):
            vec_ref[row : row + 1, start : start + values.shape[1]] = jnp.sum(values.astype(F32), 0, keepdims=True)

        valid = lax.broadcasted_iota(jnp.int32, (rows, 1), 0) < length
        g = jnp.where(valid, bgin[:rows, :].astype(F32), 0.0)
        n2 = kept["n2"][place, :rows, :].astype(F32)
        inv1 = kept["inv"][place, :rows, 0:1]
        inv2 = kept["inv"][place, :rows, 1:2]
        sum_two = norm_backward(g * gain(1), n2, inv2)
        bg = sum_two.astype(BF16)
        bbg[:rows, :] = bg
        finish(0, bbg, bg_ref.at[crop])
        column(base + 5, g)
        column(base + 7, g * n2)
        column(base + 4, bg)
        side = [sum_two]

        def cols(part):
            return slice(part * width, (part + 1) * width)

        def descend(part):
            return mm(bg, wdown[0, cols(part), :], NT)

        def slope(part, grad):
            grad = (grad * kept["gp"][place, :rows, cols(part)].astype(F32)).astype(BF16)
            bug[:rows, cols(part)] = grad
            column(part, grad)
            return grad

        def ascend(part, grad):
            side[0] = side[0] + mm(grad, wup[0, :, cols(part)], NT)

        each_lagged(base, descend, slope, ascend)
        finish(1, bug, ug_ref.at[crop])
        n1 = kept["n1"][place, :rows, :].astype(F32)
        side = side[0]
        sum_one = norm_backward(side * gain(0), n1, inv1)
        ag = sum_one.astype(BF16)
        bag[:rows, :] = ag
        finish(2, bag, ag_ref.at[crop])
        column(base + 3, side)
        column(base + 6, side * n1)
        column(base + 2, ag)
        bmg[:rows, :] = mm(ag, wout[0], NT).astype(BF16)
        att_copy().wait()
        masks = head_masks()
        scale = HEAD**-0.5
        sums = [None]

        def pair(part, head, row_count):
            start = part * width + head // 2 * 2 * HEAD
            return jnp.where(masks[head % 2], kept["qkv"][place, :row_count, start : start + 2 * HEAD], 0)

        def attention_grad(head):
            start = head // 2 * 2 * HEAD
            return mm(bmg[:rows, start : start + 2 * HEAD], pair(2, head, keys), NT)

        def score_grad(head, grad):
            wide = batt[head, :rows, :keys].astype(F32)
            both = wide * grad
            return (both - wide * jnp.sum(both, -1, keepdims=True)).astype(BF16)

        def spread(head, score):
            start = head // 2 * 2 * HEAD
            mg = jnp.where(masks[head % 2], bmg[:rows, start : start + 2 * HEAD], 0)
            parts = (
                mm(score, pair(1, head, keys)),
                mm(score, pair(0, head, rows), TN),
                mm(batt[head, :rows, :keys], mg, TN),
            )
            if head % 2 == 0:
                sums[0] = parts
                return
            dq, dk, dv = (old + new for old, new in zip(sums[0], parts))
            dq = (dq * scale).astype(BF16)
            dv = dv[:rows].astype(BF16)
            bqg[:rows, start : start + 2 * HEAD] = dq
            bqg[:rows, width + start : width + start + 2 * HEAD] = (dk[:rows] * scale).astype(BF16)
            bqg[:rows, 2 * width + start : 2 * width + start + 2 * HEAD] = dv
            column(base, dq, start)
            column(base + 1, dv, start)

        each_lagged(heads, attention_grad, score_grad, spread)
        finish(3, bqg, qg_ref.at[crop])
        xg = sum_one + mm(bqg[:rows, :], wqkv[0], NT)
        dx = xg.astype(BF16)
        dx_ref[:rows, :] = dx
        clear(dx_ref)
        bxg[:rows, :] = jnp.where(section == 0, xg, dx.astype(F32))
        finish(4, bxg, ig_ref.at[crop])
        for copy in started:
            copy.wait()

    @pl.when(jnp.logical_not(live))
    def _():
        vec_ref[...] = jnp.zeros(vec_ref.shape, F32)

    @pl.when(live)
    def _():
        if recv is not None:

            @pl.when(section == 0)
            def _():
                bgin[...] = recv[...]

        @pl.when(section != 0)
        def _():
            copy = pltpu.make_async_copy(cot.at[crop], bgin, gsem)
            copy.start()
            copy.wait()

        att_copy().start()
        dispatch(length, crop_len, body)


def backward_call(lengths, crops, cot, recv, weights, held, state, grads, order=()):
    crop_count, crop_len, width = cot.shape
    hidden = weights[2].shape[-1]
    shapes = {
        "ig": ((crop_count, crop_len, width), F32),
        "bg": ((crop_count, crop_len, width), BF16),
        "ug": ((crop_count, crop_len, hidden), BF16),
        "ag": ((crop_count, crop_len, width), BF16),
        "qg": ((crop_count, crop_len, 3 * width), BF16),
    }
    names = tuple(shapes)
    aliased = in_hbm(*[grads[name] for name in names]) if grads else []
    arrived = [] if recv is None else [recv]
    operands = [lengths, *in_hbm(cot), *arrived, *in_vmem(*held), weights[6]]
    order = list(order)
    operands += in_vmem(*[state[name] for name in VMEM_NAMES]) + in_hbm(state["att"]) + order + aliased
    first = 8 + len(arrived) + len(VMEM_NAMES) + len(order)
    outs = pl.pallas_call(
        functools.partial(backward_kernel, crops, recv is None, len(order) + len(aliased)),
        out_shape=[
            jax.ShapeDtypeStruct((crop_len, width), BF16),
            jax.ShapeDtypeStruct((hidden // width + 8, width), F32),
        ]
        + [pltpu.HBM(*shapes[name]) for name in names],
        in_specs=[SMEM, ANY] + [VMEM] * (len(arrived) + 5 + len(VMEM_NAMES)) + [ANY] * (1 + len(order) + len(aliased)),
        out_specs=[VMEM, VMEM] + [ANY] * len(names),
        input_output_aliases={first + i: 2 + i for i in range(len(aliased))},
        scratch_shapes=[
            pltpu.VMEM((width // HEAD, crop_len, crop_len), BF16),
            pltpu.VMEM((crop_len, width), BF16),
            pltpu.VMEM((crop_len, width), BF16),
            pltpu.VMEM((crop_len, hidden), BF16),
            pltpu.VMEM((crop_len, width), BF16),
            pltpu.VMEM((crop_len, 3 * width), BF16),
            pltpu.VMEM((crop_len, width), BF16),
            pltpu.VMEM((crop_len, width), F32),
            pltpu.SemaphoreType.DMA,
            pltpu.SemaphoreType.DMA,
            pltpu.SemaphoreType.DMA((5,)),
        ],
        compiler_params=pltpu.CompilerParams(vmem_limit_bytes=HELD_LIMIT),
        cost_estimate=crop_cost(weights, crop_len),
        name="backward_crop",
    )(*operands)
    return outs[0], outs[1], dict(zip(names, outs[2:]))


def weight_kernel(info, left, right, out):
    out[...] = mm(left[...], right[...], TN).astype(BF16)


def weight_call(info, left, right, mine):
    left = left.reshape(-1, left.shape[-1])
    right = right.reshape(-1, right.shape[-1])
    tokens, rows, columns = right.shape[0], left.shape[1] // 2, right.shape[1]
    half = lambda info: info[0] if mine else 1 - info[0]
    if rows >= columns:
        count = rows // 384
        tile = rows // count
        spec_left = pl.BlockSpec((tokens, tile), lambda i, info: (0, half(info) * count + i))
        spec_right = pl.BlockSpec((tokens, columns), lambda i, info: (0, 0))
        spec_out = pl.BlockSpec((tile, columns), lambda i, info: (i, 0))
    else:
        tile = 768
        count = columns // tile
        spec_left = pl.BlockSpec((tokens, rows), lambda i, info: (0, half(info)))
        spec_right = pl.BlockSpec((tokens, tile), lambda i, info: (0, i))
        spec_out = pl.BlockSpec((rows, tile), lambda i, info: (0, i))
    return pl.pallas_call(
        weight_kernel,
        out_shape=jax.ShapeDtypeStruct((rows, columns), BF16),
        grid_spec=pltpu.PrefetchScalarGridSpec(
            num_scalar_prefetch=1, grid=(count,), in_specs=[spec_left, spec_right], out_specs=spec_out
        ),
        compiler_params=pltpu.CompilerParams(vmem_limit_bytes=VMEM_LIMIT),
        cost_estimate=pl.CostEstimate(flops=2 * tokens * rows * columns, bytes_accessed=2 * tokens * (rows + columns) + 2 * rows * columns, transcendentals=0),
        name="weight_half",
    )(info, *in_hbm(left, right))


def last_weight_kernel(info, left, right, left_out, right_out, out):
    step = pl.program_id(0)

    @pl.when(step < pl.num_programs(0) - 1)
    def _():
        out[...] = mm(left[...], right[...], TN).astype(BF16)

    @pl.when(step == pl.num_programs(0) - 1)
    def _():
        out[...] = mm(left_out[...], right_out[...], TN).astype(BF16)


def last_weight_call(info, left, right, left_out, right_out, mine):
    left, right, left_out, right_out = (a.reshape(-1, a.shape[-1]) for a in (left, right, left_out, right_out))
    (tokens, columns), width = right.shape, left.shape[1]
    rows, parts = width // 2, columns // width
    half = lambda info: info[0] if mine else 1 - info[0]
    return pl.pallas_call(
        last_weight_kernel,
        out_shape=jax.ShapeDtypeStruct((rows, (parts + 1) * width), BF16),
        grid_spec=pltpu.PrefetchScalarGridSpec(
            num_scalar_prefetch=1,
            grid=(parts + 1,),
            in_specs=[
                pl.BlockSpec((tokens, rows), lambda i, info: (0, half(info))),
                pl.BlockSpec((tokens, width), lambda i, info: (0, jnp.minimum(i, parts - 1))),
                pl.BlockSpec((tokens, rows), lambda i, info: (0, half(info))),
                pl.BlockSpec((tokens, width), lambda i, info: (0, 0)),
            ],
            out_specs=pl.BlockSpec((rows, width), lambda i, info: (0, i)),
        ),
        compiler_params=pltpu.CompilerParams(vmem_limit_bytes=VMEM_LIMIT),
        cost_estimate=pl.CostEstimate(flops=2 * tokens * rows * width * (parts + 1), bytes_accessed=12_000_000, transcendentals=0),
        name="weight_half_two",
    )(info, *in_hbm(left, right, left_out, right_out))


def ring_plan(dp, rep):
    chips = [(0, z) for z in range(rep)] + [(1, z) for z in reversed(range(rep))]
    count = len(chips)
    position = [0] * (dp * rep)
    pairs = []
    for core in range(2):
        order = chips if core == 0 else chips[::-1]
        index = [(2 * y + core) * rep + z for y, z in order]
        for place, device in enumerate(index):
            position[device] = place
            pairs.append((device, index[(place + 1) % count]))
    return count, position, pairs


def place_kernel(info, half, *refs):
    outs = refs[len(refs) // 2 :]
    start = 0
    for out in outs:
        out[...] = half[:, start : start + out.shape[1]].astype(F32)
        start += out.shape[1]


def place_call(info, half, widths, outs):
    rows, columns = half.shape
    count = 4
    tile = rows // count
    return pl.pallas_call(
        place_kernel if outs else lambda info, half, *refs: place_kernel(info, half, *refs, *refs),
        out_shape=[jax.ShapeDtypeStruct((2 * rows, width), F32) for width in widths],
        grid_spec=pltpu.PrefetchScalarGridSpec(
            num_scalar_prefetch=1,
            grid=(count,),
            in_specs=[pl.BlockSpec((tile, columns), lambda i, info: (i, 0))] + [ANY] * len(outs),
            out_specs=[pl.BlockSpec((tile, width), lambda i, info: (info[0] * count + i, 0)) for width in widths],
        ),
        input_output_aliases={2 + n: n for n in range(len(outs))},
        compiler_params=pltpu.CompilerParams(vmem_limit_bytes=VMEM_LIMIT),
        cost_estimate=pl.CostEstimate(flops=0, bytes_accessed=6 * rows * columns, transcendentals=0),
        name="place_half",
    )(info, half, *outs)


def tied(value, *others):
    return lax.optimization_barrier((value, *others))[0]


class RingSum:
    def __init__(self, own, other, core, place, plan, swap, widths):
        self.count, _, self.pairs = plan
        self.own, self.other = (a.reshape(self.count, -1, a.shape[-1]) for a in (own, other))
        self.core, self.place, self.swap = core, place, swap
        self.moving = self.block(place).astype(BF16)
        self.step, self.half = 0, None
        self.widths, self.outs, self.finished = widths, [], False

    def block(self, number):
        number = jnp.mod(number, self.count)
        take = lambda a: lax.dynamic_index_in_dim(a, number, 0, keepdims=False).astype(F32)
        return take(self.own) + take(self.other)

    def done(self):
        return self.step == 2 * self.count - 2

    def put(self, number):
        self.half = lax.dynamic_update_index_in_dim(self.half, self.moving, jnp.mod(number, self.count), 0)

    def advance(self, last):
        self.step += 1
        moving = tied(lax.ppermute(self.moving, AXES, self.pairs), last)
        if self.step < self.count:
            self.moving = (moving.astype(F32) + self.block(self.place - self.step)).astype(BF16)
            if self.step == self.count - 1:
                self.half = jnp.zeros(self.own.shape, BF16)
                self.put(self.place + 1)
            return
        self.moving = moving
        self.put(self.place - (self.step - self.count))

    def finish(self, last):
        if not self.outs:
            self.half = self.half.reshape(-1, self.own.shape[-1])
            self.swapped = lax.ppermute(self.half, AXES, self.swap)
            self.outs = place_call(tied(self.core[None], last), self.half, self.widths, [])
        else:
            swapped = tied(self.swapped, last)
            self.outs = place_call((1 - self.core)[None], swapped, self.widths, self.outs)
            self.finished = True
        return self.outs[0]


class RingGather:
    def __init__(self, value, cuts, core, place, rep, plan, swap):
        self.cuts = cuts
        self.count, _, self.pairs = plan
        self.core, self.place, self.rep, self.swap = core, place, rep, swap
        self.moving = value
        self.parts = [value]
        self.finished = False

    def done(self):
        return len(self.parts) == self.count

    def advance(self, last):
        self.moving = tied(lax.ppermute(self.moving, AXES, self.pairs), last)
        self.parts.append(self.moving)

    def finish(self, last):
        core, rep = self.core, self.rep
        count = self.count
        own = jnp.stack(self.parts[::-1])
        own = jnp.roll(own, self.place + 1, 0)
        other = lax.ppermute(own, AXES, self.swap)
        first = jnp.where(core == 0, own, other)
        second = jnp.where(core == 0, other, own)[::-1]
        both = jnp.stack([first, second], 1)
        low, high = both[: count // 2], both[count // 2 :][::-1]
        whole = jnp.stack([low, high])
        whole = jnp.moveaxis(whole, 1, 2)
        whole = whole.reshape((2 * 2 * rep,) + whole.shape[3:])
        starts = [sum(self.cuts[:number]) for number in range(len(self.cuts))]
        parts = [whole[:, start : start + cut] for start, cut in zip(starts, self.cuts)]
        self.outs = [jnp.sum(parts[0], 0)] + [part.reshape(-1, part.shape[-1]) for part in parts[1:]]
        self.outs = lax.optimization_barrier((*self.outs, last))[:-1]
        self.finished = True
        return self.outs[-1]


AXES = ("dp", "rep")


def on_device(
    query_input,
    key_input,
    query_lengths,
    key_lengths,
    cotangent,
    w_qkv,
    w_out,
    w_up,
    w_down,
    b_up,
    biases,
    gains,
):
    section = lax.axis_index("section")
    dp, rep = lax.axis_size("dp"), lax.axis_size("rep")
    crops, crop_len, width = query_input.shape
    hidden = w_up.shape[-1]
    weights = (w_qkv, w_out, w_up, w_down, b_up, biases, gains)

    core = jnp.mod(lax.axis_index("dp"), 2).astype(jnp.int32)
    place = jnp.zeros((), jnp.int32)
    if dp == 4:
        plan = ring_plan(dp, rep)
        place = jnp.asarray(plan[1], jnp.int32)[lax.axis_index(AXES)]
    query_lengths, core, place, section = lax.optimization_barrier((query_lengths, core, place, section))

    def sum_of(vectors):
        return sum(lax.optimization_barrier(tuple(vectors)))

    def up(value):
        return lax.ppermute(value, "section", [(0, 1)])

    def down(value):
        return lax.ppermute(value, "section", [(1, 0)])

    state, grads = {}, {}
    vectors = []

    lengths = (query_lengths, key_lengths)
    idle = (0, -1)
    query = lambda crop: (0, crop) if 0 <= crop < crops else idle
    key = lambda crop: (1, crop) if 0 <= crop < crops else idle
    plan_of_calls = [(query(0), idle), (key(0), idle)]
    for crop in range(1, crops):
        plan_of_calls += [(query(crop), query(crop - 1)), None]
    plan_of_calls += [(key(1), query(crops - 1)), None, (key(2), key(0)), None]
    late_calls = [(key(crop), key(crop - 2)) for crop in range(3, crops + 2)]
    sent_on, pooled_rows = {}, {}

    def forward(mode, call, held, state, order, lengths=lengths):
        sent, pooled, loaded, state = forward_call(
            mode, lengths, call, key_input if call[0][0] else query_input, sent_on.get(call[1]), weights, held, state, order
        )
        for number, done in enumerate(call):
            if done[1] >= 0:
                pooled_rows[number, *done] = pooled
        if call[0][1] >= 0:
            sent_on[call[0]] = up(sent)
        return pooled, loaded or held, state

    def pool(member):
        first, second = (jnp.concatenate([pooled_rows[number, member, crop] for crop in range(crops)]) for number in range(2))
        return jnp.where(section == 0, first, second)

    returned = held = None
    order = []
    backs = 0
    for number, call in enumerate(plan_of_calls):
        if call is not None:
            pooled, held, state = forward("held" if number > 1 else "load", call, held, state, order)
            order = [pooled]
        else:
            assignment = (backs - 1, backs if backs < crops else -1)
            back, vector, grads = backward_call(
                query_lengths, assignment, cotangent, returned, weights, held, state, grads, order
            )
            order = [vector]
            vectors.append(vector)
            returned = down(back)
            backs += 1

    section, core, place, vector = lax.optimization_barrier((section, core, place, sum_of(vectors)))
    core_info = core[None]
    swap = [(d * rep + z, (d ^ 1) * rep + z) for d in range(dp) for z in range(rep)]
    products = (
        lambda mine, core_info: weight_call(core_info, state["act"], grads["bg"], mine),
        lambda mine, core_info: weight_call(core_info, state["low"], grads["ug"], mine),
        lambda mine, core_info: last_weight_call(
            core_info, state["xs"], grads["qg"], state["mix"], grads["ag"], mine
        ),
    )
    widths = [(width,), (hidden,), (3 * width, width)]
    if dp == 4:
        rings, last = [], vector

        def advance(last):
            for ring in rings:
                if not ring.done():
                    ring.advance(last)
                    last = ring.moving
                elif not ring.finished:
                    last = ring.finish(last)
            return last

        for product, cut in zip(products, widths):
            theirs = product(False, tied(core_info, last))
            last = advance(theirs)
            other = lax.ppermute(theirs, AXES, swap)
            own = product(True, tied(core_info, last))
            last = advance(own)
            rings.append(RingSum(own, other, core, place, plan, swap, cut))
            last = rings[-1].moving
        sums = list(rings)
        for call in late_calls:
            pooled, _, _ = forward("pass", call, None, {}, [], (query_lengths, tied(key_lengths, last)))
            last = advance(pooled)
        small = jnp.concatenate([vector, pool(0), pool(1)])
        gather = RingGather(small, (vector.shape[0], crops, crops), core, place, rep, plan, swap)
        rings.insert(0, gather)
        while not all(ring.finished for ring in rings):
            last = advance(last)
        totals = [out for ring in sums for out in ring.outs]
        vector, pooled_query, pooled_key = gather.outs
    else:
        totals = []
        for product in products:
            theirs, own = product(False, core_info), product(True, core_info)
            both = jnp.where(core == 0, jnp.stack([own, theirs]), jnp.stack([theirs, own]))
            totals.append(lax.psum(both.reshape(-1, own.shape[-1]), AXES).astype(F32))
        totals += [totals[2][:, 3 * width :]]
        totals[2] = totals[2][:, : 3 * width]
        for call in late_calls:
            forward("pass", call, None, {}, [])
        vector = lax.psum(vector, AXES)
        pooled_query = lax.all_gather(pool(0), AXES, axis=0, tiled=True)
        pooled_key = lax.all_gather(pool(1), AXES, axis=0, tiled=True)
    ratio = hidden // width
    return (
        pooled_query[None],
        pooled_key[None],
        grads["ig"][None],
        totals[2][None],
        totals[3][None],
        totals[1][None],
        totals[0][None],
        vector[:ratio].reshape(1, hidden),
        vector[None, ratio : ratio + 6],
        vector[None, ratio + 6 : ratio + 8],
    )


def solution(mesh):
    placed = (
        P(("dp", "rep"), None, None),
        P(("dp", "rep"), None, None),
        P(("dp", "rep")),
        P(("dp", "rep")),
        P(("dp", "rep"), None, None),
        P("section", None, None, None),
        P("section", None, None, None),
        P("section", None, None, None),
        P("section", None, None, None),
        P("section", None, None),
        P("section", None, None, None),
        P("section", None, None, None),
    )
    return jax.shard_map(
        on_device,
        mesh=mesh,
        in_specs=placed,
        out_specs=(
            P("section", None, None),
            P("section", None, None),
            P("section", ("dp", "rep"), None, None),
            P("section", None, None),
            P("section", None, None),
            P("section", None, None),
            P("section", None, None),
            P("section", None),
            P("section", None, None),
            P("section", None, None),
        ),
        check_vma=False,
    )
```

time: 513 us -> 392 us (0.76)
  Pallas kernels: 242 us -> 192 us
  waiting for transfers between devices: 73.9 us -> 47.4 us
  other arithmetic: 52.9 us -> 29 us
  local copies, waits for them, and re-layouts: 40.3 us -> 23.3 us
    pallas_call x17 -> x21, Pallas kernels: 201 us -> 154 us  [the longest x10 91.1 us: forward_call(): pl.pallas_call(functools.partial(forward_kernel, mode, crops, recv is Non...]
    ppermute x8, waiting for transfers between devices: 26.6 us -> 7.29 us  [up(): return lax.ppermute(value, 'section', [(0, 1)])]
    convert_element_type x4 -> x0, other arithmetic: 11.8 us -> none  [the longest x3 11.1 us: result(): return both.reshape(-1, half.shape[-1]).astype(F32)]
    unnamed x94 -> x57, local copies, waits for them, and re-layouts: 12.1 us -> 4.96 us
    select_n x6 -> x1, other arithmetic: 6.69 us -> 0.05 us  [pool(): return jnp.where(section == 0, first, second)]
    optimization_barrier x9 -> x0, local copies, waits for them, and re-layouts: 6.21 us -> none  [tied(): return lax.optimization_barrier((value, *others))[0]]
    ppermute x42, waiting for transfers between devices: 45.4 us -> 40.1 us  [advance(): moving = tied(lax.ppermute(self.moving, AXES, self.pairs), last)]
    broadcast_in_dim x2 -> x0, local copies, waits for them, and re-layouts: 5.13 us -> none  [the longest x1 3.53 us: on_device(): totals[2][None, :, :3 * width]]
  transfers between devices with their start and end apart: 68 -> 68, of which waited for: 27 -> 24; matrix products, arithmetic and copies ran while one was open for 14% -> 12% of each run, Pallas kernels for 42% -> 42%
where the time goes in v3:
time: 392 us; the launch traced here: 384 us
  Pallas kernels  192 us (49%)
  starting transfers between devices  83.8 us (21%)
  waiting for transfers between devices  47.4 us (12%)
  other arithmetic  29 us (7%)
  local copies, waits for them, and re-layouts  23.3 us (6%)
  between operations  9.18 us (2%)
    pallas_call x10, Pallas kernels, forward_call(): pl.pallas_call(functools.partial(forward_kernel, mode, crops, recv is Non...  91.1 us
    pallas_call x5, Pallas kernels, backward_call(): pl.pallas_call(functools.partial(backward_kernel, crops, recv is None, le...  43.3 us
    ppermute x42, waiting for transfers between devices, advance(): moving = tied(lax.ppermute(self.moving, AXES, self.pairs), last)  40.1 us
    ppermute x42, starting transfers between devices, advance(): moving = tied(lax.ppermute(self.moving, AXES, self.pairs), last)  39.1 us
    pallas_call x4, Pallas kernels, weight_call(): pl.pallas_call(weight_kernel, out_shape=jax.ShapeDtypeStruct((rows, colum...  24.2 us
    convert_element_type x18, other arithmetic, advance(): (moving.astype(F32) + self.block(self.place - self.step)).astype(BF16)  20.4 us
    pallas_call x6, Pallas kernels, place_call(): pl.pallas_call(place_kernel if outs else lambda info, half, *refs: place_...  19.1 us
    pallas_call x2, Pallas kernels, last_weight_call(): pl.pallas_call(last_weight_kernel, out_shape=jax.ShapeDtypeStruct((rows,...  13.8 us
  transfers between devices with their start and end apart: 68, of which 24 were waited for; matrix products, arithmetic and copies ran while one was open for 12% of the time, Pallas kernels for 42%

profile of v3, /device:TPU:3, one launch (start us, length us, event | category | flops | bytes accessed | tf_op | source)
XLA Modules:
  0.0 384.2 jit_solution(9256291162817996977)
XLA Ops:
  5.4 5.8 %forward_crop.10 = (bf16[256,768]{1,0:T(8,128)(2,1)S(1)}, f32[1,768]{1,0:T(1,128)S(1)}, bf16[3,256,2304]{2,1,0:T(8,128)(2,1)S(1)}, bf16[3,256,768]{2,1,0:T(8,128...) custom-call(s32[4]{0:T(128)S(1)} %copy-done.8, ...), custom_call_target="tpu_custom_call" | custom-call | flops 3623878656 | bytes 8000000 | tf_op jit(solution)/shard_map/forward_crop/pallas_call | solution.py:317
  12.6 10.9 %forward_crop.11 = (bf16[256,768]{1,0:T(8,128)(2,1)S(1)}, f32[1,768]{1,0:T(1,128)S(1)}, bf16[3,256,2304]{2,1,0:T(8,128)(2,1)S(1)}, bf16[3,256,768]{2,1,0:T(8,128...) custom-call(s32[4]{0:T(128)S(1)} %copy-done.9, ...), custom_call_target="tpu_custom_call", output_to_operand_aliasing={{2}: (11, {}), {3}: (12, {}), {4}: (13, {}), {5}: (14, {}),... | custom-call | flops 3623878656 | bytes 8000000 | tf_op jit(solution)/shard_map/forward_crop/pallas_call | solution.py:317
  23.5 4.5 %collective-permute-done.refs_0_ = bf16[256,768]{1,0:T(8,128)(2,1)S(1)} collective-permute-done((bf16[256,768]{1,0:T(8,128)(2,1)S(1)}, bf16[256,768]{1,0:T(8,128)(2,1)S(1)}, u32[]{:S(2)}, u32[]{:S(2)}) %collective-permute-start) | collective-permute-done | bytes 393248 | tf_op jit(solution)/shard_map/ppermute | solution.py:791
  28.0 7.8 %forward_crop.12 = (bf16[256,768]{1,0:T(8,128)(2,1)S(1)}, f32[1,768]{1,0:T(1,128)S(1)}, bf16[3,256,2304]{2,1,0:T(8,128)(2,1)S(1)}, bf16[3,256,768]{2,1,0:T(8,128...) custom-call(s32[4]{0:T(128)S(1)} %copy-done.9, ...), custom_call_target="tpu_custom_call", output_to_operand_aliasing={{2}: (12, {}), {3}: (13, {}), {4}: (14, {}), {5}: (15, {}),... | custom-call | flops 3623878656 | bytes 8000000 | tf_op jit(solution)/shard_map/forward_crop/pallas_call | solution.py:317
  37.2 10.5 %backward_crop.5 = (bf16[256,768]{1,0:T(8,128)(2,1)S(1)}, f32[12,768]{1,0:T(8,128)S(1)}, f32[4,256,768]{2,1,0:T(8,128)}, bf16[4,256,768]{2,1,0:T(8,128)(2,1)}, b...) custom-call(s32[4]{0:T(128)S(1)} %copy-done.9, ...), custom_call_target="tpu_custom_call" | custom-call | flops 3623878656 | bytes 8000000 | tf_op jit(solution)/shard_map/backward_crop/pallas_call | solution.py:530
  49.0 1.4 collective-permute-done.2.refs_0_
  50.4 7.8 %forward_crop.13 = (bf16[256,768]{1,0:T(8,128)(2,1)S(1)}, f32[1,768]{1,0:T(1,128)S(1)}, bf16[3,256,2304]{2,1,0:T(8,128)(2,1)S(1)}, bf16[3,256,768]{2,1,0:T(8,128...) custom-call(s32[4]{0:T(128)S(1)} %copy-done.9, ...), custom_call_target="tpu_custom_call", output_to_operand_aliasing={{2}: (12, {}), {3}: (13, {}), {4}: (14, {}), {5}: (15, {}),... | custom-call | flops 3623878656 | bytes 8000000 | tf_op jit(solution)/shard_map/forward_crop/pallas_call | solution.py:317
  59.5 10.5 %backward_crop.6 = (bf16[256,768]{1,0:T(8,128)(2,1)S(1)}, f32[12,768]{1,0:T(8,128)S(1)}, f32[4,256,768]{2,1,0:T(8,128)}, bf16[4,256,768]{2,1,0:T(8,128)(2,1)}, b...) custom-call(s32[4]{0:T(128)S(1)} %copy-done.9, ...), custom_call_target="tpu_custom_call", output_to_operand_aliasing={{2}: (15, {}), {3}: (16, {}), {4}: (17, {}), {5}: (18, {}),... | custom-call | flops 3623878656 | bytes 8000000 | tf_op jit(solution)/shard_map/backward_crop/pallas_call | solution.py:530
  70.1 3.1 collective-permute-start.3
  73.2 8.0 %forward_crop.14 = (bf16[256,768]{1,0:T(8,128)(2,1)S(1)}, f32[1,768]{1,0:T(1,128)S(1)}, bf16[3,256,2304]{2,1,0:T(8,128)(2,1)S(1)}, bf16[3,256,768]{2,1,0:T(8,128...) custom-call(s32[4]{0:T(128)S(1)} %copy-done.9, ...), custom_call_target="tpu_custom_call", output_to_operand_aliasing={{2}: (12, {}), {3}: (13, {}), {4}: (14, {}), {5}: (15, {}),... | custom-call | flops 3623878656 | bytes 8000000 | tf_op jit(solution)/shard_map/forward_crop/pallas_call | solution.py:317
  82.5 10.2 %backward_crop.7 = (bf16[256,768]{1,0:T(8,128)(2,1)S(1)}, f32[12,768]{1,0:T(8,128)S(1)}, f32[4,256,768]{2,1,0:T(8,128)}, bf16[4,256,768]{2,1,0:T(8,128)(2,1)}, b...) custom-call(s32[4]{0:T(128)S(1)} %copy-done.9, ...), custom_call_target="tpu_custom_call", output_to_operand_aliasing={{2}: (15, {}), {3}: (16, {}), {4}: (17, {}), {5}: (18, {}),... | custom-call | flops 3623878656 | bytes 8000000 | tf_op jit(solution)/shard_map/backward_crop/pallas_call | solution.py:530
  92.7 3.1 collective-permute-start.5
  97.1 10.4 %forward_crop.15 = (bf16[256,768]{1,0:T(8,128)(2,1)}, f32[1,768]{1,0:T(1,128)S(1)}, bf16[3,256,2304]{2,1,0:T(8,128)(2,1)S(1)}, bf16[3,256,768]{2,1,0:T(8,128)(2,...) custom-call(s32[4]{0:T(128)S(1)} %copy-done.9, ...), custom_call_target="tpu_custom_call", output_to_operand_aliasing={{2}: (12, {}), {3}: (13, {}), {4}: (14, {}), {5}: (15, {}),... | custom-call | flops 3623878656 | bytes 8000000 | tf_op jit(solution)/shard_map/forward_crop/pallas_call | solution.py:317
  107.5 10.5 %backward_crop.8 = (bf16[256,768]{1,0:T(8,128)(2,1)S(1)}, f32[12,768]{1,0:T(8,128)S(1)}, f32[4,256,768]{2,1,0:T(8,128)}, bf16[4,256,768]{2,1,0:T(8,128)(2,1)}, b...) custom-call(s32[4]{0:T(128)S(1)} %copy-done.9, ...), custom_call_target="tpu_custom_call", output_to_operand_aliasing={{2}: (15, {}), {3}: (16, {}), {4}: (17, {}), {5}: (18, {}),... | custom-call | flops 3623878656 | bytes 8000000 | tf_op jit(solution)/shard_map/backward_crop/pallas_call | solution.py:530
  117.9 4.0 %collective-permute-start.7 = (bf16[256,768]{1,0:T(8,128)(2,1)S(1)}, bf16[256,768]{1,0:T(8,128)(2,1)S(1)}, u32[]{:S(2)}, u32[]{:S(2)}) collective-permute-start(bf16[256,768]{1,0:T(8,128)(2,1)S(1)} %get-tuple-element.324), channel_id=1, source_target_pairs={{16,0},{17,1},{18,2},{19,3},{20,4},{21,5},{22,6},{23,7},{24,8},{25... | collective-permute-start | bytes 1179656 | tf_op jit(solution)/shard_map/ppermute | solution.py:794
  122.0 10.2 %forward_crop.16 = (bf16[256,768]{1,0:T(8,128)(2,1)}, f32[1,768]{1,0:T(1,128)S(1)}, bf16[3,256,2304]{2,1,0:T(8,128)(2,1)S(1)}, bf16[3,256,768]{2,1,0:T(8,128)(2,...) custom-call(s32[4]{0:T(128)S(1)} %copy-done.9, ...), custom_call_target="tpu_custom_call", output_to_operand_aliasing={{2}: (12, {}), {3}: (13, {}), {4}: (14, {}), {5}: (15, {}),... | custom-call | flops 3623878656 | bytes 8000000 | tf_op jit(solution)/shard_map/forward_crop/pallas_call | solution.py:317
  132.1 1.6 backward_crop.9
  133.8 6.4 %weight_half.4 = bf16[1536,768]{1,0:T(8,128)(2,1)} custom-call(s32[1]{0:T(128)} %bitcast.1.info, bf16[1280,3072]{1,0:T(8,128)(2,1)} %bitcast.237, bf16[1024,768]{1,0:T(8,128)(2,1)} %bitcast.251), custom_call_target="tpu_custom_call" | custom-call | flops 2415919104 | bytes 7077888 | tf_op jit(solution)/shard_map/weight_half/pallas_call | solution.py:581
  140.2 2.3 collective-permute-start.9
  144.5 5.4 %weight_half.5 = bf16[1536,768]{1,0:T(8,128)(2,1)S(1)} custom-call(s32[1]{0:T(128)} %bitcast.1.info, bf16[1280,3072]{1,0:T(8,128)(2,1)} %bitcast.238, bf16[1024,768]{1,0:T(8,128)(2,1)} %bitcast.252), custom_call_target="tpu_custom_call" | custom-call | flops 2415919104 | bytes 7077888 | tf_op jit(solution)/shard_map/weight_half/pallas_call | solution.py:581
  151.2 6.7 %weight_half.6 = bf16[384,3072]{1,0:T(8,128)(2,1)} custom-call(s32[1]{0:T(128)} %bitcast.1.info, bf16[1280,768]{1,0:T(8,128)(2,1)} %bitcast.247, bf16[1024,3072]{1,0:T(8,128)(2,1)} %bitcast.239), custom_call_target="tpu_custom_call" | custom-call | flops 2415919104 | bytes 9437184 | tf_op jit(solution)/shard_map/weight_half/pallas_call | solution.py:581
  157.9 2.1 collective-permute-start.10
  160.6 3.8 collective-permute-done.10
  165.5 1.5 collective-permute-start.13
  167.6 5.7 %weight_half.7 = bf16[384,3072]{1,0:T(8,128)(2,1)S(1)} custom-call(s32[1]{0:T(128)} %bitcast.1.info, bf16[1280,768]{1,0:T(8,128)(2,1)} %bitcast.248, bf16[1024,3072]{1,0:T(8,128)(2,1)} %bitcast.240), custom_call_target="tpu_custom_call" | custom-call | flops 2415919104 | bytes 9437184 | tf_op jit(solution)/shard_map/weight_half/pallas_call | solution.py:581
  173.4 1.9 fusion.22
  176.6 1.7 fusion.25
  178.3 7.3 %weight_half_two.2 = bf16[384,3072]{1,0:T(8,128)(2,1)} custom-call(s32[1]{0:T(128)} %bitcast.1.info, bf16[1280,768]{1,0:T(8,128)(2,1)} %bitcast.243, bf16[1024,2304]{1,0:T(8,128)(2,1)} %bitcast.241, bf16[1280,768]{1,0:T(8,128)(2,1)} %bitcast.245, bf16[1024,768]{1,0:T(8,128)(2,1)} %bitcast.249), custom_call_target="tpu_custom_call" | custom-call | flops 2415919104 | bytes 12000000 | tf_op jit(solution)/shard_map/weight_half_two/pallas_call | solution.py:610
  185.7 2.0 collective-permute-start.15
  198.4 6.5 %weight_half_two.3 = bf16[384,3072]{1,0:T(8,128)(2,1)S(1)} custom-call(s32[1]{0:T(128)} %bitcast.1.info, bf16[1280,768]{1,0:T(8,128)(2,1)} %bitcast.244, bf16[1024,2304]{1,0:T(8,128)(2,1)} %bitcast.242, bf16[1280,768]{1,0:T(8,128)(2,1)} %bitcast.246, bf16[1024,768]{1,0:T(8,128)(2,1)} %bitcast.250), custom_call_target="tpu_custom_call" | custom-call | flops 2415919104 | bytes 12000000 | tf_op jit(solution)/shard_map/weight_half_two/pallas_call | solution.py:610
  212.1 9.5 %forward_crop.17 = (bf16[256,768]{1,0:T(8,128)(2,1)S(1)}, f32[1,768]{1,0:T(1,128)S(1)}) custom-call(s32[4]{0:T(128)S(1)} %copy-done.9, s32[4]{0:T(128)S(1)} %copy-done.11, bf16[4,256,768]{2,1,0:T(8,128)(2,1)} %own.17, bf16[256,768]{1,0:T(8,128)(2,1)S(1)} %collective-permute-done.16.refs_0_, bf16[1,2,768,2304]{3,2,1,0:T(8,128)(2,1)} %refs_1_.9, ...), custom_call_target="tpu_custom_call" | custom-call | flops 3623878656 | bytes 8000000 | tf_op jit(solution)/shard_map/forward_crop/pallas_call | solution.py:317
  227.1 10.5 %forward_crop.18 = (bf16[256,768]{1,0:T(8,128)(2,1)}, f32[1,768]{1,0:T(1,128)S(1)}) custom-call(s32[4]{0:T(128)S(1)} %copy-done.9, s32[4]{0:T(128)S(1)} %copy-done.11, bf16[4,256,768]{2,1,0:T(8,128)(2,1)} %own.19, bf16[256,768]{1,0:T(8,128)(2,1)S(1)} %collective-permute-done.22.refs_0_, bf16[1,2,768,2304]{3,2,1,0:T(8,128)(2,1)} %refs_1_.9, ...), custom_call_target="tpu_custom_call" | custom-call | flops 3623878656 | bytes 8000000 | tf_op jit(solution)/shard_map/forward_crop/pallas_call | solution.py:317
  243.6 1.4 collective-permute-done.26.refs_0_
  245.0 10.3 %forward_crop.19 = (bf16[256,768]{1,0:T(8,128)(2,1)}, f32[1,768]{1,0:T(1,128)S(1)}) custom-call(s32[4]{0:T(128)S(1)} %copy-done.9, s32[4]{0:T(128)S(1)} %copy-done.11, bf16[4,256,768]{2,1,0:T(8,128)(2,1)} %own.19, bf16[256,768]{1,0:T(8,128)(2,1)S(1)} %collective-permute-done.26.refs_0_, bf16[1,2,768,2304]{3,2,1,0:T(8,128)(2,1)} %refs_1_.9, ...), custom_call_target="tpu_custom_call" | custom-call | flops 3623878656 | bytes 8000000 | tf_op jit(solution)/shard_map/forward_crop/pallas_call | solution.py:317
  255.6 1.6 broadcast_in_dim.124
  257.2 1.8 bitcast_dynamic-update-slice_fusion.19
  264.9 1.4 collective-permute-start.38
  266.3 1.7 collective-permute-done.33
  273.7 1.4 collective-permute-done.38
  276.2 2.1 collective-permute-done.37
  284.0 1.4 collective-permute-done.42
  286.4 2.1 collective-permute-done.41
  290.4 1.4 collective-permute-done.40
  294.2 1.4 collective-permute-done.46
  296.7 2.1 collective-permute-done.45
  300.6 1.4 collective-permute-done.44
  307.0 2.1 collective-permute-done.49
  310.9 1.4 collective-permute-done.48
  314.1 2.1 collective-permute-done.54
  317.2 2.1 collective-permute-done.53
  324.2 5.5 %collective-permute-start.55 = (f32[8,20,768]{2,0,1:T(8,128)S(1)}, f32[8,20,768]{2,0,1:T(8,128)S(1)}, u32[]{:S(2)}, u32[]{:S(2)}) collective-permute-start(f32[8,20,768]{2,0,1:T(8,128)S(1)} %copy.131), channel_id=1, source_target_pairs={{0,4},{1,5},{2,6},{3,7},{4,0},{5,1},{6,2},{7,3},{8,12},{9,13},{10,... | collective-permute-start | bytes 1474568 | tf_op jit(solution)/shard_map/ppermute | solution.py:741
  331.5 5.5 %collective-permute-start.63 = (bf16[1536,768]{1,0:T(8,128)(2,1)}, bf16[1536,768]{1,0:T(8,128)(2,1)}, u32[]{:S(2)}, u32[]{:S(2)}) collective-permute-start(bf16[1536,768]{1,0:T(8,128)(2,1)} %bitcast.71.half), channel_id=1, source_target_pairs={{0,4},{1,5},{2,6},{3,7},{4,0},{5,1},{6,2},{7,3},{8,12},{9,13},{10,... | collective-permute-start | bytes 7077896 | tf_op jit(solution)/shard_map/ppermute | solution.py:711
  340.3 1.7 reshape.181
  342.0 1.7 reshape.182
  343.7 4.5 %place_half.6.refs_0_ = f32[3072,768]{1,0:T(8,128)} custom-call(s32[1]{0:T(128)} %bitcast.1.info, bf16[1536,768]{1,0:T(8,128)(2,1)} %bitcast.71.half), custom_call_target="tpu_custom_call" | custom-call | bytes 7077888 | tf_op jit(solution)/shard_map/place_half/pallas_call | solution.py:656
  349.7 4.4 %place_half.7 = f32[3072,768]{1,0:T(8,128)} custom-call(s32[1]{0:T(128)} %bitcast.58.info, bf16[1536,768]{1,0:T(8,128)(2,1)} %collective-permute-done.63.half, f32[3072,768]{1,0:T(8,128)} %place_half.6.refs_0_), custom_call_target="tpu_custom_call", output_to_operand_aliasing={{}: (2, {})} | custom-call | bytes 7077888 | tf_op jit(solution)/shard_map/place_half/pallas_call | solution.py:656
  358.1 4.6 %collective-permute-done.61 = bf16[48,3072]{1,0:T(8,128)(2,1)S(1)} collective-permute-done((bf16[48,3072]{1,0:T(8,128)(2,1)}, bf16[48,3072]{1,0:T(8,128)(2,1)S(1)}, u32[]{:S(2)}, u32[]{:S(2)}) %collective-permute-start.61) | collective-permute-done | bytes 294944 | tf_op jit(solution)/shard_map/ppermute | solution.py:698
  363.2 2.6 place_half.8.refs_0_
  365.8 2.8 collective-permute-done.64
  369.1 2.6 place_half.9
  371.7 2.8 collective-permute-done.65
  374.5 2.6 collective-permute-start.67
  379.0 2.5 place_half.10
  381.5 2.5 place_half.11
  (224 shorter events, 95.9 us)
Async XLA Ops:
  11.2 16.8 %collective-permute-start = (bf16[256,768]{1,0:T(8,128)(2,1)S(1)}, bf16[256,768]{1,0:T(8,128)(2,1)S(1)}, u32[]{:S(2)}, u32[]{:S(2)}) collective-permute-start(bf16[256,768]{1,0:T(8,128)(2,1)S(1)} %get-tuple-element.247), channel_id=1, source_target_pairs={{0,16},{1,17},{2,18},{3,19},{4,20},{5,21},{6,22},{7,23},{8,24},{9,... | collective-permute-start | bytes 1179656 | tf_op jit(solution)/shard_map/ppermute | solution.py:791
  35.9 14.5 %collective-permute-start.2 = (bf16[256,768]{1,0:T(8,128)(2,1)S(1)}, bf16[256,768]{1,0:T(8,128)(2,1)S(1)}, u32[]{:S(2)}, u32[]{:S(2)}) collective-permute-start(bf16[256,768]{1,0:T(8,128)(2,1)S(1)} %get-tuple-element.268), channel_id=1, source_target_pairs={{0,16},{1,17},{2,18},{3,19},{4,20},{5,21},{6,22},{7,23},{8,24},{9,... | collective-permute-start | bytes 1179656 | tf_op jit(solution)/shard_map/ppermute | solution.py:791
  47.7 11.8 %collective-permute-start.1 = (bf16[256,768]{1,0:T(8,128)(2,1)S(1)}, bf16[256,768]{1,0:T(8,128)(2,1)S(1)}, u32[]{:S(2)}, u32[]{:S(2)}) collective-permute-start(bf16[256,768]{1,0:T(8,128)(2,1)S(1)} %get-tuple-element.267), channel_id=1, source_target_pairs={{16,0},{17,1},{18,2},{19,3},{20,4},{21,5},{22,6},{23,7},{24,8},{25... | collective-permute-start | bytes 1179656 | tf_op jit(solution)/shard_map/ppermute | solution.py:794
  58.2 14.9 %collective-permute-start.4 = (bf16[256,768]{1,0:T(8,128)(2,1)S(1)}, bf16[256,768]{1,0:T(8,128)(2,1)S(1)}, u32[]{:S(2)}, u32[]{:S(2)}) collective-permute-start(bf16[256,768]{1,0:T(8,128)(2,1)S(1)} %get-tuple-element.287), channel_id=1, source_target_pairs={{0,16},{1,17},{2,18},{3,19},{4,20},{5,21},{6,22},{7,23},{8,24},{9,... | collective-permute-start | bytes 1179656 | tf_op jit(solution)/shard_map/ppermute | solution.py:791
  70.1 12.4 %collective-permute-start.3 = (bf16[256,768]{1,0:T(8,128)(2,1)S(1)}, bf16[256,768]{1,0:T(8,128)(2,1)S(1)}, u32[]{:S(2)}, u32[]{:S(2)}) collective-permute-start(bf16[256,768]{1,0:T(8,128)(2,1)S(1)} %get-tuple-element.286), channel_id=1, source_target_pairs={{16,0},{17,1},{18,2},{19,3},{20,4},{21,5},{22,6},{23,7},{24,8},{25... | collective-permute-start | bytes 1179656 | tf_op jit(solution)/shard_map/ppermute | solution.py:794
  81.2 15.9 %collective-permute-start.6 = (bf16[256,768]{1,0:T(8,128)(2,1)S(1)}, bf16[256,768]{1,0:T(8,128)(2,1)S(1)}, u32[]{:S(2)}, u32[]{:S(2)}) collective-permute-start(bf16[256,768]{1,0:T(8,128)(2,1)S(1)} %get-tuple-element.306), channel_id=1, source_target_pairs={{0,16},{1,17},{2,18},{3,19},{4,20},{5,21},{6,22},{7,23},{8,24},{9,... | collective-permute-start | bytes 1179656 | tf_op jit(solution)/shard_map/ppermute | solution.py:791
  92.7 14.8 %collective-permute-start.5 = (bf16[256,768]{1,0:T(8,128)(2,1)S(1)}, bf16[256,768]{1,0:T(8,128)(2,1)S(1)}, u32[]{:S(2)}, u32[]{:S(2)}) collective-permute-start(bf16[256,768]{1,0:T(8,128)(2,1)S(1)} %get-tuple-element.305), channel_id=1, source_target_pairs={{16,0},{17,1},{18,2},{19,3},{20,4},{21,5},{22,6},{23,7},{24,8},{25... | collective-permute-start | bytes 1179656 | tf_op jit(solution)/shard_map/ppermute | solution.py:794
  95.8 26.2 %collective-permute-start.8 = (bf16[256,768]{1,0:T(8,128)(2,1)S(1)}, bf16[256,768]{1,0:T(8,128)(2,1)S(1)}, u32[]{:S(2)}, u32[]{:S(2)}) collective-permute-start(bf16[256,768]{1,0:T(8,128)(2,1)S(1)} %get-tuple-element.325), channel_id=1, source_target_pairs={{0,16},{1,17},{2,18},{3,19},{4,20},{5,21},{6,22},{7,23},{8,24},{9,... | collective-permute-start | bytes 1179656 | tf_op jit(solution)/shard_map/ppermute | solution.py:791
  117.9 14.2 %collective-permute-start.7 = (bf16[256,768]{1,0:T(8,128)(2,1)S(1)}, bf16[256,768]{1,0:T(8,128)(2,1)S(1)}, u32[]{:S(2)}, u32[]{:S(2)}) collective-permute-start(bf16[256,768]{1,0:T(8,128)(2,1)S(1)} %get-tuple-element.324), channel_id=1, source_target_pairs={{16,0},{17,1},{18,2},{19,3},{20,4},{21,5},{22,6},{23,7},{24,8},{25... | collective-permute-start | bytes 1179656 | tf_op jit(solution)/shard_map/ppermute | solution.py:794
  140.2 9.7 %collective-permute-start.9 = (bf16[1536,768]{1,0:T(8,128)(2,1)}, bf16[1536,768]{1,0:T(8,128)(2,1)}, u32[]{:S(2)}, u32[]{:S(2)}) collective-permute-start(bf16[1536,768]{1,0:T(8,128)(2,1)} %weight_half.4), channel_id=1, source_target_pairs={{0,4},{1,5},{2,6},{3,7},{4,0},{5,1},{6,2},{7,3},{8,12},{9,13},{10,... | collective-permute-start | bytes 7077896 | tf_op jit(solution)/shard_map/ppermute | solution.py:868
  157.9 18.7 %collective-permute-start.11 = (bf16[384,3072]{1,0:T(8,128)(2,1)}, bf16[384,3072]{1,0:T(8,128)(2,1)}, u32[]{:S(2)}, u32[]{:S(2)}) collective-permute-start(bf16[384,3072]{1,0:T(8,128)(2,1)} %weight_half.6), channel_id=1, source_target_pairs={{0,4},{1,5},{2,6},{3,7},{4,0},{5,1},{6,2},{7,3},{8,12},{9,13},{10,... | collective-permute-start | bytes 7077896 | tf_op jit(solution)/shard_map/ppermute | solution.py:868
  157.9 6.5 %collective-permute-start.10 = (bf16[192,768]{1,0:T(8,128)(2,1)S(1)}, bf16[192,768]{1,0:T(8,128)(2,1)S(1)}, u32[]{:S(2)}, u32[]{:S(2)}) collective-permute-start(bf16[192,768]{1,0:T(8,128)(2,1)S(1)} %fusion.24), channel_id=1, source_target_pairs={{0,1},{1,2},{2,3},{3,11},{11,10},{10,9},{9,8},{8,0},{12,13},{13,14... | collective-permute-start | bytes 884744 | tf_op jit(solution)/shard_map/ppermute | solution.py:698
  165.5 7.9 %collective-permute-start.13 = (bf16[192,768]{1,0:T(8,128)(2,1)S(1)}, bf16[192,768]{1,0:T(8,128)(2,1)S(1)}, u32[]{:S(2)}, u32[]{:S(2)}) collective-permute-start(bf16[192,768]{1,0:T(8,128)(2,1)S(1)} %fusion.23), channel_id=1, source_target_pairs={{0,1},{1,2},{2,3},{3,11},{11,10},{10,9},{9,8},{8,0},{12,13},{13,14... | collective-permute-start | bytes 884744 | tf_op jit(solution)/shard_map/ppermute | solution.py:698
  175.3 19.1 %collective-permute-start.14 = (bf16[192,768]{1,0:T(8,128)(2,1)}, bf16[192,768]{1,0:T(8,128)(2,1)}, u32[]{:S(2)}, u32[]{:S(2)}) collective-permute-start(bf16[192,768]{1,0:T(8,128)(2,1)} %fusion.22), channel_id=1, source_target_pairs={{0,1},{1,2},{2,3},{3,11},{11,10},{10,9},{9,8},{8,0},{12,13},{13,14... | collective-permute-start | bytes 884744 | tf_op jit(solution)/shard_map/ppermute | solution.py:698
  185.7 24.0 %collective-permute-start.15 = (bf16[384,3072]{1,0:T(8,128)(2,1)}, bf16[384,3072]{1,0:T(8,128)(2,1)}, u32[]{:S(2)}, u32[]{:S(2)}) collective-permute-start(bf16[384,3072]{1,0:T(8,128)(2,1)} %weight_half_two.2), channel_id=1, source_target_pairs={{0,4},{1,5},{2,6},{3,7},{4,0},{5,1},{6,2},{7,3},{8,12},{9,13},{10,... | collective-permute-start | bytes 7077896 | tf_op jit(solution)/shard_map/ppermute | solution.py:868
  187.6 8.5 %collective-permute-start.12 = (bf16[48,3072]{1,0:T(8,128)(2,1)}, bf16[48,3072]{1,0:T(8,128)(2,1)}, u32[]{:S(2)}, u32[]{:S(2)}) collective-permute-start(bf16[48,3072]{1,0:T(8,128)(2,1)} %fusion.25), channel_id=1, source_target_pairs={{0,1},{1,2},{2,3},{3,11},{11,10},{10,9},{9,8},{8,0},{12,13},{13,14... | collective-permute-start | bytes 884744 | tf_op jit(solution)/shard_map/ppermute | solution.py:698
  187.8 24.3 %collective-permute-start.16 = (bf16[256,768]{1,0:T(8,128)(2,1)}, bf16[256,768]{1,0:T(8,128)(2,1)S(1)}, u32[]{:S(2)}, u32[]{:S(2)}) collective-permute-start(bf16[256,768]{1,0:T(8,128)(2,1)} %get-tuple-element.371), channel_id=1, source_target_pairs={{0,16},{1,17},{2,18},{3,19},{4,20},{5,21},{6,22},{7,23},{8,24},{9,... | collective-permute-start | bytes 1179656 | tf_op jit(solution)/shard_map/ppermute | solution.py:791
  189.1 38.0 %collective-permute-start.22 = (bf16[256,768]{1,0:T(8,128)(2,1)}, bf16[256,768]{1,0:T(8,128)(2,1)S(1)}, u32[]{:S(2)}, u32[]{:S(2)}) collective-permute-start(bf16[256,768]{1,0:T(8,128)(2,1)} %get-tuple-element.379), channel_id=1, source_target_pairs={{0,16},{1,17},{2,18},{3,19},{4,20},{5,21},{6,22},{7,23},{8,24},{9,... | collective-permute-start | bytes 1179656 | tf_op jit(solution)/shard_map/ppermute | solution.py:791
  195.7 9.2 %collective-permute-start.19 = (bf16[192,768]{1,0:T(8,128)(2,1)S(1)}, bf16[192,768]{1,0:T(8,128)(2,1)S(1)}, u32[]{:S(2)}, u32[]{:S(2)}) collective-permute-start(bf16[192,768]{1,0:T(8,128)(2,1)S(1)} %fusion.21), channel_id=1, source_target_pairs={{0,1},{1,2},{2,3},{3,11},{11,10},{10,9},{9,8},{8,0},{12,13},{13,14... | collective-permute-start | bytes 884744 | tf_op jit(solution)/shard_map/ppermute | solution.py:698
  197.4 9.9 %collective-permute-start.18 = (bf16[48,3072]{1,0:T(8,128)(2,1)S(1)}, bf16[48,3072]{1,0:T(8,128)(2,1)S(1)}, u32[]{:S(2)}, u32[]{:S(2)}) collective-permute-start(bf16[48,3072]{1,0:T(8,128)(2,1)S(1)} %fusion.20), channel_id=1, source_target_pairs={{0,1},{1,2},{2,3},{3,11},{11,10},{10,9},{9,8},{8,0},{12,13},{13,14... | collective-permute-start | bytes 884744 | tf_op jit(solution)/shard_map/ppermute | solution.py:698
  205.9 15.7 %collective-permute-start.21 = (bf16[192,768]{1,0:T(8,128)(2,1)S(1)}, bf16[192,768]{1,0:T(8,128)(2,1)S(1)}, u32[]{:S(2)}, u32[]{:S(2)}) collective-permute-start(bf16[192,768]{1,0:T(8,128)(2,1)S(1)} %fusion.19), channel_id=1, source_target_pairs={{0,1},{1,2},{2,3},{3,11},{11,10},{10,9},{9,8},{8,0},{12,13},{13,14... | collective-permute-start | bytes 884744 | tf_op jit(solution)/shard_map/ppermute | solution.py:698
  208.4 14.8 %collective-permute-start.20 = (bf16[48,3072]{1,0:T(8,128)(2,1)S(1)}, bf16[48,3072]{1,0:T(8,128)(2,1)S(1)}, u32[]{:S(2)}, u32[]{:S(2)}) collective-permute-start(bf16[48,3072]{1,0:T(8,128)(2,1)S(1)} %fusion.18), channel_id=1, source_target_pairs={{0,1},{1,2},{2,3},{3,11},{11,10},{10,9},{9,8},{8,0},{12,13},{13,14... | collective-permute-start | bytes 884744 | tf_op jit(solution)/shard_map/ppermute | solution.py:698
  210.7 15.0 %collective-permute-start.17 = (bf16[48,3072]{1,0:T(8,128)(2,1)S(1)}, bf16[48,3072]{1,0:T(8,128)(2,1)S(1)}, u32[]{:S(2)}, u32[]{:S(2)}) collective-permute-start(bf16[48,3072]{1,0:T(8,128)(2,1)S(1)} %fusion.26), channel_id=1, source_target_pairs={{0,1},{1,2},{2,3},{3,11},{11,10},{10,9},{9,8},{8,0},{12,13},{13,14... | collective-permute-start | bytes 884744 | tf_op jit(solution)/shard_map/ppermute | solution.py:698
  222.7 14.8 %collective-permute-start.25 = (bf16[192,768]{1,0:T(8,128)(2,1)S(1)}, bf16[192,768]{1,0:T(8,128)(2,1)S(1)}, u32[]{:S(2)}, u32[]{:S(2)}) collective-permute-start(bf16[192,768]{1,0:T(8,128)(2,1)S(1)} %fusion.17), channel_id=1, source_target_pairs={{0,1},{1,2},{2,3},{3,11},{11,10},{10,9},{9,8},{8,0},{12,13},{13,14... | collective-permute-start | bytes 884744 | tf_op jit(solution)/shard_map/ppermute | solution.py:698
  224.2 15.0 %collective-permute-start.24 = (bf16[48,3072]{1,0:T(8,128)(2,1)S(1)}, bf16[48,3072]{1,0:T(8,128)(2,1)S(1)}, u32[]{:S(2)}, u32[]{:S(2)}) collective-permute-start(bf16[48,3072]{1,0:T(8,128)(2,1)S(1)} %fusion.16), channel_id=1, source_target_pairs={{0,1},{1,2},{2,3},{3,11},{11,10},{10,9},{9,8},{8,0},{12,13},{13,14... | collective-permute-start | bytes 884744 | tf_op jit(solution)/shard_map/ppermute | solution.py:698
  224.4 20.5 %collective-permute-start.26 = (bf16[256,768]{1,0:T(8,128)(2,1)S(1)}, bf16[256,768]{1,0:T(8,128)(2,1)S(1)}, u32[]{:S(2)}, u32[]{:S(2)}) collective-permute-start(bf16[256,768]{1,0:T(8,128)(2,1)S(1)} %get-tuple-element.385), channel_id=1, source_target_pairs={{0,16},{1,17},{2,18},{3,19},{4,20},{5,21},{6,22},{7,23},{8,24},{9,... | collective-permute-start | bytes 1179656 | tf_op jit(solution)/shard_map/ppermute | solution.py:791
  226.8 14.3 %collective-permute-start.23 = (bf16[48,3072]{1,0:T(8,128)(2,1)S(1)}, bf16[48,3072]{1,0:T(8,128)(2,1)S(1)}, u32[]{:S(2)}, u32[]{:S(2)}) collective-permute-start(bf16[48,3072]{1,0:T(8,128)(2,1)S(1)} %fusion.15), channel_id=1, source_target_pairs={{0,1},{1,2},{2,3},{3,11},{11,10},{10,9},{9,8},{8,0},{12,13},{13,14... | collective-permute-start | bytes 884744 | tf_op jit(solution)/shard_map/ppermute | solution.py:698
  238.6 17.0 %collective-permute-start.30 = (bf16[192,768]{1,0:T(8,128)(2,1)S(1)}, bf16[192,768]{1,0:T(8,128)(2,1)S(1)}, u32[]{:S(2)}, u32[]{:S(2)}) collective-permute-start(bf16[192,768]{1,0:T(8,128)(2,1)S(1)} %fusion.14), channel_id=1, source_target_pairs={{0,1},{1,2},{2,3},{3,11},{11,10},{10,9},{9,8},{8,0},{12,13},{13,14... | collective-permute-start | bytes 884744 | tf_op jit(solution)/shard_map/ppermute | solution.py:698
  240.3 19.8 %collective-permute-start.29 = (bf16[48,3072]{1,0:T(8,128)(2,1)S(1)}, bf16[48,3072]{1,0:T(8,128)(2,1)S(1)}, u32[]{:S(2)}, u32[]{:S(2)}) collective-permute-start(bf16[48,3072]{1,0:T(8,128)(2,1)S(1)} %fusion.13), channel_id=1, source_target_pairs={{0,1},{1,2},{2,3},{3,11},{11,10},{10,9},{9,8},{8,0},{12,13},{13,14... | collective-permute-start | bytes 884744 | tf_op jit(solution)/shard_map/ppermute | solution.py:698
  242.2 19.3 %collective-permute-start.28 = (bf16[48,3072]{1,0:T(8,128)(2,1)S(1)}, bf16[48,3072]{1,0:T(8,128)(2,1)S(1)}, u32[]{:S(2)}, u32[]{:S(2)}) collective-permute-start(bf16[48,3072]{1,0:T(8,128)(2,1)S(1)} %fusion.12), channel_id=1, source_target_pairs={{0,1},{1,2},{2,3},{3,11},{11,10},{10,9},{9,8},{8,0},{12,13},{13,14... | collective-permute-start | bytes 884744 | tf_op jit(solution)/shard_map/ppermute | solution.py:698
  255.4 8.1 %collective-permute-start.27 = (f32[20,768]{1,0:T(8,128)S(1)}, f32[20,768]{1,0:T(8,128)S(1)}, u32[]{:S(2)}, u32[]{:S(2)}) collective-permute-start(f32[20,768]{1,0:T(8,128)S(1)} %pad_maximum_fusion.2), channel_id=1, source_target_pairs={{0,1},{1,2},{2,3},{3,11},{11,10},{10,9},{9,8},{8,0},{12,13},{13,14... | collective-permute-start | bytes 184328 | tf_op jit(solution)/shard_map/ppermute | solution.py:733
  261.1 6.9 %collective-permute-start.33 = (bf16[48,3072]{1,0:T(8,128)(2,1)S(1)}, bf16[48,3072]{1,0:T(8,128)(2,1)S(1)}, u32[]{:S(2)}, u32[]{:S(2)}) collective-permute-start(bf16[48,3072]{1,0:T(8,128)(2,1)S(1)} %fusion.10), channel_id=1, source_target_pairs={{0,1},{1,2},{2,3},{3,11},{11,10},{10,9},{9,8},{8,0},{12,13},{13,14... | collective-permute-start | bytes 884744 | tf_op jit(solution)/shard_map/ppermute | solution.py:698
  262.6 8.6 %collective-permute-start.32 = (bf16[48,3072]{1,0:T(8,128)(2,1)S(1)}, bf16[48,3072]{1,0:T(8,128)(2,1)S(1)}, u32[]{:S(2)}, u32[]{:S(2)}) collective-permute-start(bf16[48,3072]{1,0:T(8,128)(2,1)S(1)} %fusion.9), channel_id=1, source_target_pairs={{0,1},{1,2},{2,3},{3,11},{11,10},{10,9},{9,8},{8,0},{12,13},{13,14... | collective-permute-start | bytes 884744 | tf_op jit(solution)/shard_map/ppermute | solution.py:698
  263.5 9.8 %collective-permute-start.31 = (f32[20,768]{1,0:T(8,128)S(1)}, f32[20,768]{1,0:T(8,128)S(1)}, u32[]{:S(2)}, u32[]{:S(2)}) collective-permute-start(f32[20,768]{1,0:T(8,128)S(1)} %collective-permute-done.27), channel_id=1, source_target_pairs={{0,1},{1,2},{2,3},{3,11},{11,10},{10,9},{9,8},{8,0},{12,13},{13,14... | collective-permute-start | bytes 184328 | tf_op jit(solution)/shard_map/ppermute | solution.py:733
  264.9 10.3 %collective-permute-start.38 = (bf16[192,768]{1,0:T(8,128)(2,1)S(1)}, bf16[192,768]{1,0:T(8,128)(2,1)S(1)}, u32[]{:S(2)}, u32[]{:S(2)}) collective-permute-start(bf16[192,768]{1,0:T(8,128)(2,1)S(1)} %collective-permute-done.34), channel_id=1, source_target_pairs={{0,1},{1,2},{2,3},{3,11},{11,10},{10,9},{9,8},{8,0},{12,13},{13,14... | collective-permute-start | bytes 884744 | tf_op jit(solution)/shard_map/ppermute | solution.py:698
  269.1 9.2 %collective-permute-start.37 = (bf16[48,3072]{1,0:T(8,128)(2,1)S(1)}, bf16[48,3072]{1,0:T(8,128)(2,1)S(1)}, u32[]{:S(2)}, u32[]{:S(2)}) collective-permute-start(bf16[48,3072]{1,0:T(8,128)(2,1)S(1)} %fusion.8), channel_id=1, source_target_pairs={{0,1},{1,2},{2,3},{3,11},{11,10},{10,9},{9,8},{8,0},{12,13},{13,14... | collective-permute-start | bytes 884744 | tf_op jit(solution)/shard_map/ppermute | solution.py:698
  272.3 9.2 %collective-permute-start.36 = (bf16[48,3072]{1,0:T(8,128)(2,1)S(1)}, bf16[48,3072]{1,0:T(8,128)(2,1)S(1)}, u32[]{:S(2)}, u32[]{:S(2)}) collective-permute-start(bf16[48,3072]{1,0:T(8,128)(2,1)S(1)} %fusion.7), channel_id=1, source_target_pairs={{0,1},{1,2},{2,3},{3,11},{11,10},{10,9},{9,8},{8,0},{12,13},{13,14... | collective-permute-start | bytes 884744 | tf_op jit(solution)/shard_map/ppermute | solution.py:698
  273.3 10.3 %collective-permute-start.35 = (f32[20,768]{1,0:T(8,128)S(1)}, f32[20,768]{1,0:T(8,128)S(1)}, u32[]{:S(2)}, u32[]{:S(2)}) collective-permute-start(f32[20,768]{1,0:T(8,128)S(1)} %collective-permute-done.31), channel_id=1, source_target_pairs={{0,1},{1,2},{2,3},{3,11},{11,10},{10,9},{9,8},{8,0},{12,13},{13,14... | collective-permute-start | bytes 184328 | tf_op jit(solution)/shard_map/ppermute | solution.py:733
  275.1 10.3 %collective-permute-start.42 = (bf16[192,768]{1,0:T(8,128)(2,1)S(1)}, bf16[192,768]{1,0:T(8,128)(2,1)S(1)}, u32[]{:S(2)}, u32[]{:S(2)}) collective-permute-start(bf16[192,768]{1,0:T(8,128)(2,1)S(1)} %collective-permute-done.38), channel_id=1, source_target_pairs={{0,1},{1,2},{2,3},{3,11},{11,10},{10,9},{9,8},{8,0},{12,13},{13,14... | collective-permute-start | bytes 884744 | tf_op jit(solution)/shard_map/ppermute | solution.py:698
  279.7 8.9 %collective-permute-start.41 = (bf16[48,3072]{1,0:T(8,128)(2,1)S(1)}, bf16[48,3072]{1,0:T(8,128)(2,1)S(1)}, u32[]{:S(2)}, u32[]{:S(2)}) collective-permute-start(bf16[48,3072]{1,0:T(8,128)(2,1)S(1)} %get-tuple-element.439), channel_id=1, source_target_pairs={{0,1},{1,2},{2,3},{3,11},{11,10},{10,9},{9,8},{8,0},{12,13},{13,14... | collective-permute-start | bytes 884744 | tf_op jit(solution)/shard_map/ppermute | solution.py:698
  282.6 9.2 %collective-permute-start.40 = (bf16[48,3072]{1,0:T(8,128)(2,1)S(1)}, bf16[48,3072]{1,0:T(8,128)(2,1)S(1)}, u32[]{:S(2)}, u32[]{:S(2)}) collective-permute-start(bf16[48,3072]{1,0:T(8,128)(2,1)S(1)} %fusion.5), channel_id=1, source_target_pairs={{0,1},{1,2},{2,3},{3,11},{11,10},{10,9},{9,8},{8,0},{12,13},{13,14... | collective-permute-start | bytes 884744 | tf_op jit(solution)/shard_map/ppermute | solution.py:698
  283.6 10.3 %collective-permute-start.39 = (f32[20,768]{1,0:T(8,128)S(1)}, f32[20,768]{1,0:T(8,128)S(1)}, u32[]{:S(2)}, u32[]{:S(2)}) collective-permute-start(f32[20,768]{1,0:T(8,128)S(1)} %collective-permute-done.35), channel_id=1, source_target_pairs={{0,1},{1,2},{2,3},{3,11},{11,10},{10,9},{9,8},{8,0},{12,13},{13,14... | collective-permute-start | bytes 184328 | tf_op jit(solution)/shard_map/ppermute | solution.py:733
  285.4 10.3 %collective-permute-start.46 = (bf16[192,768]{1,0:T(8,128)(2,1)S(1)}, bf16[192,768]{1,0:T(8,128)(2,1)S(1)}, u32[]{:S(2)}, u32[]{:S(2)}) collective-permute-start(bf16[192,768]{1,0:T(8,128)(2,1)S(1)} %collective-permute-done.42), channel_id=1, source_target_pairs={{0,1},{1,2},{2,3},{3,11},{11,10},{10,9},{9,8},{8,0},{12,13},{13,14... | collective-permute-start | bytes 884744 | tf_op jit(solution)/shard_map/ppermute | solution.py:698
  288.6 10.3 %collective-permute-start.45 = (bf16[48,3072]{1,0:T(8,128)(2,1)S(1)}, bf16[48,3072]{1,0:T(8,128)(2,1)S(1)}, u32[]{:S(2)}, u32[]{:S(2)}) collective-permute-start(bf16[48,3072]{1,0:T(8,128)(2,1)S(1)} %collective-permute-done.41), channel_id=1, source_target_pairs={{0,1},{1,2},{2,3},{3,11},{11,10},{10,9},{9,8},{8,0},{12,13},{13,14... | collective-permute-start | bytes 884744 | tf_op jit(solution)/shard_map/ppermute | solution.py:698
  292.8 9.2 %collective-permute-start.44 = (bf16[48,3072]{1,0:T(8,128)(2,1)S(1)}, bf16[48,3072]{1,0:T(8,128)(2,1)S(1)}, u32[]{:S(2)}, u32[]{:S(2)}) collective-permute-start(bf16[48,3072]{1,0:T(8,128)(2,1)S(1)} %fusion.4), channel_id=1, source_target_pairs={{0,1},{1,2},{2,3},{3,11},{11,10},{10,9},{9,8},{8,0},{12,13},{13,14... | collective-permute-start | bytes 884744 | tf_op jit(solution)/shard_map/ppermute | solution.py:698
  293.9 10.6 %collective-permute-start.43 = (f32[20,768]{1,0:T(8,128)S(1)}, f32[20,768]{1,0:T(8,128)S(1)}, u32[]{:S(2)}, u32[]{:S(2)}) collective-permute-start(f32[20,768]{1,0:T(8,128)S(1)} %collective-permute-done.39), channel_id=1, source_target_pairs={{0,1},{1,2},{2,3},{3,11},{11,10},{10,9},{9,8},{8,0},{12,13},{13,14... | collective-permute-start | bytes 184328 | tf_op jit(solution)/shard_map/ppermute | solution.py:733
  295.7 10.3 %collective-permute-start.50 = (bf16[192,768]{1,0:T(8,128)(2,1)S(1)}, bf16[192,768]{1,0:T(8,128)(2,1)S(1)}, u32[]{:S(2)}, u32[]{:S(2)}) collective-permute-start(bf16[192,768]{1,0:T(8,128)(2,1)S(1)} %collective-permute-done.46), channel_id=1, source_target_pairs={{0,1},{1,2},{2,3},{3,11},{11,10},{10,9},{9,8},{8,0},{12,13},{13,14... | collective-permute-start | bytes 884744 | tf_op jit(solution)/shard_map/ppermute | solution.py:698
  298.8 10.3 %collective-permute-start.49 = (bf16[48,3072]{1,0:T(8,128)(2,1)S(1)}, bf16[48,3072]{1,0:T(8,128)(2,1)S(1)}, u32[]{:S(2)}, u32[]{:S(2)}) collective-permute-start(bf16[48,3072]{1,0:T(8,128)(2,1)S(1)} %collective-permute-done.45), channel_id=1, source_target_pairs={{0,1},{1,2},{2,3},{3,11},{11,10},{10,9},{9,8},{8,0},{12,13},{13,14... | collective-permute-start | bytes 884744 | tf_op jit(solution)/shard_map/ppermute | solution.py:698
  303.4 8.9 %collective-permute-start.48 = (bf16[48,3072]{1,0:T(8,128)(2,1)S(1)}, bf16[48,3072]{1,0:T(8,128)(2,1)S(1)}, u32[]{:S(2)}, u32[]{:S(2)}) collective-permute-start(bf16[48,3072]{1,0:T(8,128)(2,1)S(1)} %get-tuple-element.443), channel_id=1, source_target_pairs={{0,1},{1,2},{2,3},{3,11},{11,10},{10,9},{9,8},{8,0},{12,13},{13,14... | collective-permute-start | bytes 884744 | tf_op jit(solution)/shard_map/ppermute | solution.py:698
  304.4 8.9 %collective-permute-start.47 = (f32[20,768]{1,0:T(8,128)S(1)}, f32[20,768]{1,0:T(8,128)S(1)}, u32[]{:S(2)}, u32[]{:S(2)}) collective-permute-start(f32[20,768]{1,0:T(8,128)S(1)} %collective-permute-done.43), channel_id=1, source_target_pairs={{0,1},{1,2},{2,3},{3,11},{11,10},{10,9},{9,8},{8,0},{12,13},{13,14... | collective-permute-start | bytes 184328 | tf_op jit(solution)/shard_map/ppermute | solution.py:733
  306.0 10.3 %collective-permute-start.54 = (bf16[192,768]{1,0:T(8,128)(2,1)S(1)}, bf16[192,768]{1,0:T(8,128)(2,1)S(1)}, u32[]{:S(2)}, u32[]{:S(2)}) collective-permute-start(bf16[192,768]{1,0:T(8,128)(2,1)S(1)} %collective-permute-done.50), channel_id=1, source_target_pairs={{0,1},{1,2},{2,3},{3,11},{11,10},{10,9},{9,8},{8,0},{12,13},{13,14... | collective-permute-start | bytes 884744 | tf_op jit(solution)/shard_map/ppermute | solution.py:698
  309.1 10.3 %collective-permute-start.53 = (bf16[48,3072]{1,0:T(8,128)(2,1)S(1)}, bf16[48,3072]{1,0:T(8,128)(2,1)S(1)}, u32[]{:S(2)}, u32[]{:S(2)}) collective-permute-start(bf16[48,3072]{1,0:T(8,128)(2,1)S(1)} %collective-permute-done.49), channel_id=1, source_target_pairs={{0,1},{1,2},{2,3},{3,11},{11,10},{10,9},{9,8},{8,0},{12,13},{13,14... | collective-permute-start | bytes 884744 | tf_op jit(solution)/shard_map/ppermute | solution.py:698
  312.3 10.3 %collective-permute-start.52 = (bf16[48,3072]{1,0:T(8,128)(2,1)S(1)}, bf16[48,3072]{1,0:T(8,128)(2,1)S(1)}, u32[]{:S(2)}, u32[]{:S(2)}) collective-permute-start(bf16[48,3072]{1,0:T(8,128)(2,1)S(1)} %collective-permute-done.48), channel_id=1, source_target_pairs={{0,1},{1,2},{2,3},{3,11},{11,10},{10,9},{9,8},{8,0},{12,13},{13,14... | collective-permute-start | bytes 884744 | tf_op jit(solution)/shard_map/ppermute | solution.py:698
  313.3 10.5 %collective-permute-start.51 = (f32[20,768]{1,0:T(8,128)S(1)}, f32[20,768]{1,0:T(8,128)S(1)}, u32[]{:S(2)}, u32[]{:S(2)}) collective-permute-start(f32[20,768]{1,0:T(8,128)S(1)} %collective-permute-done.47), channel_id=1, source_target_pairs={{0,1},{1,2},{2,3},{3,11},{11,10},{10,9},{9,8},{8,0},{12,13},{13,14... | collective-permute-start | bytes 184328 | tf_op jit(solution)/shard_map/ppermute | solution.py:733
  316.2 13.5 %collective-permute-start.58 = (bf16[192,768]{1,0:T(8,128)(2,1)S(1)}, bf16[192,768]{1,0:T(8,128)(2,1)S(1)}, u32[]{:S(2)}, u32[]{:S(2)}) collective-permute-start(bf16[192,768]{1,0:T(8,128)(2,1)S(1)} %collective-permute-done.54), channel_id=1, source_target_pairs={{0,1},{1,2},{2,3},{3,11},{11,10},{10,9},{9,8},{8,0},{12,13},{13,14... | collective-permute-start | bytes 884744 | tf_op jit(solution)/shard_map/ppermute | solution.py:698
  319.4 10.3 %collective-permute-start.57 = (bf16[48,3072]{1,0:T(8,128)(2,1)S(1)}, bf16[48,3072]{1,0:T(8,128)(2,1)}, u32[]{:S(2)}, u32[]{:S(2)}) collective-permute-start(bf16[48,3072]{1,0:T(8,128)(2,1)S(1)} %collective-permute-done.53), channel_id=1, source_target_pairs={{0,1},{1,2},{2,3},{3,11},{11,10},{10,9},{9,8},{8,0},{12,13},{13,14... | collective-permute-start | bytes 884744 | tf_op jit(solution)/shard_map/ppermute | solution.py:698
  322.5 15.4 %collective-permute-start.56 = (bf16[48,3072]{1,0:T(8,128)(2,1)S(1)}, bf16[48,3072]{1,0:T(8,128)(2,1)}, u32[]{:S(2)}, u32[]{:S(2)}) collective-permute-start(bf16[48,3072]{1,0:T(8,128)(2,1)S(1)} %collective-permute-done.52), channel_id=1, source_target_pairs={{0,1},{1,2},{2,3},{3,11},{11,10},{10,9},{9,8},{8,0},{12,13},{13,14... | collective-permute-start | bytes 884744 | tf_op jit(solution)/shard_map/ppermute | solution.py:698
  324.2 14.2 %collective-permute-start.55 = (f32[8,20,768]{2,0,1:T(8,128)S(1)}, f32[8,20,768]{2,0,1:T(8,128)S(1)}, u32[]{:S(2)}, u32[]{:S(2)}) collective-permute-start(f32[8,20,768]{2,0,1:T(8,128)S(1)} %copy.131), channel_id=1, source_target_pairs={{0,4},{1,5},{2,6},{3,7},{4,0},{5,1},{6,2},{7,3},{8,12},{9,13},{10,... | collective-permute-start | bytes 1474568 | tf_op jit(solution)/shard_map/ppermute | solution.py:741
  329.7 18.5 %collective-permute-start.60 = (bf16[48,3072]{1,0:T(8,128)(2,1)}, bf16[48,3072]{1,0:T(8,128)(2,1)}, u32[]{:S(2)}, u32[]{:S(2)}) collective-permute-start(bf16[48,3072]{1,0:T(8,128)(2,1)} %collective-permute-done.57), channel_id=1, source_target_pairs={{0,1},{1,2},{2,3},{3,11},{11,10},{10,9},{9,8},{8,0},{12,13},{13,14... | collective-permute-start | bytes 884744 | tf_op jit(solution)/shard_map/ppermute | solution.py:698
  331.5 18.2 %collective-permute-start.63 = (bf16[1536,768]{1,0:T(8,128)(2,1)}, bf16[1536,768]{1,0:T(8,128)(2,1)}, u32[]{:S(2)}, u32[]{:S(2)}) collective-permute-start(bf16[1536,768]{1,0:T(8,128)(2,1)} %bitcast.71.half), channel_id=1, source_target_pairs={{0,4},{1,5},{2,6},{3,7},{4,0},{5,1},{6,2},{7,3},{8,12},{9,13},{10,... | collective-permute-start | bytes 7077896 | tf_op jit(solution)/shard_map/ppermute | solution.py:711
  338.0 11.7 %collective-permute-start.59 = (bf16[48,3072]{1,0:T(8,128)(2,1)}, bf16[48,3072]{1,0:T(8,128)(2,1)}, u32[]{:S(2)}, u32[]{:S(2)}) collective-permute-start(bf16[48,3072]{1,0:T(8,128)(2,1)} %collective-permute-done.56), channel_id=1, source_target_pairs={{0,1},{1,2},{2,3},{3,11},{11,10},{10,9},{9,8},{8,0},{12,13},{13,14... | collective-permute-start | bytes 884744 | tf_op jit(solution)/shard_map/ppermute | solution.py:698
  354.4 14.7 %collective-permute-start.66 = (bf16[384,3072]{1,0:T(8,128)(2,1)S(1)}, bf16[384,3072]{1,0:T(8,128)(2,1)S(1)}, u32[]{:S(2)}, u32[]{:S(2)}) collective-permute-start(bf16[384,3072]{1,0:T(8,128)(2,1)S(1)} %bitcast.235), channel_id=1, source_target_pairs={{0,4},{1,5},{2,6},{3,7},{4,0},{5,1},{6,2},{7,3},{8,12},{9,13},{10,... | collective-permute-start | bytes 7077896 | tf_op jit(solution)/shard_map/ppermute | solution.py:711
  356.6 6.1 %collective-permute-start.61 = (bf16[48,3072]{1,0:T(8,128)(2,1)}, bf16[48,3072]{1,0:T(8,128)(2,1)S(1)}, u32[]{:S(2)}, u32[]{:S(2)}) collective-permute-start(bf16[48,3072]{1,0:T(8,128)(2,1)} %collective-permute-done.59), channel_id=1, source_target_pairs={{0,1},{1,2},{2,3},{3,11},{11,10},{10,9},{9,8},{8,0},{12,13},{13,14... | collective-permute-start | bytes 884744 | tf_op jit(solution)/shard_map/ppermute | solution.py:698
  374.5 7.0 %collective-permute-start.67 = (bf16[384,3072]{1,0:T(8,128)(2,1)S(1)}, bf16[384,3072]{1,0:T(8,128)(2,1)S(1)}, u32[]{:S(2)}, u32[]{:S(2)}) collective-permute-start(bf16[384,3072]{1,0:T(8,128)(2,1)S(1)} %bitcast.209), channel_id=1, source_target_pairs={{0,4},{1,5},{2,6},{3,7},{4,0},{5,1},{6,2},{7,3},{8,12},{9,13},{10,... | collective-permute-start | bytes 7077896 | tf_op jit(solution)/shard_map/ppermute | solution.py:711
  (24 other events, 209.0 us)

commit v4 on v3

--- a/solution.py
+++ b/solution.py
@@ -11,10 +11,10 @@
 HEAD = 64
 EPS = 1e-06
 NEG = -1000000000.0
-VMEM_LIMIT = 16 * 1024 * 1024
 HELD_CROPS = 3
 HELD_LIMIT = 10 * 1024 * 1024
 PASS_LIMIT = 22 * 1024 * 1024
+WEIGHTS_LIMIT = 50 * 1024 * 1024
 NT = (((1,), (1,)), ((), ()))
 TN = (((0,), (0,)), ((), ()))
 F32 = jnp.float32
@@ -557,116 +557,211 @@
     return outs[0], outs[1], dict(zip(names, outs[2:]))
 
 
-def weight_kernel(info, left, right, out):
-    out[...] = mm(left[...], right[...], TN).astype(BF16)
-
-
-def weight_call(info, left, right, mine):
-    left = left.reshape(-1, left.shape[-1])
-    right = right.reshape(-1, right.shape[-1])
-    tokens, rows, columns = right.shape[0], left.shape[1] // 2, right.shape[1]
-    half = lambda info: info[0] if mine else 1 - info[0]
-    if rows >= columns:
-        count = rows // 384
-        tile = rows // count
-        spec_left = pl.BlockSpec((tokens, tile), lambda i, info: (0, half(info) * count + i))
-        spec_right = pl.BlockSpec((tokens, columns), lambda i, info: (0, 0))
-        spec_out = pl.BlockSpec((tile, columns), lambda i, info: (i, 0))
-    else:
-        tile = 768
-        count = columns // tile
-        spec_left = pl.BlockSpec((tokens, rows), lambda i, info: (0, half(info)))
-        spec_right = pl.BlockSpec((tokens, tile), lambda i, info: (0, i))
-        spec_out = pl.BlockSpec((rows, tile), lambda i, info: (0, i))
+def ring_place(core, chip, count):
+    return jnp.where(core == 0, chip, count - 1 - chip)
+
+
+def chip_number(dp_index, rep_index, rep):
+    return jnp.where(lax.div(dp_index, 2) == 0, rep_index, 2 * rep - 1 - rep_index)
+
+
+def weights_kernel(groups, *refs):
+    pairs = 1 + max(dot[0] for dots in groups for dot in dots)
+    lefts, rights = refs[:pairs], refs[pairs : 2 * pairs]
+    refs = refs[-(3 * len(groups) + 2 * pairs + 3) :]
+    outs, refs = refs[: 2 * len(groups)], refs[2 * len(groups) :]
+    held_lefts, held_rights, refs = refs[:pairs], refs[pairs : 2 * pairs], refs[2 * pairs :]
+    held_outs, (lsem, rsem, osem) = refs[:-3], refs[-3:]
+    count = lax.axis_size("rep") * 2
+    core = lax.rem(lax.axis_index("dp"), 2)
+    chip = chip_number(lax.axis_index("dp"), lax.axis_index("rep"), count // 2)
+    place = ring_place(core, chip, count)
+    tile, width = held_lefts[0].shape[2], held_rights[0].shape[2]
+
+    def slot_of(number, half, part):
+        return half * (held_lefts[number].shape[0] // 2) + part
+
+    def left_copy(number, half, part):
+        which = jnp.where(half == 0, 1 - core, core)
+        start = pl.multiple_of(slot_of(number, which, part) * tile, 128)
+        source = lefts[number].at[pl.ds(0, held_lefts[number].shape[1]), pl.ds(start, tile)]
+        slot = slot_of(number, half, part)
+        return pltpu.make_async_copy(source, held_lefts[number].at[slot], lsem.at[number, slot])
+
+    def right_copy(number, part):
+        source = rights[number].at[:, pl.ds(part * width, width)]
+        return pltpu.make_async_copy(source, held_rights[number].at[part], rsem.at[number, part])
+
+    def out_copy(group, half, step, target):
+        rows = held_outs[group].shape[1] // count
+        block = lax.rem(jnp.where(half == 0, count - 1 - place, place) - step + count, count)
+        source = held_outs[group].at[half, pl.ds(pl.multiple_of(block * rows, 16), rows)]
+        return pltpu.make_async_copy(source, outs[2 * group + target].at[step], osem.at[group, half, step])
+
+    def firsts():
+        seen = set()
+        for group, dots in enumerate(groups):
+            for step, (number, left, right) in enumerate(dots):
+                fresh = [key not in seen for key in ((0, number, left), (1, number, right))]
+                seen |= {(0, number, left), (1, number, right)}
+                yield group, step, number, left, right, fresh
+
+    for half in range(2):
+        for _, _, number, left, right, fresh in firsts():
+            if fresh[0]:
+                left_copy(number, half, left).start()
+            if fresh[1] and half == 0:
+                right_copy(number, right).start()
+
+    @pl.loop(0, 2)
+    def _(half):
+        for group, step, number, left, right, fresh in firsts():
+            if fresh[0]:
+                left_copy(number, half, left).wait()
+            if fresh[1]:
+
+                @pl.when(half == 0)
+                def _():
+                    right_copy(number, right).wait()
+
+            product = mm(held_lefts[number][slot_of(number, half, left)], held_rights[number][right], TN).astype(BF16)
+            if held_outs[group].shape[1] == tile:
+                held_outs[group][half, :, step * width : (step + 1) * width] = product
+            else:
+                held_outs[group][half, step * tile : (step + 1) * tile, :] = product
+            if step == len(groups[group]) - 1:
+                for target in range(2):
+
+                    @pl.when(half == target)
+                    def _():
+                        for number in range(count):
+                            out_copy(group, half, number, target).start()
+
+    for group in range(len(groups)):
+        for half in range(2):
+            for step in range(count):
+                out_copy(group, half, step, half).wait()
+
+
+def weights_call(pairs, groups, order=()):
+    lefts, rights = ([array.reshape(-1, array.shape[-1]) for array in side] for side in zip(*pairs))
+    tokens, width = rights[0].shape
+    tile = width // 2
+    left_parts = [left.shape[1] // tile for left in lefts]
+    right_parts = [right.shape[1] // width for right in rights]
+    count = lax.axis_size("rep") * 2
+    shapes = []
+    for dots in groups:
+        down = left_parts[dots[0][0]] // 2
+        shapes.append((down * tile, len(dots) // down * width))
+    blocks = [(count, rows // count, columns) for rows, columns in shapes]
+    outs = pl.pallas_call(
+        functools.partial(weights_kernel, groups),
+        out_shape=[pltpu.HBM(block, BF16) for block in blocks for _ in range(2)],
+        in_specs=[ANY] * (2 * len(pairs) + len(order)),
+        out_specs=[ANY] * (2 * len(groups)),
+        scratch_shapes=[pltpu.VMEM((parts, tokens, tile), BF16) for parts in left_parts]
+        + [pltpu.VMEM((parts, tokens, width), BF16) for parts in right_parts]
+        + [pltpu.VMEM((2, *shape), BF16) for shape in shapes]
+        + [
+            pltpu.SemaphoreType.DMA((len(pairs), max(left_parts))),
+            pltpu.SemaphoreType.DMA((len(pairs), max(right_parts))),
+            pltpu.SemaphoreType.DMA((len(groups), 2, count)),
+        ],
+        compiler_params=pltpu.CompilerParams(vmem_limit_bytes=WEIGHTS_LIMIT),
+        cost_estimate=pl.CostEstimate(
+            flops=4 * tokens * sum(rows * columns for rows, columns in shapes), bytes_accessed=40_000_000, transcendentals=0
+        ),
+        name="weight_gradients",
+    )(*in_hbm(*lefts, *rights), *order)
+    return [(outs[2 * number], outs[2 * number + 1]) for number in range(len(groups))]
+
+
+def write_kernel(mine, outs_count, *refs):
+    value, refs = refs[0], refs[1 if mine else 1 + outs_count :]
+    outs, wide, osem = refs[:-2], refs[-2], refs[-1]
+    small = outs[-1] if outs[-1].dtype == BF16 else None
+    targets = outs if small is None else outs[:-1]
+    count, rows, _ = wide.shape
+    core = lax.rem(lax.axis_index("dp"), 2)
+    whose = core if mine else 1 - core
+    copies = []
+    for block in range(count):
+        wide[block] = value[block, :rows, :].astype(F32)
+        row = pl.multiple_of((whose * count + block) * rows, 16)
+        start = 0
+        for target in targets:
+            part = wide.at[block, :, pl.ds(start, target.shape[1])]
+            copies.append(pltpu.make_async_copy(part, target.at[pl.ds(row, rows)], osem.at[len(copies)]))
+            copies[-1].start()
+            start += target.shape[1]
+        if small is not None:
+            origin = ring_place(whose, (block - 1) % count, count)
+            part = value.at[block, pl.ds(rows, value.shape[1] - rows)]
+            copies.append(pltpu.make_async_copy(part, small.at[whose, origin], osem.at[len(copies)]))
+            copies[-1].start()
+    for copy in copies:
+        copy.wait()
+
+
+def write_call(mine, value, rows, widths, outs):
+    count, all_rows, columns = value.shape
+    shapes = [pltpu.HBM((2 * count * rows, width), F32) for width in widths]
+    if all_rows > rows:
+        shapes.append(pltpu.HBM((2, count, all_rows - rows, columns), BF16))
     return pl.pallas_call(
-        weight_kernel,
-        out_shape=jax.ShapeDtypeStruct((rows, columns), BF16),
-        grid_spec=pltpu.PrefetchScalarGridSpec(
-            num_scalar_prefetch=1, grid=(count,), in_specs=[spec_left, spec_right], out_specs=spec_out
-        ),
-        compiler_params=pltpu.CompilerParams(vmem_limit_bytes=VMEM_LIMIT),
-        cost_estimate=pl.CostEstimate(flops=2 * tokens * rows * columns, bytes_accessed=2 * tokens * (rows + columns) + 2 * rows * columns, transcendentals=0),
-        name="weight_half",
-    )(info, *in_hbm(left, right))
-
-
-def last_weight_kernel(info, left, right, left_out, right_out, out):
-    step = pl.program_id(0)
-
-    @pl.when(step < pl.num_programs(0) - 1)
-    def _():
-        out[...] = mm(left[...], right[...], TN).astype(BF16)
-
-    @pl.when(step == pl.num_programs(0) - 1)
-    def _():
-        out[...] = mm(left_out[...], right_out[...], TN).astype(BF16)
-
-
-def last_weight_call(info, left, right, left_out, right_out, mine):
-    left, right, left_out, right_out = (a.reshape(-1, a.shape[-1]) for a in (left, right, left_out, right_out))
-    (tokens, columns), width = right.shape, left.shape[1]
-    rows, parts = width // 2, columns // width
-    half = lambda info: info[0] if mine else 1 - info[0]
+        functools.partial(write_kernel, mine, len(shapes)),
+        out_shape=shapes,
+        in_specs=[VMEM] + [ANY] * len(outs),
+        out_specs=[ANY] * len(shapes),
+        input_output_aliases={1 + n: n for n in range(len(outs))},
+        scratch_shapes=[pltpu.VMEM((count, rows, columns), F32), pltpu.SemaphoreType.DMA((3 * count,))],
+        compiler_params=pltpu.CompilerParams(vmem_limit_bytes=PASS_LIMIT),
+        cost_estimate=pl.CostEstimate(flops=0, bytes_accessed=6 * value.size, transcendentals=0),
+        name="write_half",
+    )(value, *in_hbm(*outs))
+
+
+def small_kernel(rep, crops, every, b_up, biases, gains, pooled_query, pooled_key):
+    count = every.shape[1]
+    fixed = b_up.shape[1] // every.shape[3] + 8
+    total = None
+    for core in range(2):
+        for chip in range(count):
+            rows = every[core, chip].astype(F32)
+            total = rows[:fixed] if total is None else total + rows[:fixed]
+            y, z = (0, chip) if chip < rep else (1, 2 * rep - 1 - chip)
+            first = ((2 * y + core) * rep + z) * crops
+            pooled_query[first : first + crops, :] = rows[fixed : fixed + crops]
+            pooled_key[first : first + crops, :] = rows[fixed + crops : fixed + 2 * crops]
+    width = every.shape[3]
+    for row in range(fixed - 8):
+        b_up[:, row * width : (row + 1) * width] = total[row : row + 1]
+    biases[...] = total[fixed - 8 : fixed - 2]
+    gains[...] = total[fixed - 2 :]
+
+
+def small_call(every, hidden, rep, crops):
+    width = every.shape[3]
+    shapes = [(1, hidden), (6, width), (2, width), (4 * rep * crops, width), (4 * rep * crops, width)]
     return pl.pallas_call(
-        last_weight_kernel,
-        out_shape=jax.ShapeDtypeStruct((rows, (parts + 1) * width), BF16),
-        grid_spec=pltpu.PrefetchScalarGridSpec(
-            num_scalar_prefetch=1,
-            grid=(parts + 1,),
-            in_specs=[
-                pl.BlockSpec((tokens, rows), lambda i, info: (0, half(info))),
-                pl.BlockSpec((tokens, width), lambda i, info: (0, jnp.minimum(i, parts - 1))),
-                pl.BlockSpec((tokens, rows), lambda i, info: (0, half(info))),
-                pl.BlockSpec((tokens, width), lambda i, info: (0, 0)),
-            ],
-            out_specs=pl.BlockSpec((rows, width), lambda i, info: (0, i)),
-        ),
-        compiler_params=pltpu.CompilerParams(vmem_limit_bytes=VMEM_LIMIT),
-        cost_estimate=pl.CostEstimate(flops=2 * tokens * rows * width * (parts + 1), bytes_accessed=12_000_000, transcendentals=0),
-        name="weight_half_two",
-    )(info, *in_hbm(left, right, left_out, right_out))
+        functools.partial(small_kernel, rep, crops),
+        out_shape=[jax.ShapeDtypeStruct(shape, F32) for shape in shapes],
+        in_specs=[VMEM],
+        out_specs=[VMEM] * 5,
+        name="small_sums",
+    )(every)
 
 
 def ring_plan(dp, rep):
     chips = [(0, z) for z in range(rep)] + [(1, z) for z in reversed(range(rep))]
     count = len(chips)
-    position = [0] * (dp * rep)
     pairs = []
     for core in range(2):
         order = chips if core == 0 else chips[::-1]
         index = [(2 * y + core) * rep + z for y, z in order]
-        for place, device in enumerate(index):
-            position[device] = place
-            pairs.append((device, index[(place + 1) % count]))
-    return count, position, pairs
-
-
-def place_kernel(info, half, *refs):
-    outs = refs[len(refs) // 2 :]
-    start = 0
-    for out in outs:
-        out[...] = half[:, start : start + out.shape[1]].astype(F32)
-        start += out.shape[1]
-
-
-def place_call(info, half, widths, outs):
-    rows, columns = half.shape
-    count = 4
-    tile = rows // count
-    return pl.pallas_call(
-        place_kernel if outs else lambda info, half, *refs: place_kernel(info, half, *refs, *refs),
-        out_shape=[jax.ShapeDtypeStruct((2 * rows, width), F32) for width in widths],
-        grid_spec=pltpu.PrefetchScalarGridSpec(
-            num_scalar_prefetch=1,
-            grid=(count,),
-            in_specs=[pl.BlockSpec((tile, columns), lambda i, info: (i, 0))] + [ANY] * len(outs),
-            out_specs=[pl.BlockSpec((tile, width), lambda i, info: (info[0] * count + i, 0)) for width in widths],
-        ),
-        input_output_aliases={2 + n: n for n in range(len(outs))},
-        compiler_params=pltpu.CompilerParams(vmem_limit_bytes=VMEM_LIMIT),
-        cost_estimate=pl.CostEstimate(flops=0, bytes_accessed=6 * rows * columns, transcendentals=0),
-        name="place_half",
-    )(info, half, *outs)
+        pairs += [(device, index[(place + 1) % count]) for place, device in enumerate(index)]
+    return count, pairs
 
 
 def tied(value, *others):
@@ -674,84 +769,34 @@
 
 
 class RingSum:
-    def __init__(self, own, other, core, place, plan, swap, widths):
-        self.count, _, self.pairs = plan
-        self.own, self.other = (a.reshape(self.count, -1, a.shape[-1]) for a in (own, other))
-        self.core, self.place, self.swap = core, place, swap
-        self.moving = self.block(place).astype(BF16)
-        self.step, self.half = 0, None
-        self.widths, self.outs, self.finished = widths, [], False
-
-    def block(self, number):
-        number = jnp.mod(number, self.count)
-        take = lambda a: lax.dynamic_index_in_dim(a, number, 0, keepdims=False).astype(F32)
-        return take(self.own) + take(self.other)
+    def __init__(self, own, other, place, plan):
+        self.count, self.pairs = plan
+        self.own, self.other, self.place = own, other, place
+        self.moving = self.block(0).astype(BF16)
+        self.step, self.extra, self.half = 0, None, None
+
+    def block(self, step):
+        return self.own[step].astype(F32) + self.other[step].astype(F32)
 
     def done(self):
         return self.step == 2 * self.count - 2
 
-    def put(self, number):
-        self.half = lax.dynamic_update_index_in_dim(self.half, self.moving, jnp.mod(number, self.count), 0)
-
     def advance(self, last):
         self.step += 1
+        spread = self.step - self.count + 1
         moving = tied(lax.ppermute(self.moving, AXES, self.pairs), last)
-        if self.step < self.count:
-            self.moving = (moving.astype(F32) + self.block(self.place - self.step)).astype(BF16)
-            if self.step == self.count - 1:
-                self.half = jnp.zeros(self.own.shape, BF16)
-                self.put(self.place + 1)
-            return
+        if spread <= 0:
+            moving = moving.astype(F32) + self.block(self.step)
+            moving = lax.reduce_precision(moving, 8, 7).astype(BF16)
+            if spread == 0 and self.extra is not None:
+                moving = jnp.concatenate([moving, self.extra])
+            if spread == 0:
+                self.half = jnp.zeros((self.count, *moving.shape), BF16)
         self.moving = moving
-        self.put(self.place - (self.step - self.count))
-
-    def finish(self, last):
-        if not self.outs:
-            self.half = self.half.reshape(-1, self.own.shape[-1])
-            self.swapped = lax.ppermute(self.half, AXES, self.swap)
-            self.outs = place_call(tied(self.core[None], last), self.half, self.widths, [])
-        else:
-            swapped = tied(self.swapped, last)
-            self.outs = place_call((1 - self.core)[None], swapped, self.widths, self.outs)
-            self.finished = True
-        return self.outs[0]
-
-
-class RingGather:
-    def __init__(self, value, cuts, core, place, rep, plan, swap):
-        self.cuts = cuts
-        self.count, _, self.pairs = plan
-        self.core, self.place, self.rep, self.swap = core, place, rep, swap
-        self.moving = value
-        self.parts = [value]
-        self.finished = False
-
-    def done(self):
-        return len(self.parts) == self.count
-
-    def advance(self, last):
-        self.moving = tied(lax.ppermute(self.moving, AXES, self.pairs), last)
-        self.parts.append(self.moving)
-
-    def finish(self, last):
-        core, rep = self.core, self.rep
-        count = self.count
-        own = jnp.stack(self.parts[::-1])
-        own = jnp.roll(own, self.place + 1, 0)
-        other = lax.ppermute(own, AXES, self.swap)
-        first = jnp.where(core == 0, own, other)
-        second = jnp.where(core == 0, other, own)[::-1]
-        both = jnp.stack([first, second], 1)
-        low, high = both[: count // 2], both[count // 2 :][::-1]
-        whole = jnp.stack([low, high])
-        whole = jnp.moveaxis(whole, 1, 2)
-        whole = whole.reshape((2 * 2 * rep,) + whole.shape[3:])
-        starts = [sum(self.cuts[:number]) for number in range(len(self.cuts))]
-        parts = [whole[:, start : start + cut] for start, cut in zip(starts, self.cuts)]
-        self.outs = [jnp.sum(parts[0], 0)] + [part.reshape(-1, part.shape[-1]) for part in parts[1:]]
-        self.outs = lax.optimization_barrier((*self.outs, last))[:-1]
-        self.finished = True
-        return self.outs[-1]
+        if spread >= 0:
+            number = jnp.mod(self.place + 1 - spread, self.count)
+            self.half = lax.dynamic_update_index_in_dim(self.half, moving, number, 0)
+        return moving
 
 
 AXES = ("dp", "rep")
@@ -777,11 +822,10 @@
     hidden = w_up.shape[-1]
     weights = (w_qkv, w_out, w_up, w_down, b_up, biases, gains)
 
-    core = jnp.mod(lax.axis_index("dp"), 2).astype(jnp.int32)
-    place = jnp.zeros((), jnp.int32)
+    core = lax.rem(lax.axis_index("dp"), 2)
+    place = ring_place(core, chip_number(lax.axis_index("dp"), lax.axis_index("rep"), rep), 2 * rep)
     if dp == 4:
         plan = ring_plan(dp, rep)
-        place = jnp.asarray(plan[1], jnp.int32)[lax.axis_index(AXES)]
     query_lengths, core, place, section = lax.optimization_barrier((query_lengths, core, place, section))
 
     def sum_of(vectors):
@@ -804,7 +848,7 @@
     for crop in range(1, crops):
         plan_of_calls += [(query(crop), query(crop - 1)), None]
     plan_of_calls += [(key(1), query(crops - 1)), None, (key(2), key(0)), None]
-    late_calls = [(key(crop), key(crop - 2)) for crop in range(3, crops + 2)]
+    late_calls = [(key(crop), idle) for crop in range(3, crops)] + [(idle, key(crop)) for crop in range(1, crops)]
     sent_on, pooled_rows = {}, {}
 
     def forward(mode, call, held, state, order, lengths=lengths):
@@ -840,61 +884,63 @@
             backs += 1
 
     section, core, place, vector = lax.optimization_barrier((section, core, place, sum_of(vectors)))
-    core_info = core[None]
     swap = [(d * rep + z, (d ^ 1) * rep + z) for d in range(dp) for z in range(rep)]
-    products = (
-        lambda mine, core_info: weight_call(core_info, state["act"], grads["bg"], mine),
-        lambda mine, core_info: weight_call(core_info, state["low"], grads["ug"], mine),
-        lambda mine, core_info: last_weight_call(
-            core_info, state["xs"], grads["qg"], state["mix"], grads["ag"], mine
-        ),
-    )
-    widths = [(width,), (hidden,), (3 * width, width)]
     if dp == 4:
-        rings, last = [], vector
-
-        def advance(last):
+        count, ratio = 2 * rep, hidden // width
+        small = jnp.concatenate([vector, pool(0)]).astype(BF16)
+        used_rows = small.shape[0] + crops
+        small_rows = -(-used_rows // 16) * 16
+        widths = [(width,), (hidden,), (3 * width, width)]
+        pairs = [(state["act"], grads["bg"]), (state["low"], grads["ug"]), (state["xs"], grads["qg"]), (state["mix"], grads["ag"])]
+        groups = [
+            [(0, part, 0) for part in range(ratio)],
+            [(1, 0, part) for part in range(ratio)],
+            [(2, 0, part) for part in range(3)] + [(3, 0, 0)],
+        ]
+        halves = weights_call(pairs, groups, [vector])
+        waiting = [(own, lax.ppermute(theirs, AXES, swap)) for theirs, own in halves]
+        rings, last = [], halves[0][1]
+
+        def advance(last, begun=0):
             for ring in rings:
                 if not ring.done():
-                    ring.advance(last)
-                    last = ring.moving
-                elif not ring.finished:
-                    last = ring.finish(last)
+                    last = ring.advance(last)
+            while len(rings) < begun:
+                rings.append(RingSum(*waiting[len(rings)], place, plan))
+                last = rings[-1].moving
             return last
 
-        for product, cut in zip(products, widths):
-            theirs = product(False, tied(core_info, last))
-            last = advance(theirs)
-            other = lax.ppermute(theirs, AXES, swap)
-            own = product(True, tied(core_info, last))
-            last = advance(own)
-            rings.append(RingSum(own, other, core, place, plan, swap, cut))
-            last = rings[-1].moving
-        sums = list(rings)
+        last = advance(last, 1)
         for call in late_calls:
-            pooled, _, _ = forward("pass", call, None, {}, [], (query_lengths, tied(key_lengths, last)))
-            last = advance(pooled)
-        small = jnp.concatenate([vector, pool(0), pool(1)])
-        gather = RingGather(small, (vector.shape[0], crops, crops), core, place, rep, plan, swap)
-        rings.insert(0, gather)
-        while not all(ring.finished for ring in rings):
+            pooled, _, _ = forward("pass", call, None, {}, [last])
+            last = advance(pooled, 3)
+        rings[0].extra = jnp.pad(
+            jnp.concatenate([small, pool(1).astype(BF16)]), ((0, small_rows - used_rows), (0, 0))
+        )
+        while not all(ring.done() for ring in rings):
             last = advance(last)
-        totals = [out for ring in sums for out in ring.outs]
-        vector, pooled_query, pooled_key = gather.outs
+        swapped = [lax.ppermute(ring.half, AXES, swap) for ring in rings]
+        outs = [write_call(True, ring.half, ring.own.shape[1], cut, []) for ring, cut in zip(rings, widths)]
+        outs = [
+            write_call(False, other, ring.own.shape[1], cut, out)
+            for ring, other, cut, out in zip(rings, swapped, widths, outs)
+        ]
+        (grad_down, every), grad_up, grad_last = outs
+        totals = [grad_down, *grad_up, *grad_last]
+        grad_b_up, grad_biases, grad_gains, pooled_query, pooled_key = small_call(every, hidden, rep, crops)
     else:
         totals = []
-        for product in products:
-            theirs, own = product(False, core_info), product(True, core_info)
-            both = jnp.where(core == 0, jnp.stack([own, theirs]), jnp.stack([theirs, own]))
-            totals.append(lax.psum(both.reshape(-1, own.shape[-1]), AXES).astype(F32))
-        totals += [totals[2][:, 3 * width :]]
-        totals[2] = totals[2][:, : 3 * width]
+        for left, right in (("act", "bg"), ("low", "ug"), ("xs", "qg"), ("mix", "ag")):
+            left, right = (a.reshape(-1, a.shape[-1]) for a in (state[left][:crops], grads[right]))
+            totals.append(lax.psum(mm(left, right, TN), AXES))
         for call in late_calls:
             forward("pass", call, None, {}, [])
         vector = lax.psum(vector, AXES)
+        ratio = hidden // width
+        grad_b_up = vector[:ratio].reshape(1, hidden)
+        grad_biases, grad_gains = vector[ratio : ratio + 6], vector[ratio + 6 :]
         pooled_query = lax.all_gather(pool(0), AXES, axis=0, tiled=True)
         pooled_key = lax.all_gather(pool(1), AXES, axis=0, tiled=True)
-    ratio = hidden // width
     return (
         pooled_query[None],
         pooled_key[None],
@@ -903,9 +949,9 @@
         totals[3][None],
         totals[1][None],
         totals[0][None],
-        vector[:ratio].reshape(1, hidden),
-        vector[None, ratio : ratio + 6],
-        vector[None, ratio + 6 : ratio + 8],
+        grad_b_up,
+        grad_biases[None],
+        grad_gains[None],
     )
 
 

time: 392 us -> 372 us (0.949)
  the two profiles are of different devices: /device:TPU:3 before, /device:TPU:1 now
where the time goes in v4:
time: 372 us; the launch traced here: 366 us
  Pallas kernels  190 us (51%)
  waiting for transfers between devices  74.6 us (20%)
  starting transfers between devices  66.7 us (18%)
  other arithmetic  26.3 us (7%)
  local copies, waits for them, and re-layouts  6.23 us (2%)
    pallas_call x11, Pallas kernels, forward_call(): pl.pallas_call(functools.partial(forward_kernel, mode, crops, recv is Non...  98.4 us
    ppermute x42, waiting for transfers between devices, advance(): moving = tied(lax.ppermute(self.moving, AXES, self.pairs), last)  71.7 us
    pallas_call x5, Pallas kernels, backward_call(): pl.pallas_call(functools.partial(backward_kernel, crops, recv is None, le...  45.1 us
    ppermute x42, starting transfers between devices, advance(): moving = tied(lax.ppermute(self.moving, AXES, self.pairs), last)  32.8 us
    pallas_call x1, Pallas kernels, weights_call(): pl.pallas_call(functools.partial(weights_kernel, groups), out_shape=[pltp...  29.5 us
    convert_element_type x19, other arithmetic, advance(): moving = lax.reduce_precision(moving, 8, 7).astype(BF16)  20.7 us
    ppermute x8, starting transfers between devices, up(): return lax.ppermute(value, 'section', [(0, 1)])  16.8 us
    pallas_call x6, Pallas kernels, write_call(): pl.pallas_call(functools.partial(write_kernel, mine, len(shapes)), out_sh...  14.8 us
  transfers between devices with their start and end apart: 60, of which 37 were waited for; matrix products, arithmetic and copies ran while one was open for 8% of the time, Pallas kernels for 34%

profile of v4, /device:TPU:1, one launch (start us, length us, event | category | flops | bytes accessed | tf_op | source)
XLA Modules:
  0.0 365.9 jit_solution(12913346092998849819)
XLA Ops:
  4.2 12.7 %forward_crop.11 = (bf16[256,768]{1,0:T(8,128)(2,1)S(1)}, f32[1,768]{1,0:T(1,128)S(1)}, bf16[3,256,2304]{2,1,0:T(8,128)(2,1)S(1)}, bf16[3,256,768]{2,1,0:T(8,128...) custom-call(s32[4]{0:T(128)S(1)} %copy-done.4, ...), custom_call_target="tpu_custom_call" | custom-call | flops 3623878656 | bytes 8000000 | tf_op jit(solution)/shard_map/forward_crop/pallas_call | solution.py:317
  18.2 12.9 %forward_crop.12 = (bf16[256,768]{1,0:T(8,128)(2,1)S(1)}, f32[1,768]{1,0:T(1,128)S(1)}, bf16[3,256,2304]{2,1,0:T(8,128)(2,1)S(1)}, bf16[3,256,768]{2,1,0:T(8,128...) custom-call(s32[4]{0:T(128)S(1)} %copy-done.4, ...), custom_call_target="tpu_custom_call", output_to_operand_aliasing={{2}: (11, {}), {3}: (12, {}), {4}: (13, {}), {5}: (14, {}),... | custom-call | flops 3623878656 | bytes 8000000 | tf_op jit(solution)/shard_map/forward_crop/pallas_call | solution.py:317
  31.1 9.0 %forward_crop.13 = (bf16[256,768]{1,0:T(8,128)(2,1)S(1)}, f32[1,768]{1,0:T(1,128)S(1)}, bf16[3,256,2304]{2,1,0:T(8,128)(2,1)S(1)}, bf16[3,256,768]{2,1,0:T(8,128...) custom-call(s32[4]{0:T(128)S(1)} %copy-done.4, ...), custom_call_target="tpu_custom_call", output_to_operand_aliasing={{2}: (12, {}), {3}: (13, {}), {4}: (14, {}), {5}: (15, {}),... | custom-call | flops 3623878656 | bytes 8000000 | tf_op jit(solution)/shard_map/forward_crop/pallas_call | solution.py:317
  41.5 5.8 %backward_crop.5 = (bf16[256,768]{1,0:T(8,128)(2,1)S(1)}, f32[12,768]{1,0:T(8,128)S(1)}, f32[4,256,768]{2,1,0:T(8,128)}, bf16[4,256,768]{2,1,0:T(8,128)(2,1)}, b...) custom-call(s32[4]{0:T(128)S(1)} %copy-done.4, ...), custom_call_target="tpu_custom_call" | custom-call | flops 3623878656 | bytes 8000000 | tf_op jit(solution)/shard_map/backward_crop/pallas_call | solution.py:530
  48.6 1.5 collective-permute-done.3.refs_0_
  50.1 8.9 %forward_crop.14 = (bf16[256,768]{1,0:T(8,128)(2,1)S(1)}, f32[1,768]{1,0:T(1,128)S(1)}, bf16[3,256,2304]{2,1,0:T(8,128)(2,1)S(1)}, bf16[3,256,768]{2,1,0:T(8,128...) custom-call(s32[4]{0:T(128)S(1)} %copy-done.4, ...), custom_call_target="tpu_custom_call", output_to_operand_aliasing={{2}: (12, {}), {3}: (13, {}), {4}: (14, {}), {5}: (15, {}),... | custom-call | flops 3623878656 | bytes 8000000 | tf_op jit(solution)/shard_map/forward_crop/pallas_call | solution.py:317
  59.1 3.2 collective-permute-start.5
  62.3 9.5 %backward_crop.6 = (bf16[256,768]{1,0:T(8,128)(2,1)S(1)}, f32[12,768]{1,0:T(8,128)S(1)}, f32[4,256,768]{2,1,0:T(8,128)}, bf16[4,256,768]{2,1,0:T(8,128)(2,1)}, b...) custom-call(s32[4]{0:T(128)S(1)} %copy-done.4, ...), custom_call_target="tpu_custom_call", output_to_operand_aliasing={{2}: (15, {}), {3}: (16, {}), {4}: (17, {}), {5}: (18, {}),... | custom-call | flops 3623878656 | bytes 8000000 | tf_op jit(solution)/shard_map/backward_crop/pallas_call | solution.py:530
  73.1 9.3 %forward_crop.15 = (bf16[256,768]{1,0:T(8,128)(2,1)S(1)}, f32[1,768]{1,0:T(1,128)S(1)}, bf16[3,256,2304]{2,1,0:T(8,128)(2,1)S(1)}, bf16[3,256,768]{2,1,0:T(8,128...) custom-call(s32[4]{0:T(128)S(1)} %copy-done.4, ...), custom_call_target="tpu_custom_call", output_to_operand_aliasing={{2}: (12, {}), {3}: (13, {}), {4}: (14, {}), {5}: (15, {}),... | custom-call | flops 3623878656 | bytes 8000000 | tf_op jit(solution)/shard_map/forward_crop/pallas_call | solution.py:317
  82.4 3.1 collective-permute-start.7
  85.5 9.8 %backward_crop.7 = (bf16[256,768]{1,0:T(8,128)(2,1)S(1)}, f32[12,768]{1,0:T(8,128)S(1)}, f32[4,256,768]{2,1,0:T(8,128)}, bf16[4,256,768]{2,1,0:T(8,128)(2,1)}, b...) custom-call(s32[4]{0:T(128)S(1)} %copy-done.4, ...), custom_call_target="tpu_custom_call", output_to_operand_aliasing={{2}: (15, {}), {3}: (16, {}), {4}: (17, {}), {5}: (18, {}),... | custom-call | flops 3623878656 | bytes 8000000 | tf_op jit(solution)/shard_map/backward_crop/pallas_call | solution.py:530
  96.6 4.0 %collective-permute-start = (bf16[256,768]{1,0:T(8,128)(2,1)S(1)}, bf16[256,768]{1,0:T(8,128)(2,1)S(1)}, u32[]{:S(2)}, u32[]{:S(2)}) collective-permute-start(bf16[256,768]{1,0:T(8,128)(2,1)S(1)} %get-tuple-element.229), channel_id=1, source_target_pairs={{0,16},{1,17},{2,18},{3,19},{4,20},{5,21},{6,22},{7,23},{8,24},{9,... | collective-permute-start | bytes 1179656 | tf_op jit(solution)/shard_map/ppermute | solution.py:835
  100.7 10.5 %forward_crop.16 = (bf16[256,768]{1,0:T(8,128)(2,1)S(1)}, f32[1,768]{1,0:T(1,128)S(1)}, bf16[3,256,2304]{2,1,0:T(8,128)(2,1)S(1)}, bf16[3,256,768]{2,1,0:T(8,128...) custom-call(s32[4]{0:T(128)S(1)} %copy-done.4, ...), custom_call_target="tpu_custom_call", output_to_operand_aliasing={{2}: (12, {}), {3}: (13, {}), {4}: (14, {}), {5}: (15, {}),... | custom-call | flops 3623878656 | bytes 8000000 | tf_op jit(solution)/shard_map/forward_crop/pallas_call | solution.py:317
  111.2 9.5 %backward_crop.8 = (bf16[256,768]{1,0:T(8,128)(2,1)S(1)}, f32[12,768]{1,0:T(8,128)S(1)}, f32[4,256,768]{2,1,0:T(8,128)}, bf16[4,256,768]{2,1,0:T(8,128)(2,1)}, b...) custom-call(s32[4]{0:T(128)S(1)} %copy-done.4, ...), custom_call_target="tpu_custom_call", output_to_operand_aliasing={{2}: (15, {}), {3}: (16, {}), {4}: (17, {}), {5}: (18, {}),... | custom-call | flops 3623878656 | bytes 8000000 | tf_op jit(solution)/shard_map/backward_crop/pallas_call | solution.py:530
  122.0 10.6 %forward_crop.17 = (bf16[256,768]{1,0:T(8,128)(2,1)S(1)}, f32[1,768]{1,0:T(1,128)S(1)}, bf16[3,256,2304]{2,1,0:T(8,128)(2,1)S(1)}, bf16[3,256,768]{2,1,0:T(8,128...) custom-call(s32[4]{0:T(128)S(1)} %copy-done.4, ...), custom_call_target="tpu_custom_call", output_to_operand_aliasing={{2}: (12, {}), {3}: (13, {}), {4}: (14, {}), {5}: (15, {}),... | custom-call | flops 3623878656 | bytes 8000000 | tf_op jit(solution)/shard_map/forward_crop/pallas_call | solution.py:317
  132.7 10.5 %backward_crop.9 = (bf16[256,768]{1,0:T(8,128)(2,1)}, f32[12,768]{1,0:T(8,128)S(1)}, f32[4,256,768]{2,1,0:T(8,128)}, bf16[4,256,768]{2,1,0:T(8,128)(2,1)}, bf16[...) custom-call(s32[4]{0:T(128)S(1)} %copy-done.4, ...), custom_call_target="tpu_custom_call", output_to_operand_aliasing={{2}: (15, {}), {3}: (16, {}), {4}: (17, {}), {5}: (18, {}),... | custom-call | flops 3623878656 | bytes 8000000 | tf_op jit(solution)/shard_map/backward_crop/pallas_call | solution.py:530
  143.2 29.5 %weight_gradients.1 = (bf16[8,192,768]{2,1,0:T(8,128)(2,1)}, bf16[8,192,768]{2,1,0:T(8,128)(2,1)}, bf16[8,48,3072]{2,1,0:T(8,128)(2,1)}, bf16[8,48,3072]{2,1,0:T...) custom-call(bf16[1280,3072]{1,0:T(8,128)(2,1)} %bitcast.199, bf16[1280,768]{1,0:T(8,128)(2,1)} %bitcast.204, ...), custom_call_target="tpu_custom_call" | custom-call | flops 14495514624 | bytes 40000000 | tf_op jit(solution)/shard_map/weight_gradients/pallas_call | solution.py:658
  172.7 2.1 collective-permute-start.9
  180.4 2.1 collective-permute-start.10
  183.8 2.1 collective-permute-start.18
  186.0 11.7 %forward_crop.18 = (bf16[256,768]{1,0:T(8,128)(2,1)S(1)}, f32[1,768]{1,0:T(1,128)S(1)}) custom-call(s32[4]{0:T(128)S(1)} %copy-done.5, s32[4]{0:T(128)S(1)} %copy-done.7, bf16[4,256,768]{2,1,0:T(8,128)(2,1)} %own.18, bf16[1,2,768,2304]{3,2,1,0:T(8,128)(2,1)} %refs_1_.11, bf16[1,2,768,768]{3,2,1,0:T(8,128)(2,1)} %refs_2_.11, ...), custom_call_target="tpu_custom_call" | custom-call | flops 3623878656 | bytes 8000000 | tf_op jit(solution)/shard_map/forward_crop/pallas_call | solution.py:317
  203.9 1.4 forward_crop.19
  205.3 3.2 collective-permute-done.11
  215.2 10.1 %forward_crop.20 = (bf16[256,768]{1,0:T(8,128)(2,1)}, f32[1,768]{1,0:T(1,128)S(1)}) custom-call(s32[4]{0:T(128)S(1)} %copy-done.5, s32[4]{0:T(128)S(1)} %copy-done.7, bf16[4,256,768]{2,1,0:T(8,128)(2,1)} %own.21, bf16[256,768]{1,0:T(8,128)(2,1)S(1)} %collective-permute-done.15.refs_0_, bf16[1,2,768,2304]{3,2,1,0:T(8,128)(2,1)} %refs_1_.11, ...), custom_call_target="tpu_custom_call" | custom-call | flops 3623878656 | bytes 8000000 | tf_op jit(solution)/shard_map/forward_crop/pallas_call | solution.py:317
  229.7 1.4 forward_crop.21
  233.7 1.7 collective-permute-done.25
  237.2 1.4 collective-permute-done.24
  240.4 1.4 collective-permute-done.23
  243.5 1.4 collective-permute-done.28
  246.7 1.4 collective-permute-done.27
  249.9 1.4 collective-permute-done.26
  253.0 1.4 collective-permute-done.31
  256.2 1.4 collective-permute-done.30
  259.3 1.4 collective-permute-done.29
  269.0 1.7 collective-permute-done.32
  271.3 2.5 collective-permute-done.37
  279.1 1.6 collective-permute-done.35
  281.4 2.5 collective-permute-done.40
  284.5 2.5 collective-permute-done.39
  287.7 3.0 collective-permute-done.38
  291.4 2.5 collective-permute-done.43
  294.5 2.5 collective-permute-done.42
  297.7 3.0 collective-permute-done.41
  301.4 2.5 collective-permute-done.46
  304.6 2.5 collective-permute-done.45
  307.8 3.0 collective-permute-done.44
  311.4 2.5 collective-permute-done.49
  314.9 2.2 collective-permute-done.48
  317.8 3.0 collective-permute-done.47
  321.4 2.5 collective-permute-done.52
  324.6 2.5 collective-permute-done.51
  327.8 3.0 collective-permute-done.50
  330.7 3.2 collective-permute-done.55
  334.6 2.5 collective-permute-done.54
  337.8 3.4 collective-permute-start.53
  341.2 2.8 collective-permute-start.59
  344.1 3.1 collective-permute-start.58
  347.2 2.5 write_half.6
  349.7 2.4 write_half.10.refs_1_
  352.2 2.4 write_half.8
  354.6 2.4 write_half.11
  357.0 2.4 write_half.9
  359.5 2.5 write_half.7
  362.0 1.9 small_sums.1
  (174 shorter events, 79.5 us)
Async XLA Ops:
  16.9 14.2 %collective-permute-start.1 = (bf16[256,768]{1,0:T(8,128)(2,1)S(1)}, bf16[256,768]{1,0:T(8,128)(2,1)S(1)}, u32[]{:S(2)}, u32[]{:S(2)}) collective-permute-start(bf16[256,768]{1,0:T(8,128)(2,1)S(1)} %get-tuple-element.234), channel_id=1, source_target_pairs={{0,16},{1,17},{2,18},{3,19},{4,20},{5,21},{6,22},{7,23},{8,24},{9,... | collective-permute-start | bytes 1179656 | tf_op jit(solution)/shard_map/ppermute | solution.py:835
  40.1 10.0 %collective-permute-start.3 = (bf16[256,768]{1,0:T(8,128)(2,1)S(1)}, bf16[256,768]{1,0:T(8,128)(2,1)S(1)}, u32[]{:S(2)}, u32[]{:S(2)}) collective-permute-start(bf16[256,768]{1,0:T(8,128)(2,1)S(1)} %get-tuple-element.254), channel_id=1, source_target_pairs={{0,16},{1,17},{2,18},{3,19},{4,20},{5,21},{6,22},{7,23},{8,24},{9,... | collective-permute-start | bytes 1179656 | tf_op jit(solution)/shard_map/ppermute | solution.py:835
  47.3 15.0 %collective-permute-start.2 = (bf16[256,768]{1,0:T(8,128)(2,1)S(1)}, bf16[256,768]{1,0:T(8,128)(2,1)S(1)}, u32[]{:S(2)}, u32[]{:S(2)}) collective-permute-start(bf16[256,768]{1,0:T(8,128)(2,1)S(1)} %get-tuple-element.253), channel_id=1, source_target_pairs={{16,0},{17,1},{18,2},{19,3},{20,4},{21,5},{22,6},{23,7},{24,8},{25... | collective-permute-start | bytes 1179656 | tf_op jit(solution)/shard_map/ppermute | solution.py:838
  59.1 14.0 %collective-permute-start.5 = (bf16[256,768]{1,0:T(8,128)(2,1)S(1)}, bf16[256,768]{1,0:T(8,128)(2,1)S(1)}, u32[]{:S(2)}, u32[]{:S(2)}) collective-permute-start(bf16[256,768]{1,0:T(8,128)(2,1)S(1)} %get-tuple-element.273), channel_id=1, source_target_pairs={{0,16},{1,17},{2,18},{3,19},{4,20},{5,21},{6,22},{7,23},{8,24},{9,... | collective-permute-start | bytes 1179656 | tf_op jit(solution)/shard_map/ppermute | solution.py:835
  71.8 13.7 %collective-permute-start.4 = (bf16[256,768]{1,0:T(8,128)(2,1)S(1)}, bf16[256,768]{1,0:T(8,128)(2,1)S(1)}, u32[]{:S(2)}, u32[]{:S(2)}) collective-permute-start(bf16[256,768]{1,0:T(8,128)(2,1)S(1)} %get-tuple-element.272), channel_id=1, source_target_pairs={{16,0},{17,1},{18,2},{19,3},{20,4},{21,5},{22,6},{23,7},{24,8},{25... | collective-permute-start | bytes 1179656 | tf_op jit(solution)/shard_map/ppermute | solution.py:838
  82.4 18.3 %collective-permute-start.7 = (bf16[256,768]{1,0:T(8,128)(2,1)S(1)}, bf16[256,768]{1,0:T(8,128)(2,1)S(1)}, u32[]{:S(2)}, u32[]{:S(2)}) collective-permute-start(bf16[256,768]{1,0:T(8,128)(2,1)S(1)} %get-tuple-element.292), channel_id=1, source_target_pairs={{0,16},{1,17},{2,18},{3,19},{4,20},{5,21},{6,22},{7,23},{8,24},{9,... | collective-permute-start | bytes 1179656 | tf_op jit(solution)/shard_map/ppermute | solution.py:835
  95.3 15.9 %collective-permute-start.6 = (bf16[256,768]{1,0:T(8,128)(2,1)S(1)}, bf16[256,768]{1,0:T(8,128)(2,1)S(1)}, u32[]{:S(2)}, u32[]{:S(2)}) collective-permute-start(bf16[256,768]{1,0:T(8,128)(2,1)S(1)} %get-tuple-element.291), channel_id=1, source_target_pairs={{16,0},{17,1},{18,2},{19,3},{20,4},{21,5},{22,6},{23,7},{24,8},{25... | collective-permute-start | bytes 1179656 | tf_op jit(solution)/shard_map/ppermute | solution.py:838
  96.6 25.4 %collective-permute-start = (bf16[256,768]{1,0:T(8,128)(2,1)S(1)}, bf16[256,768]{1,0:T(8,128)(2,1)S(1)}, u32[]{:S(2)}, u32[]{:S(2)}) collective-permute-start(bf16[256,768]{1,0:T(8,128)(2,1)S(1)} %get-tuple-element.229), channel_id=1, source_target_pairs={{0,16},{1,17},{2,18},{3,19},{4,20},{5,21},{6,22},{7,23},{8,24},{9,... | collective-permute-start | bytes 1179656 | tf_op jit(solution)/shard_map/ppermute | solution.py:835
  120.7 11.9 %collective-permute-start.8 = (bf16[256,768]{1,0:T(8,128)(2,1)S(1)}, bf16[256,768]{1,0:T(8,128)(2,1)S(1)}, u32[]{:S(2)}, u32[]{:S(2)}) collective-permute-start(bf16[256,768]{1,0:T(8,128)(2,1)S(1)} %get-tuple-element.319), channel_id=1, source_target_pairs={{16,0},{17,1},{18,2},{19,3},{20,4},{21,5},{22,6},{23,7},{24,8},{25... | collective-permute-start | bytes 1179656 | tf_op jit(solution)/shard_map/ppermute | solution.py:838
  143.2 42.8 %copy-start.1 = (f32[1,2,2,768]{3,2,1,0:T(2,128)S(1)}, f32[1,2,2,768]{3,2,1,0:T(2,128)}, u32[]{:S(2)}) copy-start(f32[1,2,2,768]{3,2,1,0:T(2,128)} %refs_7_.15) | copy-start | bytes 36868
  143.2 42.8 %copy-start.3 = (f32[1,2,3072]{2,1,0:T(2,128)S(1)}, f32[1,2,3072]{2,1,0:T(2,128)}, u32[]{:S(2)}) copy-start(f32[1,2,3072]{2,1,0:T(2,128)} %refs_5_.26) | copy-start | bytes 73732
  143.2 42.8 %copy-start.5 = (s32[4]{0:T(128)S(1)}, s32[4]{0:T(128)}, u32[]{:S(2)}) copy-start(s32[4]{0:T(128)} %query_lengths.10) | copy-start | bytes 52
  143.2 42.8 %copy-start.7 = (s32[4]{0:T(128)S(1)}, s32[4]{0:T(128)}, u32[]{:S(2)}) copy-start(s32[4]{0:T(128)} %key_lengths.21) | copy-start | bytes 52
  172.7 6.6 %collective-permute-start.9 = (bf16[8,192,768]{2,1,0:T(8,128)(2,1)}, bf16[8,192,768]{2,1,0:T(8,128)(2,1)}, u32[]{:S(2)}, u32[]{:S(2)}) collective-permute-start(bf16[8,192,768]{2,1,0:T(8,128)(2,1)} %get-tuple-element.346), channel_id=1, source_target_pairs={{0,4},{1,5},{2,6},{3,7},{4,0},{5,1},{6,2},{7,3},{8,12},{9,13},{10,... | collective-permute-start | bytes 7077896 | tf_op jit(solution)/shard_map/ppermute | solution.py:901
  174.8 7.9 %collective-permute-start.17 = (bf16[8,48,3072]{2,1,0:T(8,128)(2,1)}, bf16[8,48,3072]{2,1,0:T(8,128)(2,1)}, u32[]{:S(2)}, u32[]{:S(2)}) collective-permute-start(bf16[8,48,3072]{2,1,0:T(8,128)(2,1)} %get-tuple-element.356), channel_id=1, source_target_pairs={{0,4},{1,5},{2,6},{3,7},{4,0},{5,1},{6,2},{7,3},{8,12},{9,13},{10,... | collective-permute-start | bytes 7077896 | tf_op jit(solution)/shard_map/ppermute | solution.py:901
  174.9 22.8 %collective-permute-start.13 = (bf16[8,48,3072]{2,1,0:T(8,128)(2,1)}, bf16[8,48,3072]{2,1,0:T(8,128)(2,1)}, u32[]{:S(2)}, u32[]{:S(2)}) collective-permute-start(bf16[8,48,3072]{2,1,0:T(8,128)(2,1)} %get-tuple-element.351), channel_id=1, source_target_pairs={{0,4},{1,5},{2,6},{3,7},{4,0},{5,1},{6,2},{7,3},{8,12},{9,13},{10,... | collective-permute-start | bytes 7077896 | tf_op jit(solution)/shard_map/ppermute | solution.py:901
  175.3 27.2 %collective-permute-start.12 = (bf16[256,768]{1,0:T(8,128)(2,1)S(1)}, bf16[256,768]{1,0:T(8,128)(2,1)S(1)}, u32[]{:S(2)}, u32[]{:S(2)}) collective-permute-start(bf16[256,768]{1,0:T(8,128)(2,1)S(1)} %get-tuple-element.349), channel_id=1, source_target_pairs={{0,16},{1,17},{2,18},{3,19},{4,20},{5,21},{6,22},{7,23},{8,24},{9,... | collective-permute-start | bytes 1179656 | tf_op jit(solution)/shard_map/ppermute | solution.py:835
  176.6 38.5 %collective-permute-start.15 = (bf16[256,768]{1,0:T(8,128)(2,1)S(1)}, bf16[256,768]{1,0:T(8,128)(2,1)S(1)}, u32[]{:S(2)}, u32[]{:S(2)}) collective-permute-start(bf16[256,768]{1,0:T(8,128)(2,1)S(1)} %get-tuple-element.354), channel_id=1, source_target_pairs={{0,16},{1,17},{2,18},{3,19},{4,20},{5,21},{6,22},{7,23},{8,24},{9,... | collective-permute-start | bytes 1179656 | tf_op jit(solution)/shard_map/ppermute | solution.py:835
  180.4 19.7 %collective-permute-start.10 = (bf16[192,768]{1,0:T(8,128)(2,1)S(1)}, bf16[192,768]{1,0:T(8,128)(2,1)S(1)}, u32[]{:S(2)}, u32[]{:S(2)}) collective-permute-start(bf16[192,768]{1,0:T(8,128)(2,1)S(1)} %fusion.42.refs_7_), channel_id=1, source_target_pairs={{0,1},{1,2},{2,3},{3,11},{11,10},{10,9},{9,8},{8,0},{12,13},{13,14... | collective-permute-start | bytes 884744 | tf_op jit(solution)/shard_map/ppermute | solution.py:787
  183.8 27.1 %collective-permute-start.18 = (bf16[48,3072]{1,0:T(8,128)(2,1)S(1)}, bf16[48,3072]{1,0:T(8,128)(2,1)S(1)}, u32[]{:S(2)}, u32[]{:S(2)}) collective-permute-start(bf16[48,3072]{1,0:T(8,128)(2,1)S(1)} %fusion.44), channel_id=1, source_target_pairs={{0,1},{1,2},{2,3},{3,11},{11,10},{10,9},{9,8},{8,0},{12,13},{13,14... | collective-permute-start | bytes 884744 | tf_op jit(solution)/shard_map/ppermute | solution.py:787
  198.8 14.3 %collective-permute-start.16 = (bf16[48,3072]{1,0:T(8,128)(2,1)S(1)}, bf16[48,3072]{1,0:T(8,128)(2,1)S(1)}, u32[]{:S(2)}, u32[]{:S(2)}) collective-permute-start(bf16[48,3072]{1,0:T(8,128)(2,1)S(1)} %fusion.43.refs_8_), channel_id=1, source_target_pairs={{0,1},{1,2},{2,3},{3,11},{11,10},{10,9},{9,8},{8,0},{12,13},{13,14... | collective-permute-start | bytes 884744 | tf_op jit(solution)/shard_map/ppermute | solution.py:787
  200.1 29.6 %collective-permute-start.20 = (bf16[256,768]{1,0:T(8,128)(2,1)S(1)}, bf16[256,768]{1,0:T(8,128)(2,1)S(1)}, u32[]{:S(2)}, u32[]{:S(2)}) collective-permute-start(bf16[256,768]{1,0:T(8,128)(2,1)S(1)} %get-tuple-element.361), channel_id=1, source_target_pairs={{0,16},{1,17},{2,18},{3,19},{4,20},{5,21},{6,22},{7,23},{8,24},{9,... | collective-permute-start | bytes 1179656 | tf_op jit(solution)/shard_map/ppermute | solution.py:835
  202.5 5.9 %collective-permute-start.11 = (bf16[192,768]{1,0:T(8,128)(2,1)S(1)}, bf16[192,768]{1,0:T(8,128)(2,1)S(1)}, u32[]{:S(2)}, u32[]{:S(2)}) collective-permute-start(bf16[192,768]{1,0:T(8,128)(2,1)S(1)} %fusion.41), channel_id=1, source_target_pairs={{0,1},{1,2},{2,3},{3,11},{11,10},{10,9},{9,8},{8,0},{12,13},{13,14... | collective-permute-start | bytes 884744 | tf_op jit(solution)/shard_map/ppermute | solution.py:787
  209.5 15.7 %collective-permute-start.14 = (bf16[192,768]{1,0:T(8,128)(2,1)S(1)}, bf16[192,768]{1,0:T(8,128)(2,1)S(1)}, u32[]{:S(2)}, u32[]{:S(2)}) collective-permute-start(bf16[192,768]{1,0:T(8,128)(2,1)S(1)} %fusion.39), channel_id=1, source_target_pairs={{0,1},{1,2},{2,3},{3,11},{11,10},{10,9},{9,8},{8,0},{12,13},{13,14... | collective-permute-start | bytes 884744 | tf_op jit(solution)/shard_map/ppermute | solution.py:787
  212.0 15.0 %collective-permute-start.22 = (bf16[48,3072]{1,0:T(8,128)(2,1)S(1)}, bf16[48,3072]{1,0:T(8,128)(2,1)S(1)}, u32[]{:S(2)}, u32[]{:S(2)}) collective-permute-start(bf16[48,3072]{1,0:T(8,128)(2,1)S(1)} %fusion.37), channel_id=1, source_target_pairs={{0,1},{1,2},{2,3},{3,11},{11,10},{10,9},{9,8},{8,0},{12,13},{13,14... | collective-permute-start | bytes 884744 | tf_op jit(solution)/shard_map/ppermute | solution.py:787
  214.1 14.2 %collective-permute-start.21 = (bf16[48,3072]{1,0:T(8,128)(2,1)S(1)}, bf16[48,3072]{1,0:T(8,128)(2,1)S(1)}, u32[]{:S(2)}, u32[]{:S(2)}) collective-permute-start(bf16[48,3072]{1,0:T(8,128)(2,1)S(1)} %fusion.35.refs_8_), channel_id=1, source_target_pairs={{0,1},{1,2},{2,3},{3,11},{11,10},{10,9},{9,8},{8,0},{12,13},{13,14... | collective-permute-start | bytes 884744 | tf_op jit(solution)/shard_map/ppermute | solution.py:787
  226.3 5.9 %collective-permute-start.19 = (bf16[192,768]{1,0:T(8,128)(2,1)S(1)}, bf16[192,768]{1,0:T(8,128)(2,1)S(1)}, u32[]{:S(2)}, u32[]{:S(2)}) collective-permute-start(bf16[192,768]{1,0:T(8,128)(2,1)S(1)} %fusion.33), channel_id=1, source_target_pairs={{0,1},{1,2},{2,3},{3,11},{11,10},{10,9},{9,8},{8,0},{12,13},{13,14... | collective-permute-start | bytes 884744 | tf_op jit(solution)/shard_map/ppermute | solution.py:787
  228.1 7.3 %collective-permute-start.25 = (bf16[48,3072]{1,0:T(8,128)(2,1)S(1)}, bf16[48,3072]{1,0:T(8,128)(2,1)S(1)}, u32[]{:S(2)}, u32[]{:S(2)}) collective-permute-start(bf16[48,3072]{1,0:T(8,128)(2,1)S(1)} %fusion.31), channel_id=1, source_target_pairs={{0,1},{1,2},{2,3},{3,11},{11,10},{10,9},{9,8},{8,0},{12,13},{13,14... | collective-permute-start | bytes 884744 | tf_op jit(solution)/shard_map/ppermute | solution.py:787
  229.5 9.1 %collective-permute-start.24 = (bf16[48,3072]{1,0:T(8,128)(2,1)S(1)}, bf16[48,3072]{1,0:T(8,128)(2,1)S(1)}, u32[]{:S(2)}, u32[]{:S(2)}) collective-permute-start(bf16[48,3072]{1,0:T(8,128)(2,1)S(1)} %fusion.29.refs_8_), channel_id=1, source_target_pairs={{0,1},{1,2},{2,3},{3,11},{11,10},{10,9},{9,8},{8,0},{12,13},{13,14... | collective-permute-start | bytes 884744 | tf_op jit(solution)/shard_map/ppermute | solution.py:787
  233.3 8.4 %collective-permute-start.23 = (bf16[192,768]{1,0:T(8,128)(2,1)S(1)}, bf16[192,768]{1,0:T(8,128)(2,1)S(1)}, u32[]{:S(2)}, u32[]{:S(2)}) collective-permute-start(bf16[192,768]{1,0:T(8,128)(2,1)S(1)} %fusion.27), channel_id=1, source_target_pairs={{0,1},{1,2},{2,3},{3,11},{11,10},{10,9},{9,8},{8,0},{12,13},{13,14... | collective-permute-start | bytes 884744 | tf_op jit(solution)/shard_map/ppermute | solution.py:787
  236.5 8.4 %collective-permute-start.28 = (bf16[48,3072]{1,0:T(8,128)(2,1)S(1)}, bf16[48,3072]{1,0:T(8,128)(2,1)S(1)}, u32[]{:S(2)}, u32[]{:S(2)}) collective-permute-start(bf16[48,3072]{1,0:T(8,128)(2,1)S(1)} %fusion.25), channel_id=1, source_target_pairs={{0,1},{1,2},{2,3},{3,11},{11,10},{10,9},{9,8},{8,0},{12,13},{13,14... | collective-permute-start | bytes 884744 | tf_op jit(solution)/shard_map/ppermute | solution.py:787
  239.7 8.4 %collective-permute-start.27 = (bf16[48,3072]{1,0:T(8,128)(2,1)S(1)}, bf16[48,3072]{1,0:T(8,128)(2,1)S(1)}, u32[]{:S(2)}, u32[]{:S(2)}) collective-permute-start(bf16[48,3072]{1,0:T(8,128)(2,1)S(1)} %fusion.23), channel_id=1, source_target_pairs={{0,1},{1,2},{2,3},{3,11},{11,10},{10,9},{9,8},{8,0},{12,13},{13,14... | collective-permute-start | bytes 884744 | tf_op jit(solution)/shard_map/ppermute | solution.py:787
  242.8 8.4 %collective-permute-start.26 = (bf16[192,768]{1,0:T(8,128)(2,1)S(1)}, bf16[192,768]{1,0:T(8,128)(2,1)S(1)}, u32[]{:S(2)}, u32[]{:S(2)}) collective-permute-start(bf16[192,768]{1,0:T(8,128)(2,1)S(1)} %fusion.21), channel_id=1, source_target_pairs={{0,1},{1,2},{2,3},{3,11},{11,10},{10,9},{9,8},{8,0},{12,13},{13,14... | collective-permute-start | bytes 884744 | tf_op jit(solution)/shard_map/ppermute | solution.py:787
  246.0 8.4 %collective-permute-start.31 = (bf16[48,3072]{1,0:T(8,128)(2,1)S(1)}, bf16[48,3072]{1,0:T(8,128)(2,1)S(1)}, u32[]{:S(2)}, u32[]{:S(2)}) collective-permute-start(bf16[48,3072]{1,0:T(8,128)(2,1)S(1)} %fusion.19), channel_id=1, source_target_pairs={{0,1},{1,2},{2,3},{3,11},{11,10},{10,9},{9,8},{8,0},{12,13},{13,14... | collective-permute-start | bytes 884744 | tf_op jit(solution)/shard_map/ppermute | solution.py:787
  249.2 8.4 %collective-permute-start.30 = (bf16[48,3072]{1,0:T(8,128)(2,1)S(1)}, bf16[48,3072]{1,0:T(8,128)(2,1)S(1)}, u32[]{:S(2)}, u32[]{:S(2)}) collective-permute-start(bf16[48,3072]{1,0:T(8,128)(2,1)S(1)} %fusion.17), channel_id=1, source_target_pairs={{0,1},{1,2},{2,3},{3,11},{11,10},{10,9},{9,8},{8,0},{12,13},{13,14... | collective-permute-start | bytes 884744 | tf_op jit(solution)/shard_map/ppermute | solution.py:787
  252.3 8.4 %collective-permute-start.29 = (bf16[192,768]{1,0:T(8,128)(2,1)S(1)}, bf16[192,768]{1,0:T(8,128)(2,1)S(1)}, u32[]{:S(2)}, u32[]{:S(2)}) collective-permute-start(bf16[192,768]{1,0:T(8,128)(2,1)S(1)} %fusion.15), channel_id=1, source_target_pairs={{0,1},{1,2},{2,3},{3,11},{11,10},{10,9},{9,8},{8,0},{12,13},{13,14... | collective-permute-start | bytes 884744 | tf_op jit(solution)/shard_map/ppermute | solution.py:787
  255.5 8.4 %collective-permute-start.34 = (bf16[48,3072]{1,0:T(8,128)(2,1)S(1)}, bf16[48,3072]{1,0:T(8,128)(2,1)S(1)}, u32[]{:S(2)}, u32[]{:S(2)}) collective-permute-start(bf16[48,3072]{1,0:T(8,128)(2,1)S(1)} %fusion.13), channel_id=1, source_target_pairs={{0,1},{1,2},{2,3},{3,11},{11,10},{10,9},{9,8},{8,0},{12,13},{13,14... | collective-permute-start | bytes 884744 | tf_op jit(solution)/shard_map/ppermute | solution.py:787
  258.6 8.4 %collective-permute-start.33 = (bf16[48,3072]{1,0:T(8,128)(2,1)S(1)}, bf16[48,3072]{1,0:T(8,128)(2,1)S(1)}, u32[]{:S(2)}, u32[]{:S(2)}) collective-permute-start(bf16[48,3072]{1,0:T(8,128)(2,1)S(1)} %fusion.11), channel_id=1, source_target_pairs={{0,1},{1,2},{2,3},{3,11},{11,10},{10,9},{9,8},{8,0},{12,13},{13,14... | collective-permute-start | bytes 884744 | tf_op jit(solution)/shard_map/ppermute | solution.py:787
  261.8 8.9 %collective-permute-start.32 = (bf16[224,768]{1,0:T(8,128)(2,1)S(1)}, bf16[224,768]{1,0:T(8,128)(2,1)S(1)}, u32[]{:S(2)}, u32[]{:S(2)}) collective-permute-start(bf16[224,768]{1,0:T(8,128)(2,1)S(1)} %pad_maximum_fusion), channel_id=1, source_target_pairs={{0,1},{1,2},{2,3},{3,11},{11,10},{10,9},{9,8},{8,0},{12,13},{13,14... | collective-permute-start | bytes 1032200 | tf_op jit(solution)/shard_map/ppermute | solution.py:787
  265.0 8.9 %collective-permute-start.37 = (bf16[48,3072]{1,0:T(8,128)(2,1)S(1)}, bf16[48,3072]{1,0:T(8,128)(2,1)S(1)}, u32[]{:S(2)}, u32[]{:S(2)}) collective-permute-start(bf16[48,3072]{1,0:T(8,128)(2,1)S(1)} %fusion.7), channel_id=1, source_target_pairs={{0,1},{1,2},{2,3},{3,11},{11,10},{10,9},{9,8},{8,0},{12,13},{13,14... | collective-permute-start | bytes 884744 | tf_op jit(solution)/shard_map/ppermute | solution.py:787
  268.1 8.9 %collective-permute-start.36 = (bf16[48,3072]{1,0:T(8,128)(2,1)S(1)}, bf16[48,3072]{1,0:T(8,128)(2,1)S(1)}, u32[]{:S(2)}, u32[]{:S(2)}) collective-permute-start(bf16[48,3072]{1,0:T(8,128)(2,1)S(1)} %fusion.5), channel_id=1, source_target_pairs={{0,1},{1,2},{2,3},{3,11},{11,10},{10,9},{9,8},{8,0},{12,13},{13,14... | collective-permute-start | bytes 884744 | tf_op jit(solution)/shard_map/ppermute | solution.py:787
  270.7 10.0 %collective-permute-start.35 = (bf16[224,768]{1,0:T(8,128)(2,1)S(1)}, bf16[224,768]{1,0:T(8,128)(2,1)S(1)}, u32[]{:S(2)}, u32[]{:S(2)}) collective-permute-start(bf16[224,768]{1,0:T(8,128)(2,1)S(1)} %collective-permute-done.32), channel_id=1, source_target_pairs={{0,1},{1,2},{2,3},{3,11},{11,10},{10,9},{9,8},{8,0},{12,13},{13,14... | collective-permute-start | bytes 1032200 | tf_op jit(solution)/shard_map/ppermute | solution.py:787
  275.2 8.6 %collective-permute-start.40 = (bf16[48,3072]{1,0:T(8,128)(2,1)S(1)}, bf16[48,3072]{1,0:T(8,128)(2,1)S(1)}, u32[]{:S(2)}, u32[]{:S(2)}) collective-permute-start(bf16[48,3072]{1,0:T(8,128)(2,1)S(1)} %get-tuple-element.427), channel_id=1, source_target_pairs={{0,1},{1,2},{2,3},{3,11},{11,10},{10,9},{9,8},{8,0},{12,13},{13,14... | collective-permute-start | bytes 884744 | tf_op jit(solution)/shard_map/ppermute | solution.py:787
  278.4 8.6 %collective-permute-start.39 = (bf16[48,3072]{1,0:T(8,128)(2,1)S(1)}, bf16[48,3072]{1,0:T(8,128)(2,1)S(1)}, u32[]{:S(2)}, u32[]{:S(2)}) collective-permute-start(bf16[48,3072]{1,0:T(8,128)(2,1)S(1)} %get-tuple-element.429), channel_id=1, source_target_pairs={{0,1},{1,2},{2,3},{3,11},{11,10},{10,9},{9,8},{8,0},{12,13},{13,14... | collective-permute-start | bytes 884744 | tf_op jit(solution)/shard_map/ppermute | solution.py:787
  280.7 10.0 %collective-permute-start.38 = (bf16[224,768]{1,0:T(8,128)(2,1)S(1)}, bf16[224,768]{1,0:T(8,128)(2,1)S(1)}, u32[]{:S(2)}, u32[]{:S(2)}) collective-permute-start(bf16[224,768]{1,0:T(8,128)(2,1)S(1)} %collective-permute-done.35), channel_id=1, source_target_pairs={{0,1},{1,2},{2,3},{3,11},{11,10},{10,9},{9,8},{8,0},{12,13},{13,14... | collective-permute-start | bytes 1032200 | tf_op jit(solution)/shard_map/ppermute | solution.py:787
  283.9 10.0 %collective-permute-start.43 = (bf16[48,3072]{1,0:T(8,128)(2,1)S(1)}, bf16[48,3072]{1,0:T(8,128)(2,1)S(1)}, u32[]{:S(2)}, u32[]{:S(2)}) collective-permute-start(bf16[48,3072]{1,0:T(8,128)(2,1)S(1)} %collective-permute-done.40), channel_id=1, source_target_pairs={{0,1},{1,2},{2,3},{3,11},{11,10},{10,9},{9,8},{8,0},{12,13},{13,14... | collective-permute-start | bytes 884744 | tf_op jit(solution)/shard_map/ppermute | solution.py:787
  287.0 10.0 %collective-permute-start.42 = (bf16[48,3072]{1,0:T(8,128)(2,1)S(1)}, bf16[48,3072]{1,0:T(8,128)(2,1)S(1)}, u32[]{:S(2)}, u32[]{:S(2)}) collective-permute-start(bf16[48,3072]{1,0:T(8,128)(2,1)S(1)} %collective-permute-done.39), channel_id=1, source_target_pairs={{0,1},{1,2},{2,3},{3,11},{11,10},{10,9},{9,8},{8,0},{12,13},{13,14... | collective-permute-start | bytes 884744 | tf_op jit(solution)/shard_map/ppermute | solution.py:787
  290.7 10.0 %collective-permute-start.41 = (bf16[224,768]{1,0:T(8,128)(2,1)S(1)}, bf16[224,768]{1,0:T(8,128)(2,1)S(1)}, u32[]{:S(2)}, u32[]{:S(2)}) collective-permute-start(bf16[224,768]{1,0:T(8,128)(2,1)S(1)} %collective-permute-done.38), channel_id=1, source_target_pairs={{0,1},{1,2},{2,3},{3,11},{11,10},{10,9},{9,8},{8,0},{12,13},{13,14... | collective-permute-start | bytes 1032200 | tf_op jit(solution)/shard_map/ppermute | solution.py:787
  293.9 10.0 %collective-permute-start.46 = (bf16[48,3072]{1,0:T(8,128)(2,1)S(1)}, bf16[48,3072]{1,0:T(8,128)(2,1)S(1)}, u32[]{:S(2)}, u32[]{:S(2)}) collective-permute-start(bf16[48,3072]{1,0:T(8,128)(2,1)S(1)} %collective-permute-done.43), channel_id=1, source_target_pairs={{0,1},{1,2},{2,3},{3,11},{11,10},{10,9},{9,8},{8,0},{12,13},{13,14... | collective-permute-start | bytes 884744 | tf_op jit(solution)/shard_map/ppermute | solution.py:787
  297.0 10.0 %collective-permute-start.45 = (bf16[48,3072]{1,0:T(8,128)(2,1)S(1)}, bf16[48,3072]{1,0:T(8,128)(2,1)S(1)}, u32[]{:S(2)}, u32[]{:S(2)}) collective-permute-start(bf16[48,3072]{1,0:T(8,128)(2,1)S(1)} %collective-permute-done.42), channel_id=1, source_target_pairs={{0,1},{1,2},{2,3},{3,11},{11,10},{10,9},{9,8},{8,0},{12,13},{13,14... | collective-permute-start | bytes 884744 | tf_op jit(solution)/shard_map/ppermute | solution.py:787
  300.7 10.0 %collective-permute-start.44 = (bf16[224,768]{1,0:T(8,128)(2,1)S(1)}, bf16[224,768]{1,0:T(8,128)(2,1)S(1)}, u32[]{:S(2)}, u32[]{:S(2)}) collective-permute-start(bf16[224,768]{1,0:T(8,128)(2,1)S(1)} %collective-permute-done.41), channel_id=1, source_target_pairs={{0,1},{1,2},{2,3},{3,11},{11,10},{10,9},{9,8},{8,0},{12,13},{13,14... | collective-permute-start | bytes 1032200 | tf_op jit(solution)/shard_map/ppermute | solution.py:787
  303.9 10.0 %collective-permute-start.49 = (bf16[48,3072]{1,0:T(8,128)(2,1)S(1)}, bf16[48,3072]{1,0:T(8,128)(2,1)S(1)}, u32[]{:S(2)}, u32[]{:S(2)}) collective-permute-start(bf16[48,3072]{1,0:T(8,128)(2,1)S(1)} %collective-permute-done.46), channel_id=1, source_target_pairs={{0,1},{1,2},{2,3},{3,11},{11,10},{10,9},{9,8},{8,0},{12,13},{13,14... | collective-permute-start | bytes 884744 | tf_op jit(solution)/shard_map/ppermute | solution.py:787
  307.0 10.0 %collective-permute-start.48 = (bf16[48,3072]{1,0:T(8,128)(2,1)S(1)}, bf16[48,3072]{1,0:T(8,128)(2,1)S(1)}, u32[]{:S(2)}, u32[]{:S(2)}) collective-permute-start(bf16[48,3072]{1,0:T(8,128)(2,1)S(1)} %collective-permute-done.45), channel_id=1, source_target_pairs={{0,1},{1,2},{2,3},{3,11},{11,10},{10,9},{9,8},{8,0},{12,13},{13,14... | collective-permute-start | bytes 884744 | tf_op jit(solution)/shard_map/ppermute | solution.py:787
  310.7 10.0 %collective-permute-start.47 = (bf16[224,768]{1,0:T(8,128)(2,1)S(1)}, bf16[224,768]{1,0:T(8,128)(2,1)S(1)}, u32[]{:S(2)}, u32[]{:S(2)}) collective-permute-start(bf16[224,768]{1,0:T(8,128)(2,1)S(1)} %collective-permute-done.44), channel_id=1, source_target_pairs={{0,1},{1,2},{2,3},{3,11},{11,10},{10,9},{9,8},{8,0},{12,13},{13,14... | collective-permute-start | bytes 1032200 | tf_op jit(solution)/shard_map/ppermute | solution.py:787
  313.9 10.0 %collective-permute-start.52 = (bf16[48,3072]{1,0:T(8,128)(2,1)S(1)}, bf16[48,3072]{1,0:T(8,128)(2,1)S(1)}, u32[]{:S(2)}, u32[]{:S(2)}) collective-permute-start(bf16[48,3072]{1,0:T(8,128)(2,1)S(1)} %collective-permute-done.49), channel_id=1, source_target_pairs={{0,1},{1,2},{2,3},{3,11},{11,10},{10,9},{9,8},{8,0},{12,13},{13,14... | collective-permute-start | bytes 884744 | tf_op jit(solution)/shard_map/ppermute | solution.py:787
  317.1 10.0 %collective-permute-start.51 = (bf16[48,3072]{1,0:T(8,128)(2,1)S(1)}, bf16[48,3072]{1,0:T(8,128)(2,1)S(1)}, u32[]{:S(2)}, u32[]{:S(2)}) collective-permute-start(bf16[48,3072]{1,0:T(8,128)(2,1)S(1)} %collective-permute-done.48), channel_id=1, source_target_pairs={{0,1},{1,2},{2,3},{3,11},{11,10},{10,9},{9,8},{8,0},{12,13},{13,14... | collective-permute-start | bytes 884744 | tf_op jit(solution)/shard_map/ppermute | solution.py:787
  320.7 10.0 %collective-permute-start.50 = (bf16[224,768]{1,0:T(8,128)(2,1)S(1)}, bf16[224,768]{1,0:T(8,128)(2,1)S(1)}, u32[]{:S(2)}, u32[]{:S(2)}) collective-permute-start(bf16[224,768]{1,0:T(8,128)(2,1)S(1)} %collective-permute-done.47), channel_id=1, source_target_pairs={{0,1},{1,2},{2,3},{3,11},{11,10},{10,9},{9,8},{8,0},{12,13},{13,14... | collective-permute-start | bytes 1032200 | tf_op jit(solution)/shard_map/ppermute | solution.py:787
  323.9 10.0 %collective-permute-start.55 = (bf16[48,3072]{1,0:T(8,128)(2,1)S(1)}, bf16[48,3072]{1,0:T(8,128)(2,1)S(1)}, u32[]{:S(2)}, u32[]{:S(2)}) collective-permute-start(bf16[48,3072]{1,0:T(8,128)(2,1)S(1)} %collective-permute-done.52), channel_id=1, source_target_pairs={{0,1},{1,2},{2,3},{3,11},{11,10},{10,9},{9,8},{8,0},{12,13},{13,14... | collective-permute-start | bytes 884744 | tf_op jit(solution)/shard_map/ppermute | solution.py:787
  327.1 10.0 %collective-permute-start.54 = (bf16[48,3072]{1,0:T(8,128)(2,1)S(1)}, bf16[48,3072]{1,0:T(8,128)(2,1)S(1)}, u32[]{:S(2)}, u32[]{:S(2)}) collective-permute-start(bf16[48,3072]{1,0:T(8,128)(2,1)S(1)} %collective-permute-done.51), channel_id=1, source_target_pairs={{0,1},{1,2},{2,3},{3,11},{11,10},{10,9},{9,8},{8,0},{12,13},{13,14... | collective-permute-start | bytes 884744 | tf_op jit(solution)/shard_map/ppermute | solution.py:787
  333.9 7.3 %collective-permute-start.57 = (bf16[48,3072]{1,0:T(8,128)(2,1)S(1)}, bf16[48,3072]{1,0:T(8,128)(2,1)S(1)}, u32[]{:S(2)}, u32[]{:S(2)}) collective-permute-start(bf16[48,3072]{1,0:T(8,128)(2,1)S(1)} %collective-permute-done.55), channel_id=1, source_target_pairs={{0,1},{1,2},{2,3},{3,11},{11,10},{10,9},{9,8},{8,0},{12,13},{13,14... | collective-permute-start | bytes 884744 | tf_op jit(solution)/shard_map/ppermute | solution.py:787
  337.1 7.0 %collective-permute-start.56 = (bf16[48,3072]{1,0:T(8,128)(2,1)S(1)}, bf16[48,3072]{1,0:T(8,128)(2,1)S(1)}, u32[]{:S(2)}, u32[]{:S(2)}) collective-permute-start(bf16[48,3072]{1,0:T(8,128)(2,1)S(1)} %collective-permute-done.54), channel_id=1, source_target_pairs={{0,1},{1,2},{2,3},{3,11},{11,10},{10,9},{9,8},{8,0},{12,13},{13,14... | collective-permute-start | bytes 884744 | tf_op jit(solution)/shard_map/ppermute | solution.py:787
  337.8 21.7 %collective-permute-start.53 = (bf16[8,224,768]{2,1,0:T(8,128)(2,1)S(1)}, bf16[8,224,768]{2,1,0:T(8,128)(2,1)S(1)}, u32[]{:S(2)}, u32[]{:S(2)}) collective-permute-start(bf16[8,224,768]{2,1,0:T(8,128)(2,1)S(1)} %bitcast_dynamic-update-slice_fusion.refs_0_), channel_id=1, source_target_pairs={{0,4},{1,5},{2,6},{3,7},{4,0},{5,1},{6,2},{7,3},{8,12},{9,13},{10,... | collective-permute-start | bytes 8257544 | tf_op jit(solution)/shard_map/ppermute | solution.py:922
  341.2 13.4 %collective-permute-start.59 = (bf16[8,48,3072]{2,1,0:T(8,128)(2,1)S(1)}, bf16[8,48,3072]{2,1,0:T(8,128)(2,1)S(1)}, u32[]{:S(2)}, u32[]{:S(2)}) collective-permute-start(bf16[8,48,3072]{2,1,0:T(8,128)(2,1)S(1)} %bitcast_dynamic-update-slice_fusion.8.refs_0_), channel_id=1, source_target_pairs={{0,4},{1,5},{2,6},{3,7},{4,0},{5,1},{6,2},{7,3},{8,12},{9,13},{10,... | collective-permute-start | bytes 7077896 | tf_op jit(solution)/shard_map/ppermute | solution.py:922
  344.1 13.0 %collective-permute-start.58 = (bf16[8,48,3072]{2,1,0:T(8,128)(2,1)S(1)}, bf16[8,48,3072]{2,1,0:T(8,128)(2,1)S(1)}, u32[]{:S(2)}, u32[]{:S(2)}) collective-permute-start(bf16[8,48,3072]{2,1,0:T(8,128)(2,1)S(1)} %bitcast_dynamic-update-slice_fusion.16.refs_0_), channel_id=1, source_target_pairs={{0,4},{1,5},{2,6},{3,7},{4,0},{5,1},{6,2},{7,3},{8,12},{9,13},{10,... | collective-permute-start | bytes 7077896 | tf_op jit(solution)/shard_map/ppermute | solution.py:922
  (15 other events, 92.4 us)

commit v5 on v4

--- a/solution.py
+++ b/solution.py
@@ -11,8 +11,8 @@
 HEAD = 64
 EPS = 1e-06
 NEG = -1000000000.0
-HELD_CROPS = 3
-HELD_LIMIT = 10 * 1024 * 1024
+HELD_CROPS = 4
+HELD_LIMIT = 12 * 1024 * 1024
 PASS_LIMIT = 22 * 1024 * 1024
 WEIGHTS_LIMIT = 50 * 1024 * 1024
 NT = (((1,), (1,)), ((), ()))
@@ -58,15 +58,15 @@
         lower = rows
 
 
-VMEM_NAMES = ("qkv", "n1", "gp", "n2", "inv")
-HBM_NAMES = ("att", "xs", "mix", "low", "act")
+VMEM_NAMES = ("n1", "gp", "n2", "inv")
+HBM_NAMES = ("qkv", "att", "xs", "mix", "low", "act")
 
 
 def save_shapes(crops, crop_len, width, hidden):
     heads = width // HEAD
     held = min(HELD_CROPS, crops)
     return {
-        "qkv": ((held, crop_len, 3 * width), BF16),
+        "qkv": ((crops + 1, crop_len, 3 * width), BF16),
         "att": ((crops + 1, heads, crop_len, crop_len), BF16),
         "n1": ((held, crop_len, width), BF16),
         "gp": ((held, crop_len, hidden), BF16),
@@ -128,8 +128,7 @@
         held = weights
     else:
         held = take(4)
-    if not save:
-        kept["qkv"] = take(1)[0]
+    bqkv = take(1)[0]
     batt = take(1)[0] if save else None
     bx, bmix, blow, bact, wsem, xsem, osem = refs
     wqkv, wout, wup, wdown = held
@@ -139,7 +138,7 @@
     base = hidden // width
     section, live, member, crop, length = assigned(crops, query_lengths, key_lengths)
     which = member if save else 0
-    place = jnp.where(member == 0, lax.rem(crop, HELD_CROPS), 1) if save else 0
+    place = jnp.where(member == 0, lax.rem(crop, HELD_CROPS), 0) if save else 0
 
     loaded = crops[0][0]
 
@@ -148,8 +147,10 @@
         return pltpu.make_async_copy(weights[number].at[0, loaded if save else 1], target, wsem.at[number])
 
     def weight_ready(number):
-        if mode != "held":
+        if mode == "pass":
             weight_copy(number).wait()
+        if mode == "load":
+            pl.when(member == loaded)(weight_copy(number).wait)
 
     def bias(row):
         return biases[0, member, row : row + 1, :]
@@ -162,7 +163,7 @@
 
     def body(rows):
         keys = -(-rows // 128) * 128
-        qkv = kept["qkv"]
+        qkv = bqkv
         started = []
 
         def clear(ref, *index):
@@ -186,15 +187,15 @@
             part = mm(x, wqkv[which, :, cols])
             if segment != 1:
                 part = part + bias(segment // 2)
-            qkv[place, :rows, cols] = part.astype(BF16)
-        clear(qkv, place)
+            qkv[:rows, cols] = part.astype(BF16)
+        finish(5, "qkv", qkv)
         masks = head_masks()
         key_valid = lax.broadcasted_iota(jnp.int32, (1, keys), 1) < length
         mixed = [None]
 
         def pair(part, head, row_count):
             start = part * width + head // 2 * 2 * HEAD
-            return qkv[place, :row_count, start : start + 2 * HEAD]
+            return qkv[:row_count, start : start + 2 * HEAD]
 
         def score(head):
             return mm(pair(0, head, rows), jnp.where(masks[head % 2], pair(1, head, keys), 0), NT)
@@ -286,6 +287,9 @@
                 bx[...] = recv[...]
 
         dispatch(length, crop_len, body)
+        if mode == "load":
+            for number in range(4):
+                pl.when(member != loaded)(weight_copy(number).wait)
 
     if mode == "load":
 
@@ -333,9 +337,8 @@
         input_output_aliases={first + i: 2 + i for i in range(len(aliased) + len(grown))},
         scratch_shapes=(weight_shapes if mode == "pass" else [])
         + [
-            pltpu.VMEM((1, crop_len, 3 * width), BF16)
-            if mode == "pass"
-            else pltpu.VMEM((width // HEAD, crop_len, crop_len), BF16)
+            pltpu.VMEM((crop_len, 3 * width), BF16),
+            *([] if mode == "pass" else [pltpu.VMEM((width // HEAD, crop_len, crop_len), BF16)]),
         ]
         + [
             pltpu.VMEM((crop_len, width), BF16),
@@ -344,7 +347,7 @@
             pltpu.VMEM((crop_len, hidden), BF16),
             pltpu.SemaphoreType.DMA((4,)),
             pltpu.SemaphoreType.DMA,
-            pltpu.SemaphoreType.DMA((5,)),
+            pltpu.SemaphoreType.DMA((6,)),
         ],
         compiler_params=pltpu.CompilerParams(vmem_limit_bytes=PASS_LIMIT if mode == "pass" else HELD_LIMIT),
         cost_estimate=crop_cost(weights, crop_len),
@@ -358,16 +361,16 @@
     return pl.CostEstimate(flops=2 * crop_len * size, bytes_accessed=8_000_000, transcendentals=0)
 
 
-def backward_kernel(crops, first, n_alias, lengths, cot, *refs):
+def backward_kernel(crops, first, n_alias, lengths, cot, sent, *refs):
     refs = list(refs)
     take = lambda count: [refs.pop(0) for _ in range(count)]
     recv = None if first else take(1)[0]
     wqkv, wout, wup, wdown, gains = take(5)
     kept = dict(zip(VMEM_NAMES, take(len(VMEM_NAMES))))
-    att = take(1)[0]
+    att, qkv = take(2)
     take(n_alias)
     dx_ref, vec_ref, ig_ref, bg_ref, ug_ref, ag_ref, qg_ref = take(7)
-    batt, bgin, bbg, bug, bag, bqg, bmg, bxg, asem, gsem, osem = refs
+    bqkv, batt, bgin, bbg, bug, bag, bqg, bmg, bxg, asem, osem = refs
     crop_len, width = bbg.shape
     hidden = bug.shape[1]
     heads = width // HEAD
@@ -379,7 +382,10 @@
         return gains[0, 0, row : row + 1, :]
 
     def att_copy():
-        return pltpu.make_async_copy(att.at[crop], batt, asem)
+        return pltpu.make_async_copy(att.at[crop], batt, asem.at[0])
+
+    def qkv_copy():
+        return pltpu.make_async_copy(qkv.at[crop], bqkv, asem.at[1])
 
     def body(rows):
         keys = -(-rows // 128) * 128
@@ -440,13 +446,14 @@
         column(base + 2, ag)
         bmg[:rows, :] = mm(ag, wout[0], NT).astype(BF16)
         att_copy().wait()
+        qkv_copy().wait()
         masks = head_masks()
         scale = HEAD**-0.5
         sums = [None]
 
         def pair(part, head, row_count):
             start = part * width + head // 2 * 2 * HEAD
-            return jnp.where(masks[head % 2], kept["qkv"][place, :row_count, start : start + 2 * HEAD], 0)
+            return jnp.where(masks[head % 2], bqkv[:row_count, start : start + 2 * HEAD], 0)
 
         def attention_grad(head):
             start = head // 2 * 2 * HEAD
@@ -481,8 +488,9 @@
         finish(3, bqg, qg_ref.at[crop])
         xg = sum_one + mm(bqg[:rows, :], wqkv[0], NT)
         dx = xg.astype(BF16)
-        dx_ref[:rows, :] = dx
-        clear(dx_ref)
+        dx_ref[:rows, :] = jnp.where(section == 0, sent[:rows, :], dx)
+        if rows < crop_len:
+            dx_ref[rows:, :] = jnp.where(section == 0, sent[rows:, :], 0)
         bxg[:rows, :] = jnp.where(section == 0, xg, dx.astype(F32))
         finish(4, bxg, ig_ref.at[crop])
         for copy in started:
@@ -491,6 +499,7 @@
     @pl.when(jnp.logical_not(live))
     def _():
         vec_ref[...] = jnp.zeros(vec_ref.shape, F32)
+        dx_ref[...] = sent[...]
 
     @pl.when(live)
     def _():
@@ -502,15 +511,14 @@
 
         @pl.when(section != 0)
         def _():
-            copy = pltpu.make_async_copy(cot.at[crop], bgin, gsem)
-            copy.start()
-            copy.wait()
+            bgin[...] = cot[crop]
 
         att_copy().start()
+        qkv_copy().start()
         dispatch(length, crop_len, body)
 
 
-def backward_call(lengths, crops, cot, recv, weights, held, state, grads, order=()):
+def backward_call(lengths, crops, cot, sent, recv, weights, held, state, grads, order=()):
     crop_count, crop_len, width = cot.shape
     hidden = weights[2].shape[-1]
     shapes = {
@@ -523,10 +531,10 @@
     names = tuple(shapes)
     aliased = in_hbm(*[grads[name] for name in names]) if grads else []
     arrived = [] if recv is None else [recv]
-    operands = [lengths, *in_hbm(cot), *arrived, *in_vmem(*held), weights[6]]
+    operands = [lengths, *in_vmem(cot), sent, *arrived, *in_vmem(*held), weights[6]]
     order = list(order)
-    operands += in_vmem(*[state[name] for name in VMEM_NAMES]) + in_hbm(state["att"]) + order + aliased
-    first = 8 + len(arrived) + len(VMEM_NAMES) + len(order)
+    operands += in_vmem(*[state[name] for name in VMEM_NAMES]) + in_hbm(state["att"], state["qkv"]) + order + aliased
+    first = 10 + len(arrived) + len(VMEM_NAMES) + len(order)
     outs = pl.pallas_call(
         functools.partial(backward_kernel, crops, recv is None, len(order) + len(aliased)),
         out_shape=[
@@ -534,10 +542,11 @@
             jax.ShapeDtypeStruct((hidden // width + 8, width), F32),
         ]
         + [pltpu.HBM(*shapes[name]) for name in names],
-        in_specs=[SMEM, ANY] + [VMEM] * (len(arrived) + 5 + len(VMEM_NAMES)) + [ANY] * (1 + len(order) + len(aliased)),
+        in_specs=[SMEM] + [VMEM] * (len(arrived) + 7 + len(VMEM_NAMES)) + [ANY] * (2 + len(order) + len(aliased)),
         out_specs=[VMEM, VMEM] + [ANY] * len(names),
         input_output_aliases={first + i: 2 + i for i in range(len(aliased))},
         scratch_shapes=[
+            pltpu.VMEM((crop_len, 3 * width), BF16),
             pltpu.VMEM((width // HEAD, crop_len, crop_len), BF16),
             pltpu.VMEM((crop_len, width), BF16),
             pltpu.VMEM((crop_len, width), BF16),
@@ -546,8 +555,7 @@
             pltpu.VMEM((crop_len, 3 * width), BF16),
             pltpu.VMEM((crop_len, width), BF16),
             pltpu.VMEM((crop_len, width), F32),
-            pltpu.SemaphoreType.DMA,
-            pltpu.SemaphoreType.DMA,
+            pltpu.SemaphoreType.DMA((2,)),
             pltpu.SemaphoreType.DMA((5,)),
         ],
         compiler_params=pltpu.CompilerParams(vmem_limit_bytes=HELD_LIMIT),
@@ -834,9 +842,6 @@
     def up(value):
         return lax.ppermute(value, "section", [(0, 1)])
 
-    def down(value):
-        return lax.ppermute(value, "section", [(1, 0)])
-
     state, grads = {}, {}
     vectors = []
 
@@ -844,23 +849,24 @@
     idle = (0, -1)
     query = lambda crop: (0, crop) if 0 <= crop < crops else idle
     key = lambda crop: (1, crop) if 0 <= crop < crops else idle
-    plan_of_calls = [(query(0), idle), (key(0), idle)]
-    for crop in range(1, crops):
-        plan_of_calls += [(query(crop), query(crop - 1)), None]
-    plan_of_calls += [(key(1), query(crops - 1)), None, (key(2), key(0)), None]
+    plan_of_calls = [(query(0), idle), (query(1), idle)]
+    for crop in range(crops):
+        ahead = query(crop + 2) if crop + 2 < crops else key(crop + 2 - crops)
+        plan_of_calls += [(ahead, query(crop)), None]
+    plan_of_calls += [(key(2), key(0)), None]
     late_calls = [(key(crop), idle) for crop in range(3, crops)] + [(idle, key(crop)) for crop in range(1, crops)]
     sent_on, pooled_rows = {}, {}
 
-    def forward(mode, call, held, state, order, lengths=lengths):
+    def forward(mode, call, held, state, order, later=False):
         sent, pooled, loaded, state = forward_call(
             mode, lengths, call, key_input if call[0][0] else query_input, sent_on.get(call[1]), weights, held, state, order
         )
         for number, done in enumerate(call):
             if done[1] >= 0:
                 pooled_rows[number, *done] = pooled
-        if call[0][1] >= 0:
+        if call[0][1] >= 0 and not later:
             sent_on[call[0]] = up(sent)
-        return pooled, loaded or held, state
+        return sent, pooled, loaded or held, state
 
     def pool(member):
         first, second = (jnp.concatenate([pooled_rows[number, member, crop] for crop in range(crops)]) for number in range(2))
@@ -868,19 +874,24 @@
 
     returned = held = None
     order = []
-    backs = 0
+    backs, encoders = 0, set()
     for number, call in enumerate(plan_of_calls):
         if call is not None:
-            pooled, held, state = forward("held" if number > 1 else "load", call, held, state, order)
+            later = 2 <= number < 2 * crops + 2
+            mode = "held" if call[0][0] in encoders else "load"
+            encoders.add(call[0][0])
+            sent, pooled, held, state = forward(mode, call, held, state, order, later)
             order = [pooled]
         else:
             assignment = (backs - 1, backs if backs < crops else -1)
             back, vector, grads = backward_call(
-                query_lengths, assignment, cotangent, returned, weights, held, state, grads, order
+                query_lengths, assignment, cotangent, sent, returned, weights, held, state, grads, order
             )
             order = [vector]
             vectors.append(vector)
-            returned = down(back)
+            if backs < crops:
+                returned = lax.ppermute(back, "section", [(0, 1), (1, 0)])
+                sent_on[plan_of_calls[number - 1][0]] = returned
             backs += 1
 
     section, core, place, vector = lax.optimization_barrier((section, core, place, sum_of(vectors)))
@@ -912,7 +923,7 @@
 
         last = advance(last, 1)
         for call in late_calls:
-            pooled, _, _ = forward("pass", call, None, {}, [last])
+            _, pooled, _, _ = forward("pass", call, None, {}, [last])
             last = advance(pooled, 3)
         rings[0].extra = jnp.pad(
             jnp.concatenate([small, pool(1).astype(BF16)]), ((0, small_rows - used_rows), (0, 0))

time: 372 us -> 363 us (0.976)
  starting transfers between devices: 66.7 us -> 38.9 us
  waiting for transfers between devices: 74.6 us -> 88.1 us
  Pallas kernels: 190 us -> 195 us
    ppermute x42, starting transfers between devices: 32.8 us -> 19.6 us  [advance(): moving = tied(lax.ppermute(self.moving, AXES, self.pairs), last)]
    ppermute x42, waiting for transfers between devices: 71.7 us -> 84.1 us  [advance(): moving = tied(lax.ppermute(self.moving, AXES, self.pairs), last)]
    ppermute x8 -> x4, starting transfers between devices: 16.8 us -> 5.24 us  [up(): return lax.ppermute(value, 'section', [(0, 1)])]
    pallas_call x11, Pallas kernels: 98.4 us -> 104 us  [forward_call(): pl.pallas_call(functools.partial(forward_kernel, mode, crops, recv is Non...]
  transfers between devices with their start and end apart: 60 -> 56, of which waited for: 37 -> 37; matrix products, arithmetic and copies ran while one was open for 8% -> 8% of each run, Pallas kernels for 34% -> 31%
where the time goes in v5:
time: 363 us; the launch traced here: 357 us
  Pallas kernels  195 us (54%)
  waiting for transfers between devices  88.1 us (24%)
  starting transfers between devices  38.9 us (11%)
  other arithmetic  26.4 us (7%)
  local copies, waits for them, and re-layouts  6.23 us (2%)
    pallas_call x11, Pallas kernels, forward_call(): pl.pallas_call(functools.partial(forward_kernel, mode, crops, recv is Non...  104 us
    ppermute x42, waiting for transfers between devices, advance(): moving = tied(lax.ppermute(self.moving, AXES, self.pairs), last)  84.1 us
    pallas_call x5, Pallas kernels, backward_call(): pl.pallas_call(functools.partial(backward_kernel, crops, recv is None, le...  44.3 us
    pallas_call x1, Pallas kernels, weights_call(): pl.pallas_call(functools.partial(weights_kernel, groups), out_shape=[pltp...  29.5 us
    convert_element_type x19, other arithmetic, advance(): moving = lax.reduce_precision(moving, 8, 7).astype(BF16)  20.7 us
    ppermute x42, starting transfers between devices, advance(): moving = tied(lax.ppermute(self.moving, AXES, self.pairs), last)  19.6 us
    pallas_call x6, Pallas kernels, write_call(): pl.pallas_call(functools.partial(write_kernel, mine, len(shapes)), out_sh...  14.8 us
    ppermute x3, starting transfers between devices, on_device(): swapped = [lax.ppermute(ring.half, AXES, swap) for ring in rings]  9.67 us
  transfers between devices with their start and end apart: 56, of which 37 were waited for; matrix products, arithmetic and copies ran while one was open for 8% of the time, Pallas kernels for 31%

profile of v5, /device:TPU:1, one launch (start us, length us, event | category | flops | bytes accessed | tf_op | source)
XLA Modules:
  0.0 356.7 jit_solution(4113481608386736304)
XLA Ops:
  4.2 13.4 %forward_crop.11 = (bf16[256,768]{1,0:T(8,128)(2,1)S(1)}, f32[1,768]{1,0:T(1,128)S(1)}, bf16[4,256,768]{2,1,0:T(8,128)(2,1)S(1)}, bf16[4,256,3072]{2,1,0:T(8,128...) custom-call(s32[4]{0:T(128)S(1)} %copy-done.5, ...), custom_call_target="tpu_custom_call" | custom-call | flops 3623878656 | bytes 8000000 | tf_op jit(solution)/shard_map/forward_crop/pallas_call | solution.py:321
  18.9 11.3 %forward_crop.12 = (bf16[256,768]{1,0:T(8,128)(2,1)S(1)}, f32[1,768]{1,0:T(1,128)S(1)}, bf16[4,256,768]{2,1,0:T(8,128)(2,1)S(1)}, bf16[4,256,3072]{2,1,0:T(8,128...) custom-call(s32[4]{0:T(128)S(1)} %copy-done.5, ...), custom_call_target="tpu_custom_call", output_to_operand_aliasing={{2}: (11, {}), {3}: (12, {}), {4}: (13, {}), {5}: (14, {}),... | custom-call | flops 3623878656 | bytes 8000000 | tf_op jit(solution)/shard_map/forward_crop/pallas_call | solution.py:321
  31.6 10.0 %forward_crop.13 = (bf16[256,768]{1,0:T(8,128)(2,1)S(1)}, f32[1,768]{1,0:T(1,128)S(1)}, bf16[4,256,768]{2,1,0:T(8,128)(2,1)S(1)}, bf16[4,256,3072]{2,1,0:T(8,128...) custom-call(s32[4]{0:T(128)S(1)} %copy-done.5, ...), custom_call_target="tpu_custom_call", output_to_operand_aliasing={{2}: (12, {}), {3}: (13, {}), {4}: (14, {}), {5}: (15, {}),... | custom-call | flops 3623878656 | bytes 8000000 | tf_op jit(solution)/shard_map/forward_crop/pallas_call | solution.py:321
  41.7 5.8 %backward_crop.5 = (bf16[256,768]{1,0:T(8,128)(2,1)S(1)}, f32[12,768]{1,0:T(8,128)S(1)}, f32[4,256,768]{2,1,0:T(8,128)}, bf16[4,256,768]{2,1,0:T(8,128)(2,1)}, b...) custom-call(s32[4]{0:T(128)S(1)} %copy-done.5, ...), custom_call_target="tpu_custom_call" | custom-call | flops 3623878656 | bytes 8000000 | tf_op jit(solution)/shard_map/backward_crop/pallas_call | solution.py:538
  48.4 10.0 %forward_crop.14 = (bf16[256,768]{1,0:T(8,128)(2,1)S(1)}, f32[1,768]{1,0:T(1,128)S(1)}, bf16[4,256,768]{2,1,0:T(8,128)(2,1)S(1)}, bf16[4,256,3072]{2,1,0:T(8,128...) custom-call(s32[4]{0:T(128)S(1)} %copy-done.5, ...), custom_call_target="tpu_custom_call", output_to_operand_aliasing={{2}: (12, {}), {3}: (13, {}), {4}: (14, {}), {5}: (15, {}),... | custom-call | flops 3623878656 | bytes 8000000 | tf_op jit(solution)/shard_map/forward_crop/pallas_call | solution.py:321
  58.4 9.3 %backward_crop.6 = (bf16[256,768]{1,0:T(8,128)(2,1)S(1)}, f32[12,768]{1,0:T(8,128)S(1)}, f32[4,256,768]{2,1,0:T(8,128)}, bf16[4,256,768]{2,1,0:T(8,128)(2,1)}, b...) custom-call(s32[4]{0:T(128)S(1)} %copy-done.5, ...), custom_call_target="tpu_custom_call", output_to_operand_aliasing={{2}: (16, {}), {3}: (17, {}), {4}: (18, {}), {5}: (19, {}),... | custom-call | flops 3623878656 | bytes 8000000 | tf_op jit(solution)/shard_map/backward_crop/pallas_call | solution.py:538
  67.8 13.6 %forward_crop.15 = (bf16[256,768]{1,0:T(8,128)(2,1)S(1)}, f32[1,768]{1,0:T(1,128)S(1)}, bf16[4,256,768]{2,1,0:T(8,128)(2,1)S(1)}, bf16[4,256,3072]{2,1,0:T(8,128...) custom-call(s32[4]{0:T(128)S(1)} %copy-done.5, ...), custom_call_target="tpu_custom_call", output_to_operand_aliasing={{2}: (12, {}), {3}: (13, {}), {4}: (14, {}), {5}: (15, {}),... | custom-call | flops 3623878656 | bytes 8000000 | tf_op jit(solution)/shard_map/forward_crop/pallas_call | solution.py:321
  81.5 9.6 %backward_crop.7 = (bf16[256,768]{1,0:T(8,128)(2,1)S(1)}, f32[12,768]{1,0:T(8,128)S(1)}, f32[4,256,768]{2,1,0:T(8,128)}, bf16[4,256,768]{2,1,0:T(8,128)(2,1)}, b...) custom-call(s32[4]{0:T(128)S(1)} %copy-done.5, ...), custom_call_target="tpu_custom_call", output_to_operand_aliasing={{2}: (16, {}), {3}: (17, {}), {4}: (18, {}), {5}: (19, {}),... | custom-call | flops 3623878656 | bytes 8000000 | tf_op jit(solution)/shard_map/backward_crop/pallas_call | solution.py:538
  91.2 10.5 %forward_crop.16 = (bf16[256,768]{1,0:T(8,128)(2,1)S(1)}, f32[1,768]{1,0:T(1,128)S(1)}, bf16[4,256,768]{2,1,0:T(8,128)(2,1)S(1)}, bf16[4,256,3072]{2,1,0:T(8,128...) custom-call(s32[4]{0:T(128)S(1)} %copy-done.5, ...), custom_call_target="tpu_custom_call", output_to_operand_aliasing={{2}: (12, {}), {3}: (13, {}), {4}: (14, {}), {5}: (15, {}),... | custom-call | flops 3623878656 | bytes 8000000 | tf_op jit(solution)/shard_map/forward_crop/pallas_call | solution.py:321
  101.7 9.3 %backward_crop.8 = (bf16[256,768]{1,0:T(8,128)(2,1)S(1)}, f32[12,768]{1,0:T(8,128)S(1)}, f32[4,256,768]{2,1,0:T(8,128)}, bf16[4,256,768]{2,1,0:T(8,128)(2,1)}, b...) custom-call(s32[4]{0:T(128)S(1)} %copy-done.5, ...), custom_call_target="tpu_custom_call", output_to_operand_aliasing={{2}: (16, {}), {3}: (17, {}), {4}: (18, {}), {5}: (19, {}),... | custom-call | flops 3623878656 | bytes 8000000 | tf_op jit(solution)/shard_map/backward_crop/pallas_call | solution.py:538
  111.6 11.0 %forward_crop.17 = (bf16[256,768]{1,0:T(8,128)(2,1)S(1)}, f32[1,768]{1,0:T(1,128)S(1)}, bf16[4,256,768]{2,1,0:T(8,128)(2,1)S(1)}, bf16[4,256,3072]{2,1,0:T(8,128...) custom-call(s32[4]{0:T(128)S(1)} %copy-done.5, ...), custom_call_target="tpu_custom_call", output_to_operand_aliasing={{2}: (12, {}), {3}: (13, {}), {4}: (14, {}), {5}: (15, {}),... | custom-call | flops 3623878656 | bytes 8000000 | tf_op jit(solution)/shard_map/forward_crop/pallas_call | solution.py:321
  122.6 10.3 %backward_crop.9 = (bf16[256,768]{1,0:T(8,128)(2,1)}, f32[12,768]{1,0:T(8,128)S(1)}, f32[4,256,768]{2,1,0:T(8,128)}, bf16[4,256,768]{2,1,0:T(8,128)(2,1)}, bf16[...) custom-call(s32[4]{0:T(128)S(1)} %copy-done.5, ...), custom_call_target="tpu_custom_call", output_to_operand_aliasing={{2}: (16, {}), {3}: (17, {}), {4}: (18, {}), {5}: (19, {}),... | custom-call | flops 3623878656 | bytes 8000000 | tf_op jit(solution)/shard_map/backward_crop/pallas_call | solution.py:538
  132.9 29.5 %weight_gradients.1 = (bf16[8,192,768]{2,1,0:T(8,128)(2,1)}, bf16[8,192,768]{2,1,0:T(8,128)(2,1)}, bf16[8,48,3072]{2,1,0:T(8,128)(2,1)}, bf16[8,48,3072]{2,1,0:T...) custom-call(bf16[1280,3072]{1,0:T(8,128)(2,1)} %bitcast.199, bf16[1280,768]{1,0:T(8,128)(2,1)} %bitcast.204, ...), custom_call_target="tpu_custom_call" | custom-call | flops 14495514624 | bytes 40000000 | tf_op jit(solution)/shard_map/weight_gradients/pallas_call | solution.py:666
  162.4 2.3 collective-permute-start.6
  166.8 2.5 collective-permute-done.6
  170.4 1.5 collective-permute-start.7
  173.8 1.5 collective-permute-start.14
  177.2 1.5 collective-permute-start.12
  178.7 11.7 %forward_crop.18 = (bf16[256,768]{1,0:T(8,128)(2,1)S(1)}, f32[1,768]{1,0:T(1,128)S(1)}) custom-call(s32[4]{0:T(128)S(1)} %copy-done.6, s32[4]{0:T(128)S(1)} %copy-done.8, bf16[4,256,768]{2,1,0:T(8,128)(2,1)} %own.18, bf16[1,2,768,2304]{3,2,1,0:T(8,128)(2,1)} %refs_1_.11, bf16[1,2,768,768]{3,2,1,0:T(8,128)(2,1)} %refs_2_.11, ...), custom_call_target="tpu_custom_call" | custom-call | flops 3623878656 | bytes 8000000 | tf_op jit(solution)/shard_map/forward_crop/pallas_call | solution.py:321
  195.6 3.2 collective-permute-done.8
  202.1 1.5 collective-permute-start.18
  206.1 10.1 %forward_crop.20 = (bf16[256,768]{1,0:T(8,128)(2,1)}, f32[1,768]{1,0:T(1,128)S(1)}) custom-call(s32[4]{0:T(128)S(1)} %copy-done.6, s32[4]{0:T(128)S(1)} %copy-done.8, bf16[4,256,768]{2,1,0:T(8,128)(2,1)} %own.21, bf16[256,768]{1,0:T(8,128)(2,1)S(1)} %collective-permute-done.11.refs_0_, bf16[1,2,768,2304]{3,2,1,0:T(8,128)(2,1)} %refs_1_.11, ...), custom_call_target="tpu_custom_call" | custom-call | flops 3623878656 | bytes 8000000 | tf_op jit(solution)/shard_map/forward_crop/pallas_call | solution.py:321
  224.6 1.8 collective-permute-done.21
  227.8 1.8 collective-permute-done.20
  230.9 1.8 collective-permute-done.19
  234.1 1.8 collective-permute-done.24
  237.2 1.8 collective-permute-done.23
  240.4 1.8 collective-permute-done.22
  243.6 1.8 collective-permute-done.27
  246.7 1.8 collective-permute-done.26
  249.9 1.8 collective-permute-done.25
  253.1 1.7 collective-permute-done.30
  256.2 1.8 collective-permute-done.29
  259.6 2.1 collective-permute-done.28
  261.9 2.9 collective-permute-done.33
  266.5 1.5 collective-permute-done.32
  269.7 2.0 collective-permute-done.31
  271.9 2.9 collective-permute-done.36
  275.1 2.9 collective-permute-done.35
  278.3 3.4 collective-permute-done.34
  281.9 2.9 collective-permute-done.39
  285.1 2.9 collective-permute-done.38
  288.3 3.4 collective-permute-done.37
  291.9 2.9 collective-permute-done.42
  295.1 2.9 collective-permute-done.41
  298.3 3.4 collective-permute-done.40
  301.9 2.9 collective-permute-done.45
  305.4 2.6 collective-permute-done.44
  308.3 3.4 collective-permute-done.43
  311.9 2.9 collective-permute-done.48
  315.1 2.9 collective-permute-done.47
  318.3 3.4 collective-permute-done.46
  321.7 3.2 collective-permute-done.51
  325.1 2.9 collective-permute-done.50
  328.3 3.5 collective-permute-start.49
  331.8 3.1 collective-permute-start.55
  334.9 3.1 collective-permute-start.54
  338.1 2.5 write_half.6
  340.6 2.4 write_half.10.refs_1_
  343.0 2.4 write_half.8
  345.5 2.4 write_half.11
  347.9 2.4 write_half.9
  350.3 2.5 write_half.7
  352.9 1.9 small_sums.1
  (168 shorter events, 59.1 us)
Async XLA Ops:
  17.6 12.7 %copy-start.9 = (f32[1,768]{1,0:T(1,128)}, f32[1,768]{1,0:T(1,128)S(1)}, u32[]{:S(2)}) copy-start(f32[1,768]{1,0:T(1,128)S(1)} %get-tuple-element.219.refs_7_) | copy-start | bytes 9220
  17.6 14.0 %collective-permute-start = (bf16[256,768]{1,0:T(8,128)(2,1)S(1)}, bf16[256,768]{1,0:T(8,128)(2,1)S(1)}, u32[]{:S(2)}, u32[]{:S(2)}) collective-permute-start(bf16[256,768]{1,0:T(8,128)(2,1)S(1)} %get-tuple-element.214), channel_id=1, source_target_pairs={{0,16},{1,17},{2,18},{3,19},{4,20},{5,21},{6,22},{7,23},{8,24},{9,... | collective-permute-start | bytes 1179656 | tf_op jit(solution)/shard_map/ppermute | solution.py:843
  30.3 11.4 %copy-start.11 = (f32[1,768]{1,0:T(1,128)}, f32[1,768]{1,0:T(1,128)S(1)}, u32[]{:S(2)}) copy-start(f32[1,768]{1,0:T(1,128)S(1)} %get-tuple-element.230.refs_8_) | copy-start | bytes 9220
  30.3 18.1 %collective-permute-start.2 = (bf16[256,768]{1,0:T(8,128)(2,1)S(1)}, bf16[256,768]{1,0:T(8,128)(2,1)S(1)}, u32[]{:S(2)}, u32[]{:S(2)}) collective-permute-start(bf16[256,768]{1,0:T(8,128)(2,1)S(1)} %get-tuple-element.250), channel_id=1, source_target_pairs={{0,16},{1,17},{2,18},{3,19},{4,20},{5,21},{6,22},{7,23},{8,24},{9,... | collective-permute-start | bytes 1179656 | tf_op jit(solution)/shard_map/ppermute | solution.py:843
  31.6 10.0 %copy-start = (bf16[4,256,768]{2,1,0:T(8,128)(2,1)S(1)}, bf16[4,256,768]{2,1,0:T(8,128)(2,1)}, u32[]{:S(2)}) copy-start(bf16[4,256,768]{2,1,0:T(8,128)(2,1)} %cot.9) | copy-start | bytes 4718596
  47.4 10.9 %collective-permute-start.1 = (bf16[256,768]{1,0:T(8,128)(2,1)S(1)}, bf16[256,768]{1,0:T(8,128)(2,1)S(1)}, u32[]{:S(2)}, u32[]{:S(2)}) collective-permute-start(bf16[256,768]{1,0:T(8,128)(2,1)S(1)} %get-tuple-element.249), channel_id=1, source_target_pairs={{0,16},{16,0},{1,17},{17,1},{2,18},{18,2},{3,19},{19,3},{4,20},{20... | collective-permute-start | bytes 1179656 | tf_op jit(solution)/shard_map/ppermute | solution.py:893
  67.7 13.7 %collective-permute-start.3 = (bf16[256,768]{1,0:T(8,128)(2,1)S(1)}, bf16[256,768]{1,0:T(8,128)(2,1)S(1)}, u32[]{:S(2)}, u32[]{:S(2)}) collective-permute-start(bf16[256,768]{1,0:T(8,128)(2,1)S(1)} %get-tuple-element.275), channel_id=1, source_target_pairs={{0,16},{16,0},{1,17},{17,1},{2,18},{18,2},{3,19},{19,3},{4,20},{20... | collective-permute-start | bytes 1179656 | tf_op jit(solution)/shard_map/ppermute | solution.py:893
  91.1 10.6 %collective-permute-start.4 = (bf16[256,768]{1,0:T(8,128)(2,1)S(1)}, bf16[256,768]{1,0:T(8,128)(2,1)S(1)}, u32[]{:S(2)}, u32[]{:S(2)}) collective-permute-start(bf16[256,768]{1,0:T(8,128)(2,1)S(1)} %get-tuple-element.292), channel_id=1, source_target_pairs={{0,16},{16,0},{1,17},{17,1},{2,18},{18,2},{3,19},{19,3},{4,20},{20... | collective-permute-start | bytes 1179656 | tf_op jit(solution)/shard_map/ppermute | solution.py:893
  111.0 11.5 %collective-permute-start.5 = (bf16[256,768]{1,0:T(8,128)(2,1)S(1)}, bf16[256,768]{1,0:T(8,128)(2,1)S(1)}, u32[]{:S(2)}, u32[]{:S(2)}) collective-permute-start(bf16[256,768]{1,0:T(8,128)(2,1)S(1)} %get-tuple-element.321), channel_id=1, source_target_pairs={{0,16},{16,0},{1,17},{17,1},{2,18},{18,2},{3,19},{19,3},{4,20},{20... | collective-permute-start | bytes 1179656 | tf_op jit(solution)/shard_map/ppermute | solution.py:893
  162.4 16.3 %copy-start.2 = (f32[1,2,2,768]{3,2,1,0:T(2,128)S(1)}, f32[1,2,2,768]{3,2,1,0:T(2,128)}, u32[]{:S(2)}) copy-start(f32[1,2,2,768]{3,2,1,0:T(2,128)} %refs_7_.15) | copy-start | bytes 36868
  162.4 16.3 %copy-start.4 = (f32[1,2,3072]{2,1,0:T(2,128)S(1)}, f32[1,2,3072]{2,1,0:T(2,128)}, u32[]{:S(2)}) copy-start(f32[1,2,3072]{2,1,0:T(2,128)} %refs_5_.26) | copy-start | bytes 73732
  162.4 16.3 %copy-start.6 = (s32[4]{0:T(128)S(1)}, s32[4]{0:T(128)}, u32[]{:S(2)}) copy-start(s32[4]{0:T(128)} %query_lengths.10) | copy-start | bytes 52
  162.4 16.3 %copy-start.8 = (s32[4]{0:T(128)S(1)}, s32[4]{0:T(128)}, u32[]{:S(2)}) copy-start(s32[4]{0:T(128)} %key_lengths.21) | copy-start | bytes 52
  162.4 6.8 %collective-permute-start.6 = (bf16[8,192,768]{2,1,0:T(8,128)(2,1)}, bf16[8,192,768]{2,1,0:T(8,128)(2,1)}, u32[]{:S(2)}, u32[]{:S(2)}) collective-permute-start(bf16[8,192,768]{2,1,0:T(8,128)(2,1)} %get-tuple-element.348), channel_id=1, source_target_pairs={{0,4},{1,5},{2,6},{3,7},{4,0},{5,1},{6,2},{7,3},{8,12},{9,13},{10,... | collective-permute-start | bytes 7077896 | tf_op jit(solution)/shard_map/ppermute | solution.py:912
  164.8 7.9 %collective-permute-start.13 = (bf16[8,48,3072]{2,1,0:T(8,128)(2,1)}, bf16[8,48,3072]{2,1,0:T(8,128)(2,1)}, u32[]{:S(2)}, u32[]{:S(2)}) collective-permute-start(bf16[8,48,3072]{2,1,0:T(8,128)(2,1)} %get-tuple-element.356), channel_id=1, source_target_pairs={{0,4},{1,5},{2,6},{3,7},{4,0},{5,1},{6,2},{7,3},{8,12},{9,13},{10,... | collective-permute-start | bytes 7077896 | tf_op jit(solution)/shard_map/ppermute | solution.py:912
  164.8 11.2 %collective-permute-start.9 = (bf16[8,48,3072]{2,1,0:T(8,128)(2,1)}, bf16[8,48,3072]{2,1,0:T(8,128)(2,1)}, u32[]{:S(2)}, u32[]{:S(2)}) collective-permute-start(bf16[8,48,3072]{2,1,0:T(8,128)(2,1)} %get-tuple-element.352), channel_id=1, source_target_pairs={{0,4},{1,5},{2,6},{3,7},{4,0},{5,1},{6,2},{7,3},{8,12},{9,13},{10,... | collective-permute-start | bytes 7077896 | tf_op jit(solution)/shard_map/ppermute | solution.py:912
  165.3 40.8 %collective-permute-start.11 = (bf16[256,768]{1,0:T(8,128)(2,1)S(1)}, bf16[256,768]{1,0:T(8,128)(2,1)S(1)}, u32[]{:S(2)}, u32[]{:S(2)}) collective-permute-start(bf16[256,768]{1,0:T(8,128)(2,1)S(1)} %get-tuple-element.320.sent), channel_id=1, source_target_pairs={{0,16},{1,17},{2,18},{3,19},{4,20},{5,21},{6,22},{7,23},{8,24},{9,... | collective-permute-start | bytes 1179656 | tf_op jit(solution)/shard_map/ppermute | solution.py:843
  170.4 21.4 %collective-permute-start.7 = (bf16[192,768]{1,0:T(8,128)(2,1)S(1)}, bf16[192,768]{1,0:T(8,128)(2,1)S(1)}, u32[]{:S(2)}, u32[]{:S(2)}) collective-permute-start(bf16[192,768]{1,0:T(8,128)(2,1)S(1)} %fusion.42.refs_7_), channel_id=1, source_target_pairs={{0,1},{1,2},{2,3},{3,11},{11,10},{10,9},{9,8},{8,0},{12,13},{13,14... | collective-permute-start | bytes 884744 | tf_op jit(solution)/shard_map/ppermute | solution.py:795
  173.8 27.3 %collective-permute-start.14 = (bf16[48,3072]{1,0:T(8,128)(2,1)S(1)}, bf16[48,3072]{1,0:T(8,128)(2,1)S(1)}, u32[]{:S(2)}, u32[]{:S(2)}) collective-permute-start(bf16[48,3072]{1,0:T(8,128)(2,1)S(1)} %fusion.44), channel_id=1, source_target_pairs={{0,1},{1,2},{2,3},{3,11},{11,10},{10,9},{9,8},{8,0},{12,13},{13,14... | collective-permute-start | bytes 884744 | tf_op jit(solution)/shard_map/ppermute | solution.py:795
  177.1 14.6 %copy-start.19 = (bf16[8,192,768]{2,1,0:T(8,128)(2,1)S(1)}, bf16[8,192,768]{2,1,0:T(8,128)(2,1)}, u32[]{:S(2)}) copy-start(bf16[8,192,768]{2,1,0:T(8,128)(2,1)} %get-tuple-element.347) | copy-start | bytes 7077892
  177.2 26.5 %collective-permute-start.12 = (bf16[48,3072]{1,0:T(8,128)(2,1)S(1)}, bf16[48,3072]{1,0:T(8,128)(2,1)S(1)}, u32[]{:S(2)}, u32[]{:S(2)}) collective-permute-start(bf16[48,3072]{1,0:T(8,128)(2,1)S(1)} %fusion.43.refs_8_), channel_id=1, source_target_pairs={{0,1},{1,2},{2,3},{3,11},{11,10},{10,9},{9,8},{8,0},{12,13},{13,14... | collective-permute-start | bytes 884744 | tf_op jit(solution)/shard_map/ppermute | solution.py:795
  190.4 29.8 %collective-permute-start.16 = (bf16[256,768]{1,0:T(8,128)(2,1)S(1)}, bf16[256,768]{1,0:T(8,128)(2,1)S(1)}, u32[]{:S(2)}, u32[]{:S(2)}) collective-permute-start(bf16[256,768]{1,0:T(8,128)(2,1)S(1)} %get-tuple-element.361), channel_id=1, source_target_pairs={{0,16},{1,17},{2,18},{3,19},{4,20},{5,21},{6,22},{7,23},{8,24},{9,... | collective-permute-start | bytes 1179656 | tf_op jit(solution)/shard_map/ppermute | solution.py:843
  192.9 5.9 %collective-permute-start.8 = (bf16[192,768]{1,0:T(8,128)(2,1)S(1)}, bf16[192,768]{1,0:T(8,128)(2,1)S(1)}, u32[]{:S(2)}, u32[]{:S(2)}) collective-permute-start(bf16[192,768]{1,0:T(8,128)(2,1)S(1)} %fusion.41), channel_id=1, source_target_pairs={{0,1},{1,2},{2,3},{3,11},{11,10},{10,9},{9,8},{8,0},{12,13},{13,14... | collective-permute-start | bytes 884744 | tf_op jit(solution)/shard_map/ppermute | solution.py:795
  199.9 16.3 %collective-permute-start.10 = (bf16[192,768]{1,0:T(8,128)(2,1)S(1)}, bf16[192,768]{1,0:T(8,128)(2,1)S(1)}, u32[]{:S(2)}, u32[]{:S(2)}) collective-permute-start(bf16[192,768]{1,0:T(8,128)(2,1)S(1)} %fusion.39), channel_id=1, source_target_pairs={{0,1},{1,2},{2,3},{3,11},{11,10},{10,9},{9,8},{8,0},{12,13},{13,14... | collective-permute-start | bytes 884744 | tf_op jit(solution)/shard_map/ppermute | solution.py:795
  202.1 15.5 %collective-permute-start.18 = (bf16[48,3072]{1,0:T(8,128)(2,1)S(1)}, bf16[48,3072]{1,0:T(8,128)(2,1)S(1)}, u32[]{:S(2)}, u32[]{:S(2)}) collective-permute-start(bf16[48,3072]{1,0:T(8,128)(2,1)S(1)} %fusion.37), channel_id=1, source_target_pairs={{0,1},{1,2},{2,3},{3,11},{11,10},{10,9},{9,8},{8,0},{12,13},{13,14... | collective-permute-start | bytes 884744 | tf_op jit(solution)/shard_map/ppermute | solution.py:795
  204.7 14.2 %collective-permute-start.17 = (bf16[48,3072]{1,0:T(8,128)(2,1)S(1)}, bf16[48,3072]{1,0:T(8,128)(2,1)S(1)}, u32[]{:S(2)}, u32[]{:S(2)}) collective-permute-start(bf16[48,3072]{1,0:T(8,128)(2,1)S(1)} %fusion.35.refs_8_), channel_id=1, source_target_pairs={{0,1},{1,2},{2,3},{3,11},{11,10},{10,9},{9,8},{8,0},{12,13},{13,14... | collective-permute-start | bytes 884744 | tf_op jit(solution)/shard_map/ppermute | solution.py:795
  217.3 5.9 %collective-permute-start.15 = (bf16[192,768]{1,0:T(8,128)(2,1)S(1)}, bf16[192,768]{1,0:T(8,128)(2,1)S(1)}, u32[]{:S(2)}, u32[]{:S(2)}) collective-permute-start(bf16[192,768]{1,0:T(8,128)(2,1)S(1)} %fusion.33), channel_id=1, source_target_pairs={{0,1},{1,2},{2,3},{3,11},{11,10},{10,9},{9,8},{8,0},{12,13},{13,14... | collective-permute-start | bytes 884744 | tf_op jit(solution)/shard_map/ppermute | solution.py:795
  218.7 7.7 %collective-permute-start.21 = (bf16[48,3072]{1,0:T(8,128)(2,1)S(1)}, bf16[48,3072]{1,0:T(8,128)(2,1)S(1)}, u32[]{:S(2)}, u32[]{:S(2)}) collective-permute-start(bf16[48,3072]{1,0:T(8,128)(2,1)S(1)} %fusion.31), channel_id=1, source_target_pairs={{0,1},{1,2},{2,3},{3,11},{11,10},{10,9},{9,8},{8,0},{12,13},{13,14... | collective-permute-start | bytes 884744 | tf_op jit(solution)/shard_map/ppermute | solution.py:795
  220.0 9.5 %collective-permute-start.20 = (bf16[48,3072]{1,0:T(8,128)(2,1)S(1)}, bf16[48,3072]{1,0:T(8,128)(2,1)S(1)}, u32[]{:S(2)}, u32[]{:S(2)}) collective-permute-start(bf16[48,3072]{1,0:T(8,128)(2,1)S(1)} %fusion.29.refs_8_), channel_id=1, source_target_pairs={{0,1},{1,2},{2,3},{3,11},{11,10},{10,9},{9,8},{8,0},{12,13},{13,14... | collective-permute-start | bytes 884744 | tf_op jit(solution)/shard_map/ppermute | solution.py:795
  224.3 8.4 %collective-permute-start.19 = (bf16[192,768]{1,0:T(8,128)(2,1)S(1)}, bf16[192,768]{1,0:T(8,128)(2,1)S(1)}, u32[]{:S(2)}, u32[]{:S(2)}) collective-permute-start(bf16[192,768]{1,0:T(8,128)(2,1)S(1)} %fusion.27), channel_id=1, source_target_pairs={{0,1},{1,2},{2,3},{3,11},{11,10},{10,9},{9,8},{8,0},{12,13},{13,14... | collective-permute-start | bytes 884744 | tf_op jit(solution)/shard_map/ppermute | solution.py:795
  227.5 8.4 %collective-permute-start.24 = (bf16[48,3072]{1,0:T(8,128)(2,1)S(1)}, bf16[48,3072]{1,0:T(8,128)(2,1)S(1)}, u32[]{:S(2)}, u32[]{:S(2)}) collective-permute-start(bf16[48,3072]{1,0:T(8,128)(2,1)S(1)} %fusion.25), channel_id=1, source_target_pairs={{0,1},{1,2},{2,3},{3,11},{11,10},{10,9},{9,8},{8,0},{12,13},{13,14... | collective-permute-start | bytes 884744 | tf_op jit(solution)/shard_map/ppermute | solution.py:795
  230.6 8.4 %collective-permute-start.23 = (bf16[48,3072]{1,0:T(8,128)(2,1)S(1)}, bf16[48,3072]{1,0:T(8,128)(2,1)S(1)}, u32[]{:S(2)}, u32[]{:S(2)}) collective-permute-start(bf16[48,3072]{1,0:T(8,128)(2,1)S(1)} %fusion.23), channel_id=1, source_target_pairs={{0,1},{1,2},{2,3},{3,11},{11,10},{10,9},{9,8},{8,0},{12,13},{13,14... | collective-permute-start | bytes 884744 | tf_op jit(solution)/shard_map/ppermute | solution.py:795
  233.8 8.4 %collective-permute-start.22 = (bf16[192,768]{1,0:T(8,128)(2,1)S(1)}, bf16[192,768]{1,0:T(8,128)(2,1)S(1)}, u32[]{:S(2)}, u32[]{:S(2)}) collective-permute-start(bf16[192,768]{1,0:T(8,128)(2,1)S(1)} %fusion.21), channel_id=1, source_target_pairs={{0,1},{1,2},{2,3},{3,11},{11,10},{10,9},{9,8},{8,0},{12,13},{13,14... | collective-permute-start | bytes 884744 | tf_op jit(solution)/shard_map/ppermute | solution.py:795
  236.9 8.4 %collective-permute-start.27 = (bf16[48,3072]{1,0:T(8,128)(2,1)S(1)}, bf16[48,3072]{1,0:T(8,128)(2,1)S(1)}, u32[]{:S(2)}, u32[]{:S(2)}) collective-permute-start(bf16[48,3072]{1,0:T(8,128)(2,1)S(1)} %fusion.19), channel_id=1, source_target_pairs={{0,1},{1,2},{2,3},{3,11},{11,10},{10,9},{9,8},{8,0},{12,13},{13,14... | collective-permute-start | bytes 884744 | tf_op jit(solution)/shard_map/ppermute | solution.py:795
  240.1 8.4 %collective-permute-start.26 = (bf16[48,3072]{1,0:T(8,128)(2,1)S(1)}, bf16[48,3072]{1,0:T(8,128)(2,1)S(1)}, u32[]{:S(2)}, u32[]{:S(2)}) collective-permute-start(bf16[48,3072]{1,0:T(8,128)(2,1)S(1)} %fusion.17), channel_id=1, source_target_pairs={{0,1},{1,2},{2,3},{3,11},{11,10},{10,9},{9,8},{8,0},{12,13},{13,14... | collective-permute-start | bytes 884744 | tf_op jit(solution)/shard_map/ppermute | solution.py:795
  243.3 8.4 %collective-permute-start.25 = (bf16[192,768]{1,0:T(8,128)(2,1)S(1)}, bf16[192,768]{1,0:T(8,128)(2,1)S(1)}, u32[]{:S(2)}, u32[]{:S(2)}) collective-permute-start(bf16[192,768]{1,0:T(8,128)(2,1)S(1)} %fusion.15), channel_id=1, source_target_pairs={{0,1},{1,2},{2,3},{3,11},{11,10},{10,9},{9,8},{8,0},{12,13},{13,14... | collective-permute-start | bytes 884744 | tf_op jit(solution)/shard_map/ppermute | solution.py:795
  246.4 8.4 %collective-permute-start.30 = (bf16[48,3072]{1,0:T(8,128)(2,1)S(1)}, bf16[48,3072]{1,0:T(8,128)(2,1)S(1)}, u32[]{:S(2)}, u32[]{:S(2)}) collective-permute-start(bf16[48,3072]{1,0:T(8,128)(2,1)S(1)} %fusion.13), channel_id=1, source_target_pairs={{0,1},{1,2},{2,3},{3,11},{11,10},{10,9},{9,8},{8,0},{12,13},{13,14... | collective-permute-start | bytes 884744 | tf_op jit(solution)/shard_map/ppermute | solution.py:795
  249.6 8.4 %collective-permute-start.29 = (bf16[48,3072]{1,0:T(8,128)(2,1)S(1)}, bf16[48,3072]{1,0:T(8,128)(2,1)S(1)}, u32[]{:S(2)}, u32[]{:S(2)}) collective-permute-start(bf16[48,3072]{1,0:T(8,128)(2,1)S(1)} %fusion.11), channel_id=1, source_target_pairs={{0,1},{1,2},{2,3},{3,11},{11,10},{10,9},{9,8},{8,0},{12,13},{13,14... | collective-permute-start | bytes 884744 | tf_op jit(solution)/shard_map/ppermute | solution.py:795
  252.8 8.9 %collective-permute-start.28 = (bf16[224,768]{1,0:T(8,128)(2,1)S(1)}, bf16[224,768]{1,0:T(8,128)(2,1)S(1)}, u32[]{:S(2)}, u32[]{:S(2)}) collective-permute-start(bf16[224,768]{1,0:T(8,128)(2,1)S(1)} %pad_maximum_fusion), channel_id=1, source_target_pairs={{0,1},{1,2},{2,3},{3,11},{11,10},{10,9},{9,8},{8,0},{12,13},{13,14... | collective-permute-start | bytes 1032200 | tf_op jit(solution)/shard_map/ppermute | solution.py:795
  255.9 8.9 %collective-permute-start.33 = (bf16[48,3072]{1,0:T(8,128)(2,1)S(1)}, bf16[48,3072]{1,0:T(8,128)(2,1)S(1)}, u32[]{:S(2)}, u32[]{:S(2)}) collective-permute-start(bf16[48,3072]{1,0:T(8,128)(2,1)S(1)} %fusion.7), channel_id=1, source_target_pairs={{0,1},{1,2},{2,3},{3,11},{11,10},{10,9},{9,8},{8,0},{12,13},{13,14... | collective-permute-start | bytes 884744 | tf_op jit(solution)/shard_map/ppermute | solution.py:795
  259.1 8.9 %collective-permute-start.32 = (bf16[48,3072]{1,0:T(8,128)(2,1)S(1)}, bf16[48,3072]{1,0:T(8,128)(2,1)S(1)}, u32[]{:S(2)}, u32[]{:S(2)}) collective-permute-start(bf16[48,3072]{1,0:T(8,128)(2,1)S(1)} %fusion.5), channel_id=1, source_target_pairs={{0,1},{1,2},{2,3},{3,11},{11,10},{10,9},{9,8},{8,0},{12,13},{13,14... | collective-permute-start | bytes 884744 | tf_op jit(solution)/shard_map/ppermute | solution.py:795
  261.7 10.0 %collective-permute-start.31 = (bf16[224,768]{1,0:T(8,128)(2,1)S(1)}, bf16[224,768]{1,0:T(8,128)(2,1)S(1)}, u32[]{:S(2)}, u32[]{:S(2)}) collective-permute-start(bf16[224,768]{1,0:T(8,128)(2,1)S(1)} %collective-permute-done.28), channel_id=1, source_target_pairs={{0,1},{1,2},{2,3},{3,11},{11,10},{10,9},{9,8},{8,0},{12,13},{13,14... | collective-permute-start | bytes 1032200 | tf_op jit(solution)/shard_map/ppermute | solution.py:795
  266.2 8.6 %collective-permute-start.36 = (bf16[48,3072]{1,0:T(8,128)(2,1)S(1)}, bf16[48,3072]{1,0:T(8,128)(2,1)S(1)}, u32[]{:S(2)}, u32[]{:S(2)}) collective-permute-start(bf16[48,3072]{1,0:T(8,128)(2,1)S(1)} %get-tuple-element.427), channel_id=1, source_target_pairs={{0,1},{1,2},{2,3},{3,11},{11,10},{10,9},{9,8},{8,0},{12,13},{13,14... | collective-permute-start | bytes 884744 | tf_op jit(solution)/shard_map/ppermute | solution.py:795
  269.3 8.6 %collective-permute-start.35 = (bf16[48,3072]{1,0:T(8,128)(2,1)S(1)}, bf16[48,3072]{1,0:T(8,128)(2,1)S(1)}, u32[]{:S(2)}, u32[]{:S(2)}) collective-permute-start(bf16[48,3072]{1,0:T(8,128)(2,1)S(1)} %get-tuple-element.429), channel_id=1, source_target_pairs={{0,1},{1,2},{2,3},{3,11},{11,10},{10,9},{9,8},{8,0},{12,13},{13,14... | collective-permute-start | bytes 884744 | tf_op jit(solution)/shard_map/ppermute | solution.py:795
  271.7 10.0 %collective-permute-start.34 = (bf16[224,768]{1,0:T(8,128)(2,1)S(1)}, bf16[224,768]{1,0:T(8,128)(2,1)S(1)}, u32[]{:S(2)}, u32[]{:S(2)}) collective-permute-start(bf16[224,768]{1,0:T(8,128)(2,1)S(1)} %collective-permute-done.31), channel_id=1, source_target_pairs={{0,1},{1,2},{2,3},{3,11},{11,10},{10,9},{9,8},{8,0},{12,13},{13,14... | collective-permute-start | bytes 1032200 | tf_op jit(solution)/shard_map/ppermute | solution.py:795
  274.8 10.0 %collective-permute-start.39 = (bf16[48,3072]{1,0:T(8,128)(2,1)S(1)}, bf16[48,3072]{1,0:T(8,128)(2,1)S(1)}, u32[]{:S(2)}, u32[]{:S(2)}) collective-permute-start(bf16[48,3072]{1,0:T(8,128)(2,1)S(1)} %collective-permute-done.36), channel_id=1, source_target_pairs={{0,1},{1,2},{2,3},{3,11},{11,10},{10,9},{9,8},{8,0},{12,13},{13,14... | collective-permute-start | bytes 884744 | tf_op jit(solution)/shard_map/ppermute | solution.py:795
  278.0 10.0 %collective-permute-start.38 = (bf16[48,3072]{1,0:T(8,128)(2,1)S(1)}, bf16[48,3072]{1,0:T(8,128)(2,1)S(1)}, u32[]{:S(2)}, u32[]{:S(2)}) collective-permute-start(bf16[48,3072]{1,0:T(8,128)(2,1)S(1)} %collective-permute-done.35), channel_id=1, source_target_pairs={{0,1},{1,2},{2,3},{3,11},{11,10},{10,9},{9,8},{8,0},{12,13},{13,14... | collective-permute-start | bytes 884744 | tf_op jit(solution)/shard_map/ppermute | solution.py:795
  281.7 10.0 %collective-permute-start.37 = (bf16[224,768]{1,0:T(8,128)(2,1)S(1)}, bf16[224,768]{1,0:T(8,128)(2,1)S(1)}, u32[]{:S(2)}, u32[]{:S(2)}) collective-permute-start(bf16[224,768]{1,0:T(8,128)(2,1)S(1)} %collective-permute-done.34), channel_id=1, source_target_pairs={{0,1},{1,2},{2,3},{3,11},{11,10},{10,9},{9,8},{8,0},{12,13},{13,14... | collective-permute-start | bytes 1032200 | tf_op jit(solution)/shard_map/ppermute | solution.py:795
  284.8 10.0 %collective-permute-start.42 = (bf16[48,3072]{1,0:T(8,128)(2,1)S(1)}, bf16[48,3072]{1,0:T(8,128)(2,1)S(1)}, u32[]{:S(2)}, u32[]{:S(2)}) collective-permute-start(bf16[48,3072]{1,0:T(8,128)(2,1)S(1)} %collective-permute-done.39), channel_id=1, source_target_pairs={{0,1},{1,2},{2,3},{3,11},{11,10},{10,9},{9,8},{8,0},{12,13},{13,14... | collective-permute-start | bytes 884744 | tf_op jit(solution)/shard_map/ppermute | solution.py:795
  288.0 10.0 %collective-permute-start.41 = (bf16[48,3072]{1,0:T(8,128)(2,1)S(1)}, bf16[48,3072]{1,0:T(8,128)(2,1)S(1)}, u32[]{:S(2)}, u32[]{:S(2)}) collective-permute-start(bf16[48,3072]{1,0:T(8,128)(2,1)S(1)} %collective-permute-done.38), channel_id=1, source_target_pairs={{0,1},{1,2},{2,3},{3,11},{11,10},{10,9},{9,8},{8,0},{12,13},{13,14... | collective-permute-start | bytes 884744 | tf_op jit(solution)/shard_map/ppermute | solution.py:795
  291.7 10.0 %collective-permute-start.40 = (bf16[224,768]{1,0:T(8,128)(2,1)S(1)}, bf16[224,768]{1,0:T(8,128)(2,1)S(1)}, u32[]{:S(2)}, u32[]{:S(2)}) collective-permute-start(bf16[224,768]{1,0:T(8,128)(2,1)S(1)} %collective-permute-done.37), channel_id=1, source_target_pairs={{0,1},{1,2},{2,3},{3,11},{11,10},{10,9},{9,8},{8,0},{12,13},{13,14... | collective-permute-start | bytes 1032200 | tf_op jit(solution)/shard_map/ppermute | solution.py:795
  294.8 10.0 %collective-permute-start.45 = (bf16[48,3072]{1,0:T(8,128)(2,1)S(1)}, bf16[48,3072]{1,0:T(8,128)(2,1)S(1)}, u32[]{:S(2)}, u32[]{:S(2)}) collective-permute-start(bf16[48,3072]{1,0:T(8,128)(2,1)S(1)} %collective-permute-done.42), channel_id=1, source_target_pairs={{0,1},{1,2},{2,3},{3,11},{11,10},{10,9},{9,8},{8,0},{12,13},{13,14... | collective-permute-start | bytes 884744 | tf_op jit(solution)/shard_map/ppermute | solution.py:795
  298.0 10.0 %collective-permute-start.44 = (bf16[48,3072]{1,0:T(8,128)(2,1)S(1)}, bf16[48,3072]{1,0:T(8,128)(2,1)S(1)}, u32[]{:S(2)}, u32[]{:S(2)}) collective-permute-start(bf16[48,3072]{1,0:T(8,128)(2,1)S(1)} %collective-permute-done.41), channel_id=1, source_target_pairs={{0,1},{1,2},{2,3},{3,11},{11,10},{10,9},{9,8},{8,0},{12,13},{13,14... | collective-permute-start | bytes 884744 | tf_op jit(solution)/shard_map/ppermute | solution.py:795
  301.7 10.0 %collective-permute-start.43 = (bf16[224,768]{1,0:T(8,128)(2,1)S(1)}, bf16[224,768]{1,0:T(8,128)(2,1)S(1)}, u32[]{:S(2)}, u32[]{:S(2)}) collective-permute-start(bf16[224,768]{1,0:T(8,128)(2,1)S(1)} %collective-permute-done.40), channel_id=1, source_target_pairs={{0,1},{1,2},{2,3},{3,11},{11,10},{10,9},{9,8},{8,0},{12,13},{13,14... | collective-permute-start | bytes 1032200 | tf_op jit(solution)/shard_map/ppermute | solution.py:795
  304.8 10.0 %collective-permute-start.48 = (bf16[48,3072]{1,0:T(8,128)(2,1)S(1)}, bf16[48,3072]{1,0:T(8,128)(2,1)S(1)}, u32[]{:S(2)}, u32[]{:S(2)}) collective-permute-start(bf16[48,3072]{1,0:T(8,128)(2,1)S(1)} %collective-permute-done.45), channel_id=1, source_target_pairs={{0,1},{1,2},{2,3},{3,11},{11,10},{10,9},{9,8},{8,0},{12,13},{13,14... | collective-permute-start | bytes 884744 | tf_op jit(solution)/shard_map/ppermute | solution.py:795
  308.0 10.0 %collective-permute-start.47 = (bf16[48,3072]{1,0:T(8,128)(2,1)S(1)}, bf16[48,3072]{1,0:T(8,128)(2,1)S(1)}, u32[]{:S(2)}, u32[]{:S(2)}) collective-permute-start(bf16[48,3072]{1,0:T(8,128)(2,1)S(1)} %collective-permute-done.44), channel_id=1, source_target_pairs={{0,1},{1,2},{2,3},{3,11},{11,10},{10,9},{9,8},{8,0},{12,13},{13,14... | collective-permute-start | bytes 884744 | tf_op jit(solution)/shard_map/ppermute | solution.py:795
  311.7 10.0 %collective-permute-start.46 = (bf16[224,768]{1,0:T(8,128)(2,1)S(1)}, bf16[224,768]{1,0:T(8,128)(2,1)S(1)}, u32[]{:S(2)}, u32[]{:S(2)}) collective-permute-start(bf16[224,768]{1,0:T(8,128)(2,1)S(1)} %collective-permute-done.43), channel_id=1, source_target_pairs={{0,1},{1,2},{2,3},{3,11},{11,10},{10,9},{9,8},{8,0},{12,13},{13,14... | collective-permute-start | bytes 1032200 | tf_op jit(solution)/shard_map/ppermute | solution.py:795
  314.8 10.0 %collective-permute-start.51 = (bf16[48,3072]{1,0:T(8,128)(2,1)S(1)}, bf16[48,3072]{1,0:T(8,128)(2,1)S(1)}, u32[]{:S(2)}, u32[]{:S(2)}) collective-permute-start(bf16[48,3072]{1,0:T(8,128)(2,1)S(1)} %collective-permute-done.48), channel_id=1, source_target_pairs={{0,1},{1,2},{2,3},{3,11},{11,10},{10,9},{9,8},{8,0},{12,13},{13,14... | collective-permute-start | bytes 884744 | tf_op jit(solution)/shard_map/ppermute | solution.py:795
  318.0 10.0 %collective-permute-start.50 = (bf16[48,3072]{1,0:T(8,128)(2,1)S(1)}, bf16[48,3072]{1,0:T(8,128)(2,1)S(1)}, u32[]{:S(2)}, u32[]{:S(2)}) collective-permute-start(bf16[48,3072]{1,0:T(8,128)(2,1)S(1)} %collective-permute-done.47), channel_id=1, source_target_pairs={{0,1},{1,2},{2,3},{3,11},{11,10},{10,9},{9,8},{8,0},{12,13},{13,14... | collective-permute-start | bytes 884744 | tf_op jit(solution)/shard_map/ppermute | solution.py:795
  324.9 6.9 %collective-permute-start.53 = (bf16[48,3072]{1,0:T(8,128)(2,1)S(1)}, bf16[48,3072]{1,0:T(8,128)(2,1)S(1)}, u32[]{:S(2)}, u32[]{:S(2)}) collective-permute-start(bf16[48,3072]{1,0:T(8,128)(2,1)S(1)} %collective-permute-done.51), channel_id=1, source_target_pairs={{0,1},{1,2},{2,3},{3,11},{11,10},{10,9},{9,8},{8,0},{12,13},{13,14... | collective-permute-start | bytes 884744 | tf_op jit(solution)/shard_map/ppermute | solution.py:795
  328.0 6.9 %collective-permute-start.52 = (bf16[48,3072]{1,0:T(8,128)(2,1)S(1)}, bf16[48,3072]{1,0:T(8,128)(2,1)S(1)}, u32[]{:S(2)}, u32[]{:S(2)}) collective-permute-start(bf16[48,3072]{1,0:T(8,128)(2,1)S(1)} %collective-permute-done.50), channel_id=1, source_target_pairs={{0,1},{1,2},{2,3},{3,11},{11,10},{10,9},{9,8},{8,0},{12,13},{13,14... | collective-permute-start | bytes 884744 | tf_op jit(solution)/shard_map/ppermute | solution.py:795
  328.3 22.0 %collective-permute-start.49 = (bf16[8,224,768]{2,1,0:T(8,128)(2,1)S(1)}, bf16[8,224,768]{2,1,0:T(8,128)(2,1)S(1)}, u32[]{:S(2)}, u32[]{:S(2)}) collective-permute-start(bf16[8,224,768]{2,1,0:T(8,128)(2,1)S(1)} %bitcast_dynamic-update-slice_fusion.refs_0_), channel_id=1, source_target_pairs={{0,4},{1,5},{2,6},{3,7},{4,0},{5,1},{6,2},{7,3},{8,12},{9,13},{10,... | collective-permute-start | bytes 8257544 | tf_op jit(solution)/shard_map/ppermute | solution.py:933
  331.8 13.6 %collective-permute-start.55 = (bf16[8,48,3072]{2,1,0:T(8,128)(2,1)S(1)}, bf16[8,48,3072]{2,1,0:T(8,128)(2,1)S(1)}, u32[]{:S(2)}, u32[]{:S(2)}) collective-permute-start(bf16[8,48,3072]{2,1,0:T(8,128)(2,1)S(1)} %bitcast_dynamic-update-slice_fusion.8.refs_0_), channel_id=1, source_target_pairs={{0,4},{1,5},{2,6},{3,7},{4,0},{5,1},{6,2},{7,3},{8,12},{9,13},{10,... | collective-permute-start | bytes 7077896 | tf_op jit(solution)/shard_map/ppermute | solution.py:933
  334.9 13.0 %collective-permute-start.54 = (bf16[8,48,3072]{2,1,0:T(8,128)(2,1)S(1)}, bf16[8,48,3072]{2,1,0:T(8,128)(2,1)S(1)}, u32[]{:S(2)}, u32[]{:S(2)}) collective-permute-start(bf16[8,48,3072]{2,1,0:T(8,128)(2,1)S(1)} %bitcast_dynamic-update-slice_fusion.16.refs_0_), channel_id=1, source_target_pairs={{0,4},{1,5},{2,6},{3,7},{4,0},{5,1},{6,2},{7,3},{8,12},{9,13},{10,... | collective-permute-start | bytes 7077896 | tf_op jit(solution)/shard_map/ppermute | solution.py:933
  (12 other events, 40.8 us)

commit v6 on v5

--- a/solution.py
+++ b/solution.py
@@ -114,7 +114,7 @@
     return lane < HEAD, lane >= HEAD
 
 
-def forward_kernel(mode, crops, first, n_alias, query_lengths, key_lengths, own, *refs):
+def forward_kernel(mode, near, crops, first, n_alias, query_lengths, key_lengths, own, *refs):
     refs = list(refs)
     take = lambda count: [refs.pop(0) for _ in range(count)]
     recv = None if first else take(1)[0]
@@ -269,16 +269,20 @@
     def _():
         @pl.when(section == 0)
         def _():
-            copy = pltpu.make_async_copy(own.at[crop], bx, xsem)
-            copy.start()
+            if near:
+                bx[...] = own[crop]
+            else:
+                pltpu.make_async_copy(own.at[crop], bx, xsem).start()
 
         if mode != "held":
             for number in range(4):
                 weight_copy(number).start()
 
-        @pl.when(section == 0)
-        def _():
-            pltpu.make_async_copy(own.at[crop], bx, xsem).wait()
+        if not near:
+
+            @pl.when(section == 0)
+            def _():
+                pltpu.make_async_copy(own.at[crop], bx, xsem).wait()
 
         if recv is not None:
 
@@ -312,21 +316,22 @@
     arrived = [] if recv is None else [recv]
     read = in_vmem(*held) if mode == "held" else in_hbm(*weights[:4])
     grown = in_vmem(*held) if mode == "load" and held else []
-    operands = [*lengths, *in_hbm(own), *arrived, *read, *weights[4:], *order, *aliased, *grown]
+    near = mode == "held" and crops[0][0] == 0
+    operands = [*lengths, *(in_vmem if near else in_hbm)(own), *arrived, *read, *weights[4:], *order, *aliased, *grown]
     first = 10 + len(arrived) + len(order)
     shape_of = lambda name: (pltpu.VMEM if name in VMEM_NAMES else pltpu.HBM)(*shapes[name])
     spec_of = lambda name: VMEM if name in VMEM_NAMES else ANY
     copies = 1 if mode == "pass" else 2
     weight_shapes = [pltpu.VMEM((copies, *weight.shape[2:]), BF16) for weight in weights[:4]]
     outs = pl.pallas_call(
-        functools.partial(forward_kernel, mode, crops, recv is None, len(order) + len(aliased) + len(grown)),
+        functools.partial(forward_kernel, mode, near, crops, recv is None, len(order) + len(aliased) + len(grown)),
         out_shape=[
             jax.ShapeDtypeStruct((crop_len, width), BF16),
             jax.ShapeDtypeStruct((1, width), F32),
         ]
         + [shape_of(name) for name in names]
         + (weight_shapes if mode == "load" else []),
-        in_specs=[SMEM, SMEM, ANY]
+        in_specs=[SMEM, SMEM, VMEM if near else ANY]
         + [VMEM] * len(arrived)
         + [VMEM if mode == "held" else ANY] * 4
         + [VMEM] * 3

time: 363 us -> 386 us (1.063)
  local copies, waits for them, and re-layouts: 6.23 us -> 30.9 us
    unnamed x42 -> x68, local copies, waits for them, and re-layouts: 4.99 us -> 29.7 us
  transfers between devices with their start and end apart: 56 -> 56, of which waited for: 37 -> 35; matrix products, arithmetic and copies ran while one was open for 8% -> 7% of each run, Pallas kernels for 31% -> 28%
where the time goes in v6:
time: 386 us; the launch traced here: 379 us
  Pallas kernels  192 us (50%)
  waiting for transfers between devices  86.4 us (22%)
  starting transfers between devices  41.3 us (11%)
  local copies, waits for them, and re-layouts  30.9 us (8%)
  other arithmetic  26.4 us (7%)
    pallas_call x11, Pallas kernels, forward_call(): pl.pallas_call(functools.partial(forward_kernel, mode, near, crops, recv...  102 us
    ppermute x42, waiting for transfers between devices, advance(): moving = tied(lax.ppermute(self.moving, AXES, self.pairs), last)  83.9 us
    pallas_call x5, Pallas kernels, backward_call(): pl.pallas_call(functools.partial(backward_kernel, crops, recv is None, le...  44.4 us
    unnamed x68, local copies, waits for them, and re-layouts  29.7 us
    pallas_call x1, Pallas kernels, weights_call(): pl.pallas_call(functools.partial(weights_kernel, groups), out_shape=[pltp...  29.5 us
    ppermute x42, starting transfers between devices, advance(): moving = tied(lax.ppermute(self.moving, AXES, self.pairs), last)  22.5 us
    convert_element_type x19, other arithmetic, advance(): moving = lax.reduce_precision(moving, 8, 7).astype(BF16)  20.7 us
    pallas_call x6, Pallas kernels, write_call(): pl.pallas_call(functools.partial(write_kernel, mine, len(shapes)), out_sh...  14.8 us
  transfers between devices with their start and end apart: 56, of which 35 were waited for; matrix products, arithmetic and copies ran while one was open for 7% of the time, Pallas kernels for 28%

profile of v6, /device:TPU:1, one launch (start us, length us, event | category | flops | bytes accessed | tf_op | source)
XLA Modules:
  0.0 379.4 jit_solution(1474220987848275741)
XLA Ops:
  4.2 13.4 %forward_crop.11 = (bf16[256,768]{1,0:T(8,128)(2,1)S(1)}, f32[1,768]{1,0:T(1,128)S(1)}, bf16[4,256,768]{2,1,0:T(8,128)(2,1)S(1)}, bf16[4,256,3072]{2,1,0:T(8,128...) custom-call(s32[4]{0:T(128)S(1)} %copy-done.18, ...), custom_call_target="tpu_custom_call" | custom-call | flops 3623878656 | bytes 8000000 | tf_op jit(solution)/shard_map/forward_crop/pallas_call | solution.py:326
  17.6 2.7 copy-done
  21.6 2.8 copy-done.1
  24.4 10.5 %forward_crop.12 = (bf16[256,768]{1,0:T(8,128)(2,1)S(1)}, f32[1,768]{1,0:T(1,128)S(1)}, bf16[4,256,768]{2,1,0:T(8,128)(2,1)S(1)}, bf16[4,256,3072]{2,1,0:T(8,128...) custom-call(s32[4]{0:T(128)S(1)} %copy-done.18, ...), custom_call_target="tpu_custom_call", output_to_operand_aliasing={{2}: (11, {}), {3}: (12, {}), {4}: (13, {}), {5}: (14, {}),... | custom-call | flops 3623878656 | bytes 8000000 | tf_op jit(solution)/shard_map/forward_crop/pallas_call | solution.py:326
  34.9 2.7 copy-done.2
  39.0 2.8 copy-done.3
  41.7 9.0 %forward_crop.13 = (bf16[256,768]{1,0:T(8,128)(2,1)S(1)}, f32[1,768]{1,0:T(1,128)S(1)}, bf16[4,256,768]{2,1,0:T(8,128)(2,1)S(1)}, bf16[4,256,3072]{2,1,0:T(8,128...) custom-call(s32[4]{0:T(128)S(1)} %copy-done.18, ...), custom_call_target="tpu_custom_call", output_to_operand_aliasing={{2}: (12, {}), {3}: (13, {}), {4}: (14, {}), {5}: (15, {}),... | custom-call | flops 3623878656 | bytes 8000000 | tf_op jit(solution)/shard_map/forward_crop/pallas_call | solution.py:326
  50.8 2.7 copy-done.4
  53.5 2.8 copy-done.5
  56.3 5.8 %backward_crop.5 = (bf16[256,768]{1,0:T(8,128)(2,1)S(1)}, f32[12,768]{1,0:T(8,128)S(1)}, f32[4,256,768]{2,1,0:T(8,128)}, bf16[4,256,768]{2,1,0:T(8,128)(2,1)}, b...) custom-call(s32[4]{0:T(128)S(1)} %copy-done.18, ...), custom_call_target="tpu_custom_call" | custom-call | flops 3623878656 | bytes 8000000 | tf_op jit(solution)/shard_map/backward_crop/pallas_call | solution.py:543
  62.2 2.8 copy-done.6
  65.0 9.0 %forward_crop.14 = (bf16[256,768]{1,0:T(8,128)(2,1)S(1)}, f32[1,768]{1,0:T(1,128)S(1)}, bf16[4,256,768]{2,1,0:T(8,128)(2,1)S(1)}, bf16[4,256,3072]{2,1,0:T(8,128...) custom-call(s32[4]{0:T(128)S(1)} %copy-done.18, ...), custom_call_target="tpu_custom_call", output_to_operand_aliasing={{2}: (12, {}), {3}: (13, {}), {4}: (14, {}), {5}: (15, {}),... | custom-call | flops 3623878656 | bytes 8000000 | tf_op jit(solution)/shard_map/forward_crop/pallas_call | solution.py:326
  74.0 2.7 copy-done.7
  76.7 2.8 copy-done.8
  79.5 9.3 %backward_crop.6 = (bf16[256,768]{1,0:T(8,128)(2,1)S(1)}, f32[12,768]{1,0:T(8,128)S(1)}, f32[4,256,768]{2,1,0:T(8,128)}, bf16[4,256,768]{2,1,0:T(8,128)(2,1)}, b...) custom-call(s32[4]{0:T(128)S(1)} %copy-done.18, ...), custom_call_target="tpu_custom_call", output_to_operand_aliasing={{2}: (16, {}), {3}: (17, {}), {4}: (18, {}), {5}: (19, {}),... | custom-call | flops 3623878656 | bytes 8000000 | tf_op jit(solution)/shard_map/backward_crop/pallas_call | solution.py:543
  90.3 13.6 %forward_crop.15 = (bf16[256,768]{1,0:T(8,128)(2,1)S(1)}, f32[1,768]{1,0:T(1,128)S(1)}, bf16[4,256,768]{2,1,0:T(8,128)(2,1)S(1)}, bf16[4,256,3072]{2,1,0:T(8,128...) custom-call(s32[4]{0:T(128)S(1)} %copy-done.18, ...), custom_call_target="tpu_custom_call", output_to_operand_aliasing={{2}: (12, {}), {3}: (13, {}), {4}: (14, {}), {5}: (15, {}),... | custom-call | flops 3623878656 | bytes 8000000 | tf_op jit(solution)/shard_map/forward_crop/pallas_call | solution.py:326
  103.9 9.6 %backward_crop.7 = (bf16[256,768]{1,0:T(8,128)(2,1)S(1)}, f32[12,768]{1,0:T(8,128)S(1)}, f32[4,256,768]{2,1,0:T(8,128)}, bf16[4,256,768]{2,1,0:T(8,128)(2,1)}, b...) custom-call(s32[4]{0:T(128)S(1)} %copy-done.18, ...), custom_call_target="tpu_custom_call", output_to_operand_aliasing={{2}: (16, {}), {3}: (17, {}), {4}: (18, {}), {5}: (19, {}),... | custom-call | flops 3623878656 | bytes 8000000 | tf_op jit(solution)/shard_map/backward_crop/pallas_call | solution.py:543
  113.6 10.5 %forward_crop.16 = (bf16[256,768]{1,0:T(8,128)(2,1)S(1)}, f32[1,768]{1,0:T(1,128)S(1)}, bf16[4,256,768]{2,1,0:T(8,128)(2,1)S(1)}, bf16[4,256,3072]{2,1,0:T(8,128...) custom-call(s32[4]{0:T(128)S(1)} %copy-done.18, ...), custom_call_target="tpu_custom_call", output_to_operand_aliasing={{2}: (12, {}), {3}: (13, {}), {4}: (14, {}), {5}: (15, {}),... | custom-call | flops 3623878656 | bytes 8000000 | tf_op jit(solution)/shard_map/forward_crop/pallas_call | solution.py:326
  124.2 9.3 %backward_crop.8 = (bf16[256,768]{1,0:T(8,128)(2,1)S(1)}, f32[12,768]{1,0:T(8,128)S(1)}, f32[4,256,768]{2,1,0:T(8,128)}, bf16[4,256,768]{2,1,0:T(8,128)(2,1)}, b...) custom-call(s32[4]{0:T(128)S(1)} %copy-done.18, ...), custom_call_target="tpu_custom_call", output_to_operand_aliasing={{2}: (16, {}), {3}: (17, {}), {4}: (18, {}), {5}: (19, {}),... | custom-call | flops 3623878656 | bytes 8000000 | tf_op jit(solution)/shard_map/backward_crop/pallas_call | solution.py:543
  134.1 11.0 %forward_crop.17 = (bf16[256,768]{1,0:T(8,128)(2,1)S(1)}, f32[1,768]{1,0:T(1,128)S(1)}, bf16[4,256,768]{2,1,0:T(8,128)(2,1)S(1)}, bf16[4,256,3072]{2,1,0:T(8,128...) custom-call(s32[4]{0:T(128)S(1)} %copy-done.18, ...), custom_call_target="tpu_custom_call", output_to_operand_aliasing={{2}: (12, {}), {3}: (13, {}), {4}: (14, {}), {5}: (15, {}),... | custom-call | flops 3623878656 | bytes 8000000 | tf_op jit(solution)/shard_map/forward_crop/pallas_call | solution.py:326
  145.1 10.3 %backward_crop.9 = (bf16[256,768]{1,0:T(8,128)(2,1)}, f32[12,768]{1,0:T(8,128)S(1)}, f32[4,256,768]{2,1,0:T(8,128)}, bf16[4,256,768]{2,1,0:T(8,128)(2,1)}, bf16[...) custom-call(s32[4]{0:T(128)S(1)} %copy-done.18, ...), custom_call_target="tpu_custom_call", output_to_operand_aliasing={{2}: (16, {}), {3}: (17, {}), {4}: (18, {}), {5}: (19, {}),... | custom-call | flops 3623878656 | bytes 8000000 | tf_op jit(solution)/shard_map/backward_crop/pallas_call | solution.py:543
  155.4 29.5 %weight_gradients.1 = (bf16[8,192,768]{2,1,0:T(8,128)(2,1)}, bf16[8,192,768]{2,1,0:T(8,128)(2,1)}, bf16[8,48,3072]{2,1,0:T(8,128)(2,1)}, bf16[8,48,3072]{2,1,0:T...) custom-call(bf16[1280,3072]{1,0:T(8,128)(2,1)} %bitcast.199, bf16[1280,768]{1,0:T(8,128)(2,1)} %bitcast.204, ...), custom_call_target="tpu_custom_call" | custom-call | flops 14495514624 | bytes 40000000 | tf_op jit(solution)/shard_map/weight_gradients/pallas_call | solution.py:671
  188.2 2.5 collective-permute-done.6
  191.8 2.7 collective-permute-start.7
  195.7 2.2 collective-permute-start.14
  199.1 2.2 collective-permute-start.12
  201.3 11.7 %forward_crop.18 = (bf16[256,768]{1,0:T(8,128)(2,1)S(1)}, f32[1,768]{1,0:T(1,128)S(1)}) custom-call(s32[4]{0:T(128)S(1)} %copy-done.19, s32[4]{0:T(128)S(1)} %copy-done.21, bf16[4,256,768]{2,1,0:T(8,128)(2,1)} %own.18, bf16[1,2,768,2304]{3,2,1,0:T(8,128)(2,1)} %refs_1_.11, bf16[1,2,768,768]{3,2,1,0:T(8,128)(2,1)} %refs_2_.11, ...), custom_call_target="tpu_custom_call" | custom-call | flops 3623878656 | bytes 8000000 | tf_op jit(solution)/shard_map/forward_crop/pallas_call | solution.py:326
  218.3 3.2 collective-permute-done.8
  228.7 10.1 %forward_crop.20 = (bf16[256,768]{1,0:T(8,128)(2,1)}, f32[1,768]{1,0:T(1,128)S(1)}) custom-call(s32[4]{0:T(128)S(1)} %copy-done.19, s32[4]{0:T(128)S(1)} %copy-done.21, bf16[4,256,768]{2,1,0:T(8,128)(2,1)} %own.21, bf16[256,768]{1,0:T(8,128)(2,1)S(1)} %collective-permute-done.11.refs_0_, bf16[1,2,768,2304]{3,2,1,0:T(8,128)(2,1)} %refs_1_.11, ...), custom_call_target="tpu_custom_call" | custom-call | flops 3623878656 | bytes 8000000 | tf_op jit(solution)/shard_map/forward_crop/pallas_call | solution.py:326
  247.2 1.8 collective-permute-done.21
  250.4 1.8 collective-permute-done.20
  253.6 1.8 collective-permute-done.19
  256.7 1.8 collective-permute-done.24
  272.5 1.8 collective-permute-done.25
  282.2 2.1 collective-permute-done.28
  284.5 2.9 collective-permute-done.33
  292.3 2.0 collective-permute-done.31
  294.5 2.9 collective-permute-done.36
  297.7 2.9 collective-permute-done.35
  300.9 3.4 collective-permute-done.34
  304.6 2.9 collective-permute-done.39
  307.7 2.9 collective-permute-done.38
  310.9 3.4 collective-permute-done.37
  314.6 2.9 collective-permute-done.42
  317.7 2.9 collective-permute-done.41
  320.9 3.4 collective-permute-done.40
  324.6 2.9 collective-permute-done.45
  328.1 2.6 collective-permute-done.44
  331.0 3.4 collective-permute-done.43
  334.6 2.9 collective-permute-done.48
  337.8 2.9 collective-permute-done.47
  341.0 3.4 collective-permute-done.46
  344.3 3.2 collective-permute-done.51
  347.8 2.9 collective-permute-done.50
  351.0 3.5 collective-permute-start.49
  354.5 3.1 collective-permute-start.55
  357.6 3.1 collective-permute-start.54
  360.7 2.5 write_half.6
  363.2 2.4 write_half.10.refs_1_
  365.7 2.4 write_half.8
  368.1 2.4 write_half.11
  370.5 2.4 write_half.9
  373.0 2.5 write_half.7
  375.5 1.9 small_sums.1
  (194 shorter events, 73.3 us)
Async XLA Ops:
  4.2 17.4 %copy-start.10 = (bf16[4,256,768]{2,1,0:T(8,128)(2,1)S(1)}, bf16[4,256,768]{2,1,0:T(8,128)(2,1)}, u32[]{:S(2)}) copy-start(bf16[4,256,768]{2,1,0:T(8,128)(2,1)} %own.21) | copy-start | bytes 4718596
  20.3 14.6 %copy-start.22 = (f32[1,768]{1,0:T(1,128)}, f32[1,768]{1,0:T(1,128)S(1)}, u32[]{:S(2)}) copy-start(f32[1,768]{1,0:T(1,128)S(1)} %get-tuple-element.219.refs_7_) | copy-start | bytes 9220
  20.3 18.7 %collective-permute-start = (bf16[256,768]{1,0:T(8,128)(2,1)S(1)}, bf16[256,768]{1,0:T(8,128)(2,1)S(1)}, u32[]{:S(2)}, u32[]{:S(2)}) collective-permute-start(bf16[256,768]{1,0:T(8,128)(2,1)S(1)} %get-tuple-element.214), channel_id=1, source_target_pairs={{0,16},{1,17},{2,18},{3,19},{4,20},{5,21},{6,22},{7,23},{8,24},{9,... | collective-permute-start | bytes 1179656 | tf_op jit(solution)/shard_map/ppermute | solution.py:848
  37.6 24.5 %collective-permute-start.2 = (bf16[256,768]{1,0:T(8,128)(2,1)S(1)}, bf16[256,768]{1,0:T(8,128)(2,1)S(1)}, u32[]{:S(2)}, u32[]{:S(2)}) collective-permute-start(bf16[256,768]{1,0:T(8,128)(2,1)S(1)} %get-tuple-element.250), channel_id=1, source_target_pairs={{0,16},{1,17},{2,18},{3,19},{4,20},{5,21},{6,22},{7,23},{8,24},{9,... | collective-permute-start | bytes 1179656 | tf_op jit(solution)/shard_map/ppermute | solution.py:848
  62.1 14.6 %collective-permute-start.1 = (bf16[256,768]{1,0:T(8,128)(2,1)S(1)}, bf16[256,768]{1,0:T(8,128)(2,1)S(1)}, u32[]{:S(2)}, u32[]{:S(2)}) collective-permute-start(bf16[256,768]{1,0:T(8,128)(2,1)S(1)} %get-tuple-element.249), channel_id=1, source_target_pairs={{0,16},{16,0},{1,17},{17,1},{2,18},{18,2},{3,19},{19,3},{4,20},{20... | collective-permute-start | bytes 1179656 | tf_op jit(solution)/shard_map/ppermute | solution.py:898
  88.8 15.1 %collective-permute-start.3 = (bf16[256,768]{1,0:T(8,128)(2,1)S(1)}, bf16[256,768]{1,0:T(8,128)(2,1)S(1)}, u32[]{:S(2)}, u32[]{:S(2)}) collective-permute-start(bf16[256,768]{1,0:T(8,128)(2,1)S(1)} %get-tuple-element.275), channel_id=1, source_target_pairs={{0,16},{16,0},{1,17},{17,1},{2,18},{18,2},{3,19},{19,3},{4,20},{20... | collective-permute-start | bytes 1179656 | tf_op jit(solution)/shard_map/ppermute | solution.py:898
  90.3 13.6 %copy-start.13 = (bf16[4,256,768]{2,1,0:T(8,128)(2,1)S(1)}, bf16[4,256,768]{2,1,0:T(8,128)(2,1)}, u32[]{:S(2)}) copy-start(bf16[4,256,768]{2,1,0:T(8,128)(2,1)} %cot.9) | copy-start | bytes 4718596
  113.6 10.6 %collective-permute-start.4 = (bf16[256,768]{1,0:T(8,128)(2,1)S(1)}, bf16[256,768]{1,0:T(8,128)(2,1)S(1)}, u32[]{:S(2)}, u32[]{:S(2)}) collective-permute-start(bf16[256,768]{1,0:T(8,128)(2,1)S(1)} %get-tuple-element.292), channel_id=1, source_target_pairs={{0,16},{16,0},{1,17},{17,1},{2,18},{18,2},{3,19},{19,3},{4,20},{20... | collective-permute-start | bytes 1179656 | tf_op jit(solution)/shard_map/ppermute | solution.py:898
  133.5 11.5 %collective-permute-start.5 = (bf16[256,768]{1,0:T(8,128)(2,1)S(1)}, bf16[256,768]{1,0:T(8,128)(2,1)S(1)}, u32[]{:S(2)}, u32[]{:S(2)}) collective-permute-start(bf16[256,768]{1,0:T(8,128)(2,1)S(1)} %get-tuple-element.321), channel_id=1, source_target_pairs={{0,16},{16,0},{1,17},{17,1},{2,18},{18,2},{3,19},{19,3},{4,20},{20... | collective-permute-start | bytes 1179656 | tf_op jit(solution)/shard_map/ppermute | solution.py:898
  184.9 16.4 %copy-start.15 = (f32[1,2,2,768]{3,2,1,0:T(2,128)S(1)}, f32[1,2,2,768]{3,2,1,0:T(2,128)}, u32[]{:S(2)}) copy-start(f32[1,2,2,768]{3,2,1,0:T(2,128)} %refs_7_.15) | copy-start | bytes 36868
  184.9 16.4 %copy-start.17 = (f32[1,2,3072]{2,1,0:T(2,128)S(1)}, f32[1,2,3072]{2,1,0:T(2,128)}, u32[]{:S(2)}) copy-start(f32[1,2,3072]{2,1,0:T(2,128)} %refs_5_.26) | copy-start | bytes 73732
  184.9 16.4 %copy-start.19 = (s32[4]{0:T(128)S(1)}, s32[4]{0:T(128)}, u32[]{:S(2)}) copy-start(s32[4]{0:T(128)} %query_lengths.10) | copy-start | bytes 52
  184.9 16.4 %copy-start.21 = (s32[4]{0:T(128)S(1)}, s32[4]{0:T(128)}, u32[]{:S(2)}) copy-start(s32[4]{0:T(128)} %key_lengths.21) | copy-start | bytes 52
  184.9 5.8 %collective-permute-start.6 = (bf16[8,192,768]{2,1,0:T(8,128)(2,1)}, bf16[8,192,768]{2,1,0:T(8,128)(2,1)}, u32[]{:S(2)}, u32[]{:S(2)}) collective-permute-start(bf16[8,192,768]{2,1,0:T(8,128)(2,1)} %get-tuple-element.348), channel_id=1, source_target_pairs={{0,4},{1,5},{2,6},{3,7},{4,0},{5,1},{6,2},{7,3},{8,12},{9,13},{10,... | collective-permute-start | bytes 7077896 | tf_op jit(solution)/shard_map/ppermute | solution.py:917
  186.2 8.4 %collective-permute-start.13 = (bf16[8,48,3072]{2,1,0:T(8,128)(2,1)}, bf16[8,48,3072]{2,1,0:T(8,128)(2,1)}, u32[]{:S(2)}, u32[]{:S(2)}) collective-permute-start(bf16[8,48,3072]{2,1,0:T(8,128)(2,1)} %get-tuple-element.356), channel_id=1, source_target_pairs={{0,4},{1,5},{2,6},{3,7},{4,0},{5,1},{6,2},{7,3},{8,12},{9,13},{10,... | collective-permute-start | bytes 7077896 | tf_op jit(solution)/shard_map/ppermute | solution.py:917
  186.3 11.7 %collective-permute-start.9 = (bf16[8,48,3072]{2,1,0:T(8,128)(2,1)}, bf16[8,48,3072]{2,1,0:T(8,128)(2,1)}, u32[]{:S(2)}, u32[]{:S(2)}) collective-permute-start(bf16[8,48,3072]{2,1,0:T(8,128)(2,1)} %get-tuple-element.352), channel_id=1, source_target_pairs={{0,4},{1,5},{2,6},{3,7},{4,0},{5,1},{6,2},{7,3},{8,12},{9,13},{10,... | collective-permute-start | bytes 7077896 | tf_op jit(solution)/shard_map/ppermute | solution.py:917
  186.7 42.0 %collective-permute-start.11 = (bf16[256,768]{1,0:T(8,128)(2,1)S(1)}, bf16[256,768]{1,0:T(8,128)(2,1)S(1)}, u32[]{:S(2)}, u32[]{:S(2)}) collective-permute-start(bf16[256,768]{1,0:T(8,128)(2,1)S(1)} %get-tuple-element.320.sent), channel_id=1, source_target_pairs={{0,16},{1,17},{2,18},{3,19},{4,20},{5,21},{6,22},{7,23},{8,24},{9,... | collective-permute-start | bytes 1179656 | tf_op jit(solution)/shard_map/ppermute | solution.py:848
  191.8 22.6 %collective-permute-start.7 = (bf16[192,768]{1,0:T(8,128)(2,1)S(1)}, bf16[192,768]{1,0:T(8,128)(2,1)S(1)}, u32[]{:S(2)}, u32[]{:S(2)}) collective-permute-start(bf16[192,768]{1,0:T(8,128)(2,1)S(1)} %fusion.42.refs_7_), channel_id=1, source_target_pairs={{0,1},{1,2},{2,3},{3,11},{11,10},{10,9},{9,8},{8,0},{12,13},{13,14... | collective-permute-start | bytes 884744 | tf_op jit(solution)/shard_map/ppermute | solution.py:800
  195.7 27.9 %collective-permute-start.14 = (bf16[48,3072]{1,0:T(8,128)(2,1)S(1)}, bf16[48,3072]{1,0:T(8,128)(2,1)S(1)}, u32[]{:S(2)}, u32[]{:S(2)}) collective-permute-start(bf16[48,3072]{1,0:T(8,128)(2,1)S(1)} %fusion.44), channel_id=1, source_target_pairs={{0,1},{1,2},{2,3},{3,11},{11,10},{10,9},{9,8},{8,0},{12,13},{13,14... | collective-permute-start | bytes 884744 | tf_op jit(solution)/shard_map/ppermute | solution.py:800
  199.1 15.3 %copy-start.32 = (bf16[8,192,768]{2,1,0:T(8,128)(2,1)S(1)}, bf16[8,192,768]{2,1,0:T(8,128)(2,1)}, u32[]{:S(2)}) copy-start(bf16[8,192,768]{2,1,0:T(8,128)(2,1)} %get-tuple-element.347) | copy-start | bytes 7077892
  199.1 27.2 %collective-permute-start.12 = (bf16[48,3072]{1,0:T(8,128)(2,1)S(1)}, bf16[48,3072]{1,0:T(8,128)(2,1)S(1)}, u32[]{:S(2)}, u32[]{:S(2)}) collective-permute-start(bf16[48,3072]{1,0:T(8,128)(2,1)S(1)} %fusion.43.refs_8_), channel_id=1, source_target_pairs={{0,1},{1,2},{2,3},{3,11},{11,10},{10,9},{9,8},{8,0},{12,13},{13,14... | collective-permute-start | bytes 884744 | tf_op jit(solution)/shard_map/ppermute | solution.py:800
  213.1 29.8 %collective-permute-start.16 = (bf16[256,768]{1,0:T(8,128)(2,1)S(1)}, bf16[256,768]{1,0:T(8,128)(2,1)S(1)}, u32[]{:S(2)}, u32[]{:S(2)}) collective-permute-start(bf16[256,768]{1,0:T(8,128)(2,1)S(1)} %get-tuple-element.361), channel_id=1, source_target_pairs={{0,16},{1,17},{2,18},{3,19},{4,20},{5,21},{6,22},{7,23},{8,24},{9,... | collective-permute-start | bytes 1179656 | tf_op jit(solution)/shard_map/ppermute | solution.py:848
  215.5 5.9 %collective-permute-start.8 = (bf16[192,768]{1,0:T(8,128)(2,1)S(1)}, bf16[192,768]{1,0:T(8,128)(2,1)S(1)}, u32[]{:S(2)}, u32[]{:S(2)}) collective-permute-start(bf16[192,768]{1,0:T(8,128)(2,1)S(1)} %fusion.41), channel_id=1, source_target_pairs={{0,1},{1,2},{2,3},{3,11},{11,10},{10,9},{9,8},{8,0},{12,13},{13,14... | collective-permute-start | bytes 884744 | tf_op jit(solution)/shard_map/ppermute | solution.py:800
  222.5 16.3 %collective-permute-start.10 = (bf16[192,768]{1,0:T(8,128)(2,1)S(1)}, bf16[192,768]{1,0:T(8,128)(2,1)S(1)}, u32[]{:S(2)}, u32[]{:S(2)}) collective-permute-start(bf16[192,768]{1,0:T(8,128)(2,1)S(1)} %fusion.39), channel_id=1, source_target_pairs={{0,1},{1,2},{2,3},{3,11},{11,10},{10,9},{9,8},{8,0},{12,13},{13,14... | collective-permute-start | bytes 884744 | tf_op jit(solution)/shard_map/ppermute | solution.py:800
  224.6 15.6 %collective-permute-start.18 = (bf16[48,3072]{1,0:T(8,128)(2,1)S(1)}, bf16[48,3072]{1,0:T(8,128)(2,1)S(1)}, u32[]{:S(2)}, u32[]{:S(2)}) collective-permute-start(bf16[48,3072]{1,0:T(8,128)(2,1)S(1)} %fusion.37), channel_id=1, source_target_pairs={{0,1},{1,2},{2,3},{3,11},{11,10},{10,9},{9,8},{8,0},{12,13},{13,14... | collective-permute-start | bytes 884744 | tf_op jit(solution)/shard_map/ppermute | solution.py:800
  227.4 14.1 %collective-permute-start.17 = (bf16[48,3072]{1,0:T(8,128)(2,1)S(1)}, bf16[48,3072]{1,0:T(8,128)(2,1)S(1)}, u32[]{:S(2)}, u32[]{:S(2)}) collective-permute-start(bf16[48,3072]{1,0:T(8,128)(2,1)S(1)} %fusion.35.refs_8_), channel_id=1, source_target_pairs={{0,1},{1,2},{2,3},{3,11},{11,10},{10,9},{9,8},{8,0},{12,13},{13,14... | collective-permute-start | bytes 884744 | tf_op jit(solution)/shard_map/ppermute | solution.py:800
  239.9 5.9 %collective-permute-start.15 = (bf16[192,768]{1,0:T(8,128)(2,1)S(1)}, bf16[192,768]{1,0:T(8,128)(2,1)S(1)}, u32[]{:S(2)}, u32[]{:S(2)}) collective-permute-start(bf16[192,768]{1,0:T(8,128)(2,1)S(1)} %fusion.33), channel_id=1, source_target_pairs={{0,1},{1,2},{2,3},{3,11},{11,10},{10,9},{9,8},{8,0},{12,13},{13,14... | collective-permute-start | bytes 884744 | tf_op jit(solution)/shard_map/ppermute | solution.py:800
  241.3 7.7 %collective-permute-start.21 = (bf16[48,3072]{1,0:T(8,128)(2,1)S(1)}, bf16[48,3072]{1,0:T(8,128)(2,1)S(1)}, u32[]{:S(2)}, u32[]{:S(2)}) collective-permute-start(bf16[48,3072]{1,0:T(8,128)(2,1)S(1)} %fusion.31), channel_id=1, source_target_pairs={{0,1},{1,2},{2,3},{3,11},{11,10},{10,9},{9,8},{8,0},{12,13},{13,14... | collective-permute-start | bytes 884744 | tf_op jit(solution)/shard_map/ppermute | solution.py:800
  242.7 9.5 %collective-permute-start.20 = (bf16[48,3072]{1,0:T(8,128)(2,1)S(1)}, bf16[48,3072]{1,0:T(8,128)(2,1)S(1)}, u32[]{:S(2)}, u32[]{:S(2)}) collective-permute-start(bf16[48,3072]{1,0:T(8,128)(2,1)S(1)} %fusion.29.refs_8_), channel_id=1, source_target_pairs={{0,1},{1,2},{2,3},{3,11},{11,10},{10,9},{9,8},{8,0},{12,13},{13,14... | collective-permute-start | bytes 884744 | tf_op jit(solution)/shard_map/ppermute | solution.py:800
  246.9 8.4 %collective-permute-start.19 = (bf16[192,768]{1,0:T(8,128)(2,1)S(1)}, bf16[192,768]{1,0:T(8,128)(2,1)S(1)}, u32[]{:S(2)}, u32[]{:S(2)}) collective-permute-start(bf16[192,768]{1,0:T(8,128)(2,1)S(1)} %fusion.27), channel_id=1, source_target_pairs={{0,1},{1,2},{2,3},{3,11},{11,10},{10,9},{9,8},{8,0},{12,13},{13,14... | collective-permute-start | bytes 884744 | tf_op jit(solution)/shard_map/ppermute | solution.py:800
  250.1 8.4 %collective-permute-start.24 = (bf16[48,3072]{1,0:T(8,128)(2,1)S(1)}, bf16[48,3072]{1,0:T(8,128)(2,1)S(1)}, u32[]{:S(2)}, u32[]{:S(2)}) collective-permute-start(bf16[48,3072]{1,0:T(8,128)(2,1)S(1)} %fusion.25), channel_id=1, source_target_pairs={{0,1},{1,2},{2,3},{3,11},{11,10},{10,9},{9,8},{8,0},{12,13},{13,14... | collective-permute-start | bytes 884744 | tf_op jit(solution)/shard_map/ppermute | solution.py:800
  253.2 8.4 %collective-permute-start.23 = (bf16[48,3072]{1,0:T(8,128)(2,1)S(1)}, bf16[48,3072]{1,0:T(8,128)(2,1)S(1)}, u32[]{:S(2)}, u32[]{:S(2)}) collective-permute-start(bf16[48,3072]{1,0:T(8,128)(2,1)S(1)} %fusion.23), channel_id=1, source_target_pairs={{0,1},{1,2},{2,3},{3,11},{11,10},{10,9},{9,8},{8,0},{12,13},{13,14... | collective-permute-start | bytes 884744 | tf_op jit(solution)/shard_map/ppermute | solution.py:800
  256.4 8.4 %collective-permute-start.22 = (bf16[192,768]{1,0:T(8,128)(2,1)S(1)}, bf16[192,768]{1,0:T(8,128)(2,1)S(1)}, u32[]{:S(2)}, u32[]{:S(2)}) collective-permute-start(bf16[192,768]{1,0:T(8,128)(2,1)S(1)} %fusion.21), channel_id=1, source_target_pairs={{0,1},{1,2},{2,3},{3,11},{11,10},{10,9},{9,8},{8,0},{12,13},{13,14... | collective-permute-start | bytes 884744 | tf_op jit(solution)/shard_map/ppermute | solution.py:800
  259.6 8.4 %collective-permute-start.27 = (bf16[48,3072]{1,0:T(8,128)(2,1)S(1)}, bf16[48,3072]{1,0:T(8,128)(2,1)S(1)}, u32[]{:S(2)}, u32[]{:S(2)}) collective-permute-start(bf16[48,3072]{1,0:T(8,128)(2,1)S(1)} %fusion.19), channel_id=1, source_target_pairs={{0,1},{1,2},{2,3},{3,11},{11,10},{10,9},{9,8},{8,0},{12,13},{13,14... | collective-permute-start | bytes 884744 | tf_op jit(solution)/shard_map/ppermute | solution.py:800
  262.7 8.4 %collective-permute-start.26 = (bf16[48,3072]{1,0:T(8,128)(2,1)S(1)}, bf16[48,3072]{1,0:T(8,128)(2,1)S(1)}, u32[]{:S(2)}, u32[]{:S(2)}) collective-permute-start(bf16[48,3072]{1,0:T(8,128)(2,1)S(1)} %fusion.17), channel_id=1, source_target_pairs={{0,1},{1,2},{2,3},{3,11},{11,10},{10,9},{9,8},{8,0},{12,13},{13,14... | collective-permute-start | bytes 884744 | tf_op jit(solution)/shard_map/ppermute | solution.py:800
  265.9 8.4 %collective-permute-start.25 = (bf16[192,768]{1,0:T(8,128)(2,1)S(1)}, bf16[192,768]{1,0:T(8,128)(2,1)S(1)}, u32[]{:S(2)}, u32[]{:S(2)}) collective-permute-start(bf16[192,768]{1,0:T(8,128)(2,1)S(1)} %fusion.15), channel_id=1, source_target_pairs={{0,1},{1,2},{2,3},{3,11},{11,10},{10,9},{9,8},{8,0},{12,13},{13,14... | collective-permute-start | bytes 884744 | tf_op jit(solution)/shard_map/ppermute | solution.py:800
  269.1 8.4 %collective-permute-start.30 = (bf16[48,3072]{1,0:T(8,128)(2,1)S(1)}, bf16[48,3072]{1,0:T(8,128)(2,1)S(1)}, u32[]{:S(2)}, u32[]{:S(2)}) collective-permute-start(bf16[48,3072]{1,0:T(8,128)(2,1)S(1)} %fusion.13), channel_id=1, source_target_pairs={{0,1},{1,2},{2,3},{3,11},{11,10},{10,9},{9,8},{8,0},{12,13},{13,14... | collective-permute-start | bytes 884744 | tf_op jit(solution)/shard_map/ppermute | solution.py:800
  272.2 8.4 %collective-permute-start.29 = (bf16[48,3072]{1,0:T(8,128)(2,1)S(1)}, bf16[48,3072]{1,0:T(8,128)(2,1)S(1)}, u32[]{:S(2)}, u32[]{:S(2)}) collective-permute-start(bf16[48,3072]{1,0:T(8,128)(2,1)S(1)} %fusion.11), channel_id=1, source_target_pairs={{0,1},{1,2},{2,3},{3,11},{11,10},{10,9},{9,8},{8,0},{12,13},{13,14... | collective-permute-start | bytes 884744 | tf_op jit(solution)/shard_map/ppermute | solution.py:800
  275.4 8.9 %collective-permute-start.28 = (bf16[224,768]{1,0:T(8,128)(2,1)S(1)}, bf16[224,768]{1,0:T(8,128)(2,1)S(1)}, u32[]{:S(2)}, u32[]{:S(2)}) collective-permute-start(bf16[224,768]{1,0:T(8,128)(2,1)S(1)} %pad_maximum_fusion), channel_id=1, source_target_pairs={{0,1},{1,2},{2,3},{3,11},{11,10},{10,9},{9,8},{8,0},{12,13},{13,14... | collective-permute-start | bytes 1032200 | tf_op jit(solution)/shard_map/ppermute | solution.py:800
  278.5 8.9 %collective-permute-start.33 = (bf16[48,3072]{1,0:T(8,128)(2,1)S(1)}, bf16[48,3072]{1,0:T(8,128)(2,1)S(1)}, u32[]{:S(2)}, u32[]{:S(2)}) collective-permute-start(bf16[48,3072]{1,0:T(8,128)(2,1)S(1)} %fusion.7), channel_id=1, source_target_pairs={{0,1},{1,2},{2,3},{3,11},{11,10},{10,9},{9,8},{8,0},{12,13},{13,14... | collective-permute-start | bytes 884744 | tf_op jit(solution)/shard_map/ppermute | solution.py:800
  281.7 8.9 %collective-permute-start.32 = (bf16[48,3072]{1,0:T(8,128)(2,1)S(1)}, bf16[48,3072]{1,0:T(8,128)(2,1)S(1)}, u32[]{:S(2)}, u32[]{:S(2)}) collective-permute-start(bf16[48,3072]{1,0:T(8,128)(2,1)S(1)} %fusion.5), channel_id=1, source_target_pairs={{0,1},{1,2},{2,3},{3,11},{11,10},{10,9},{9,8},{8,0},{12,13},{13,14... | collective-permute-start | bytes 884744 | tf_op jit(solution)/shard_map/ppermute | solution.py:800
  284.3 10.0 %collective-permute-start.31 = (bf16[224,768]{1,0:T(8,128)(2,1)S(1)}, bf16[224,768]{1,0:T(8,128)(2,1)S(1)}, u32[]{:S(2)}, u32[]{:S(2)}) collective-permute-start(bf16[224,768]{1,0:T(8,128)(2,1)S(1)} %collective-permute-done.28), channel_id=1, source_target_pairs={{0,1},{1,2},{2,3},{3,11},{11,10},{10,9},{9,8},{8,0},{12,13},{13,14... | collective-permute-start | bytes 1032200 | tf_op jit(solution)/shard_map/ppermute | solution.py:800
  288.8 8.6 %collective-permute-start.36 = (bf16[48,3072]{1,0:T(8,128)(2,1)S(1)}, bf16[48,3072]{1,0:T(8,128)(2,1)S(1)}, u32[]{:S(2)}, u32[]{:S(2)}) collective-permute-start(bf16[48,3072]{1,0:T(8,128)(2,1)S(1)} %get-tuple-element.427), channel_id=1, source_target_pairs={{0,1},{1,2},{2,3},{3,11},{11,10},{10,9},{9,8},{8,0},{12,13},{13,14... | collective-permute-start | bytes 884744 | tf_op jit(solution)/shard_map/ppermute | solution.py:800
  292.0 8.6 %collective-permute-start.35 = (bf16[48,3072]{1,0:T(8,128)(2,1)S(1)}, bf16[48,3072]{1,0:T(8,128)(2,1)S(1)}, u32[]{:S(2)}, u32[]{:S(2)}) collective-permute-start(bf16[48,3072]{1,0:T(8,128)(2,1)S(1)} %get-tuple-element.429), channel_id=1, source_target_pairs={{0,1},{1,2},{2,3},{3,11},{11,10},{10,9},{9,8},{8,0},{12,13},{13,14... | collective-permute-start | bytes 884744 | tf_op jit(solution)/shard_map/ppermute | solution.py:800
  294.3 10.0 %collective-permute-start.34 = (bf16[224,768]{1,0:T(8,128)(2,1)S(1)}, bf16[224,768]{1,0:T(8,128)(2,1)S(1)}, u32[]{:S(2)}, u32[]{:S(2)}) collective-permute-start(bf16[224,768]{1,0:T(8,128)(2,1)S(1)} %collective-permute-done.31), channel_id=1, source_target_pairs={{0,1},{1,2},{2,3},{3,11},{11,10},{10,9},{9,8},{8,0},{12,13},{13,14... | collective-permute-start | bytes 1032200 | tf_op jit(solution)/shard_map/ppermute | solution.py:800
  297.5 10.0 %collective-permute-start.39 = (bf16[48,3072]{1,0:T(8,128)(2,1)S(1)}, bf16[48,3072]{1,0:T(8,128)(2,1)S(1)}, u32[]{:S(2)}, u32[]{:S(2)}) collective-permute-start(bf16[48,3072]{1,0:T(8,128)(2,1)S(1)} %collective-permute-done.36), channel_id=1, source_target_pairs={{0,1},{1,2},{2,3},{3,11},{11,10},{10,9},{9,8},{8,0},{12,13},{13,14... | collective-permute-start | bytes 884744 | tf_op jit(solution)/shard_map/ppermute | solution.py:800
  300.6 10.0 %collective-permute-start.38 = (bf16[48,3072]{1,0:T(8,128)(2,1)S(1)}, bf16[48,3072]{1,0:T(8,128)(2,1)S(1)}, u32[]{:S(2)}, u32[]{:S(2)}) collective-permute-start(bf16[48,3072]{1,0:T(8,128)(2,1)S(1)} %collective-permute-done.35), channel_id=1, source_target_pairs={{0,1},{1,2},{2,3},{3,11},{11,10},{10,9},{9,8},{8,0},{12,13},{13,14... | collective-permute-start | bytes 884744 | tf_op jit(solution)/shard_map/ppermute | solution.py:800
  304.3 10.0 %collective-permute-start.37 = (bf16[224,768]{1,0:T(8,128)(2,1)S(1)}, bf16[224,768]{1,0:T(8,128)(2,1)S(1)}, u32[]{:S(2)}, u32[]{:S(2)}) collective-permute-start(bf16[224,768]{1,0:T(8,128)(2,1)S(1)} %collective-permute-done.34), channel_id=1, source_target_pairs={{0,1},{1,2},{2,3},{3,11},{11,10},{10,9},{9,8},{8,0},{12,13},{13,14... | collective-permute-start | bytes 1032200 | tf_op jit(solution)/shard_map/ppermute | solution.py:800
  307.5 10.0 %collective-permute-start.42 = (bf16[48,3072]{1,0:T(8,128)(2,1)S(1)}, bf16[48,3072]{1,0:T(8,128)(2,1)S(1)}, u32[]{:S(2)}, u32[]{:S(2)}) collective-permute-start(bf16[48,3072]{1,0:T(8,128)(2,1)S(1)} %collective-permute-done.39), channel_id=1, source_target_pairs={{0,1},{1,2},{2,3},{3,11},{11,10},{10,9},{9,8},{8,0},{12,13},{13,14... | collective-permute-start | bytes 884744 | tf_op jit(solution)/shard_map/ppermute | solution.py:800
  310.6 10.0 %collective-permute-start.41 = (bf16[48,3072]{1,0:T(8,128)(2,1)S(1)}, bf16[48,3072]{1,0:T(8,128)(2,1)S(1)}, u32[]{:S(2)}, u32[]{:S(2)}) collective-permute-start(bf16[48,3072]{1,0:T(8,128)(2,1)S(1)} %collective-permute-done.38), channel_id=1, source_target_pairs={{0,1},{1,2},{2,3},{3,11},{11,10},{10,9},{9,8},{8,0},{12,13},{13,14... | collective-permute-start | bytes 884744 | tf_op jit(solution)/shard_map/ppermute | solution.py:800
  314.3 10.0 %collective-permute-start.40 = (bf16[224,768]{1,0:T(8,128)(2,1)S(1)}, bf16[224,768]{1,0:T(8,128)(2,1)S(1)}, u32[]{:S(2)}, u32[]{:S(2)}) collective-permute-start(bf16[224,768]{1,0:T(8,128)(2,1)S(1)} %collective-permute-done.37), channel_id=1, source_target_pairs={{0,1},{1,2},{2,3},{3,11},{11,10},{10,9},{9,8},{8,0},{12,13},{13,14... | collective-permute-start | bytes 1032200 | tf_op jit(solution)/shard_map/ppermute | solution.py:800
  317.5 10.0 %collective-permute-start.45 = (bf16[48,3072]{1,0:T(8,128)(2,1)S(1)}, bf16[48,3072]{1,0:T(8,128)(2,1)S(1)}, u32[]{:S(2)}, u32[]{:S(2)}) collective-permute-start(bf16[48,3072]{1,0:T(8,128)(2,1)S(1)} %collective-permute-done.42), channel_id=1, source_target_pairs={{0,1},{1,2},{2,3},{3,11},{11,10},{10,9},{9,8},{8,0},{12,13},{13,14... | collective-permute-start | bytes 884744 | tf_op jit(solution)/shard_map/ppermute | solution.py:800
  320.6 10.0 %collective-permute-start.44 = (bf16[48,3072]{1,0:T(8,128)(2,1)S(1)}, bf16[48,3072]{1,0:T(8,128)(2,1)S(1)}, u32[]{:S(2)}, u32[]{:S(2)}) collective-permute-start(bf16[48,3072]{1,0:T(8,128)(2,1)S(1)} %collective-permute-done.41), channel_id=1, source_target_pairs={{0,1},{1,2},{2,3},{3,11},{11,10},{10,9},{9,8},{8,0},{12,13},{13,14... | collective-permute-start | bytes 884744 | tf_op jit(solution)/shard_map/ppermute | solution.py:800
  324.3 10.0 %collective-permute-start.43 = (bf16[224,768]{1,0:T(8,128)(2,1)S(1)}, bf16[224,768]{1,0:T(8,128)(2,1)S(1)}, u32[]{:S(2)}, u32[]{:S(2)}) collective-permute-start(bf16[224,768]{1,0:T(8,128)(2,1)S(1)} %collective-permute-done.40), channel_id=1, source_target_pairs={{0,1},{1,2},{2,3},{3,11},{11,10},{10,9},{9,8},{8,0},{12,13},{13,14... | collective-permute-start | bytes 1032200 | tf_op jit(solution)/shard_map/ppermute | solution.py:800
  327.5 10.0 %collective-permute-start.48 = (bf16[48,3072]{1,0:T(8,128)(2,1)S(1)}, bf16[48,3072]{1,0:T(8,128)(2,1)S(1)}, u32[]{:S(2)}, u32[]{:S(2)}) collective-permute-start(bf16[48,3072]{1,0:T(8,128)(2,1)S(1)} %collective-permute-done.45), channel_id=1, source_target_pairs={{0,1},{1,2},{2,3},{3,11},{11,10},{10,9},{9,8},{8,0},{12,13},{13,14... | collective-permute-start | bytes 884744 | tf_op jit(solution)/shard_map/ppermute | solution.py:800
  330.6 10.0 %collective-permute-start.47 = (bf16[48,3072]{1,0:T(8,128)(2,1)S(1)}, bf16[48,3072]{1,0:T(8,128)(2,1)S(1)}, u32[]{:S(2)}, u32[]{:S(2)}) collective-permute-start(bf16[48,3072]{1,0:T(8,128)(2,1)S(1)} %collective-permute-done.44), channel_id=1, source_target_pairs={{0,1},{1,2},{2,3},{3,11},{11,10},{10,9},{9,8},{8,0},{12,13},{13,14... | collective-permute-start | bytes 884744 | tf_op jit(solution)/shard_map/ppermute | solution.py:800
  334.3 10.0 %collective-permute-start.46 = (bf16[224,768]{1,0:T(8,128)(2,1)S(1)}, bf16[224,768]{1,0:T(8,128)(2,1)S(1)}, u32[]{:S(2)}, u32[]{:S(2)}) collective-permute-start(bf16[224,768]{1,0:T(8,128)(2,1)S(1)} %collective-permute-done.43), channel_id=1, source_target_pairs={{0,1},{1,2},{2,3},{3,11},{11,10},{10,9},{9,8},{8,0},{12,13},{13,14... | collective-permute-start | bytes 1032200 | tf_op jit(solution)/shard_map/ppermute | solution.py:800
  337.5 10.0 %collective-permute-start.51 = (bf16[48,3072]{1,0:T(8,128)(2,1)S(1)}, bf16[48,3072]{1,0:T(8,128)(2,1)S(1)}, u32[]{:S(2)}, u32[]{:S(2)}) collective-permute-start(bf16[48,3072]{1,0:T(8,128)(2,1)S(1)} %collective-permute-done.48), channel_id=1, source_target_pairs={{0,1},{1,2},{2,3},{3,11},{11,10},{10,9},{9,8},{8,0},{12,13},{13,14... | collective-permute-start | bytes 884744 | tf_op jit(solution)/shard_map/ppermute | solution.py:800
  340.6 10.0 %collective-permute-start.50 = (bf16[48,3072]{1,0:T(8,128)(2,1)S(1)}, bf16[48,3072]{1,0:T(8,128)(2,1)S(1)}, u32[]{:S(2)}, u32[]{:S(2)}) collective-permute-start(bf16[48,3072]{1,0:T(8,128)(2,1)S(1)} %collective-permute-done.47), channel_id=1, source_target_pairs={{0,1},{1,2},{2,3},{3,11},{11,10},{10,9},{9,8},{8,0},{12,13},{13,14... | collective-permute-start | bytes 884744 | tf_op jit(solution)/shard_map/ppermute | solution.py:800
  347.5 7.0 %collective-permute-start.53 = (bf16[48,3072]{1,0:T(8,128)(2,1)S(1)}, bf16[48,3072]{1,0:T(8,128)(2,1)S(1)}, u32[]{:S(2)}, u32[]{:S(2)}) collective-permute-start(bf16[48,3072]{1,0:T(8,128)(2,1)S(1)} %collective-permute-done.51), channel_id=1, source_target_pairs={{0,1},{1,2},{2,3},{3,11},{11,10},{10,9},{9,8},{8,0},{12,13},{13,14... | collective-permute-start | bytes 884744 | tf_op jit(solution)/shard_map/ppermute | solution.py:800
  350.6 6.9 %collective-permute-start.52 = (bf16[48,3072]{1,0:T(8,128)(2,1)S(1)}, bf16[48,3072]{1,0:T(8,128)(2,1)S(1)}, u32[]{:S(2)}, u32[]{:S(2)}) collective-permute-start(bf16[48,3072]{1,0:T(8,128)(2,1)S(1)} %collective-permute-done.50), channel_id=1, source_target_pairs={{0,1},{1,2},{2,3},{3,11},{11,10},{10,9},{9,8},{8,0},{12,13},{13,14... | collective-permute-start | bytes 884744 | tf_op jit(solution)/shard_map/ppermute | solution.py:800
  351.0 22.0 %collective-permute-start.49 = (bf16[8,224,768]{2,1,0:T(8,128)(2,1)S(1)}, bf16[8,224,768]{2,1,0:T(8,128)(2,1)S(1)}, u32[]{:S(2)}, u32[]{:S(2)}) collective-permute-start(bf16[8,224,768]{2,1,0:T(8,128)(2,1)S(1)} %bitcast_dynamic-update-slice_fusion.refs_0_), channel_id=1, source_target_pairs={{0,4},{1,5},{2,6},{3,7},{4,0},{5,1},{6,2},{7,3},{8,12},{9,13},{10,... | collective-permute-start | bytes 8257544 | tf_op jit(solution)/shard_map/ppermute | solution.py:938
  354.5 13.6 %collective-permute-start.55 = (bf16[8,48,3072]{2,1,0:T(8,128)(2,1)S(1)}, bf16[8,48,3072]{2,1,0:T(8,128)(2,1)S(1)}, u32[]{:S(2)}, u32[]{:S(2)}) collective-permute-start(bf16[8,48,3072]{2,1,0:T(8,128)(2,1)S(1)} %bitcast_dynamic-update-slice_fusion.8.refs_0_), channel_id=1, source_target_pairs={{0,4},{1,5},{2,6},{3,7},{4,0},{5,1},{6,2},{7,3},{8,12},{9,13},{10,... | collective-permute-start | bytes 7077896 | tf_op jit(solution)/shard_map/ppermute | solution.py:938
  357.6 13.0 %collective-permute-start.54 = (bf16[8,48,3072]{2,1,0:T(8,128)(2,1)S(1)}, bf16[8,48,3072]{2,1,0:T(8,128)(2,1)S(1)}, u32[]{:S(2)}, u32[]{:S(2)}) collective-permute-start(bf16[8,48,3072]{2,1,0:T(8,128)(2,1)S(1)} %bitcast_dynamic-update-slice_fusion.16.refs_0_), channel_id=1, source_target_pairs={{0,4},{1,5},{2,6},{3,7},{4,0},{5,1},{6,2},{7,3},{8,12},{9,13},{10,... | collective-permute-start | bytes 7077896 | tf_op jit(solution)/shard_map/ppermute | solution.py:938
  (25 other events, 118.5 us)
